TPU v7x, 128 devices: a whole 4x4x4 slice. The times are simulated.
128 devices in a mesh: ctx: 16 (over y_lo, x, core), tp: 8 (over y_hi, z).
Axes of the slice: x: 4, y: 4 (y_hi: 2, y_lo: 2; y = y_hi * 2 + y_lo), z: 4, core: 2. Of those that a mesh axis runs over, the one named last changes fastest.
Arguments:
- query_rows: bfloat16 [8192, 7168], P('ctx', 'tp'), may hold values from -32 to 32
- key_rows: bfloat16 [8192, 7168], P('ctx', 'tp'), may hold values from -32 to 32
- value_rows: bfloat16 [8192, 7168], P('ctx', 'tp'), may hold values from -6 to 6
- ssm_inputs: bfloat16 [8192, 7168], P('ctx', 'tp'), may hold values from -6 to 6
- ssm_gate: bfloat16 [8192, 7168], P('ctx', 'tp'), may hold values from -20 to 20
- write_vecs: bfloat16 [8192, 64], P('ctx'), may hold values from -0.75 to 0.75
- read_vecs: bfloat16 [8192, 64], P('ctx'), may hold values from -0.75 to 0.75
- step_raw: float32 [8192, 112], P('ctx', 'tp'), may hold values from -4 to 4
- decay_log: float32 [112], P('tp'), may hold values from -12 to -3
- skip_gain: float32 [112], P('tp'), may hold values from 0.5 to 2.5
- norm_gain: float32 [7168], P('tp'), may hold values from 0.1 to 1.9
Outputs:
- attention_out: bfloat16 [8192, 7168], P('ctx', 'tp')
- mixer_out: bfloat16 [8192, 7168], P('ctx', 'tp')
All inputs are finite; a program needn't handle non-finite values.
Results may differ from a plain program's by a relative error of at most 0.014.
Values may be sent and summed in bfloat16 or wider, within the bound.
No kernel may reach another device: no remote copies, remote signals or barrier semaphores. Data moves between devices by JAX's collectives and lax.ppermute only.
A program may use at most 256 MiB of HBM per device.

v0:
```python
import jax
import jax.numpy as jnp
from jax import lax
from jax.sharding import PartitionSpec as P

ATT_DIM = 224
SSM_DIM = 64
STATE_DIM = 64
BLOCK_LEN = 256
SSM_WIDTH = 7168


def carried_in(shard, axis, combine, identity):
    count, mine = (lax.axis_size(axis), lax.axis_index(axis))
    everything = jax.tree.map(
        lambda part, kind: lax.all_gather(part.astype(kind), axis),
        shard,
        (jnp.bfloat16, jnp.bfloat16),
    )
    start = jax.tree.map(
        lambda part, zero: jnp.broadcast_to(jnp.asarray(zero, part.dtype), part.shape),
        shard,
        identity,
    )

    def lap(k, before):
        reached = k < mine
        new = combine(
            before, jax.tree.map(lambda part, own: part[k].astype(own.dtype), everything, shard)
        )
        return jax.tree.map(lambda a, b: jnp.where(reached, a, b), new, before)

    return lax.fori_loop(0, count, lap, start)


def block_pass(state, block):
    inputs, write_low, read_low, step, log_decay = block
    high = lax.Precision.HIGHEST
    write_f = write_low.astype(jnp.float32)
    read_f = read_low.astype(jnp.float32)
    length = inputs.shape[0]
    cumul = jnp.cumsum(log_decay, axis=0).T
    lower = jnp.tril(jnp.ones((length, length), dtype=bool))[None, :, :]
    spread = cumul[:, :, None] - cumul[:, None, :]
    decay = jnp.where(lower, jnp.exp(jnp.where(lower, spread, 0.0)), 0.0)
    intersection = jnp.dot(read_low, write_low.T, preferred_element_type=jnp.float32)
    weights = decay * intersection[None, :, :] * step.T[:, None, :]
    inner = jnp.einsum("hts,shp->thp", weights, inputs, precision=high)
    carried = (
        jnp.einsum("tn,hpn->thp", read_f, state, precision=high) * jnp.exp(cumul).T[:, :, None]
    )
    last = cumul[:, -1]
    tail = jnp.exp(last[:, None] - cumul).T * step
    weighted = inputs * tail[:, :, None]
    new_state = jnp.exp(last)[:, None, None] * state + jnp.einsum(
        "shp,sn->hpn", weighted, write_f, precision=high
    )
    return (new_state, inner + carried)


def attention_part(query_rows, key_rows, value_rows):
    tokens = query_rows.shape[0]
    heads = query_rows.shape[1] // ATT_DIM
    scale = ATT_DIM ** (-0.5)
    query_heads = query_rows.reshape(tokens, heads, ATT_DIM).transpose(1, 0, 2)
    first_row = lax.axis_index("ctx") * tokens
    query_pos = first_row + jnp.arange(tokens, dtype=jnp.int32)
    run_max = jnp.full((heads, tokens), -1e30, jnp.float32)
    key_piece = lax.all_gather(key_rows, "ctx", axis=0, tiled=True)
    value_piece = lax.all_gather(value_rows, "ctx", axis=0, tiled=True)
    count = key_piece.shape[0]
    key_heads = key_piece.reshape(count, heads, ATT_DIM)
    value_heads = value_piece.reshape(count, heads, ATT_DIM)
    scores = (
        jnp.einsum("hqd,khd->hqk", query_heads, key_heads, preferred_element_type=jnp.float32)
        * scale
    )
    key_pos = jnp.arange(count, dtype=jnp.int32)
    visible = (key_pos[None, :] <= query_pos[:, None])[None]
    scores = jnp.where(visible, scores, -1e30)
    new_max = jnp.maximum(run_max, jnp.max(scores, axis=2))
    weights = jnp.where(visible, jnp.exp(scores - new_max[:, :, None]), 0.0)
    new_sum = jnp.sum(weights, axis=2)
    mixed = jnp.einsum(
        "hqk,khd->hqd",
        weights.astype(jnp.bfloat16),
        value_heads,
        preferred_element_type=jnp.float32,
    )
    result = (mixed / new_sum[:, :, None]).astype(jnp.bfloat16)
    return result.transpose(1, 0, 2).reshape(tokens, heads * ATT_DIM)


def mixer_part(
    ssm_inputs, ssm_gate, write_vecs, read_vecs, step_raw, decay_log, skip_gain, norm_gain
):
    tokens = ssm_inputs.shape[0]
    heads = decay_log.shape[0]
    inputs = ssm_inputs.astype(jnp.float32).reshape(tokens, heads, SSM_DIM)
    read_f = read_vecs.astype(jnp.float32)
    step = jax.nn.softplus(step_raw)
    log_decay = -jnp.exp(decay_log)[None, :] * step
    blocks = tokens // BLOCK_LEN

    def split(array):
        return array.reshape((blocks, BLOCK_LEN) + array.shape[1:])

    zero_state = jnp.zeros((heads, SSM_DIM, STATE_DIM), jnp.float32)
    end_state, outputs = lax.scan(
        block_pass,
        zero_state,
        (split(inputs), split(write_vecs), split(read_vecs), split(step), split(log_decay)),
    )
    outputs = outputs.reshape(tokens, heads, SSM_DIM)
    total_decay = jnp.exp(jnp.sum(log_decay, axis=0))

    def combine(earlier, later):
        return (earlier[0] * later[0], later[0][:, None, None] * earlier[1] + later[1])

    identity_pair = (jnp.ones((heads,), jnp.float32), jnp.zeros_like(end_state))
    carried = carried_in((total_decay, end_state), "ctx", combine, identity_pair)
    incoming = carried[1]
    reach = jnp.exp(jnp.cumsum(log_decay, axis=0))
    outputs = (
        outputs
        + jnp.einsum("tn,hpn->thp", read_f, incoming, precision=lax.Precision.HIGHEST)
        * reach[:, :, None]
    )
    mixed = outputs + skip_gain[None, :, None] * inputs
    gated = mixed.reshape(tokens, heads * SSM_DIM) * jax.nn.silu(ssm_gate.astype(jnp.float32))
    local_squares = jnp.sum(gated * gated, axis=1)
    all_squares = lax.psum(local_squares, "tp")
    scaled = gated * lax.rsqrt(all_squares / SSM_WIDTH + 1e-05)[:, None] * norm_gain[None, :]
    return scaled.astype(jnp.bfloat16)


def on_device(
    query_rows,
    key_rows,
    value_rows,
    ssm_inputs,
    ssm_gate,
    write_vecs,
    read_vecs,
    step_raw,
    decay_log,
    skip_gain,
    norm_gain,
):
    attention_out = attention_part(query_rows, key_rows, value_rows)
    mixer_out = mixer_part(
        ssm_inputs, ssm_gate, write_vecs, read_vecs, step_raw, decay_log, skip_gain, norm_gain
    )
    return (attention_out, mixer_out)


def solution(mesh):
    placed = (
        P("ctx", "tp"),
        P("ctx", "tp"),
        P("ctx", "tp"),
        P("ctx", "tp"),
        P("ctx", "tp"),
        P("ctx", None),
        P("ctx", None),
        P("ctx", "tp"),
        P("tp"),
        P("tp"),
        P("tp"),
    )
    return jax.shard_map(
        on_device,
        mesh=mesh,
        in_specs=placed,
        out_specs=(P("ctx", "tp"), P("ctx", "tp")),
        check_vma=False,
    )
```

profile of v0, /device:TPU:0, one launch (start us, length us, event | category | flops | bytes accessed | tf_op | source)
XLA Modules:
  0.0 345.2 jit_solution(4709139733660394722)
XLA Ops:
  7.2 0.7 exponential_negate_fusion
  7.9 0.9 fusion.63
  8.9 0.6 copy-done.3
  9.4 4.1 %reshape.184 = f32[2,256,14,64]{3,2,1,0:T(8,128)} reshape(bf16[512,896]{1,0:T(8,128)(2,1)} %param.18) | data formatting | bytes 2752512 | tf_op jit(solution)/shard_map/reshape;reshape | solution.py:106
  13.5 3.3 copy.66
  16.9 0.6 reshape.160
  17.5 0.7 copy_bitcast_fusion.3
  18.1 60.8 %while.27 = (s32[]{:T(128)}, f32[14,64,64]{2,1,0:T(8,128)S(1)}, f32[2,256,14,64]{1,0,3,2:T(2,128)}, f32[2,256,14]{1,0,2:T(2,128)S(1)}, f32[2,256,14,64]{1,3,2,0:...) while((s32[]{:T(128)}, f32[14,64,64]{2,1,0:T(8,128)S(1)}, ...), condition=%wide.region_5.6_spmd.clone, body=%wide.region_2.5_spmd.clone.sunk | while | flops 1071389760 | bytes 10438907 | solution.py:109
  18.1 0.8 constant_dynamic-slice_fusion.3
  18.9 1.0 fusion.90
  20.0 0.6 reduce-window.26
  20.9 4.3 %fusion.91 = f32[256,14,64]{0,2,1:T(8,128)S(1)} fusion(f32[14,256]{1,0:T(8,128)S(1)} %bitcast.140, f32[256,256]{1,0:T(8,128)S(1)} %fusion.90, f32[14,256]{1,0:T(8,128)S(1)} %bitcast.132, pred[256,256]{1,0:T(8,128)(4,1)S(1)} %iota_compare_fusion.3, f32[2,256,14,64]{1,3,2,0:T(8,128)S(1)} %get-tuple-element.364, s32[]{:T(128)S(6)} %copy.118), kind=kOutput, calls=%fused_computation.16.clone.1 | convolution fusion | flops 709230592 | bytes 2211844 | tf_op jit(solution)/shard_map/while/body/eval_jaxpr/hts,shp->thp/dot_general | solution.py:48
  25.3 1.3 fusion.92
  26.8 1.5 convolution_add_fusion.2
  28.3 0.9 copy.113
  29.2 19.3 %dynamic_update_slice.6 = f32[2,256,14,64]{1,0,3,2:T(2,128)} dynamic-update-slice(f32[2,256,14,64]{1,0,3,2:T(2,128)} %get-tuple-element.351, f32[1,256,14,64]{1,0,3,2:T(1,128)S(1)} %copy.113, s32[]{:T(128)S(6)} %copy.118, s32[]{:T(128)} %constant.75.clone.1..sunk, s32[]{:T(128)} %constant.75.clone.1..sunk, s32[]{:T(128)} %constant.75.clone.1..sunk) | dynamic-update-slice | bytes 1835012 | tf_op jit(solution)/shard_map/while/body/jit(dynamic_update_index_in_dim)/dynamic_update_slice | solution.py:109
  48.5 0.8 constant_dynamic-slice_fusion.3
  49.3 1.0 fusion.90
  50.4 0.6 reduce-window.26
  51.3 4.3 %fusion.91 = f32[256,14,64]{0,2,1:T(8,128)S(1)} fusion(f32[14,256]{1,0:T(8,128)S(1)} %bitcast.140, f32[256,256]{1,0:T(8,128)S(1)} %fusion.90, f32[14,256]{1,0:T(8,128)S(1)} %bitcast.132, pred[256,256]{1,0:T(8,128)(4,1)S(1)} %iota_compare_fusion.3, f32[2,256,14,64]{1,3,2,0:T(8,128)S(1)} %get-tuple-element.364, s32[]{:T(128)S(6)} %copy.118), kind=kOutput, calls=%fused_computation.16.clone.1 | convolution fusion | flops 709230592 | bytes 2211844 | tf_op jit(solution)/shard_map/while/body/eval_jaxpr/hts,shp->thp/dot_general | solution.py:48
  55.6 1.3 fusion.92
  57.2 1.5 convolution_add_fusion.2
  58.7 0.9 copy.113
  59.6 19.3 %dynamic_update_slice.6 = f32[2,256,14,64]{1,0,3,2:T(2,128)} dynamic-update-slice(f32[2,256,14,64]{1,0,3,2:T(2,128)} %get-tuple-element.351, f32[1,256,14,64]{1,0,3,2:T(1,128)S(1)} %copy.113, s32[]{:T(128)S(6)} %copy.118, s32[]{:T(128)} %constant.75.clone.1..sunk, s32[]{:T(128)} %constant.75.clone.1..sunk, s32[]{:T(128)} %constant.75.clone.1..sunk) | dynamic-update-slice | bytes 1835012 | tf_op jit(solution)/shard_map/while/body/jit(dynamic_update_index_in_dim)/dynamic_update_slice | solution.py:109
  78.9 0.7 convert_element_type.64
  79.7 0.7 all-gather.6.cloned.1.call-update
  80.5 0.7 all-gather.8.cloned.1.call-update
  81.2 2.5 copy.73
  83.7 1.3 copy.61
  85.0 2.7 reshape.163
  87.8 0.6 dynamic-slice
  89.3 31.2 %all-reduce = bf16[224]{0:T(256)(128)(2,1)S(1)} all-reduce(bf16[224]{0:T(256)(128)(2,1)S(1)} %dynamic-update-slice), channel_id=2, replica_groups=mesh['ctx'=16,'tp'=8] {'ctx'}, use_global_device_ids=true, to_apply=%add | all-reduce | flops 224 | bytes 896
  120.6 1.2 reduce-window.16
  122.2 5.2 %iota_compare_fusion.1 = pred[512,8192]{1,0:T(8,128)(4,1)} fusion(s32[512]{0:T(512)S(1)} %iota_add_fusion), kind=kLoop, calls=%fused_computation.63 | loop fusion | flops 4194304 | bytes 4196352 | tf_op jit(solution)/shard_map/le | solution.py:79
  127.4 18.0 %while.28 = (s32[]{:T(128)}, f32[14,64,64]{2,1,0:T(8,128)S(1)}, s32[]{:T(128)}, bf16[16,14]{1,0:T(8,128)(2,1)S(1)}, bf16[16,14,64,64]{3,2,1,0:T(8,128)(2,1)}, /*index=5*/s32[]{:T(128)}, s32[]{:T(128)}) while((s32[]{:T(128)}, f32[14,64,64]{2,1,0:T(8,128)S(1)}, s32[]{:T(128)}, bf16[16,14]{1,0:T(8,128)(2,1)S(1)}, ...), condition=%wide.region_8.9_spmd.clone, body=%wide.region_7.8_spmd.clone.sunk | while | flops 286738 | bytes 573693 | solution.py:33
  127.4 1.1 fusion.93
  128.6 1.1 fusion.93
  129.7 1.1 fusion.93
  130.8 1.1 fusion.93
  132.0 1.1 fusion.93
  133.1 1.1 fusion.93
  134.2 1.1 fusion.93
  135.3 1.1 fusion.93
  136.4 1.1 fusion.93
  137.6 1.1 fusion.93
  138.7 1.1 fusion.93
  139.8 1.2 fusion.93
  141.0 1.1 fusion.93
  142.1 1.1 fusion.93
  143.2 1.1 fusion.93
  144.4 1.1 fusion.93
  145.5 3.8 %fusion.55 = f32[512,14,64]{0,2,1:T(8,128)} fusion(f32[512,14,64]{0,2,1:T(8,128)S(1)} %reshape.163, f32[512,14,64]{0,2,1:T(8,128)} %bitcast.131, f32[14,64,64]{2,1,0:T(8,128)S(1)} %get-tuple-element.141, f32[14]{0:T(128)S(1)} %copy-done.9, f32[512,14]{0,1:T(8,128)S(1)} %bitcast.144, bf16[512,64]{0,1:T(8,128)(2,1)S(1)} %copy-done.6), kind=kOutput, calls=%fused_computation.72 | convolution fusion | flops 354156544 | bytes 5828664 | tf_op jit(solution)/shard_map/tn,hpn->thp/dot_general | solution.py:126
  149.3 1.9 copy.74
  151.2 0.7 multiply_reduce_fusion
  151.9 25.5 %psum.7 = f32[512]{0:T(512)S(1)} all-reduce(f32[512]{0:T(512)S(1)} %multiply_reduce_fusion), channel_id=1, replica_groups=mesh['ctx'=16,'tp'=8] {'tp'}, use_global_device_ids=true, to_apply=%region_12.13 | all-reduce | flops 512 | bytes 4096 | tf_op jit(solution)/shard_map/psum | solution.py:132
  177.5 1.6 multiply_convert_fusion
  179.0 23.7 %all-gather.6.cloned.1.call-done = bf16[8192,896]{1,0:T(8,128)(2,1)} async-done(((bf16[512,896]{1,0:T(8,128)(2,1)}), bf16[8192,896]{1,0:T(8,128)(2,1)}) %all-gather.6.cloned.1.call-update) | async-done | bytes 14680080 | tf_op jit(solution)/shard_map/all_gather | solution.py:69
  202.7 19.5 %copy.62 = bf16[8192,896]{0,1:T(8,128)(2,1)} copy(bf16[8192,896]{1,0:T(8,128)(2,1)} %all-gather.6.cloned.1.call-done) | data formatting | bytes 29360128 | tf_op jit(solution)/shard_map/all_gather | solution.py:69
  222.2 34.0 %fusion.44 = (f32[4,512]{1,0:T(4,128)S(1)}, f32[4,512,8192]{2,1,0:T(8,128)}) fusion(pred[512,8192]{1,0:T(8,128)(4,1)} %iota_compare_fusion.1, bf16[4,512,224]{1,2,0:T(8,128)(2,1)S(1)} %bitcast.138, bf16[8192,4,224]{0,2,1:T(8,128)(2,1)} %bitcast.129), kind=kOutput, calls=%fused_computation.58 | convolution fusion | flops 7566522368 | bytes 86908928 | tf_op jit(solution)/shard_map/hqd,khd->hqk/dot_general | solution.py:75
  256.2 24.1 %fusion.45 = f32[4,512]{1,0:T(4,128)S(1)} fusion(f32[4,512,8192]{2,1,0:T(8,128)} %get-tuple-element.251, f32[4,512]{1,0:T(4,128)S(1)} %broadcast_maximum_fusion, pred[512,8192]{1,0:T(8,128)(4,1)} %iota_compare_fusion.1), kind=kLoop, calls=%fused_computation.59 | loop fusion | flops 83884032 | bytes 71319552 | tf_op jit(solution)/shard_map/reduce_sum | solution.py:83
  280.4 6.3 %all-gather.8.cloned.1.call-done = bf16[8192,896]{1,0:T(8,128)(2,1)} async-done(((bf16[512,896]{1,0:T(8,128)(2,1)}), bf16[8192,896]{1,0:T(8,128)(2,1)}) %all-gather.8.cloned.1.call-update) | async-done | bytes 14680080 | tf_op jit(solution)/shard_map/all_gather | solution.py:70
  286.7 19.5 %copy.63 = bf16[8192,896]{0,1:T(8,128)(2,1)} copy(bf16[8192,896]{1,0:T(8,128)(2,1)} %all-gather.8.cloned.1.call-done) | data formatting | bytes 29360128 | tf_op jit(solution)/shard_map/all_gather | solution.py:70
  306.2 31.2 %fusion.56 = bf16[512,4,224]{0,2,1:T(8,128)(2,1)S(1)} fusion(bf16[8192,4,224]{0,2,1:T(8,128)(2,1)} %bitcast.128, f32[4,512,8192]{2,1,0:T(8,128)} %get-tuple-element.251, f32[4,512]{1,0:T(4,128)S(1)} %broadcast_maximum_fusion, pred[512,8192]{1,0:T(8,128)(4,1)} %iota_compare_fusion.1, f32[512,4]{0,1:T(4,128)S(1)} %bitcast.147), kind=kOutput, calls=%fused_computation.74 | convolution fusion | flops 7600996352 | bytes 86917120 | tf_op jit(solution)/shard_map/hqk,khd->hqd/dot_general | solution.py:84
  337.4 1.3 copy.75
  (94 shorter events, 2.3 us)
Async XLA Ops:
  7.2 120.2 %all-gather.10.cloned.1.call-start = ((), (), s32[]{:S(2)}) async-start(), calls=%async_computation.2 | async-start | bytes 3899392 | tf_op jit(solution)/shard_map/all_gather | solution.py:16
  8.8 0.6 copy-start.3
  13.5 3.9 %copy-start.5 = (bf16[512,64]{0,1:T(8,128)(2,1)S(1)}, bf16[512,64]{0,1:T(8,128)(2,1)}, u32[]{:S(2)}) copy-start(bf16[512,64]{0,1:T(8,128)(2,1)} %param.21) | copy-start | bytes 196612
  13.5 3.9 %copy-start.7 = (bf16[512,64]{0,1:T(8,128)(2,1)S(1)}, bf16[512,64]{0,1:T(8,128)(2,1)}, u32[]{:S(2)}) copy-start(bf16[512,64]{0,1:T(8,128)(2,1)} %param.20) | copy-start | bytes 196612
  78.9 4.8 %copy-start.1 = (bf16[512,896]{1,0:T(8,128)(2,1)S(1)}, bf16[512,896]{1,0:T(8,128)(2,1)}, u32[]{:S(2)}) copy-start(bf16[512,896]{1,0:T(8,128)(2,1)} %param.15) | copy-start | bytes 2752516
  79.7 123.0 %all-gather.6.cloned.1.call-start = ((), (), s32[]{:S(2)}) async-start(), calls=%async_computation | async-start | bytes 15597568 | tf_op jit(solution)/shard_map/all_gather | solution.py:69
  80.4 206.3 %all-gather.8.cloned.1.call-start = ((), (), s32[]{:S(2)}) async-start(), calls=%async_computation.1 | async-start | bytes 15597568 | tf_op jit(solution)/shard_map/all_gather | solution.py:70
  81.2 6.6 %copy-start.10 = (u32[128]{0:T(128)S(1)}, u32[128]{0:T(128)}, u32[]{:S(2)}) copy-start(u32[128]{0:T(128)} %constant.84) | copy-start | bytes 1540
  81.2 39.4 %copy-start.4 = (f32[512,14]{0,1:T(8,128)S(1)}, f32[512,14]{0,1:T(8,128)}, u32[]{:S(2)}) copy-start(f32[512,14]{0,1:T(8,128)} %copy-done.3) | copy-start | bytes 86020
  127.4 18.0 %copy-start.6 = (bf16[512,64]{0,1:T(8,128)(2,1)S(1)}, bf16[512,64]{0,1:T(8,128)(2,1)}, u32[]{:S(2)}) copy-start(bf16[512,64]{0,1:T(8,128)(2,1)} %param.21) | copy-start | bytes 196612
  127.4 18.1 %copy-start.9 = (f32[14]{0:T(128)S(1)}, f32[14]{0:T(128)}, u32[]{:S(2)}) copy-start(f32[14]{0:T(128)} %param.24) | copy-start | bytes 172
  145.5 5.8 %copy-start = (bf16[512,896]{1,0:T(8,128)(2,1)S(1)}, bf16[512,896]{1,0:T(8,128)(2,1)}, u32[]{:S(2)}) copy-start(bf16[512,896]{1,0:T(8,128)(2,1)} %param.19) | copy-start | bytes 2752516
  149.3 28.1 %copy-start.8 = (f32[896]{0:T(1024)S(1)}, f32[896]{0:T(1024)}, u32[]{:S(2)}) copy-start(f32[896]{0:T(1024)} %param.25) | copy-start | bytes 10756
  179.0 43.2 %copy-start.2 = (bf16[512,896]{0,1:T(8,128)(2,1)S(1)}, bf16[512,896]{0,1:T(8,128)(2,1)}, u32[]{:S(2)}) copy-start(bf16[512,896]{0,1:T(8,128)(2,1)} %copy.61) | copy-start | bytes 2752516
Sparse Core Ops, SparseCore 0:
  79.8 39.0 all-gather.9
  120.6 82.0 all-gather.5
  204.4 82.2 all-gather.7
where the time goes:
time: 351 us; the launch traced here: 345 us
  local copies, waits for them, and re-layouts  102 us (29%)
  matrix products  85.2 us (24%)
  blocking collectives  56.7 us (16%)
  other arithmetic  54.3 us (15%)
  waiting for transfers between devices  31.4 us (9%)
  between operations  14.6 us (4%)
    dynamic_update_slice x4, local copies, waits for them, and re-layouts, mixer_part(): lax.scan(block_pass, zero_state, (split(inputs), split(write_vecs), split...  40.5 us
    dot_general x1, matrix products, attention_part(): jnp.einsum('hqd,khd->hqk', query_heads, key_heads, preferred_element_type...  34 us
    dot_general x1, matrix products, attention_part(): jnp.einsum('hqk,khd->hqd', weights.astype(jnp.bfloat16), value_heads, pre...  31.2 us
    unnamed x1, blocking collectives  31.2 us
    psum x1, blocking collectives, mixer_part(): all_squares = lax.psum(local_squares, 'tp')  25.5 us
    reduce_sum x1, other arithmetic, attention_part(): new_sum = jnp.sum(weights, axis=2)  24.1 us
    all_gather x1, waiting for transfers between devices, attention_part(): key_piece = lax.all_gather(key_rows, 'ctx', axis=0, tiled=True)  23.7 us
    all_gather x1, local copies, waits for them, and re-layouts, attention_part(): key_piece = lax.all_gather(key_rows, 'ctx', axis=0, tiled=True)  19.5 us
  transfers between devices with their start and end apart: 3, of which 2 were waited for; matrix products, arithmetic and copies ran while one was open for 34% of the time, Pallas kernels for 0%

commit v1 on v0

v1 whole, which is shorter than its diff:
```python
import math

import jax
import jax.numpy as jnp
from jax import lax
from jax.experimental import pallas as pl
from jax.experimental.pallas import tpu as pltpu
from jax.sharding import PartitionSpec as P

ATT_DIM = 224
SSM_DIM = 64
STATE_DIM = 64
SSM_WIDTH = 7168
TOK = 512
HEADS = 4
CTX = 16
HALF = 256
LOG2E = math.log2(math.e)
F32 = jnp.float32
BF16 = jnp.bfloat16


def exchanged(i, r):
    y, x, c = i >> 3, (i >> 1) & 3, i & 1
    if r & 1:
        x = 3 - x
    if r & 2:
        y = 1 - y
    return y * 8 + x * 2 + c


def head_swap(value, r):
    return lax.ppermute(value, "ctx", [(i, exchanged(i, r)) for i in range(CTX)])


def class_swap(value):
    return lax.ppermute(value, "ctx", [(i, i ^ 2) for i in range(CTX)])


def core_swap(value):
    return lax.ppermute(value, "ctx", [(i, i ^ 1) for i in range(CTX)])


def head_rows(head):
    return pl.ds(pl.multiple_of(head * ATT_DIM, 16), ATT_DIM)


def pack_kernel(info, q_ref, k_ref, v_ref, *refs):
    q_out, kv_out, (qs, ks, vs) = refs[:4], refs[4:8], refs[8:]
    qs[...] = q_ref[...].T
    ks[...] = k_ref[...].T
    vs[...] = v_ref[...].T
    for r in range(4):
        rows = head_rows(info[0] ^ r)
        q_out[r][...] = qs[rows, :]
        kv_out[r][0:ATT_DIM, :] = ks[rows, :]
        kv_out[r][ATT_DIM : 2 * ATT_DIM, :] = vs[rows, :]


def unpack_kernel(info, *refs):
    pieces, out_ref, rows_ref = refs[:4], refs[4], refs[5]
    for r in range(4):
        rows_ref[head_rows(info[0] ^ r), :] = pieces[r][...]
    out_ref[...] = rows_ref[...].T


def token_block(chip, kind, core):
    return (chip >> 1) * 8 + (kind + (chip & 1) * (3 - 2 * kind)) * 2 + core


def attend_kernel(info, *refs):
    q_in, kv_in, o_out = refs[:4], refs[4:20], refs[20:24]
    qs, ks, vs, os, acc = refs[24:]
    hid, kind, core = info[0], info[1], info[2]
    scale = ATT_DIM ** (-0.5) * LOG2E

    for cl in range(2):
        for co in range(2):
            for r in range(4):
                piece = kv_in[(cl * 2 + co) * 4 + r]
                block = token_block(hid ^ r, kind ^ cl, core ^ co)
                ks[pl.ds(pl.multiple_of(block * TOK, TOK), TOK), :] = piece[0:ATT_DIM, :].T
                lanes = pl.ds(pl.multiple_of((block & 1) * TOK, TOK), TOK)
                vs[block >> 1, :, lanes] = piece[ATT_DIM : 2 * ATT_DIM, :]
    for r in range(4):
        qs[r] = q_in[r][...]

    def one_queries(r, carry):
        block = token_block(hid ^ r, kind, core)
        acc[...] = jnp.zeros_like(acc)

        def visit(keys, values, stats, masked):
            new_stats = []
            for half in range(2):
                top, total = stats[half]
                lanes = slice(half * HALF, (half + 1) * HALF)
                s = jnp.dot(keys, qs[r, :, lanes], preferred_element_type=F32)
                if masked:
                    k_pos = lax.broadcasted_iota(jnp.int32, s.shape, 0)
                    q_pos = lax.broadcasted_iota(jnp.int32, s.shape, 1) + half * HALF
                    s = jnp.where(k_pos <= q_pos, s, -1e30)
                new_top = jnp.maximum(top, jnp.max(s, axis=0, keepdims=True))
                p = jnp.exp2((s - new_top) * scale)
                shrink = jnp.exp2((top - new_top) * scale)
                total = total * shrink + jnp.sum(p, axis=0, keepdims=True)
                acc[:, lanes] = acc[:, lanes] * shrink + jnp.dot(
                    values, p.astype(BF16), preferred_element_type=F32
                )
                new_stats.append((new_top, total))
            return tuple(new_stats)

        def chip_block(j, stats):
            rows = pl.ds(pl.multiple_of(j * 2 * TOK, 2 * TOK), 2 * TOK)
            return visit(ks[rows, :], vs[j], stats, False)

        def core_block(j, stats, masked):
            rows = pl.ds(pl.multiple_of(j * TOK, TOK), TOK)
            lanes = pl.ds(pl.multiple_of((j & 1) * TOK, TOK), TOK)
            return visit(ks[rows, :], vs[j >> 1, :, lanes], stats, masked)

        first = (jnp.full((1, HALF), -1e30, F32), jnp.zeros((1, HALF), F32))
        stats = lax.fori_loop(0, block >> 1, chip_block, (first, first))
        stats = lax.fori_loop(
            0, block & 1, lambda k, now: core_block(block - 1, now, False), stats
        )
        stats = core_block(block, stats, True)
        for half in range(2):
            lanes = slice(half * HALF, (half + 1) * HALF)
            os[r, :, lanes] = (acc[:, lanes] / stats[half][1]).astype(BF16)
        return carry

    lax.fori_loop(0, 4, one_queries, 0)
    for r in range(4):
        o_out[r][...] = os[r]


def pair_of(low, columns, h):
    return jnp.where(low, columns[:, h : h + 1], columns[:, h + 1 : h + 2])


def softplus(v):
    return jnp.maximum(v, 0.0) + jnp.log1p(jnp.exp(-jnp.abs(v)))


PAYLOAD = 80


def ssm_local_kernel(
    x_ref, write_ref, read_ref, step_ref, step_t_ref, rate_ref, rate_t_ref, gain_ref, out_ref, pay_ref, cum_ref
):
    heads = step_ref.shape[1]
    high = lax.Precision.HIGHEST
    row = lax.broadcasted_iota(jnp.int32, (TOK, TOK), 0)
    col = lax.broadcasted_iota(jnp.int32, (TOK, TOK), 1)
    step = softplus(step_ref[...])
    decay = -jnp.exp(rate_ref[...]) * step * LOG2E
    cum = jnp.dot(jnp.where(col <= row, 1.0, 0.0), decay, precision=high, preferred_element_type=F32)
    step_t = softplus(step_t_ref[...])
    decay_t = -jnp.exp(rate_t_ref[...]) * step_t * LOG2E
    cum_t = jnp.dot(decay_t, jnp.where(row <= col, 1.0, 0.0), precision=high, preferred_element_type=F32)
    key_row = jnp.log2(step_t) - cum_t
    cum_ref[...] = cum
    last = cum[TOK - 1 : TOK, :]
    tail = jnp.exp2(last - cum) * step

    near = lax.dot_general(
        read_ref[...], write_ref[...], (((1,), (1,)), ((), ())), preferred_element_type=F32
    )
    near = jnp.where(col <= row, near, 0.0)
    low = lax.broadcasted_iota(jnp.int32, (1, 128), 1) < SSM_DIM
    for h in range(0, heads, 2):
        lanes = slice(h * SSM_DIM, (h + 2) * SSM_DIM)
        x_pair = x_ref[:, lanes]
        x_f = x_pair.astype(F32)
        weighted = (x_f * pair_of(low, tail, h)).astype(BF16)
        pay_ref[0:STATE_DIM, lanes] = lax.dot_general(
            write_ref[...], weighted, (((0,), (0,)), ((), ())), preferred_element_type=F32
        ).astype(BF16)
        span = pair_of(low, last, h)
        span_high = span.astype(BF16)
        span_low = (span - span_high.astype(F32)).astype(BF16)
        pay_ref[STATE_DIM : STATE_DIM + 8, lanes] = jnp.broadcast_to(span_high, (8, 128))
        pay_ref[STATE_DIM + 8 : PAYLOAD, lanes] = jnp.broadcast_to(span_low, (8, 128))
        for t in range(2):
            t_rows = slice(t * HALF, (t + 1) * HALF)
            both = []
            for k in range(2):
                total = None
                for s in range(t + 1):
                    s_rows = slice(s * HALF, (s + 1) * HALF)
                    weights = (
                        jnp.exp2(cum[t_rows, h + k : h + k + 1] + key_row[h + k : h + k + 1, s_rows])
                        * near[t_rows, s_rows]
                    )
                    part = jnp.dot(weights.astype(BF16), x_pair[s_rows, :], preferred_element_type=F32)
                    total = part if total is None else total + part
                both.append(total)
            out_ref[t_rows, lanes] = (
                jnp.where(low, both[0], both[1]) + gain_ref[:, lanes] * x_f[t_rows, :]
            )


def ssm_carry_kernel(info, pay_ref, mixed_ref, cum_ref, read_ref, gate_ref, gated_ref, square_ref):
    heads = cum_ref.shape[1]

    def lap(k, state):
        block = pay_ref[k]
        span = (block[STATE_DIM : STATE_DIM + 8, :].astype(F32) + block[STATE_DIM + 8 : PAYLOAD, :].astype(F32))[0:1, :]
        return state * jnp.exp2(span) + block[0:STATE_DIM, :].astype(F32)

    state = lax.fori_loop(0, info[3], lap, jnp.zeros((STATE_DIM, heads * SSM_DIM), F32))
    state_high = state.astype(BF16)
    state_low = (state - state_high.astype(F32)).astype(BF16)
    reach = jnp.exp2(cum_ref[...])
    low = lax.broadcasted_iota(jnp.int32, (1, 128), 1) < SSM_DIM
    squares = jnp.zeros((TOK, 128), F32)
    for h in range(0, heads, 2):
        lanes = slice(h * SSM_DIM, (h + 2) * SSM_DIM)
        carried = jnp.dot(read_ref[...], state_high[:, lanes], preferred_element_type=F32) + jnp.dot(
            read_ref[...], state_low[:, lanes], preferred_element_type=F32
        )
        mixed = mixed_ref[:, lanes] + carried * pair_of(low, reach, h)
        gate = gate_ref[:, lanes].astype(F32)
        gated = mixed * (gate / (1.0 + jnp.exp(-gate)))
        gated_ref[:, lanes] = gated
        squares = squares + gated * gated
    square_ref[...] = jnp.sum(squares, axis=1, keepdims=True)


def vmem(count):
    return [pl.BlockSpec(memory_space=pltpu.VMEM)] * count


SMEM = pl.BlockSpec(memory_space=pltpu.SMEM)


def params(mib):
    return pltpu.CompilerParams(vmem_limit_bytes=mib * 1024 * 1024)


def shape(dims, kind):
    return jax.ShapeDtypeStruct(dims, kind)


def attention_part(info, query_rows, key_rows, value_rows):
    width = HEADS * ATT_DIM
    packed = pl.pallas_call(
        pack_kernel,
        out_shape=[shape((ATT_DIM, TOK), BF16)] * 4 + [shape((2 * ATT_DIM, TOK), BF16)] * 4,
        in_specs=[SMEM] + vmem(3),
        out_specs=vmem(8),
        scratch_shapes=[pltpu.VMEM((width, TOK), BF16)] * 3,
        compiler_params=params(40),
    )(info, query_rows, key_rows, value_rows)
    q_own, kv_own = packed[:4], packed[4:]
    kv_here = [kv_own[0]] + [head_swap(kv_own[r], r) for r in range(1, 4)]
    q_here = [q_own[0]] + [head_swap(q_own[r], r) for r in range(1, 4)]
    kv_there = [class_swap(piece) for piece in kv_here]
    kv_here_core = [core_swap(piece) for piece in kv_here]
    kv_there_core = [core_swap(piece) for piece in kv_there]
    results = pl.pallas_call(
        attend_kernel,
        out_shape=[shape((ATT_DIM, TOK), BF16)] * 4,
        in_specs=[SMEM] + vmem(20),
        out_specs=vmem(4),
        scratch_shapes=[
            pltpu.VMEM((4, ATT_DIM, TOK), BF16),
            pltpu.VMEM((CTX * TOK, ATT_DIM), BF16),
            pltpu.VMEM((CTX // 2, ATT_DIM, 2 * TOK), BF16),
            pltpu.VMEM((4, ATT_DIM, TOK), BF16),
            pltpu.VMEM((ATT_DIM, TOK), F32),
        ],
        compiler_params=params(56),
    )(info, *q_here, *kv_here, *kv_here_core, *kv_there, *kv_there_core)
    back = [results[0]] + [head_swap(results[r], r) for r in range(1, 4)]
    return pl.pallas_call(
        unpack_kernel,
        out_shape=shape((TOK, width), BF16),
        in_specs=[SMEM] + vmem(4),
        out_specs=vmem(1)[0],
        scratch_shapes=[pltpu.VMEM((width, TOK), BF16)],
        compiler_params=params(40),
    )(info, *back)


def mixer_part(
    info, ssm_inputs, ssm_gate, write_vecs, read_vecs, step_raw, decay_log, skip_gain, norm_gain
):
    tokens, width = ssm_inputs.shape
    heads = decay_log.shape[0]
    gain = jnp.repeat(skip_gain, SSM_DIM)[None, :]
    mixed, payload, cum = pl.pallas_call(
        ssm_local_kernel,
        out_shape=[
            shape((tokens, width), F32),
            shape((PAYLOAD, width), BF16),
            shape((tokens, heads), F32),
        ],
        in_specs=vmem(8),
        out_specs=vmem(3),
        compiler_params=params(40),
    )(ssm_inputs, write_vecs, read_vecs, step_raw, step_raw.T, decay_log[None, :], decay_log[:, None], gain)
    everything = lax.all_gather(payload, "ctx")
    gated, squares = pl.pallas_call(
        ssm_carry_kernel,
        out_shape=[shape((tokens, width), F32), shape((tokens, 1), F32)],
        in_specs=[SMEM] + vmem(5),
        out_specs=vmem(2),
        compiler_params=params(40),
    )(info, everything, mixed, cum, read_vecs, ssm_gate)
    squares = squares.reshape(tokens // 128, 128)
    count = lax.axis_size("tp")
    total = squares
    for d in range(1, count):
        total = total + lax.ppermute(squares, "tp", [(i, i ^ d) for i in range(count)])
    factor = lax.rsqrt(total.reshape(tokens) / SSM_WIDTH + 1e-05)
    return (gated * factor[:, None] * norm_gain[None, :]).astype(BF16)


def on_device(
    query_rows,
    key_rows,
    value_rows,
    ssm_inputs,
    ssm_gate,
    write_vecs,
    read_vecs,
    step_raw,
    decay_log,
    skip_gain,
    norm_gain,
):
    me = lax.axis_index("ctx")
    y, x, core = me >> 3, (me >> 1) & 3, me & 1
    info = jnp.stack([y * 2 + (x >> 1), (x ^ (x >> 1)) & 1, core, me]).astype(jnp.int32)
    mixer_out = mixer_part(
        info, ssm_inputs, ssm_gate, write_vecs, read_vecs, step_raw, decay_log, skip_gain, norm_gain
    )
    attention_out = attention_part(info, query_rows, key_rows, value_rows)
    return (attention_out, mixer_out)


def solution(mesh):
    placed = (
        P("ctx", "tp"),
        P("ctx", "tp"),
        P("ctx", "tp"),
        P("ctx", "tp"),
        P("ctx", "tp"),
        P("ctx", None),
        P("ctx", None),
        P("ctx", "tp"),
        P("tp"),
        P("tp"),
        P("tp"),
    )
    return jax.shard_map(
        on_device,
        mesh=mesh,
        in_specs=placed,
        out_specs=(P("ctx", "tp"), P("ctx", "tp")),
        check_vma=False,
    )
```

time: 351 us -> 178 us (0.51)
  local copies, waits for them, and re-layouts: 102 us -> 16 us
  matrix products: 85.2 us -> 0 us
  blocking collectives: 56.7 us -> 0 us
  other arithmetic: 54.3 us -> 1.38 us
  Pallas kernels: 0 us -> 43.6 us
  starting transfers between devices: 0.12 us -> 36.5 us
  waiting for transfers between devices: 31.4 us -> 63.1 us
    dot_general x11 -> x0, matrix products: 85.2 us -> none  [the longest x1 34 us: attention_part(): jnp.einsum('hqd,khd->hqk', query_heads, key_heads, preferred_element_type...]
    ppermute x0 -> x28, waiting for transfers between devices: none -> 63 us  [the longest x9 30.6 us: head_swap(): lax.ppermute(value, 'ctx', [(i, exchanged(i, r)) for i in range(CTX)])]
    pallas_call x0 -> x5, Pallas kernels: none -> 43.6 us  [the longest x1 33.1 us: attention_part(): pl.pallas_call(attend_kernel, out_shape=[shape((ATT_DIM, TOK), BF16)] * 4...]
    dynamic_update_slice x4 -> x0, local copies, waits for them, and re-layouts: 40.5 us -> none  [mixer_part(): lax.scan(block_pass, zero_state, (split(inputs), split(write_vecs), split...]
    all_gather x3 -> x0, local copies, waits for them, and re-layouts: 39 us -> none  [the longest x1 19.5 us: attention_part(): key_piece = lax.all_gather(key_rows, 'ctx', axis=0, tiled=True)]
    ppermute x0 -> x28, starting transfers between devices: none -> 36.5 us  [the longest x9 18 us: head_swap(): lax.ppermute(value, 'ctx', [(i, exchanged(i, r)) for i in range(CTX)])]
    unnamed x1 -> x0, blocking collectives: 31.2 us -> none
    all_gather x3 -> x1, waiting for transfers between devices: 30 us -> 0.01 us  [mixer_part(): everything = lax.all_gather(payload, 'ctx')]
  transfers between devices with their start and end apart: 3 -> 29, of which waited for: 2 -> 10; matrix products, arithmetic and copies ran while one was open for 34% -> 0% of each run, Pallas kernels for 0% -> 22%
where the time goes in v1:
time: 178 us; the launch traced here: 175 us
  waiting for transfers between devices  63.1 us (35%)
  Pallas kernels  43.6 us (24%)
  starting transfers between devices  36.5 us (21%)
  local copies, waits for them, and re-layouts  16 us (9%)
  between operations  14.4 us (8%)
    pallas_call x1, Pallas kernels, attention_part(): pl.pallas_call(attend_kernel, out_shape=[shape((ATT_DIM, TOK), BF16)] * 4...  33.1 us
    ppermute x9, waiting for transfers between devices, head_swap(): lax.ppermute(value, 'ctx', [(i, exchanged(i, r)) for i in range(CTX)])  30.6 us
    ppermute x4, waiting for transfers between devices, class_swap(): return lax.ppermute(value, 'ctx', [(i, i ^ 2) for i in range(CTX)])  29.8 us
    ppermute x9, starting transfers between devices, head_swap(): lax.ppermute(value, 'ctx', [(i, exchanged(i, r)) for i in range(CTX)])  18 us
    ppermute x7, starting transfers between devices, mixer_part(): lax.ppermute(squares, 'tp', [(i, i ^ d) for i in range(count)])  14.5 us
    unnamed x73, local copies, waits for them, and re-layouts  14.4 us
    pallas_call x1, Pallas kernels, mixer_part(): pl.pallas_call(ssm_local_kernel, out_shape=[shape((tokens, width), F32),...  4.86 us
  transfers between devices with their start and end apart: 29, of which 10 were waited for; matrix products, arithmetic and copies ran while one was open for 0% of the time, Pallas kernels for 22%

profile of v1, /device:TPU:0, one launch (start us, length us, event | category | flops | bytes accessed | tf_op | source)
XLA Modules:
  0.0 174.9 jit_solution(13892155374422395611)
XLA Ops:
  7.2 0.0 all-gather.3.cloned.1.call-start
  7.2 1.0 copy.18.write_ref
  8.2 1.0 copy.19.read_ref
  9.1 0.9 copy.20.step_ref
  10.0 0.7 copy.21.rate_t_ref
  10.8 0.7 broadcast_in_dim.13
  11.5 0.1 broadcast_in_dim_reshape.3.gain_ref
  11.6 1.2 copy-done.3
  12.8 0.8 copy-done.12
  13.5 0.7 copy-done.15
  14.2 4.9 %shard_map.125 = (f32[512,896]{1,0:T(8,128)S(1)}, bf16[80,896]{1,0:T(8,128)(2,1)S(1)}, f32[512,14]{1,0:T(8,128)S(1)}) custom-call(bf16[512,896]{1,0:T(8,128)(2,1)S(1)} %copy-done.3, bf16[512,64]{1,0:T(8,128)(2,1)S(1)} %copy.18.write_ref, bf16[512,64]{1,0:T(8,128)(2,1)S(1)} %copy.19.read_ref, f32[512,14]{1,0:T(8,128)S(1)} %copy.20.step_ref, ...), custom_call_target="tpu_custom_call" | custom-call | tf_op jit(solution)/shard_map/pallas_call | solution.py:292
  19.1 0.6 copy-done.11
  19.7 0.0 all-gather.3.cloned.1.call-update
  19.7 0.1 pad_add_fusion.info
  19.8 1.2 copy-done.5
  21.0 1.2 copy-done.6
  22.2 1.4 shard_map.122
  23.6 0.7 copy-done.9
  24.3 2.8 %collective-permute-start = (bf16[224,512]{1,0:T(8,128)(2,1)S(1)}, bf16[224,512]{1,0:T(8,128)(2,1)S(1)}, u32[]{:S(2)}, u32[]{:S(2)}) collective-permute-start(bf16[224,512]{1,0:T(8,128)(2,1)S(1)} %get-tuple-element.20), channel_id=1, source_target_pairs={{0,48},{8,56},{16,32},{24,40},{32,16},{40,24},{48,0},{56,8},{64,11... | collective-permute-start | bytes 688136 | tf_op jit(solution)/shard_map/ppermute | solution.py:33
  27.2 1.6 collective-permute-start.1
  28.7 0.3 collective-permute-start.2
  29.0 2.8 %collective-permute-start.3 = (bf16[448,512]{1,0:T(8,128)(2,1)S(1)}, bf16[448,512]{1,0:T(8,128)(2,1)S(1)}, u32[]{:S(2)}, u32[]{:S(2)}) collective-permute-start(bf16[448,512]{1,0:T(8,128)(2,1)S(1)} %get-tuple-element.24), channel_id=1, source_target_pairs={{0,48},{8,56},{16,32},{24,40},{32,16},{40,24},{48,0},{56,8},{64,11... | collective-permute-start | bytes 1376264 | tf_op jit(solution)/shard_map/ppermute | solution.py:33
  31.9 1.6 collective-permute-start.4
  33.4 0.3 collective-permute-done.refs_1_
  33.7 4.1 %collective-permute-start.5 = (bf16[448,512]{1,0:T(8,128)(2,1)S(1)}, bf16[448,512]{1,0:T(8,128)(2,1)S(1)}, u32[]{:S(2)}, u32[]{:S(2)}) collective-permute-start(bf16[448,512]{1,0:T(8,128)(2,1)S(1)} %get-tuple-element.26), channel_id=1, source_target_pairs={{0,112},{8,120},{16,96},{24,104},{32,80},{40,88},{48,64},{56,72},{... | collective-permute-start | bytes 1376264 | tf_op jit(solution)/shard_map/ppermute | solution.py:33
  37.9 4.7 %collective-permute-done.1.refs_2_ = bf16[224,512]{1,0:T(8,128)(2,1)S(1)} collective-permute-done((bf16[224,512]{1,0:T(8,128)(2,1)S(1)}, bf16[224,512]{1,0:T(8,128)(2,1)S(1)}, u32[]{:S(2)}, u32[]{:S(2)}) %collective-permute-start.1) | collective-permute-done | bytes 229408 | tf_op jit(solution)/shard_map/ppermute | solution.py:33
  42.5 0.0 collective-permute-start.6
  42.5 0.0 collective-permute-done.2.refs_3_
  42.6 1.2 collective-permute-start.10
  43.7 4.8 %collective-permute-done.3.refs_5_ = bf16[448,512]{1,0:T(8,128)(2,1)S(1)} collective-permute-done((bf16[448,512]{1,0:T(8,128)(2,1)S(1)}, bf16[448,512]{1,0:T(8,128)(2,1)S(1)}, u32[]{:S(2)}, u32[]{:S(2)}) %collective-permute-start.3) | collective-permute-done | bytes 458784 | tf_op jit(solution)/shard_map/ppermute | solution.py:33
  48.5 0.0 collective-permute-start.7
  48.5 20.8 %collective-permute-done.4.refs_6_ = bf16[448,512]{1,0:T(8,128)(2,1)S(1)} collective-permute-done((bf16[448,512]{1,0:T(8,128)(2,1)S(1)}, bf16[448,512]{1,0:T(8,128)(2,1)S(1)}, u32[]{:S(2)}, u32[]{:S(2)}) %collective-permute-start.4) | collective-permute-done | bytes 458784 | tf_op jit(solution)/shard_map/ppermute | solution.py:33
  69.4 0.1 collective-permute-start.11
  69.5 2.0 %collective-permute-start.12 = (bf16[448,512]{1,0:T(8,128)(2,1)S(1)}, bf16[448,512]{1,0:T(8,128)(2,1)S(1)}, u32[]{:S(2)}, u32[]{:S(2)}) collective-permute-start(bf16[448,512]{1,0:T(8,128)(2,1)S(1)} %collective-permute-done.4.refs_6_), channel_id=1, source_target_pairs={{0,16},{8,24},{16,0},{24,8},{32,48},{40,56},{48,32},{56,40},{64,80... | collective-permute-start | bytes 1376264 | tf_op jit(solution)/shard_map/ppermute | solution.py:37
  71.5 0.2 collective-permute-start.13
  71.7 0.0 collective-permute-start.9
  71.7 0.5 collective-permute-start.14
  72.2 10.6 %collective-permute-done.11.refs_13_ = bf16[448,512]{1,0:T(8,128)(2,1)S(1)} collective-permute-done((bf16[448,512]{1,0:T(8,128)(2,1)S(1)}, bf16[448,512]{1,0:T(8,128)(2,1)S(1)}, u32[]{:S(2)}, u32[]{:S(2)}) %collective-permute-start.11) | collective-permute-done | bytes 458784 | tf_op jit(solution)/shard_map/ppermute | solution.py:37
  82.8 9.8 %collective-permute-done.12.refs_14_ = bf16[448,512]{1,0:T(8,128)(2,1)S(1)} collective-permute-done((bf16[448,512]{1,0:T(8,128)(2,1)S(1)}, bf16[448,512]{1,0:T(8,128)(2,1)S(1)}, u32[]{:S(2)}, u32[]{:S(2)}) %collective-permute-start.12) | collective-permute-done | bytes 458784 | tf_op jit(solution)/shard_map/ppermute | solution.py:37
  92.6 9.4 %collective-permute-done.13.refs_15_ = bf16[448,512]{1,0:T(8,128)(2,1)S(1)} collective-permute-done((bf16[448,512]{1,0:T(8,128)(2,1)S(1)}, bf16[448,512]{1,0:T(8,128)(2,1)S(1)}, u32[]{:S(2)}, u32[]{:S(2)}) %collective-permute-start.13) | collective-permute-done | bytes 458784 | tf_op jit(solution)/shard_map/ppermute | solution.py:37
  102.0 0.0 collective-permute-start.17
  102.1 1.7 collective-permute-done.17.refs_19_
  103.8 0.8 copy-done.30
  104.7 0.0 copy-start.7
  104.7 33.1 %shard_map.123 = (bf16[224,512]{1,0:T(8,128)(2,1)}, bf16[224,512]{1,0:T(8,128)(2,1)}, bf16[224,512]{1,0:T(8,128)(2,1)}, bf16[224,512]{1,0:T(8,128)(2,1)}) custom-call(s32[4]{0:T(128)} %copy-done.13, bf16[224,512]{1,0:T(8,128)(2,1)} %copy-done.9, bf16[224,512]{1,0:T(8,128)(2,1)} %copy-done.31, bf16[224,512]{1,0:T(8,128)(2,1)} %copy-done.32, ...), custom_call_target="tpu_custom_call" | custom-call | tf_op jit(solution)/shard_map/pallas_call | solution.py:261
  137.8 0.1 collective-permute-start.18
  137.8 1.7 collective-permute-start.19
  139.5 3.0 %collective-permute-start.20 = (bf16[224,512]{1,0:T(8,128)(2,1)}, bf16[224,512]{1,0:T(8,128)(2,1)}, u32[]{:S(2)}, u32[]{:S(2)}) collective-permute-start(bf16[224,512]{1,0:T(8,128)(2,1)} %get-tuple-element.30), channel_id=1, source_target_pairs={{0,112},{8,120},{16,96},{24,104},{32,80},{40,88},{48,64},{56,72},{... | collective-permute-start | bytes 688136 | tf_op jit(solution)/shard_map/ppermute | solution.py:33
  142.5 1.6 copy-done
  144.2 0.6 copy-done.14
  144.8 1.8 %shard_map.126 = (f32[512,896]{1,0:T(8,128)S(1)}, f32[512,1]{1,0:T(8,128)S(1)}) custom-call(s32[4]{0:T(128)S(1)} %copy-done.14, bf16[16,80,896]{2,1,0:T(8,128)(2,1)S(1)} %bitcast.12, f32[512,896]{1,0:T(8,128)S(1)} %get-tuple-element.32.mixed_ref, f32[512,14]{1,0:T(8,128)S(1)} %get-tuple-element.33.cum_ref, bf16[512,64]{1,0:T(8,128)(2,1)S(1)} %copy.19.read_ref, ...), custom_call_target="tpu_custom_call" | custom-call | tf_op jit(solution)/shard_map/pallas_call | solution.py:304
  146.6 1.2 copy-done.1
  147.9 0.1 reduce
  148.0 6.9 %collective-permute-start.27 = (f32[4,128]{1,0:T(4,128)S(1)}, f32[4,128]{1,0:T(4,128)S(1)}, u32[]{:S(2)}, u32[]{:S(2)}) collective-permute-start(f32[4,128]{1,0:T(4,128)S(1)} %bitcast.16), channel_id=1, source_target_pairs={{0,7},{1,6},{2,5},{3,4},{4,3},{5,2},{6,1},{7,0},{8,15},{9,14},{10,... | collective-permute-start | bytes 6152 | tf_op jit(solution)/shard_map/ppermute | solution.py:315
  155.0 2.3 %collective-permute-start.25 = (f32[4,128]{1,0:T(4,128)S(1)}, f32[4,128]{1,0:T(4,128)S(1)}, u32[]{:S(2)}, u32[]{:S(2)}) collective-permute-start(f32[4,128]{1,0:T(4,128)S(1)} %bitcast.18), channel_id=1, source_target_pairs={{0,5},{1,4},{2,7},{3,6},{4,1},{5,0},{6,3},{7,2},{8,13},{9,12},{10,... | collective-permute-start | bytes 6152 | tf_op jit(solution)/shard_map/ppermute | solution.py:315
  157.2 1.6 collective-permute-start.24
  158.9 2.9 %collective-permute-start.23 = (f32[4,128]{1,0:T(4,128)S(1)}, f32[4,128]{1,0:T(4,128)S(1)}, u32[]{:S(2)}, u32[]{:S(2)}) collective-permute-start(f32[4,128]{1,0:T(4,128)S(1)} %bitcast.20), channel_id=1, source_target_pairs={{0,3},{1,2},{2,1},{3,0},{4,7},{5,6},{6,5},{7,4},{8,11},{9,10},{10,... | collective-permute-start | bytes 6152 | tf_op jit(solution)/shard_map/ppermute | solution.py:315
  161.8 0.2 collective-permute-start.22
  162.0 0.4 collective-permute-done.26
  162.5 0.5 collective-permute-start.21
  163.0 0.9 copy-done.10
  163.9 2.4 %shard_map.124 = bf16[512,896]{1,0:T(8,128)(2,1)} custom-call(s32[4]{0:T(128)S(1)} %copy-done.14, bf16[224,512]{1,0:T(8,128)(2,1)S(1)} %copy-done.10, bf16[224,512]{1,0:T(8,128)(2,1)} %collective-permute-done.18.refs_1_, bf16[224,512]{1,0:T(8,128)(2,1)} %collective-permute-done.19.refs_2_, bf16[224,512]{1,0:T(8,128)(2,1)} %collective-permute-done.20.refs_3_), custom_call_target="tpu_custom_call" | custom-call | tf_op jit(solution)/shard_map/pallas_call | solution.py:276
  166.4 0.5 collective-permute-done.22
  166.9 1.1 multiply_convert_fusion
  (80 shorter events, 0.2 us)
Async XLA Ops:
  7.2 135.4 %all-gather.3.cloned.1.call-start = ((), (), s32[]{:S(2)}) async-start(), calls=%async_computation | async-start | bytes 2437120 | tf_op jit(solution)/shard_map/all_gather | solution.py:303
  11.6 1.2 copy-start.3
  12.8 0.8 copy-start.12
  13.5 0.7 copy-start.15
  14.2 5.6 %copy-start.4 = (bf16[512,896]{1,0:T(8,128)(2,1)S(1)}, bf16[512,896]{1,0:T(8,128)(2,1)}, u32[]{:S(2)}) copy-start(bf16[512,896]{1,0:T(8,128)(2,1)} %q_ref.1) | copy-start | bytes 2752516
  19.1 0.7 copy-start.11
  19.8 1.2 copy-start.5
  21.0 1.2 copy-start.6
  22.2 82.4 %copy-start.13 = (s32[4]{0:T(128)}, s32[4]{0:T(128)S(1)}, u32[]{:S(2)}) copy-start(s32[4]{0:T(128)S(1)} %pad_add_fusion.info) | copy-start | bytes 52
  23.6 0.7 copy-start.9
  24.3 80.3 %copy-start.8 = (bf16[448,512]{1,0:T(8,128)(2,1)}, bf16[448,512]{1,0:T(8,128)(2,1)S(1)}, u32[]{:S(2)}) copy-start(bf16[448,512]{1,0:T(8,128)(2,1)S(1)} %get-tuple-element.23.refs_4_) | copy-start | bytes 1376260
  24.3 9.4 %collective-permute-start = (bf16[224,512]{1,0:T(8,128)(2,1)S(1)}, bf16[224,512]{1,0:T(8,128)(2,1)S(1)}, u32[]{:S(2)}, u32[]{:S(2)}) collective-permute-start(bf16[224,512]{1,0:T(8,128)(2,1)S(1)} %get-tuple-element.20), channel_id=1, source_target_pairs={{0,48},{8,56},{16,32},{24,40},{32,16},{40,24},{48,0},{56,8},{64,11... | collective-permute-start | bytes 688136 | tf_op jit(solution)/shard_map/ppermute | solution.py:33
  27.2 15.4 %collective-permute-start.1 = (bf16[224,512]{1,0:T(8,128)(2,1)S(1)}, bf16[224,512]{1,0:T(8,128)(2,1)S(1)}, u32[]{:S(2)}, u32[]{:S(2)}) collective-permute-start(bf16[224,512]{1,0:T(8,128)(2,1)S(1)} %get-tuple-element.21), channel_id=1, source_target_pairs={{0,64},{8,72},{16,80},{24,88},{32,96},{40,104},{48,112},{56,120},{... | collective-permute-start | bytes 688136 | tf_op jit(solution)/shard_map/ppermute | solution.py:33
  28.7 13.8 %collective-permute-start.2 = (bf16[224,512]{1,0:T(8,128)(2,1)S(1)}, bf16[224,512]{1,0:T(8,128)(2,1)S(1)}, u32[]{:S(2)}, u32[]{:S(2)}) collective-permute-start(bf16[224,512]{1,0:T(8,128)(2,1)S(1)} %get-tuple-element.22), channel_id=1, source_target_pairs={{0,112},{8,120},{16,96},{24,104},{32,80},{40,88},{48,64},{56,72},{... | collective-permute-start | bytes 688136 | tf_op jit(solution)/shard_map/ppermute | solution.py:33
  29.0 19.5 %collective-permute-start.3 = (bf16[448,512]{1,0:T(8,128)(2,1)S(1)}, bf16[448,512]{1,0:T(8,128)(2,1)S(1)}, u32[]{:S(2)}, u32[]{:S(2)}) collective-permute-start(bf16[448,512]{1,0:T(8,128)(2,1)S(1)} %get-tuple-element.24), channel_id=1, source_target_pairs={{0,48},{8,56},{16,32},{24,40},{32,16},{40,24},{48,0},{56,8},{64,11... | collective-permute-start | bytes 1376264 | tf_op jit(solution)/shard_map/ppermute | solution.py:33
  31.9 37.5 %collective-permute-start.4 = (bf16[448,512]{1,0:T(8,128)(2,1)S(1)}, bf16[448,512]{1,0:T(8,128)(2,1)S(1)}, u32[]{:S(2)}, u32[]{:S(2)}) collective-permute-start(bf16[448,512]{1,0:T(8,128)(2,1)S(1)} %get-tuple-element.25), channel_id=1, source_target_pairs={{0,64},{8,72},{16,80},{24,88},{32,96},{40,104},{48,112},{56,120},{... | collective-permute-start | bytes 1376264 | tf_op jit(solution)/shard_map/ppermute | solution.py:33
  33.7 70.9 %copy-start.31 = (bf16[224,512]{1,0:T(8,128)(2,1)}, bf16[224,512]{1,0:T(8,128)(2,1)S(1)}, u32[]{:S(2)}) copy-start(bf16[224,512]{1,0:T(8,128)(2,1)S(1)} %collective-permute-done.refs_1_) | copy-start | bytes 688132
  33.7 35.6 %collective-permute-start.5 = (bf16[448,512]{1,0:T(8,128)(2,1)S(1)}, bf16[448,512]{1,0:T(8,128)(2,1)S(1)}, u32[]{:S(2)}, u32[]{:S(2)}) collective-permute-start(bf16[448,512]{1,0:T(8,128)(2,1)S(1)} %get-tuple-element.26), channel_id=1, source_target_pairs={{0,112},{8,120},{16,96},{24,104},{32,80},{40,88},{48,64},{56,72},{... | collective-permute-start | bytes 1376264 | tf_op jit(solution)/shard_map/ppermute | solution.py:33
  42.5 61.3 %copy-start.32 = (bf16[224,512]{1,0:T(8,128)(2,1)}, bf16[224,512]{1,0:T(8,128)(2,1)S(1)}, u32[]{:S(2)}) copy-start(bf16[224,512]{1,0:T(8,128)(2,1)S(1)} %collective-permute-done.1.refs_2_) | copy-start | bytes 688132
  42.5 26.9 %collective-permute-start.6 = (bf16[448,512]{1,0:T(8,128)(2,1)S(1)}, bf16[448,512]{1,0:T(8,128)(2,1)S(1)}, u32[]{:S(2)}, u32[]{:S(2)}) collective-permute-start(bf16[448,512]{1,0:T(8,128)(2,1)S(1)} %get-tuple-element.23.refs_4_), channel_id=1, source_target_pairs={{0,8},{8,0},{16,24},{24,16},{32,40},{40,32},{48,56},{56,48},{64,72... | collective-permute-start | bytes 1376264 | tf_op jit(solution)/shard_map/ppermute | solution.py:41
  42.5 28.9 %copy-start.33 = (bf16[224,512]{1,0:T(8,128)(2,1)}, bf16[224,512]{1,0:T(8,128)(2,1)S(1)}, u32[]{:S(2)}) copy-start(bf16[224,512]{1,0:T(8,128)(2,1)S(1)} %collective-permute-done.2.refs_3_) | copy-start | bytes 688132
  42.6 28.9 %collective-permute-start.10 = (bf16[448,512]{1,0:T(8,128)(2,1)S(1)}, bf16[448,512]{1,0:T(8,128)(2,1)S(1)}, u32[]{:S(2)}, u32[]{:S(2)}) collective-permute-start(bf16[448,512]{1,0:T(8,128)(2,1)S(1)} %get-tuple-element.23.refs_4_), channel_id=1, source_target_pairs={{0,16},{8,24},{16,0},{24,8},{32,48},{40,56},{48,32},{56,40},{64,80... | collective-permute-start | bytes 1376264 | tf_op jit(solution)/shard_map/ppermute | solution.py:37
  48.5 56.1 %copy-start.16 = (bf16[448,512]{1,0:T(8,128)(2,1)}, bf16[448,512]{1,0:T(8,128)(2,1)S(1)}, u32[]{:S(2)}) copy-start(bf16[448,512]{1,0:T(8,128)(2,1)S(1)} %collective-permute-done.3.refs_5_) | copy-start | bytes 1376260
  48.5 23.1 %collective-permute-start.7 = (bf16[448,512]{1,0:T(8,128)(2,1)S(1)}, bf16[448,512]{1,0:T(8,128)(2,1)S(1)}, u32[]{:S(2)}, u32[]{:S(2)}) collective-permute-start(bf16[448,512]{1,0:T(8,128)(2,1)S(1)} %collective-permute-done.3.refs_5_), channel_id=1, source_target_pairs={{0,8},{8,0},{16,24},{24,16},{32,40},{40,32},{48,56},{56,48},{64,72... | collective-permute-start | bytes 1376264 | tf_op jit(solution)/shard_map/ppermute | solution.py:41
  69.4 35.3 %copy-start.17 = (bf16[448,512]{1,0:T(8,128)(2,1)}, bf16[448,512]{1,0:T(8,128)(2,1)S(1)}, u32[]{:S(2)}) copy-start(bf16[448,512]{1,0:T(8,128)(2,1)S(1)} %collective-permute-done.4.refs_6_) | copy-start | bytes 1376260
  69.4 2.3 %collective-permute-start.8 = (bf16[448,512]{1,0:T(8,128)(2,1)S(1)}, bf16[448,512]{1,0:T(8,128)(2,1)S(1)}, u32[]{:S(2)}, u32[]{:S(2)}) collective-permute-start(bf16[448,512]{1,0:T(8,128)(2,1)S(1)} %collective-permute-done.4.refs_6_), channel_id=1, source_target_pairs={{0,8},{8,0},{16,24},{24,16},{32,40},{40,32},{48,56},{56,48},{64,72... | collective-permute-start | bytes 1376264 | tf_op jit(solution)/shard_map/ppermute | solution.py:41
  69.4 35.3 %copy-start.18 = (bf16[448,512]{1,0:T(8,128)(2,1)}, bf16[448,512]{1,0:T(8,128)(2,1)S(1)}, u32[]{:S(2)}) copy-start(bf16[448,512]{1,0:T(8,128)(2,1)S(1)} %collective-permute-done.5.refs_7_) | copy-start | bytes 1376260
  69.4 13.4 %collective-permute-start.11 = (bf16[448,512]{1,0:T(8,128)(2,1)S(1)}, bf16[448,512]{1,0:T(8,128)(2,1)S(1)}, u32[]{:S(2)}, u32[]{:S(2)}) collective-permute-start(bf16[448,512]{1,0:T(8,128)(2,1)S(1)} %collective-permute-done.3.refs_5_), channel_id=1, source_target_pairs={{0,16},{8,24},{16,0},{24,8},{32,48},{40,56},{48,32},{56,40},{64,80... | collective-permute-start | bytes 1376264 | tf_op jit(solution)/shard_map/ppermute | solution.py:37
  69.5 35.2 %copy-start.19 = (bf16[448,512]{1,0:T(8,128)(2,1)}, bf16[448,512]{1,0:T(8,128)(2,1)S(1)}, u32[]{:S(2)}) copy-start(bf16[448,512]{1,0:T(8,128)(2,1)S(1)} %collective-permute-done.6.refs_8_) | copy-start | bytes 1376260
  69.5 23.1 %collective-permute-start.12 = (bf16[448,512]{1,0:T(8,128)(2,1)S(1)}, bf16[448,512]{1,0:T(8,128)(2,1)S(1)}, u32[]{:S(2)}, u32[]{:S(2)}) collective-permute-start(bf16[448,512]{1,0:T(8,128)(2,1)S(1)} %collective-permute-done.4.refs_6_), channel_id=1, source_target_pairs={{0,16},{8,24},{16,0},{24,8},{32,48},{40,56},{48,32},{56,40},{64,80... | collective-permute-start | bytes 1376264 | tf_op jit(solution)/shard_map/ppermute | solution.py:37
  71.5 33.2 %copy-start.20 = (bf16[448,512]{1,0:T(8,128)(2,1)}, bf16[448,512]{1,0:T(8,128)(2,1)S(1)}, u32[]{:S(2)}) copy-start(bf16[448,512]{1,0:T(8,128)(2,1)S(1)} %collective-permute-done.10.refs_12_) | copy-start | bytes 1376260
  71.5 30.5 %collective-permute-start.13 = (bf16[448,512]{1,0:T(8,128)(2,1)S(1)}, bf16[448,512]{1,0:T(8,128)(2,1)S(1)}, u32[]{:S(2)}, u32[]{:S(2)}) collective-permute-start(bf16[448,512]{1,0:T(8,128)(2,1)S(1)} %collective-permute-done.5.refs_7_), channel_id=1, source_target_pairs={{0,16},{8,24},{16,0},{24,8},{32,48},{40,56},{48,32},{56,40},{64,80... | collective-permute-start | bytes 1376264 | tf_op jit(solution)/shard_map/ppermute | solution.py:37
  71.7 33.0 %copy-start.21 = (bf16[448,512]{1,0:T(8,128)(2,1)}, bf16[448,512]{1,0:T(8,128)(2,1)S(1)}, u32[]{:S(2)}) copy-start(bf16[448,512]{1,0:T(8,128)(2,1)S(1)} %collective-permute-done.7.refs_9_) | copy-start | bytes 1376260
  71.7 30.3 %collective-permute-start.9 = (bf16[448,512]{1,0:T(8,128)(2,1)S(1)}, bf16[448,512]{1,0:T(8,128)(2,1)S(1)}, u32[]{:S(2)}, u32[]{:S(2)}) collective-permute-start(bf16[448,512]{1,0:T(8,128)(2,1)S(1)} %collective-permute-done.5.refs_7_), channel_id=1, source_target_pairs={{0,8},{8,0},{16,24},{24,16},{32,40},{40,32},{48,56},{56,48},{64,72... | collective-permute-start | bytes 1376264 | tf_op jit(solution)/shard_map/ppermute | solution.py:41
  71.7 33.0 %copy-start.22 = (bf16[448,512]{1,0:T(8,128)(2,1)}, bf16[448,512]{1,0:T(8,128)(2,1)S(1)}, u32[]{:S(2)}) copy-start(bf16[448,512]{1,0:T(8,128)(2,1)S(1)} %collective-permute-done.8.refs_10_) | copy-start | bytes 1376260
  71.7 30.3 %collective-permute-start.14 = (bf16[448,512]{1,0:T(8,128)(2,1)S(1)}, bf16[448,512]{1,0:T(8,128)(2,1)S(1)}, u32[]{:S(2)}, u32[]{:S(2)}) collective-permute-start(bf16[448,512]{1,0:T(8,128)(2,1)S(1)} %collective-permute-done.10.refs_12_), channel_id=1, source_target_pairs={{0,8},{8,0},{16,24},{24,16},{32,40},{40,32},{48,56},{56,48},{64,72... | collective-permute-start | bytes 1376264 | tf_op jit(solution)/shard_map/ppermute | solution.py:41
  82.8 21.9 %copy-start.23 = (bf16[448,512]{1,0:T(8,128)(2,1)}, bf16[448,512]{1,0:T(8,128)(2,1)S(1)}, u32[]{:S(2)}) copy-start(bf16[448,512]{1,0:T(8,128)(2,1)S(1)} %collective-permute-done.11.refs_13_) | copy-start | bytes 1376260
  82.8 19.2 %collective-permute-start.15 = (bf16[448,512]{1,0:T(8,128)(2,1)S(1)}, bf16[448,512]{1,0:T(8,128)(2,1)S(1)}, u32[]{:S(2)}, u32[]{:S(2)}) collective-permute-start(bf16[448,512]{1,0:T(8,128)(2,1)S(1)} %collective-permute-done.11.refs_13_), channel_id=1, source_target_pairs={{0,8},{8,0},{16,24},{24,16},{32,40},{40,32},{48,56},{56,48},{64,72... | collective-permute-start | bytes 1376264 | tf_op jit(solution)/shard_map/ppermute | solution.py:41
  92.6 12.1 %copy-start.24 = (bf16[448,512]{1,0:T(8,128)(2,1)}, bf16[448,512]{1,0:T(8,128)(2,1)S(1)}, u32[]{:S(2)}) copy-start(bf16[448,512]{1,0:T(8,128)(2,1)S(1)} %collective-permute-done.12.refs_14_) | copy-start | bytes 1376260
  92.6 9.4 %collective-permute-start.16 = (bf16[448,512]{1,0:T(8,128)(2,1)S(1)}, bf16[448,512]{1,0:T(8,128)(2,1)S(1)}, u32[]{:S(2)}, u32[]{:S(2)}) collective-permute-start(bf16[448,512]{1,0:T(8,128)(2,1)S(1)} %collective-permute-done.12.refs_14_), channel_id=1, source_target_pairs={{0,8},{8,0},{16,24},{24,16},{32,40},{40,32},{48,56},{56,48},{64,72... | collective-permute-start | bytes 1376264 | tf_op jit(solution)/shard_map/ppermute | solution.py:41
  102.0 1.8 %copy-start.25 = (bf16[448,512]{1,0:T(8,128)(2,1)}, bf16[448,512]{1,0:T(8,128)(2,1)S(1)}, u32[]{:S(2)}) copy-start(bf16[448,512]{1,0:T(8,128)(2,1)S(1)} %collective-permute-done.13.refs_15_) | copy-start | bytes 1376260
  102.0 1.8 %collective-permute-start.17 = (bf16[448,512]{1,0:T(8,128)(2,1)S(1)}, bf16[448,512]{1,0:T(8,128)(2,1)S(1)}, u32[]{:S(2)}, u32[]{:S(2)}) collective-permute-start(bf16[448,512]{1,0:T(8,128)(2,1)S(1)} %collective-permute-done.13.refs_15_), channel_id=1, source_target_pairs={{0,8},{8,0},{16,24},{24,16},{32,40},{40,32},{48,56},{56,48},{64,72... | collective-permute-start | bytes 1376264 | tf_op jit(solution)/shard_map/ppermute | solution.py:41
  102.0 1.8 %copy-start.26 = (bf16[448,512]{1,0:T(8,128)(2,1)}, bf16[448,512]{1,0:T(8,128)(2,1)S(1)}, u32[]{:S(2)}) copy-start(bf16[448,512]{1,0:T(8,128)(2,1)S(1)} %collective-permute-done.9.refs_11_) | copy-start | bytes 1376260
  102.0 1.8 %copy-start.27 = (bf16[448,512]{1,0:T(8,128)(2,1)}, bf16[448,512]{1,0:T(8,128)(2,1)S(1)}, u32[]{:S(2)}) copy-start(bf16[448,512]{1,0:T(8,128)(2,1)S(1)} %collective-permute-done.14.refs_16_) | copy-start | bytes 1376260
  102.0 1.8 %copy-start.28 = (bf16[448,512]{1,0:T(8,128)(2,1)}, bf16[448,512]{1,0:T(8,128)(2,1)S(1)}, u32[]{:S(2)}) copy-start(bf16[448,512]{1,0:T(8,128)(2,1)S(1)} %collective-permute-done.15.refs_17_) | copy-start | bytes 1376260
  102.1 1.8 %copy-start.29 = (bf16[448,512]{1,0:T(8,128)(2,1)}, bf16[448,512]{1,0:T(8,128)(2,1)S(1)}, u32[]{:S(2)}) copy-start(bf16[448,512]{1,0:T(8,128)(2,1)S(1)} %collective-permute-done.16.refs_18_) | copy-start | bytes 1376260
  103.8 0.8 copy-start.30
  104.7 37.8 %copy-start.7 = (bf16[512,896]{1,0:T(8,128)(2,1)S(1)}, bf16[512,896]{1,0:T(8,128)(2,1)}, u32[]{:S(2)}) copy-start(bf16[512,896]{1,0:T(8,128)(2,1)} %gate_ref.1) | copy-start | bytes 2752516
  137.8 17.2 %collective-permute-start.18 = (bf16[224,512]{1,0:T(8,128)(2,1)}, bf16[224,512]{1,0:T(8,128)(2,1)}, u32[]{:S(2)}, u32[]{:S(2)}) collective-permute-start(bf16[224,512]{1,0:T(8,128)(2,1)} %get-tuple-element.28), channel_id=1, source_target_pairs={{0,48},{8,56},{16,32},{24,40},{32,16},{40,24},{48,0},{56,8},{64,11... | collective-permute-start | bytes 688136 | tf_op jit(solution)/shard_map/ppermute | solution.py:33
  137.8 19.4 %collective-permute-start.19 = (bf16[224,512]{1,0:T(8,128)(2,1)}, bf16[224,512]{1,0:T(8,128)(2,1)}, u32[]{:S(2)}, u32[]{:S(2)}) collective-permute-start(bf16[224,512]{1,0:T(8,128)(2,1)} %get-tuple-element.29), channel_id=1, source_target_pairs={{0,64},{8,72},{16,80},{24,88},{32,96},{40,104},{48,112},{56,120},{... | collective-permute-start | bytes 688136 | tf_op jit(solution)/shard_map/ppermute | solution.py:33
  139.5 19.4 %collective-permute-start.20 = (bf16[224,512]{1,0:T(8,128)(2,1)}, bf16[224,512]{1,0:T(8,128)(2,1)}, u32[]{:S(2)}, u32[]{:S(2)}) collective-permute-start(bf16[224,512]{1,0:T(8,128)(2,1)} %get-tuple-element.30), channel_id=1, source_target_pairs={{0,112},{8,120},{16,96},{24,104},{32,80},{40,88},{48,64},{56,72},{... | collective-permute-start | bytes 688136 | tf_op jit(solution)/shard_map/ppermute | solution.py:33
  142.5 1.6 copy-start
  144.2 0.6 copy-start.14
  144.8 22.1 %copy-start.34 = (f32[896]{0:T(1024)S(1)}, f32[896]{0:T(1024)}, u32[]{:S(2)}) copy-start(f32[896]{0:T(1024)} %param.21) | copy-start | bytes 10756
  146.6 1.3 copy-start.1
  147.9 19.1 %copy-start.2 = (f32[512,896]{1,0:T(8,128)S(1)}, f32[512,896]{1,0:T(8,128)}, u32[]{:S(2)}) copy-start(f32[512,896]{1,0:T(8,128)} %copy-done.1) | copy-start | bytes 5505028
  148.0 13.8 %collective-permute-start.27 = (f32[4,128]{1,0:T(4,128)S(1)}, f32[4,128]{1,0:T(4,128)S(1)}, u32[]{:S(2)}, u32[]{:S(2)}) collective-permute-start(f32[4,128]{1,0:T(4,128)S(1)} %bitcast.16), channel_id=1, source_target_pairs={{0,7},{1,6},{2,5},{3,4},{4,3},{5,2},{6,1},{7,0},{8,15},{9,14},{10,... | collective-permute-start | bytes 6152 | tf_op jit(solution)/shard_map/ppermute | solution.py:315
  155.0 7.5 %collective-permute-start.26 = (f32[4,128]{1,0:T(4,128)S(1)}, f32[4,128]{1,0:T(4,128)S(1)}, u32[]{:S(2)}, u32[]{:S(2)}) collective-permute-start(f32[4,128]{1,0:T(4,128)S(1)} %bitcast.17), channel_id=1, source_target_pairs={{0,6},{1,7},{2,4},{3,5},{4,2},{5,3},{6,0},{7,1},{8,14},{9,15},{10,... | collective-permute-start | bytes 6152 | tf_op jit(solution)/shard_map/ppermute | solution.py:315
  155.0 11.4 %collective-permute-start.25 = (f32[4,128]{1,0:T(4,128)S(1)}, f32[4,128]{1,0:T(4,128)S(1)}, u32[]{:S(2)}, u32[]{:S(2)}) collective-permute-start(f32[4,128]{1,0:T(4,128)S(1)} %bitcast.18), channel_id=1, source_target_pairs={{0,5},{1,4},{2,7},{3,6},{4,1},{5,0},{6,3},{7,2},{8,13},{9,12},{10,... | collective-permute-start | bytes 6152 | tf_op jit(solution)/shard_map/ppermute | solution.py:315
  157.2 9.1 %collective-permute-start.24 = (f32[4,128]{1,0:T(4,128)S(1)}, f32[4,128]{1,0:T(4,128)S(1)}, u32[]{:S(2)}, u32[]{:S(2)}) collective-permute-start(f32[4,128]{1,0:T(4,128)S(1)} %bitcast.19), channel_id=1, source_target_pairs={{0,4},{1,5},{2,6},{3,7},{4,0},{5,1},{6,2},{7,3},{8,12},{9,13},{10,... | collective-permute-start | bytes 6152 | tf_op jit(solution)/shard_map/ppermute | solution.py:315
  158.9 7.5 %collective-permute-start.23 = (f32[4,128]{1,0:T(4,128)S(1)}, f32[4,128]{1,0:T(4,128)S(1)}, u32[]{:S(2)}, u32[]{:S(2)}) collective-permute-start(f32[4,128]{1,0:T(4,128)S(1)} %bitcast.20), channel_id=1, source_target_pairs={{0,3},{1,2},{2,1},{3,0},{4,7},{5,6},{6,5},{7,4},{8,11},{9,10},{10,... | collective-permute-start | bytes 6152 | tf_op jit(solution)/shard_map/ppermute | solution.py:315
  161.8 5.1 %collective-permute-start.22 = (f32[4,128]{1,0:T(4,128)S(1)}, f32[4,128]{1,0:T(4,128)S(1)}, u32[]{:S(2)}, u32[]{:S(2)}) collective-permute-start(f32[4,128]{1,0:T(4,128)S(1)} %bitcast.21), channel_id=1, source_target_pairs={{0,2},{1,3},{2,0},{3,1},{4,6},{5,7},{6,4},{7,5},{8,10},{9,11},{10,... | collective-permute-start | bytes 6152 | tf_op jit(solution)/shard_map/ppermute | solution.py:315
  162.5 4.4 %collective-permute-start.21 = (f32[4,128]{1,0:T(4,128)S(1)}, f32[4,128]{1,0:T(4,128)S(1)}, u32[]{:S(2)}, u32[]{:S(2)}) collective-permute-start(f32[4,128]{1,0:T(4,128)S(1)} %bitcast.22), channel_id=1, source_target_pairs={{0,1},{1,0},{2,3},{3,2},{4,5},{5,4},{6,7},{7,6},{8,9},{9,8},{10,11... | collective-permute-start | bytes 6152 | tf_op jit(solution)/shard_map/ppermute | solution.py:315
  163.0 0.9 copy-start.10
Sparse Core Ops, SparseCore 0:
  19.9 52.5 all-gather.2

commit v2 on v1

v2 whole, which is shorter than its diff:
```python
import functools
import math

import jax
import jax.numpy as jnp
from jax import lax
from jax.experimental import pallas as pl
from jax.experimental.pallas import tpu as pltpu
from jax.sharding import PartitionSpec as P

ATT_DIM = 224
SSM_DIM = 64
STATE_DIM = 64
SSM_WIDTH = 7168
TOK = 512
HEADS = 4
CTX = 16
HALF = 256
LOG2E = math.log2(math.e)
F32 = jnp.float32
BF16 = jnp.bfloat16


def exchanged(i, r):
    y, x, c = i >> 3, (i >> 1) & 3, i & 1
    if r & 1:
        x = 3 - x
    if r & 2:
        y = 1 - y
    return y * 8 + x * 2 + c


def head_swap(value, r):
    return lax.ppermute(value, "ctx", [(i, exchanged(i, r)) for i in range(CTX)])


def class_swap(value):
    return lax.ppermute(value, "ctx", [(i, i ^ 2) for i in range(CTX)])


def core_swap(value):
    return lax.ppermute(value, "ctx", [(i, i ^ 1) for i in range(CTX)])


def block_swap(value, step):
    return lax.ppermute(value, "ctx", [(i, i ^ step) for i in range(CTX)])


def head_rows(head):
    return pl.ds(pl.multiple_of(head * ATT_DIM, 16), ATT_DIM)


Q_ROWS = slice(0, ATT_DIM)
K_ROWS = slice(ATT_DIM, 2 * ATT_DIM)
V_ROWS = slice(2 * ATT_DIM, 3 * ATT_DIM)


def pack_kernel(info, q_in, k_in, v_in, q_own, kv_own, all_1, all_2, all_3, raw, rows_ref, sems):
    copies = [pltpu.make_async_copy(src, raw.at[i], sems.at[i]) for i, src in enumerate((q_in, k_in, v_in))]
    for copy in copies:
        copy.start()
    for i, (out, first) in enumerate(((q_own, 0), (kv_own, 0), (kv_own, ATT_DIM))):
        copies[i].wait()
        rows_ref[i] = raw[i].T
        out[first : first + ATT_DIM, :] = rows_ref[i, head_rows(info[0]), :]
        for r, away in ((1, all_1), (2, all_2), (3, all_3)):
            away[i * ATT_DIM : (i + 1) * ATT_DIM, :] = rows_ref[i, head_rows(info[0] ^ r), :]


def unpack_kernel(info, *refs):
    pieces, out_ref, rows_ref = refs[:4], refs[4], refs[5]
    for r in range(4):
        rows_ref[head_rows(info[0] ^ r), :] = pieces[r][...]
    out_ref[...] = rows_ref[...].T


def attend_kernel(own, info, *refs):
    hid, kind, core = info[0], info[1], info[2]
    scale = ATT_DIM ** (-0.5) * LOG2E

    if own:
        queries, pieces, refs = refs[:4], refs[4:12], refs[12:]
        acc, stats_out, qs, mark, ks, vs = refs
        for r in range(4):
            qs[r] = queries[r][Q_ROWS, :]
        for i, piece in enumerate(pieces):
            k_first = ATT_DIM if i & 3 else 0
            v_first = k_first + ATT_DIM
            start = pl.multiple_of((core ^ (i >> 2)) * TOK, TOK)
            ks[hid ^ (i & 3), pl.ds(start, TOK), :] = piece[k_first:v_first, :].T
            vs[hid ^ (i & 3), :, pl.ds(start, TOK)] = piece[v_first : v_first + ATT_DIM, :]
    else:
        pieces, refs = refs[:8], refs[8:]
        _, queries, acc_in, stats_in, *o_out, mark, qs, ks, vs, raw, acc, os, sems = refs
        loads = [
            pltpu.make_async_copy(queries, qs, sems.at[16]),
            pltpu.make_async_copy(acc_in, acc, sems.at[17]),
        ]
        key_loads, value_loads = [], []
        for i, piece in enumerate(pieces):
            start = pl.multiple_of((core ^ (i >> 2)) * TOK, TOK)
            key_loads.append(pltpu.make_async_copy(piece.at[0:ATT_DIM, :], raw.at[i], sems.at[i]))
            value_loads.append(
                pltpu.make_async_copy(
                    piece.at[ATT_DIM : 2 * ATT_DIM, :],
                    vs.at[hid ^ (i & 3), :, pl.ds(start, TOK)],
                    sems.at[8 + i],
                )
            )
        for load in key_loads + loads + value_loads:
            load.start()
        for i, load in enumerate(key_loads):
            load.wait()
            start = pl.multiple_of((core ^ (i >> 2)) * TOK, TOK)
            ks[hid ^ (i & 3), pl.ds(start, TOK), :] = raw[i].T
        for load in loads + value_loads:
            load.wait()
    mark[...] = jnp.zeros_like(mark)

    def one_queries(r, carry):
        chip = hid ^ r

        def visit(keys, values, stats, masked):
            lanes = [slice(half * HALF, (half + 1) * HALF) for half in range(2)]
            scores = [
                jnp.dot(keys, qs[r, :, lanes[half]], preferred_element_type=F32) for half in range(2)
            ]
            new_stats, low, shrinks = [], [], []
            for half in range(2):
                (top, total), s = stats[half], scores[half]
                if masked:
                    k_pos = lax.broadcasted_iota(jnp.int32, s.shape, 0)
                    q_pos = lax.broadcasted_iota(jnp.int32, s.shape, 1) + half * HALF
                    s = jnp.where(k_pos <= q_pos, s, -1e30)
                new_top = jnp.maximum(top, jnp.max(s, axis=0, keepdims=True))
                p = jnp.exp2((s - new_top) * scale)
                shrink = jnp.exp2((top - new_top) * scale)
                total = total * shrink + jnp.sum(p, axis=0, keepdims=True)
                new_stats.append((new_top, total))
                low.append(p.astype(BF16))
                shrinks.append(shrink)
            for half in range(2):
                acc[r, :, lanes[half]] = acc[r, :, lanes[half]] * shrinks[half] + jnp.dot(
                    values, low[half], preferred_element_type=F32
                )
            return tuple(new_stats)

        def chip_block(j, stats):
            return visit(ks[j], vs[j], stats, False)

        def core_block(start, stats, masked):
            start = pl.multiple_of(start, TOK)
            return visit(
                ks[chip, pl.ds(start, TOK), :], vs[chip, :, pl.ds(start, TOK)], stats, masked
            )

        if own:
            acc[r] = jnp.zeros((ATT_DIM, TOK), F32)
            first = (jnp.full((1, HALF), -1e30, F32), jnp.zeros((1, HALF), F32))
            stats = lax.fori_loop(0, chip, chip_block, (first, first))
            stats = lax.fori_loop(0, core, lambda k, now: core_block(0, now, False), stats)
            stats = core_block(core * TOK, stats, True)
            for half in range(2):
                lanes = slice(half * HALF, (half + 1) * HALF)
                stats_out[r, 0:8, lanes] = jnp.broadcast_to(stats[half][0], (8, HALF))
                stats_out[r, 8:16, lanes] = jnp.broadcast_to(stats[half][1], (8, HALF))
        else:
            stats = tuple(
                (
                    stats_in[r, 0:1, half * HALF : (half + 1) * HALF],
                    stats_in[r, 8:9, half * HALF : (half + 1) * HALF],
                )
                for half in range(2)
            )
            count = jnp.where(kind == 0, ((chip + 1) >> 1) * 2, (chip >> 1) * 2 + 1)
            stats = lax.fori_loop(0, count, chip_block, stats)
            for half in range(2):
                lanes = slice(half * HALF, (half + 1) * HALF)
                os[r, :, lanes] = (acc[r, :, lanes] / stats[half][1]).astype(BF16)
        return carry

    lax.fori_loop(0, 4, one_queries, 0)
    if not own:
        for r in range(4):
            o_out[r][...] = os[r]


def pair_of(low, columns, h):
    return jnp.where(low, columns[:, h : h + 1], columns[:, h + 1 : h + 2])


def softplus(v):
    return jnp.maximum(v, 0.0) + jnp.log1p(jnp.exp(-jnp.abs(v)))


SPAN = slice(STATE_DIM, STATE_DIM + 8)
SPAN_LOW = slice(STATE_DIM + 8, STATE_DIM + 16)
HELD, SENT = STATE_DIM + 8, STATE_DIM + 16


def send_state(pay_ref, lanes, state, span):
    span_high = span.astype(BF16)
    pay_ref[0:STATE_DIM, lanes] = state.astype(BF16)
    pay_ref[STATE_DIM:SENT, lanes] = jnp.concatenate(
        [span_high.astype(F32), span - span_high.astype(F32)], axis=0
    ).astype(BF16)


def ssm_local_kernel(
    x_ref, write_t_ref, read_t_ref, step_t_ref, rate_ref, gain_ref, out_ref, total_ref, pay_ref, cum_ref
):
    heads = step_t_ref.shape[0]
    high = lax.Precision.HIGHEST
    row = lax.broadcasted_iota(jnp.int32, (TOK, TOK), 0)
    col = lax.broadcasted_iota(jnp.int32, (TOK, TOK), 1)
    rate = jnp.broadcast_to(-jnp.exp(rate_ref[...]) * LOG2E, (8, heads)).T[:, 0:1]
    step_t = softplus(step_t_ref[...])
    cum_t = jnp.dot(
        rate * step_t, jnp.where(row <= col, 1.0, 0.0), precision=high, preferred_element_type=F32
    )
    key_row = jnp.log2(step_t) - cum_t
    cum = cum_t.T
    step = step_t.T
    cum_ref[...] = cum
    last = cum[TOK - 1 : TOK, :]
    tail = jnp.exp2(last - cum) * step
    gain = gain_ref[...]

    near = lax.dot_general(
        read_t_ref[...], write_t_ref[...], (((0,), (0,)), ((), ())), preferred_element_type=F32
    )
    near = jnp.where(col <= row, near, 0.0)
    low = lax.broadcasted_iota(jnp.int32, (1, 128), 1) < SSM_DIM
    for h in range(0, heads, 2):
        lanes = slice(h * SSM_DIM, (h + 2) * SSM_DIM)
        x_pair = x_ref[:, lanes]
        x_f = x_pair.astype(F32)
        weighted = (x_f * pair_of(low, tail, h)).astype(BF16)
        state = jnp.dot(write_t_ref[...], weighted, preferred_element_type=F32)
        span = jnp.broadcast_to(pair_of(low, last, h), (8, 128))
        total_ref[0:STATE_DIM, lanes] = state
        total_ref[SPAN, lanes] = span
        send_state(pay_ref, lanes, state, span)
        for t in range(2):
            t_rows = slice(t * HALF, (t + 1) * HALF)
            both = []
            for k in range(2):
                total = None
                for s in range(t + 1):
                    s_rows = slice(s * HALF, (s + 1) * HALF)
                    weights = (
                        jnp.exp2(cum[t_rows, h + k : h + k + 1] + key_row[h + k : h + k + 1, s_rows])
                        * near[t_rows, s_rows]
                    )
                    part = jnp.dot(weights.astype(BF16), x_pair[s_rows, :], preferred_element_type=F32)
                    total = part if total is None else total + part
                both.append(total)
            out_ref[t_rows, lanes] = (
                jnp.where(low, both[0], both[1]) + pair_of(low, gain, h) * x_f[t_rows, :]
            )


def ssm_merge_kernel(level, info, got_ref, total_ref, before_ref, total_out, before_out, pay_ref):
    later = ((info[3] >> level) & 1).astype(F32)
    got = got_ref[0:STATE_DIM, :].astype(F32)
    got_span = got_ref[STATE_DIM:SENT, :].astype(F32)
    got_span = got_span[0:8, :] + got_span[8:16, :]
    total, total_span = total_ref[0:STATE_DIM, :], total_ref[SPAN, :]
    before, before_span = before_ref[0:STATE_DIM, :], before_ref[SPAN, :]
    before_out[0:STATE_DIM, :] = before + later * (got * jnp.exp2(before_span[0:1, :]))
    before_out[SPAN, :] = before_span + later * got_span
    after_got = got * jnp.exp2(total_span[0:1, :]) + total
    after_total = total * jnp.exp2(got_span[0:1, :]) + got
    total = later * after_got + (1.0 - later) * after_total
    span = total_span + got_span
    total_out[0:STATE_DIM, :] = total
    total_out[SPAN, :] = span
    send_state(pay_ref, slice(None), total, span)


def ssm_carry_kernel(state_ref, mixed_ref, cum_ref, read_t_ref, gate_ref, gated_ref, square_ref):
    heads = cum_ref.shape[1]
    state = state_ref[0:STATE_DIM, :]
    state_high = state.astype(BF16)
    state_low = (state - state_high.astype(F32)).astype(BF16)
    reach = jnp.exp2(cum_ref[...])
    read = read_t_ref[...].T
    low = lax.broadcasted_iota(jnp.int32, (1, 128), 1) < SSM_DIM
    squares = jnp.zeros((TOK, 128), F32)
    for h in range(0, heads, 2):
        lanes = slice(h * SSM_DIM, (h + 2) * SSM_DIM)
        carried = jnp.dot(read, state_high[:, lanes], preferred_element_type=F32)
        carried = carried + jnp.dot(read, state_low[:, lanes], preferred_element_type=F32)
        mixed = mixed_ref[:, lanes] + carried * pair_of(low, reach, h)
        gate = gate_ref[:, lanes].astype(F32)
        gated = mixed * (gate / (1.0 + jnp.exp(-gate)))
        gated_ref[:, lanes] = gated
        squares = squares + gated * gated
    square_ref[...] = jnp.broadcast_to(jnp.sum(squares.T, axis=0, keepdims=True), square_ref.shape)


def vmem(count):
    return [pl.BlockSpec(memory_space=pltpu.VMEM)] * count


SMEM = pl.BlockSpec(memory_space=pltpu.SMEM)
ANY = pl.BlockSpec(memory_space=pl.ANY)


SMALL = pl.CostEstimate(flops=1000, bytes_accessed=1000, transcendentals=0)


def params(mib):
    return pltpu.CompilerParams(vmem_limit_bytes=mib * 1024 * 1024)


def shape(dims, kind):
    return jax.ShapeDtypeStruct(dims, kind)


def pack(info, query_rows, key_rows, value_rows):
    width = HEADS * ATT_DIM
    rows = [ATT_DIM, 2 * ATT_DIM] + [3 * ATT_DIM] * 3
    return pl.pallas_call(
        pack_kernel,
        out_shape=[shape((count, TOK), BF16) for count in rows],
        in_specs=[SMEM] + [ANY] * 3,
        out_specs=vmem(len(rows)),
        scratch_shapes=[
            pltpu.VMEM((3, TOK, width), BF16),
            pltpu.VMEM((3, width, TOK), BF16),
            pltpu.SemaphoreType.DMA((3,)),
        ],
        compiler_params=params(60),
    )(info, query_rows, key_rows, value_rows)


def attend(own, info, *operands):
    queries = pltpu.VMEM((4, ATT_DIM, TOK), BF16)
    scratch = [pltpu.VMEM((4, 2 * TOK, ATT_DIM), BF16), pltpu.VMEM((4, ATT_DIM, 2 * TOK), BF16)]
    if own:
        out = [shape((4, ATT_DIM, TOK), F32), shape((4, 16, TOK), F32), shape((4, ATT_DIM, TOK), BF16)]
        specs = vmem(len(operands))
    else:
        out = [shape((ATT_DIM, TOK), BF16)] * 4
        scratch = [queries] + scratch + [
            pltpu.VMEM((8, ATT_DIM, TOK), BF16),
            pltpu.VMEM((4, ATT_DIM, TOK), F32),
            queries,
            pltpu.SemaphoreType.DMA((18,)),
        ]
        specs = [ANY] * (len(operands) - 1) + vmem(1)
    out = out + [shape((8, 128), F32)]
    return pl.pallas_call(
        functools.partial(attend_kernel, own),
        out_shape=out,
        in_specs=[SMEM] + specs,
        out_specs=vmem(len(out)),
        scratch_shapes=scratch,
        compiler_params=params(24),
        cost_estimate=SMALL,
    )(info, *operands)


def unpack(info, pieces):
    width = HEADS * ATT_DIM
    return pl.pallas_call(
        unpack_kernel,
        out_shape=shape((TOK, width), BF16),
        in_specs=[SMEM] + vmem(4),
        out_specs=vmem(1)[0],
        scratch_shapes=[pltpu.VMEM((width, TOK), BF16)],
        compiler_params=params(40),
    )(info, *pieces)


def ssm_local(ssm_inputs, write_t, read_t, step_t, rate, gain):
    tokens, width = ssm_inputs.shape
    heads = step_t.shape[0]
    return pl.pallas_call(
        ssm_local_kernel,
        out_shape=[
            shape((tokens, width), F32),
            shape((HELD, width), F32),
            shape((SENT, width), BF16),
            shape((tokens, heads), F32),
        ],
        in_specs=vmem(6),
        out_specs=vmem(4),
        compiler_params=params(40),
        cost_estimate=SMALL,
    )(ssm_inputs, write_t, read_t, step_t, rate, gain)


def ssm_merge(level, info, got, total, before):
    held, sent = shape(total.shape, F32), shape(got.shape, BF16)
    return pl.pallas_call(
        functools.partial(ssm_merge_kernel, level),
        out_shape=[held, held, sent],
        in_specs=[SMEM] + vmem(3),
        out_specs=vmem(3),
        compiler_params=params(40),
        cost_estimate=SMALL,
    )(info, got, total, before)


def ssm_carry(state, mixed, cum, read_t, gate):
    tokens, width = mixed.shape
    return pl.pallas_call(
        ssm_carry_kernel,
        out_shape=[shape((tokens, width), F32), shape((8, tokens), F32)],
        in_specs=vmem(5),
        out_specs=vmem(2),
        compiler_params=params(40),
        cost_estimate=SMALL,
    )(state, mixed, cum, read_t, gate)


def on_device(
    query_rows,
    key_rows,
    value_rows,
    ssm_inputs,
    ssm_gate,
    write_vecs,
    read_vecs,
    step_raw,
    decay_log,
    skip_gain,
    norm_gain,
):
    me = lax.axis_index("ctx")
    y, x, core = me >> 3, (me >> 1) & 3, me & 1
    info = jnp.stack([y * 2 + (x >> 1), (x ^ (x >> 1)) & 1, core, me]).astype(jnp.int32)
    tie = lax.optimization_barrier

    q_own, kv_own, *away = pack(info, query_rows, key_rows, value_rows)
    here, near, from_core = [None] * 4, [None] * 4, [None] * 4
    here[0] = kv_own
    here[1], here[2] = head_swap(away[0], 1), head_swap(away[1], 2)
    near[0] = class_swap(kv_own)
    from_core[0] = core_swap(kv_own)

    from_core[0], ssm_inputs = tie((from_core[0], ssm_inputs))
    read_t = read_vecs.T
    mixed, total, sent, cum = ssm_local(
        ssm_inputs, write_vecs.T, read_t, step_raw.T, decay_log[None, :], skip_gain[None, :]
    )
    before = jnp.zeros_like(total)
    total, before, sent = ssm_merge(0, info, core_swap(sent), total, before)
    total, before, sent = ssm_merge(1, info, class_swap(sent), total, before)

    here[1], here[2], near[0], away[2], sent = tie((here[1], here[2], near[0], away[2], sent))
    got = block_swap(sent, 4)
    here[3] = head_swap(away[2], 3)
    for r in (1, 2):
        near[r] = class_swap(here[r][ATT_DIM:])
    from_core[1] = core_swap(here[1])
    from_core[1], piece = tie((from_core[1], here[2]))
    from_core[2] = core_swap(piece)

    here[3], near[1], near[2], got = tie((here[3], near[1], near[2], got))
    near[3] = class_swap(here[3][ATT_DIM:])
    from_core[3] = core_swap(here[3])
    total, before, sent = ssm_merge(2, info, got, total, before)
    got = block_swap(sent, 8)
    partial, stats, queries, mark = attend(True, info, q_own, *here[1:], *here, *from_core)

    near[3], got, mark = tie((near[3], got, mark))
    near_core = [core_swap(piece) for piece in near]
    total, before, sent = ssm_merge(3, info, got, total, before)
    gated, squares = ssm_carry(before, mixed, cum, read_t, ssm_gate)
    squares = lax.all_gather(squares, "tp")
    *results, _ = attend(False, info, *near, *near_core, mark, queries, partial, stats)
    back = [results[0]] + [head_swap(results[r], r) for r in range(1, 4)]
    back[1], squares = tie((back[1], squares))
    factor = lax.rsqrt(jnp.sum(squares[:, 0], axis=0) / SSM_WIDTH + 1e-05)
    mixer_out = (gated * factor[:, None] * norm_gain[None, :]).astype(BF16)
    return (unpack(info, back), mixer_out)


def solution(mesh):
    placed = (
        P("ctx", "tp"),
        P("ctx", "tp"),
        P("ctx", "tp"),
        P("ctx", "tp"),
        P("ctx", "tp"),
        P("ctx", None),
        P("ctx", None),
        P("ctx", "tp"),
        P("tp"),
        P("tp"),
        P("tp"),
    )
    return jax.shard_map(
        on_device,
        mesh=mesh,
        in_specs=placed,
        out_specs=(P("ctx", "tp"), P("ctx", "tp")),
        check_vma=False,
    )
```

time: 178 us -> 138 us (0.78); the launches traced: 175 us -> 138 us
  blocking collectives: 0 us -> 35.3 us
  waiting for transfers between devices: 63.1 us -> 38.2 us
  local copies, waits for them, and re-layouts: 16 us -> 0.16 us
  starting transfers between devices: 36.5 us -> 22.3 us
  between operations: 14.4 us -> 0.96 us
  Pallas kernels: 43.6 us -> 39.3 us
    all_gather x0 -> x1, blocking collectives: none -> 35.3 us  [on_device(): squares = lax.all_gather(squares, 'tp')]
    ppermute x9 -> x6, waiting for transfers between devices: 30.6 us -> 4.43 us  [head_swap(): lax.ppermute(value, 'ctx', [(i, exchanged(i, r)) for i in range(CTX)])]
    ppermute x7 -> x2, waiting for transfers between devices: 0.93 us -> 23.3 us  [block_swap(): return lax.ppermute(value, 'ctx', [(i, i ^ step) for i in range(CTX)])]
    ppermute x4 -> x5, waiting for transfers between devices: 29.8 us -> 7.64 us  [class_swap(): return lax.ppermute(value, 'ctx', [(i, i ^ 2) for i in range(CTX)])]
    unnamed x73 -> x24, local copies, waits for them, and re-layouts: 14.4 us -> 0.05 us
    ppermute x7 -> x2, starting transfers between devices: 14.5 us -> 2 us  [block_swap(): return lax.ppermute(value, 'ctx', [(i, i ^ step) for i in range(CTX)])]
    ppermute x9 -> x6, starting transfers between devices: 18 us -> 11.6 us  [head_swap(): lax.ppermute(value, 'ctx', [(i, exchanged(i, r)) for i in range(CTX)])]
    pallas_call x5 -> x10, Pallas kernels: 43.6 us -> 39.3 us  [the longest x2 24.6 us: attend(): pl.pallas_call(functools.partial(attend_kernel, own), out_shape=out, in_s...]
  transfers between devices with their start and end apart: 29 -> 22, of which waited for: 10 -> 6; matrix products, arithmetic and copies ran while one was open for 0% -> 1% of each run, Pallas kernels for 22% -> 14%
where the time goes in v2:
time: 138 us
  Pallas kernels  39.3 us (28%)
  waiting for transfers between devices  38.2 us (28%)
  blocking collectives  35.3 us (26%)
  starting transfers between devices  22.3 us (16%)
  other arithmetic  1.74 us (1%)
    all_gather x1, blocking collectives, on_device(): squares = lax.all_gather(squares, 'tp')  35.3 us
    pallas_call x2, Pallas kernels, attend(): pl.pallas_call(functools.partial(attend_kernel, own), out_shape=out, in_s...  24.6 us
    ppermute x2, waiting for transfers between devices, block_swap(): return lax.ppermute(value, 'ctx', [(i, i ^ step) for i in range(CTX)])  23.3 us
    ppermute x6, starting transfers between devices, head_swap(): lax.ppermute(value, 'ctx', [(i, exchanged(i, r)) for i in range(CTX)])  11.6 us
    ppermute x5, waiting for transfers between devices, class_swap(): return lax.ppermute(value, 'ctx', [(i, i ^ 2) for i in range(CTX)])  7.64 us
    ppermute x6, waiting for transfers between devices, head_swap(): lax.ppermute(value, 'ctx', [(i, exchanged(i, r)) for i in range(CTX)])  4.43 us
    pallas_call x1, Pallas kernels, pack(): pl.pallas_call(pack_kernel, out_shape=[shape((count, TOK), BF16) for coun...  4.42 us
    ppermute x5, starting transfers between devices, class_swap(): return lax.ppermute(value, 'ctx', [(i, i ^ 2) for i in range(CTX)])  4.36 us
  transfers between devices with their start and end apart: 22, of which 6 were waited for; matrix products, arithmetic and copies ran while one was open for 1% of the time, Pallas kernels for 14%

profile of v2, /device:TPU:0, one launch (start us, length us, event | category | flops | bytes accessed | tf_op | source)
XLA Modules:
  0.0 138.0 jit_solution(11889447339805817967)
XLA Ops:
  0.6 0.0 copy-start
  0.6 0.0 copy-start.3
  0.7 0.0 copy-start.5
  0.7 0.6 pad_add_fusion.info
  1.3 4.4 %shard_map.122 = (bf16[224,512]{1,0:T(8,128)(2,1)}, bf16[448,512]{1,0:T(8,128)(2,1)}, bf16[672,512]{1,0:T(8,128)(2,1)}, bf16[672,512]{1,0:T(8,128)(2,1)}, bf16[672,512]{1,0:T(8,128)(2,1)}) custom-call(s32[4]{0:T(128)} %pad_add_fusion.info, bf16[512,896]{1,0:T(8,128)(2,1)} %q_in.1, bf16[512,896]{1,0:T(8,128)(2,1)} %k_in.1, bf16[512,896]{1,0:T(8,128)(2,1)} %v_in.1), custom_call_target="tpu_custom_call" | custom-call | tf_op jit(solution)/shard_map/pallas_call | solution.py:324
  5.7 0.1 collective-permute-start.3
  5.8 2.9 %collective-permute-start = (bf16[672,512]{1,0:T(8,128)(2,1)}, bf16[672,512]{1,0:T(8,128)(2,1)S(1)}, u32[]{:S(2)}, u32[]{:S(2)}) collective-permute-start(bf16[672,512]{1,0:T(8,128)(2,1)} %get-tuple-element.49), channel_id=1, source_target_pairs={{0,48},{8,56},{16,32},{24,40},{32,16},{40,24},{48,0},{56,8},{64,11... | collective-permute-start | bytes 2064392 | tf_op jit(solution)/shard_map/ppermute | solution.py:34
  8.7 1.6 %collective-permute-start.1 = (bf16[672,512]{1,0:T(8,128)(2,1)}, bf16[672,512]{1,0:T(8,128)(2,1)S(1)}, u32[]{:S(2)}, u32[]{:S(2)}) collective-permute-start(bf16[672,512]{1,0:T(8,128)(2,1)} %get-tuple-element.50), channel_id=1, source_target_pairs={{0,64},{8,72},{16,80},{24,88},{32,96},{40,104},{48,112},{56,120},{... | collective-permute-start | bytes 2064392 | tf_op jit(solution)/shard_map/ppermute | solution.py:34
  10.3 0.2 collective-permute-start.2
  10.5 0.0 collective-permute-done.3.refs_8_
  10.6 3.6 %shard_map.123 = (f32[512,896]{1,0:T(8,128)S(1)}, f32[72,896]{1,0:T(8,128)S(1)}, bf16[80,896]{1,0:T(8,128)(2,1)S(1)}, f32[512,14]{1,0:T(8,128)S(1)}) custom-call(bf16[512,896]{1,0:T(8,128)(2,1)S(1)} %copy-done, bf16[64,512]{1,0:T(8,128)(2,1)S(1)} %bitcast.12, bf16[64,512]{1,0:T(8,128)(2,1)S(1)} %bitcast.10, f32[14,512]{1,0:T(8,128)S(1)} %bitcast.13, ...), custom_call_target="tpu_custom_call" | custom-call | flops 1000 | bytes 1000 | tf_op jit(solution)/shard_map/pallas_call | solution.py:380
  14.2 0.1 collective-permute-start.4
  14.3 1.4 collective-permute-done.4.got_ref
  15.7 0.0 copy-done.6
  15.7 0.7 shard_map.124
  16.4 1.9 %collective-permute-start.5 = (bf16[80,896]{1,0:T(8,128)(2,1)S(1)}, bf16[80,896]{1,0:T(8,128)(2,1)S(1)}, u32[]{:S(2)}, u32[]{:S(2)}) collective-permute-start(bf16[80,896]{1,0:T(8,128)(2,1)S(1)} %get-tuple-element.56), channel_id=1, source_target_pairs={{0,16},{8,24},{16,0},{24,8},{32,48},{40,56},{48,32},{56,40},{64,80... | collective-permute-start | bytes 430088 | tf_op jit(solution)/shard_map/ppermute | solution.py:38
  18.2 7.6 %collective-permute-done.5.got_ref = bf16[80,896]{1,0:T(8,128)(2,1)S(1)} collective-permute-done((bf16[80,896]{1,0:T(8,128)(2,1)S(1)}, bf16[80,896]{1,0:T(8,128)(2,1)S(1)}, u32[]{:S(2)}, u32[]{:S(2)}) %collective-permute-start.5) | collective-permute-done | bytes 143392 | tf_op jit(solution)/shard_map/ppermute | solution.py:38
  25.9 0.7 shard_map.125
  26.6 0.0 collective-permute-done.2.refs_0_
  26.6 0.0 collective-permute-done.refs_1_.refs_5_
  26.6 0.0 collective-permute-done.1.refs_2_.refs_6_
  26.6 0.1 collective-permute-start.12
  26.7 0.0 copy-done.11
  26.7 2.3 %collective-permute-start.6 = (bf16[672,512]{1,0:T(8,128)(2,1)S(1)}, bf16[672,512]{1,0:T(8,128)(2,1)S(1)}, u32[]{:S(2)}, u32[]{:S(2)}) collective-permute-start(bf16[672,512]{1,0:T(8,128)(2,1)S(1)} %copy-done.11), channel_id=1, source_target_pairs={{0,112},{8,120},{16,96},{24,104},{32,80},{40,88},{48,64},{56,72},{... | collective-permute-start | bytes 2064392 | tf_op jit(solution)/shard_map/ppermute | solution.py:34
  29.1 0.1 collective-permute-start.7
  29.2 2.1 %collective-permute-start.8 = (bf16[448,512]{1,0:T(8,128)(2,1)S(1)}, bf16[448,512]{1,0:T(8,128)(2,1)S(1)}, u32[]{:S(2)}, u32[]{:S(2)}) collective-permute-start(bf16[448,512]{1,0:T(8,128)(2,1)S(1)} %slice.13), channel_id=1, source_target_pairs={{0,16},{8,24},{16,0},{24,8},{32,48},{40,56},{48,32},{56,40},{64,80... | collective-permute-start | bytes 1376264 | tf_op jit(solution)/shard_map/ppermute | solution.py:38
  31.3 1.2 collective-permute-start.9
  32.5 0.0 collective-permute-done.12.refs_9_
  32.5 0.0 collective-permute-start.13
  32.5 23.3 %collective-permute-done.9.got_ref = bf16[80,896]{1,0:T(8,128)(2,1)S(1)} collective-permute-done((bf16[80,896]{1,0:T(8,128)(2,1)S(1)}, bf16[80,896]{1,0:T(8,128)(2,1)S(1)}, u32[]{:S(2)}, u32[]{:S(2)}) %collective-permute-start.9) | collective-permute-done | bytes 143392 | tf_op jit(solution)/shard_map/ppermute | solution.py:46
  55.8 0.0 collective-permute-done.7.refs_1_
  55.8 0.0 collective-permute-done.8.refs_2_
  55.8 0.0 collective-permute-done.6.refs_3_.refs_7_
  55.8 0.1 collective-permute-start.14
  55.9 0.1 collective-permute-start.10
  56.0 0.7 shard_map.126
  56.7 0.8 collective-permute-start.11
  57.5 0.2 collective-permute-start.15
  57.7 0.0 collective-permute-done.13.refs_10_
  57.7 0.3 collective-permute-start.16
  58.0 0.0 collective-permute-done.14.refs_11_
  58.0 0.2 collective-permute-start.17
  58.3 0.0 copy-done.4
  58.3 10.8 %shard_map.127 = (f32[4,224,512]{2,1,0:T(8,128)S(1)}, f32[4,16,512]{2,1,0:T(8,128)S(1)}, bf16[4,224,512]{2,1,0:T(8,128)(2,1)S(1)}, f32[8,128]{1,0:T(8,128)S(1)}) custom-call(s32[4]{0:T(128)S(1)} %copy-done.6, bf16[224,512]{1,0:T(8,128)(2,1)S(1)} %copy-done.4, bf16[672,512]{1,0:T(8,128)(2,1)S(1)} %collective-permute-done.refs_1_.refs_5_, ...), custom_call_target="tpu_custom_call" | custom-call | flops 1000 | bytes 1000 | tf_op jit(solution)/shard_map/pallas_call | solution.py:354
  69.0 0.0 collective-permute-done.11.got_ref
  69.0 0.0 collective-permute-done.10.refs_3_
  69.0 3.3 %collective-permute-start.18 = (bf16[448,512]{1,0:T(8,128)(2,1)S(1)}, bf16[448,512]{1,0:T(8,128)(2,1)S(1)}, u32[]{:S(2)}, u32[]{:S(2)}) collective-permute-start(bf16[448,512]{1,0:T(8,128)(2,1)S(1)} %collective-permute-done.10.refs_3_), channel_id=1, source_target_pairs={{0,8},{8,0},{16,24},{24,16},{32,40},{40,32},{48,56},{56,48},{64,72... | collective-permute-start | bytes 1376264 | tf_op jit(solution)/shard_map/ppermute | solution.py:42
  72.3 0.0 collective-permute-done.15.refs_4_
  72.3 0.0 collective-permute-done.16.refs_5_
  72.3 0.0 collective-permute-done.17.refs_6_
  72.3 1.4 %collective-permute-done.18.refs_7_ = bf16[448,512]{1,0:T(8,128)(2,1)S(1)} collective-permute-done((bf16[448,512]{1,0:T(8,128)(2,1)S(1)}, bf16[448,512]{1,0:T(8,128)(2,1)S(1)}, u32[]{:S(2)}, u32[]{:S(2)}) %collective-permute-start.18) | collective-permute-done | bytes 458784 | tf_op jit(solution)/shard_map/ppermute | solution.py:42
  73.8 13.9 %shard_map.128 = (bf16[224,512]{1,0:T(8,128)(2,1)S(1)}, bf16[224,512]{1,0:T(8,128)(2,1)S(1)}, bf16[224,512]{1,0:T(8,128)(2,1)S(1)}, bf16[224,512]{1,0:T(8,128)(2,1)S(1)}, f32[8,128]{1,0:T(8,128)}) custom-call(s32[4]{0:T(128)S(1)} %copy-done.6, bf16[448,512]{1,0:T(8,128)(2,1)S(1)} %collective-permute-done.2.refs_0_, ...), custom_call_target="tpu_custom_call" | custom-call | flops 1000 | bytes 1000 | tf_op jit(solution)/shard_map/pallas_call | solution.py:354
  87.6 1.6 %collective-permute-start.19 = (bf16[224,512]{1,0:T(8,128)(2,1)S(1)}, bf16[224,512]{1,0:T(8,128)(2,1)S(1)}, u32[]{:S(2)}, u32[]{:S(2)}) collective-permute-start(bf16[224,512]{1,0:T(8,128)(2,1)S(1)} %get-tuple-element.83), channel_id=1, source_target_pairs={{0,48},{8,56},{16,32},{24,40},{32,16},{40,24},{48,0},{56,8},{64,11... | collective-permute-start | bytes 688136 | tf_op jit(solution)/shard_map/ppermute | solution.py:34
  89.2 1.4 shard_map.129
  90.6 0.0 copy-done.1
  90.6 1.4 %shard_map.130 = (f32[512,896]{1,0:T(8,128)S(1)}, f32[8,512]{1,0:T(8,128)S(1)}) custom-call(f32[72,896]{1,0:T(8,128)S(1)} %get-tuple-element.87.state_ref, f32[512,896]{1,0:T(8,128)S(1)} %get-tuple-element.88.mixed_ref, f32[512,14]{1,0:T(8,128)S(1)} %get-tuple-element.89.cum_ref, bf16[64,512]{1,0:T(8,128)(2,1)S(1)} %bitcast.11, bf16[512,896]{1,0:T(8,128)(2,1)S(1)} %copy-done.1), custom_call_target="tpu_custom_call" | custom-call | flops 1000 | bytes 1000 | tf_op jit(solution)/shard_map/pallas_call | solution.py:409
  92.0 35.3 %all-gather = f32[64,512]{1,0:T(8,128)S(1)} all-gather(f32[8,512]{1,0:T(8,128)S(1)} %get-tuple-element.90), channel_id=2, replica_groups=mesh['ctx'=16,'tp'=8] {'tp'}, dimensions={0}, use_global_device_ids=true | all-gather | bytes 147456 | tf_op jit(solution)/shard_map/all_gather | solution.py:473
  127.3 0.7 collective-permute-start.20
  128.0 2.5 %collective-permute-start.21 = (bf16[224,512]{1,0:T(8,128)(2,1)S(1)}, bf16[224,512]{1,0:T(8,128)(2,1)S(1)}, u32[]{:S(2)}, u32[]{:S(2)}) collective-permute-start(bf16[224,512]{1,0:T(8,128)(2,1)S(1)} %get-tuple-element.93), channel_id=1, source_target_pairs={{0,112},{8,120},{16,96},{24,104},{32,80},{40,88},{48,64},{56,72},{... | collective-permute-start | bytes 688136 | tf_op jit(solution)/shard_map/ppermute | solution.py:34
  130.6 0.0 collective-permute-done.19.refs_1_
  130.6 1.1 multiply_convert_fusion
  131.8 1.6 %collective-permute-done.20.refs_2_ = bf16[224,512]{1,0:T(8,128)(2,1)S(1)} collective-permute-done((bf16[224,512]{1,0:T(8,128)(2,1)S(1)}, bf16[224,512]{1,0:T(8,128)(2,1)S(1)}, u32[]{:S(2)}, u32[]{:S(2)}) %collective-permute-start.20) | collective-permute-done | bytes 229408 | tf_op jit(solution)/shard_map/ppermute | solution.py:34
  133.4 2.8 %collective-permute-done.21.refs_3_ = bf16[224,512]{1,0:T(8,128)(2,1)S(1)} collective-permute-done((bf16[224,512]{1,0:T(8,128)(2,1)S(1)}, bf16[224,512]{1,0:T(8,128)(2,1)S(1)}, u32[]{:S(2)}, u32[]{:S(2)}) %collective-permute-start.21) | collective-permute-done | bytes 229408 | tf_op jit(solution)/shard_map/ppermute | solution.py:34
  136.2 1.8 %shard_map.131 = bf16[512,896]{1,0:T(8,128)(2,1)} custom-call(s32[4]{0:T(128)S(1)} %copy-done.6, bf16[224,512]{1,0:T(8,128)(2,1)S(1)} %get-tuple-element.82.refs_0_, bf16[224,512]{1,0:T(8,128)(2,1)S(1)} %collective-permute-done.19.refs_1_, bf16[224,512]{1,0:T(8,128)(2,1)S(1)} %collective-permute-done.20.refs_2_, ...), custom_call_target="tpu_custom_call" | custom-call | tf_op jit(solution)/shard_map/pallas_call | solution.py:367
  (23 shorter events, 0.2 us)
Async XLA Ops:
  0.6 9.9 %copy-start = (bf16[512,896]{1,0:T(8,128)(2,1)S(1)}, bf16[512,896]{1,0:T(8,128)(2,1)}, u32[]{:S(2)}) copy-start(bf16[512,896]{1,0:T(8,128)(2,1)} %x_ref) | copy-start | bytes 2752516
  0.6 9.9 %copy-start.3 = (bf16[512,64]{0,1:T(8,128)(2,1)S(1)}, bf16[512,64]{0,1:T(8,128)(2,1)}, u32[]{:S(2)}) copy-start(bf16[512,64]{0,1:T(8,128)(2,1)} %param.17) | copy-start | bytes 196612
  0.7 9.9 %copy-start.5 = (bf16[512,64]{0,1:T(8,128)(2,1)S(1)}, bf16[512,64]{0,1:T(8,128)(2,1)}, u32[]{:S(2)}) copy-start(bf16[512,64]{0,1:T(8,128)(2,1)} %param.16) | copy-start | bytes 196612
  0.7 9.9 %copy-start.7 = (f32[512,14]{0,1:T(8,128)S(1)}, f32[512,14]{0,1:T(8,128)}, u32[]{:S(2)}) copy-start(f32[512,14]{0,1:T(8,128)} %param.18) | copy-start | bytes 86020
  0.7 9.9 %copy-start.8 = (f32[14]{0:T(128)S(1)}, f32[14]{0:T(128)}, u32[]{:S(2)}) copy-start(f32[14]{0:T(128)} %param.19) | copy-start | bytes 172
  0.7 9.9 %copy-start.9 = (f32[14]{0:T(128)S(1)}, f32[14]{0:T(128)}, u32[]{:S(2)}) copy-start(f32[14]{0:T(128)} %param.20) | copy-start | bytes 172
  1.3 14.4 %copy-start.6 = (s32[4]{0:T(128)S(1)}, s32[4]{0:T(128)}, u32[]{:S(2)}) copy-start(s32[4]{0:T(128)} %pad_add_fusion.info) | copy-start | bytes 52
  5.7 21.0 %copy-start.11 = (bf16[672,512]{1,0:T(8,128)(2,1)S(1)}, bf16[672,512]{1,0:T(8,128)(2,1)}, u32[]{:S(2)}) copy-start(bf16[672,512]{1,0:T(8,128)(2,1)} %get-tuple-element.61) | copy-start | bytes 2064388
  5.7 4.8 %collective-permute-start.3 = (bf16[448,512]{1,0:T(8,128)(2,1)}, bf16[448,512]{1,0:T(8,128)(2,1)S(1)}, u32[]{:S(2)}, u32[]{:S(2)}) collective-permute-start(bf16[448,512]{1,0:T(8,128)(2,1)} %get-tuple-element.51.refs_4_), channel_id=1, source_target_pairs={{0,8},{8,0},{16,24},{24,16},{32,40},{40,32},{48,56},{56,48},{64,72... | collective-permute-start | bytes 1376264 | tf_op jit(solution)/shard_map/ppermute | solution.py:42
  5.8 20.8 %collective-permute-start = (bf16[672,512]{1,0:T(8,128)(2,1)}, bf16[672,512]{1,0:T(8,128)(2,1)S(1)}, u32[]{:S(2)}, u32[]{:S(2)}) collective-permute-start(bf16[672,512]{1,0:T(8,128)(2,1)} %get-tuple-element.49), channel_id=1, source_target_pairs={{0,48},{8,56},{16,32},{24,40},{32,16},{40,24},{48,0},{56,8},{64,11... | collective-permute-start | bytes 2064392 | tf_op jit(solution)/shard_map/ppermute | solution.py:34
  8.7 17.9 %collective-permute-start.1 = (bf16[672,512]{1,0:T(8,128)(2,1)}, bf16[672,512]{1,0:T(8,128)(2,1)S(1)}, u32[]{:S(2)}, u32[]{:S(2)}) collective-permute-start(bf16[672,512]{1,0:T(8,128)(2,1)} %get-tuple-element.50), channel_id=1, source_target_pairs={{0,64},{8,72},{16,80},{24,88},{32,96},{40,104},{48,112},{56,120},{... | collective-permute-start | bytes 2064392 | tf_op jit(solution)/shard_map/ppermute | solution.py:34
  10.3 16.3 %collective-permute-start.2 = (bf16[448,512]{1,0:T(8,128)(2,1)}, bf16[448,512]{1,0:T(8,128)(2,1)S(1)}, u32[]{:S(2)}, u32[]{:S(2)}) collective-permute-start(bf16[448,512]{1,0:T(8,128)(2,1)} %get-tuple-element.51.refs_4_), channel_id=1, source_target_pairs={{0,16},{8,24},{16,0},{24,8},{32,48},{40,56},{48,32},{56,40},{64,80... | collective-permute-start | bytes 1376264 | tf_op jit(solution)/shard_map/ppermute | solution.py:38
  14.2 1.4 %collective-permute-start.4 = (bf16[80,896]{1,0:T(8,128)(2,1)S(1)}, bf16[80,896]{1,0:T(8,128)(2,1)S(1)}, u32[]{:S(2)}, u32[]{:S(2)}) collective-permute-start(bf16[80,896]{1,0:T(8,128)(2,1)S(1)} %get-tuple-element.54), channel_id=1, source_target_pairs={{0,8},{8,0},{16,24},{24,16},{32,40},{40,32},{48,56},{56,48},{64,72... | collective-permute-start | bytes 430088 | tf_op jit(solution)/shard_map/ppermute | solution.py:42
  16.4 9.5 %collective-permute-start.5 = (bf16[80,896]{1,0:T(8,128)(2,1)S(1)}, bf16[80,896]{1,0:T(8,128)(2,1)S(1)}, u32[]{:S(2)}, u32[]{:S(2)}) collective-permute-start(bf16[80,896]{1,0:T(8,128)(2,1)S(1)} %get-tuple-element.56), channel_id=1, source_target_pairs={{0,16},{8,24},{16,0},{24,8},{32,48},{40,56},{48,32},{56,40},{64,80... | collective-permute-start | bytes 430088 | tf_op jit(solution)/shard_map/ppermute | solution.py:38
  26.5 31.7 %copy-start.2 = (bf16[448,512]{1,0:T(8,128)(2,1)S(1)}, bf16[448,512]{1,0:T(8,128)(2,1)}, u32[]{:S(2)}) copy-start(bf16[448,512]{1,0:T(8,128)(2,1)} %get-tuple-element.51.refs_4_) | copy-start | bytes 1376260
  26.5 31.7 %copy-start.4 = (bf16[224,512]{1,0:T(8,128)(2,1)S(1)}, bf16[224,512]{1,0:T(8,128)(2,1)}, u32[]{:S(2)}) copy-start(bf16[224,512]{1,0:T(8,128)(2,1)} %get-tuple-element.72.refs_0_) | copy-start | bytes 688132
  26.6 5.9 %collective-permute-start.12 = (bf16[672,512]{1,0:T(8,128)(2,1)S(1)}, bf16[672,512]{1,0:T(8,128)(2,1)S(1)}, u32[]{:S(2)}, u32[]{:S(2)}) collective-permute-start(bf16[672,512]{1,0:T(8,128)(2,1)S(1)} %collective-permute-done.refs_1_.refs_5_), channel_id=1, source_target_pairs={{0,8},{8,0},{16,24},{24,16},{32,40},{40,32},{48,56},{56,48},{64,72... | collective-permute-start | bytes 2064392 | tf_op jit(solution)/shard_map/ppermute | solution.py:42
  26.7 29.1 %collective-permute-start.6 = (bf16[672,512]{1,0:T(8,128)(2,1)S(1)}, bf16[672,512]{1,0:T(8,128)(2,1)S(1)}, u32[]{:S(2)}, u32[]{:S(2)}) collective-permute-start(bf16[672,512]{1,0:T(8,128)(2,1)S(1)} %copy-done.11), channel_id=1, source_target_pairs={{0,112},{8,120},{16,96},{24,104},{32,80},{40,88},{48,64},{56,72},{... | collective-permute-start | bytes 2064392 | tf_op jit(solution)/shard_map/ppermute | solution.py:34
  29.1 26.7 %collective-permute-start.7 = (bf16[448,512]{1,0:T(8,128)(2,1)S(1)}, bf16[448,512]{1,0:T(8,128)(2,1)S(1)}, u32[]{:S(2)}, u32[]{:S(2)}) collective-permute-start(bf16[448,512]{1,0:T(8,128)(2,1)S(1)} %slice.12), channel_id=1, source_target_pairs={{0,16},{8,24},{16,0},{24,8},{32,48},{40,56},{48,32},{56,40},{64,80... | collective-permute-start | bytes 1376264 | tf_op jit(solution)/shard_map/ppermute | solution.py:38
  29.2 26.6 %collective-permute-start.8 = (bf16[448,512]{1,0:T(8,128)(2,1)S(1)}, bf16[448,512]{1,0:T(8,128)(2,1)S(1)}, u32[]{:S(2)}, u32[]{:S(2)}) collective-permute-start(bf16[448,512]{1,0:T(8,128)(2,1)S(1)} %slice.13), channel_id=1, source_target_pairs={{0,16},{8,24},{16,0},{24,8},{32,48},{40,56},{48,32},{56,40},{64,80... | collective-permute-start | bytes 1376264 | tf_op jit(solution)/shard_map/ppermute | solution.py:38
  31.3 24.5 %collective-permute-start.9 = (bf16[80,896]{1,0:T(8,128)(2,1)S(1)}, bf16[80,896]{1,0:T(8,128)(2,1)S(1)}, u32[]{:S(2)}, u32[]{:S(2)}) collective-permute-start(bf16[80,896]{1,0:T(8,128)(2,1)S(1)} %get-tuple-element.64), channel_id=1, source_target_pairs={{0,32},{8,40},{16,48},{24,56},{32,0},{40,8},{48,16},{56,24},{64,96... | collective-permute-start | bytes 430088 | tf_op jit(solution)/shard_map/ppermute | solution.py:46
  32.5 25.2 %collective-permute-start.13 = (bf16[672,512]{1,0:T(8,128)(2,1)S(1)}, bf16[672,512]{1,0:T(8,128)(2,1)S(1)}, u32[]{:S(2)}, u32[]{:S(2)}) collective-permute-start(bf16[672,512]{1,0:T(8,128)(2,1)S(1)} %collective-permute-done.1.refs_2_.refs_6_), channel_id=1, source_target_pairs={{0,8},{8,0},{16,24},{24,16},{32,40},{40,32},{48,56},{56,48},{64,72... | collective-permute-start | bytes 2064392 | tf_op jit(solution)/shard_map/ppermute | solution.py:42
  55.8 2.2 %collective-permute-start.14 = (bf16[672,512]{1,0:T(8,128)(2,1)S(1)}, bf16[672,512]{1,0:T(8,128)(2,1)S(1)}, u32[]{:S(2)}, u32[]{:S(2)}) collective-permute-start(bf16[672,512]{1,0:T(8,128)(2,1)S(1)} %collective-permute-done.6.refs_3_.refs_7_), channel_id=1, source_target_pairs={{0,8},{8,0},{16,24},{24,16},{32,40},{40,32},{48,56},{56,48},{64,72... | collective-permute-start | bytes 2064392 | tf_op jit(solution)/shard_map/ppermute | solution.py:42
  55.9 13.1 %collective-permute-start.10 = (bf16[448,512]{1,0:T(8,128)(2,1)S(1)}, bf16[448,512]{1,0:T(8,128)(2,1)S(1)}, u32[]{:S(2)}, u32[]{:S(2)}) collective-permute-start(bf16[448,512]{1,0:T(8,128)(2,1)S(1)} %slice.14), channel_id=1, source_target_pairs={{0,16},{8,24},{16,0},{24,8},{32,48},{40,56},{48,32},{56,40},{64,80... | collective-permute-start | bytes 1376264 | tf_op jit(solution)/shard_map/ppermute | solution.py:38
  56.7 12.3 %collective-permute-start.11 = (bf16[80,896]{1,0:T(8,128)(2,1)S(1)}, bf16[80,896]{1,0:T(8,128)(2,1)S(1)}, u32[]{:S(2)}, u32[]{:S(2)}) collective-permute-start(bf16[80,896]{1,0:T(8,128)(2,1)S(1)} %get-tuple-element.71), channel_id=1, source_target_pairs={{0,64},{8,72},{16,80},{24,88},{32,96},{40,104},{48,112},{56,120},{... | collective-permute-start | bytes 430088 | tf_op jit(solution)/shard_map/ppermute | solution.py:46
  57.5 14.8 %collective-permute-start.15 = (bf16[448,512]{1,0:T(8,128)(2,1)S(1)}, bf16[448,512]{1,0:T(8,128)(2,1)S(1)}, u32[]{:S(2)}, u32[]{:S(2)}) collective-permute-start(bf16[448,512]{1,0:T(8,128)(2,1)S(1)} %collective-permute-done.2.refs_0_), channel_id=1, source_target_pairs={{0,8},{8,0},{16,24},{24,16},{32,40},{40,32},{48,56},{56,48},{64,72... | collective-permute-start | bytes 1376264 | tf_op jit(solution)/shard_map/ppermute | solution.py:42
  57.7 14.6 %collective-permute-start.16 = (bf16[448,512]{1,0:T(8,128)(2,1)S(1)}, bf16[448,512]{1,0:T(8,128)(2,1)S(1)}, u32[]{:S(2)}, u32[]{:S(2)}) collective-permute-start(bf16[448,512]{1,0:T(8,128)(2,1)S(1)} %collective-permute-done.7.refs_1_), channel_id=1, source_target_pairs={{0,8},{8,0},{16,24},{24,16},{32,40},{40,32},{48,56},{56,48},{64,72... | collective-permute-start | bytes 1376264 | tf_op jit(solution)/shard_map/ppermute | solution.py:42
  58.0 14.3 %collective-permute-start.17 = (bf16[448,512]{1,0:T(8,128)(2,1)S(1)}, bf16[448,512]{1,0:T(8,128)(2,1)S(1)}, u32[]{:S(2)}, u32[]{:S(2)}) collective-permute-start(bf16[448,512]{1,0:T(8,128)(2,1)S(1)} %collective-permute-done.8.refs_2_), channel_id=1, source_target_pairs={{0,8},{8,0},{16,24},{24,16},{32,40},{40,32},{48,56},{56,48},{64,72... | collective-permute-start | bytes 1376264 | tf_op jit(solution)/shard_map/ppermute | solution.py:42
  69.0 4.7 %collective-permute-start.18 = (bf16[448,512]{1,0:T(8,128)(2,1)S(1)}, bf16[448,512]{1,0:T(8,128)(2,1)S(1)}, u32[]{:S(2)}, u32[]{:S(2)}) collective-permute-start(bf16[448,512]{1,0:T(8,128)(2,1)S(1)} %collective-permute-done.10.refs_3_), channel_id=1, source_target_pairs={{0,8},{8,0},{16,24},{24,16},{32,40},{40,32},{48,56},{56,48},{64,72... | collective-permute-start | bytes 1376264 | tf_op jit(solution)/shard_map/ppermute | solution.py:42
  73.8 16.8 %copy-start.1 = (bf16[512,896]{1,0:T(8,128)(2,1)S(1)}, bf16[512,896]{1,0:T(8,128)(2,1)}, u32[]{:S(2)}) copy-start(bf16[512,896]{1,0:T(8,128)(2,1)} %gate_ref.1) | copy-start | bytes 2752516
  87.6 42.9 %collective-permute-start.19 = (bf16[224,512]{1,0:T(8,128)(2,1)S(1)}, bf16[224,512]{1,0:T(8,128)(2,1)S(1)}, u32[]{:S(2)}, u32[]{:S(2)}) collective-permute-start(bf16[224,512]{1,0:T(8,128)(2,1)S(1)} %get-tuple-element.83), channel_id=1, source_target_pairs={{0,48},{8,56},{16,32},{24,40},{32,16},{40,24},{48,0},{56,8},{64,11... | collective-permute-start | bytes 688136 | tf_op jit(solution)/shard_map/ppermute | solution.py:34
  90.6 40.0 %copy-start.10 = (f32[896]{0:T(1024)S(1)}, f32[896]{0:T(1024)}, u32[]{:S(2)}) copy-start(f32[896]{0:T(1024)} %param.21) | copy-start | bytes 10756
  127.3 6.0 %collective-permute-start.20 = (bf16[224,512]{1,0:T(8,128)(2,1)S(1)}, bf16[224,512]{1,0:T(8,128)(2,1)S(1)}, u32[]{:S(2)}, u32[]{:S(2)}) collective-permute-start(bf16[224,512]{1,0:T(8,128)(2,1)S(1)} %get-tuple-element.92), channel_id=1, source_target_pairs={{0,64},{8,72},{16,80},{24,88},{32,96},{40,104},{48,112},{56,120},{... | collective-permute-start | bytes 688136 | tf_op jit(solution)/shard_map/ppermute | solution.py:34
  128.0 8.1 %collective-permute-start.21 = (bf16[224,512]{1,0:T(8,128)(2,1)S(1)}, bf16[224,512]{1,0:T(8,128)(2,1)S(1)}, u32[]{:S(2)}, u32[]{:S(2)}) collective-permute-start(bf16[224,512]{1,0:T(8,128)(2,1)S(1)} %get-tuple-element.93), channel_id=1, source_target_pairs={{0,112},{8,120},{16,96},{24,104},{32,80},{40,88},{48,64},{56,72},{... | collective-permute-start | bytes 688136 | tf_op jit(solution)/shard_map/ppermute | solution.py:34

commit v3 on v2

--- a/solution.py
+++ b/solution.py
@@ -55,19 +55,19 @@
 V_ROWS = slice(2 * ATT_DIM, 3 * ATT_DIM)
 
 
-def pack_kernel(info, q_in, k_in, v_in, q_own, kv_own, all_1, all_2, all_3, raw, rows_ref, sems):
-    copies = [pltpu.make_async_copy(src, raw.at[i], sems.at[i]) for i, src in enumerate((q_in, k_in, v_in))]
+def pack_kernel(info, q_in, k_in, v_in, q_own, q_1, q_2, kv_own, kv_1, kv_2, all_3, raw, rows_ref, sems):
+    copies = [pltpu.make_async_copy(src, raw.at[i], sems.at[i]) for i, src in enumerate((k_in, v_in, q_in))]
     for copy in copies:
         copy.start()
-    for i, (out, first) in enumerate(((q_own, 0), (kv_own, 0), (kv_own, ATT_DIM))):
+    for i, (own, one, two, first) in enumerate(((kv_own, kv_1, kv_2, 0), (kv_own, kv_1, kv_2, ATT_DIM), (q_own, q_1, q_2, 0))):
         copies[i].wait()
         rows_ref[i] = raw[i].T
-        out[first : first + ATT_DIM, :] = rows_ref[i, head_rows(info[0]), :]
-        for r, away in ((1, all_1), (2, all_2), (3, all_3)):
-            away[i * ATT_DIM : (i + 1) * ATT_DIM, :] = rows_ref[i, head_rows(info[0] ^ r), :]
-
-
-def unpack_kernel(info, *refs):
+        for r, out in enumerate((own, one, two)):
+            out[first : first + ATT_DIM, :] = rows_ref[i, head_rows(info[0] ^ r), :]
+        all_3[(K_ROWS, V_ROWS, Q_ROWS)[i], :] = rows_ref[i, head_rows(info[0] ^ 3), :]
+
+
+def unpack_kernel(info, _, *refs):
     pieces, out_ref, rows_ref = refs[:4], refs[4], refs[5]
     for r in range(4):
         rows_ref[head_rows(info[0] ^ r), :] = pieces[r][...]
@@ -83,38 +83,15 @@
         acc, stats_out, qs, mark, ks, vs = refs
         for r in range(4):
             qs[r] = queries[r][Q_ROWS, :]
-        for i, piece in enumerate(pieces):
-            k_first = ATT_DIM if i & 3 else 0
-            v_first = k_first + ATT_DIM
-            start = pl.multiple_of((core ^ (i >> 2)) * TOK, TOK)
-            ks[hid ^ (i & 3), pl.ds(start, TOK), :] = piece[k_first:v_first, :].T
-            vs[hid ^ (i & 3), :, pl.ds(start, TOK)] = piece[v_first : v_first + ATT_DIM, :]
     else:
         pieces, refs = refs[:8], refs[8:]
-        _, queries, acc_in, stats_in, *o_out, mark, qs, ks, vs, raw, acc, os, sems = refs
-        loads = [
-            pltpu.make_async_copy(queries, qs, sems.at[16]),
-            pltpu.make_async_copy(acc_in, acc, sems.at[17]),
-        ]
-        key_loads, value_loads = [], []
-        for i, piece in enumerate(pieces):
-            start = pl.multiple_of((core ^ (i >> 2)) * TOK, TOK)
-            key_loads.append(pltpu.make_async_copy(piece.at[0:ATT_DIM, :], raw.at[i], sems.at[i]))
-            value_loads.append(
-                pltpu.make_async_copy(
-                    piece.at[ATT_DIM : 2 * ATT_DIM, :],
-                    vs.at[hid ^ (i & 3), :, pl.ds(start, TOK)],
-                    sems.at[8 + i],
-                )
-            )
-        for load in key_loads + loads + value_loads:
-            load.start()
-        for i, load in enumerate(key_loads):
-            load.wait()
-            start = pl.multiple_of((core ^ (i >> 2)) * TOK, TOK)
-            ks[hid ^ (i & 3), pl.ds(start, TOK), :] = raw[i].T
-        for load in loads + value_loads:
-            load.wait()
+        _, qs, acc_in, stats_in, *o_out, mark, ks, vs, acc, os = refs
+    for i, piece in enumerate(pieces):
+        k_first = ATT_DIM if own and i & 3 == 3 else 0
+        v_first = k_first + ATT_DIM
+        start = pl.multiple_of((core ^ (i >> 2)) * TOK, TOK)
+        ks[hid ^ (i & 3), pl.ds(start, TOK), :] = piece[k_first:v_first, :].T
+        vs[hid ^ (i & 3), :, pl.ds(start, TOK)] = piece[v_first : v_first + ATT_DIM, :]
     mark[...] = jnp.zeros_like(mark)
 
     def one_queries(r, carry):
@@ -165,6 +142,7 @@
                 stats_out[r, 0:8, lanes] = jnp.broadcast_to(stats[half][0], (8, HALF))
                 stats_out[r, 8:16, lanes] = jnp.broadcast_to(stats[half][1], (8, HALF))
         else:
+            acc[r] = acc_in[r]
             stats = tuple(
                 (
                     stats_in[r, 0:1, half * HALF : (half + 1) * HALF],
@@ -308,6 +286,7 @@
 
 
 SMALL = pl.CostEstimate(flops=1000, bytes_accessed=1000, transcendentals=0)
+LARGE = pl.CostEstimate(flops=4 * 10**10, bytes_accessed=6 * 2**20, transcendentals=10**6)
 
 
 def params(mib):
@@ -320,7 +299,7 @@
 
 def pack(info, query_rows, key_rows, value_rows):
     width = HEADS * ATT_DIM
-    rows = [ATT_DIM, 2 * ATT_DIM] + [3 * ATT_DIM] * 3
+    rows = [ATT_DIM] * 3 + [2 * ATT_DIM] * 3 + [3 * ATT_DIM]
     return pl.pallas_call(
         pack_kernel,
         out_shape=[shape((count, TOK), BF16) for count in rows],
@@ -336,25 +315,17 @@
 
 
 def attend(own, info, *operands):
-    queries = pltpu.VMEM((4, ATT_DIM, TOK), BF16)
     scratch = [pltpu.VMEM((4, 2 * TOK, ATT_DIM), BF16), pltpu.VMEM((4, ATT_DIM, 2 * TOK), BF16)]
     if own:
         out = [shape((4, ATT_DIM, TOK), F32), shape((4, 16, TOK), F32), shape((4, ATT_DIM, TOK), BF16)]
-        specs = vmem(len(operands))
     else:
         out = [shape((ATT_DIM, TOK), BF16)] * 4
-        scratch = [queries] + scratch + [
-            pltpu.VMEM((8, ATT_DIM, TOK), BF16),
-            pltpu.VMEM((4, ATT_DIM, TOK), F32),
-            queries,
-            pltpu.SemaphoreType.DMA((18,)),
-        ]
-        specs = [ANY] * (len(operands) - 1) + vmem(1)
+        scratch += [pltpu.VMEM((4, ATT_DIM, TOK), F32), pltpu.VMEM((4, ATT_DIM, TOK), BF16)]
     out = out + [shape((8, 128), F32)]
     return pl.pallas_call(
         functools.partial(attend_kernel, own),
         out_shape=out,
-        in_specs=[SMEM] + specs,
+        in_specs=[SMEM] + vmem(len(operands)),
         out_specs=vmem(len(out)),
         scratch_shapes=scratch,
         compiler_params=params(24),
@@ -362,16 +333,16 @@
     )(info, *operands)
 
 
-def unpack(info, pieces):
+def unpack(info, mark, pieces):
     width = HEADS * ATT_DIM
     return pl.pallas_call(
         unpack_kernel,
         out_shape=shape((TOK, width), BF16),
-        in_specs=[SMEM] + vmem(4),
+        in_specs=[SMEM, ANY] + vmem(4),
         out_specs=vmem(1)[0],
         scratch_shapes=[pltpu.VMEM((width, TOK), BF16)],
         compiler_params=params(40),
-    )(info, *pieces)
+    )(info, mark, *pieces)
 
 
 def ssm_local(ssm_inputs, write_t, read_t, step_t, rate, gain):
@@ -400,19 +371,19 @@
         in_specs=[SMEM] + vmem(3),
         out_specs=vmem(3),
         compiler_params=params(40),
-        cost_estimate=SMALL,
+        cost_estimate=LARGE if level == 3 else SMALL,
     )(info, got, total, before)
 
 
-def ssm_carry(state, mixed, cum, read_t, gate):
+def ssm_carry(count, state, mixed, cum, read_t, gate):
     tokens, width = mixed.shape
     return pl.pallas_call(
         ssm_carry_kernel,
-        out_shape=[shape((tokens, width), F32), shape((8, tokens), F32)],
+        out_shape=[shape((tokens, width), F32), shape((8 * count, tokens), F32)],
         in_specs=vmem(5),
         out_specs=vmem(2),
         compiler_params=params(40),
-        cost_estimate=SMALL,
+        cost_estimate=LARGE,
     )(state, mixed, cum, read_t, gate)
 
 
@@ -434,10 +405,9 @@
     info = jnp.stack([y * 2 + (x >> 1), (x ^ (x >> 1)) & 1, core, me]).astype(jnp.int32)
     tie = lax.optimization_barrier
 
-    q_own, kv_own, *away = pack(info, query_rows, key_rows, value_rows)
-    here, near, from_core = [None] * 4, [None] * 4, [None] * 4
-    here[0] = kv_own
-    here[1], here[2] = head_swap(away[0], 1), head_swap(away[1], 2)
+    q_own, q_1, q_2, kv_own, kv_1, kv_2, all_3 = pack(info, query_rows, key_rows, value_rows)
+    here, near, from_core = [kv_own] + [None] * 3, [None] * 4, [None] * 4
+    here[1], here[2] = head_swap(kv_1, 1), head_swap(kv_2, 2)
     near[0] = class_swap(kv_own)
     from_core[0] = core_swap(kv_own)
 
@@ -448,35 +418,37 @@
     )
     before = jnp.zeros_like(total)
     total, before, sent = ssm_merge(0, info, core_swap(sent), total, before)
-    total, before, sent = ssm_merge(1, info, class_swap(sent), total, before)
-
-    here[1], here[2], near[0], away[2], sent = tie((here[1], here[2], near[0], away[2], sent))
+    got = class_swap(sent)
+
+    here[1], here[2], near[0], all_3, got = tie((here[1], here[2], near[0], all_3, got))
+    near[1], near[2] = class_swap(here[1]), class_swap(here[2])
+    here[3] = head_swap(all_3, 3)
+    total, before, sent = ssm_merge(1, info, got, total, before)
+    q_1, q_2, sent = tie((q_1, q_2, sent))
+    q_1, q_2 = head_swap(q_1, 1), head_swap(q_2, 2)
+
+    here[3], near[1], near[2], q_1, q_2, sent = tie((here[3], near[1], near[2], q_1, q_2, sent))
+    near[3] = class_swap(here[3][ATT_DIM:])
+    for r in range(1, 4):
+        from_core[r] = core_swap(here[r])
     got = block_swap(sent, 4)
-    here[3] = head_swap(away[2], 3)
-    for r in (1, 2):
-        near[r] = class_swap(here[r][ATT_DIM:])
-    from_core[1] = core_swap(here[1])
-    from_core[1], piece = tie((from_core[1], here[2]))
-    from_core[2] = core_swap(piece)
-
-    here[3], near[1], near[2], got = tie((here[3], near[1], near[2], got))
-    near[3] = class_swap(here[3][ATT_DIM:])
-    from_core[3] = core_swap(here[3])
+    partial, stats, queries, mark = attend(True, info, q_own, q_1, q_2, here[3], *here, *from_core)
+
+    near[3], got, mark = tie((near[3], got, mark))
+    near_core = [core_swap(piece) for piece in near]
     total, before, sent = ssm_merge(2, info, got, total, before)
     got = block_swap(sent, 8)
-    partial, stats, queries, mark = attend(True, info, q_own, *here[1:], *here, *from_core)
-
-    near[3], got, mark = tie((near[3], got, mark))
-    near_core = [core_swap(piece) for piece in near]
+    *results, mark = attend(False, info, *near, *near_core, mark, queries, partial, stats)
+    back = [results[0]] + [head_swap(results[r], r) for r in range(1, 4)]
+    got, mark = tie((got, mark))
     total, before, sent = ssm_merge(3, info, got, total, before)
-    gated, squares = ssm_carry(before, mixed, cum, read_t, ssm_gate)
-    squares = lax.all_gather(squares, "tp")
-    *results, _ = attend(False, info, *near, *near_core, mark, queries, partial, stats)
-    back = [results[0]] + [head_swap(results[r], r) for r in range(1, 4)]
-    back[1], squares = tie((back[1], squares))
+    count = lax.axis_size("tp")
+    gated, squares = ssm_carry(count, before, mixed, cum, read_t, ssm_gate)
+    squares = lax.all_to_all(squares, "tp", 0, 0, tiled=True).reshape(count, 8, TOK)
+    *back, squares = tie((*back, squares))
     factor = lax.rsqrt(jnp.sum(squares[:, 0], axis=0) / SSM_WIDTH + 1e-05)
     mixer_out = (gated * factor[:, None] * norm_gain[None, :]).astype(BF16)
-    return (unpack(info, back), mixer_out)
+    return (unpack(info, mark, back), mixer_out)
 
 
 def solution(mesh):

time: 138 us -> 105 us (0.76)
  blocking collectives: 35.3 us -> 15.5 us
  waiting for transfers between devices: 38.2 us -> 26.1 us
  Pallas kernels: 39.3 us -> 35.2 us
  starting transfers between devices: 22.3 us -> 24.7 us
    all_gather x1 -> x0, blocking collectives: 35.3 us -> none  [on_device(): squares = lax.all_gather(squares, 'tp')]
    ppermute x2, waiting for transfers between devices: 23.3 us -> 2.38 us  [block_swap(): return lax.ppermute(value, 'ctx', [(i, i ^ step) for i in range(CTX)])]
    all_to_all x0 -> x1, blocking collectives: none -> 15.5 us  [on_device(): lax.all_to_all(squares, 'tp', 0, 0, tiled=True).reshape(count, 8, TOK)]
    ppermute x6 -> x8, waiting for transfers between devices: 4.43 us -> 19.3 us  [head_swap(): lax.ppermute(value, 'ctx', [(i, exchanged(i, r)) for i in range(CTX)])]
    ppermute x5, waiting for transfers between devices: 7.64 us -> 3.05 us  [class_swap(): return lax.ppermute(value, 'ctx', [(i, i ^ 2) for i in range(CTX)])]
    pallas_call x2, Pallas kernels: 24.6 us -> 20.8 us  [attend(): pl.pallas_call(functools.partial(attend_kernel, own), out_shape=out, in_s...]
    ppermute x2, starting transfers between devices: 2 us -> 4.39 us  [block_swap(): return lax.ppermute(value, 'ctx', [(i, i ^ step) for i in range(CTX)])]
    ppermute x9, starting transfers between devices: 4.35 us -> 2.37 us  [core_swap(): return lax.ppermute(value, 'ctx', [(i, i ^ 1) for i in range(CTX)])]
  transfers between devices with their start and end apart: 22 -> 24, of which waited for: 6 -> 8; matrix products, arithmetic and copies ran while one was open for 1% -> 0% of each run, Pallas kernels for 14% -> 28%
where the time goes in v3:
time: 105 us; the launch traced here: 104 us
  Pallas kernels  35.2 us (34%)
  waiting for transfers between devices  26.1 us (25%)
  starting transfers between devices  24.7 us (24%)
  blocking collectives  15.5 us (15%)
  other arithmetic  1.8 us (2%)
    pallas_call x2, Pallas kernels, attend(): pl.pallas_call(functools.partial(attend_kernel, own), out_shape=out, in_s...  20.8 us
    ppermute x8, waiting for transfers between devices, head_swap(): lax.ppermute(value, 'ctx', [(i, exchanged(i, r)) for i in range(CTX)])  19.3 us
    all_to_all x1, blocking collectives, on_device(): lax.all_to_all(squares, 'tp', 0, 0, tiled=True).reshape(count, 8, TOK)  15.5 us
    ppermute x8, starting transfers between devices, head_swap(): lax.ppermute(value, 'ctx', [(i, exchanged(i, r)) for i in range(CTX)])  13.2 us
    ppermute x5, starting transfers between devices, class_swap(): return lax.ppermute(value, 'ctx', [(i, i ^ 2) for i in range(CTX)])  4.71 us
    ppermute x2, starting transfers between devices, block_swap(): return lax.ppermute(value, 'ctx', [(i, i ^ step) for i in range(CTX)])  4.39 us
    pallas_call x1, Pallas kernels, pack(): pl.pallas_call(pack_kernel, out_shape=[shape((count, TOK), BF16) for coun...  4.18 us
    pallas_call x1, Pallas kernels, ssm_local(): pl.pallas_call(ssm_local_kernel, out_shape=[shape((tokens, width), F32),...  3.65 us
  transfers between devices with their start and end apart: 24, of which 8 were waited for; matrix products, arithmetic and copies ran while one was open for 0% of the time, Pallas kernels for 28%

profile of v3, /device:TPU:0, one launch (start us, length us, event | category | flops | bytes accessed | tf_op | source)
XLA Modules:
  0.0 104.4 jit_solution(11529372757119109901)
XLA Ops:
  0.7 0.6 pad_add_fusion.info
  1.3 4.2 %shard_map.122 = (bf16[224,512]{1,0:T(8,128)(2,1)}, bf16[224,512]{1,0:T(8,128)(2,1)}, bf16[224,512]{1,0:T(8,128)(2,1)}, bf16[448,512]{1,0:T(8,128)(2,1)}, bf16[4...) custom-call(s32[4]{0:T(128)} %pad_add_fusion.info, bf16[512,896]{1,0:T(8,128)(2,1)} %q_in.1, ...), custom_call_target="tpu_custom_call" | custom-call | tf_op jit(solution)/shard_map/pallas_call | solution.py:303
  5.5 0.0 copy-start.11
  5.5 0.0 copy-start.13
  5.5 0.0 copy-start.1
  5.6 0.1 collective-permute-start.3
  5.7 1.7 %collective-permute-start.2 = (bf16[448,512]{1,0:T(8,128)(2,1)}, bf16[448,512]{1,0:T(8,128)(2,1)S(1)}, u32[]{:S(2)}, u32[]{:S(2)}) collective-permute-start(bf16[448,512]{1,0:T(8,128)(2,1)} %get-tuple-element.62.refs_4_), channel_id=1, source_target_pairs={{0,16},{8,24},{16,0},{24,8},{32,48},{40,56},{48,32},{56,40},{64,80... | collective-permute-start | bytes 1376264 | tf_op jit(solution)/shard_map/ppermute | solution.py:38
  7.3 2.1 %collective-permute-start = (bf16[448,512]{1,0:T(8,128)(2,1)}, bf16[448,512]{1,0:T(8,128)(2,1)S(1)}, u32[]{:S(2)}, u32[]{:S(2)}) collective-permute-start(bf16[448,512]{1,0:T(8,128)(2,1)} %get-tuple-element.60), channel_id=1, source_target_pairs={{0,48},{8,56},{16,32},{24,40},{32,16},{40,24},{48,0},{56,8},{64,11... | collective-permute-start | bytes 1376264 | tf_op jit(solution)/shard_map/ppermute | solution.py:34
  9.4 1.6 %collective-permute-start.1 = (bf16[448,512]{1,0:T(8,128)(2,1)}, bf16[448,512]{1,0:T(8,128)(2,1)S(1)}, u32[]{:S(2)}, u32[]{:S(2)}) collective-permute-start(bf16[448,512]{1,0:T(8,128)(2,1)} %get-tuple-element.61), channel_id=1, source_target_pairs={{0,64},{8,72},{16,80},{24,88},{32,96},{40,104},{48,112},{56,120},{... | collective-permute-start | bytes 1376264 | tf_op jit(solution)/shard_map/ppermute | solution.py:34
  11.0 0.0 collective-permute-done.3.refs_8_
  11.0 3.6 %shard_map.123 = (f32[512,896]{1,0:T(8,128)S(1)}, f32[72,896]{1,0:T(8,128)S(1)}, bf16[80,896]{1,0:T(8,128)(2,1)S(1)}, f32[512,14]{1,0:T(8,128)S(1)}) custom-call(bf16[512,896]{1,0:T(8,128)(2,1)S(1)} %copy-done, bf16[64,512]{1,0:T(8,128)(2,1)S(1)} %bitcast.11, bf16[64,512]{1,0:T(8,128)(2,1)S(1)} %bitcast.12, f32[14,512]{1,0:T(8,128)S(1)} %bitcast.14, ...), custom_call_target="tpu_custom_call" | custom-call | flops 1000 | bytes 1000 | tf_op jit(solution)/shard_map/pallas_call | solution.py:351
  14.7 0.1 collective-permute-start.4
  14.8 1.4 %collective-permute-done.4.got_ref = bf16[80,896]{1,0:T(8,128)(2,1)S(1)} collective-permute-done((bf16[80,896]{1,0:T(8,128)(2,1)S(1)}, bf16[80,896]{1,0:T(8,128)(2,1)S(1)}, u32[]{:S(2)}, u32[]{:S(2)}) %collective-permute-start.4) | collective-permute-done | bytes 143392 | tf_op jit(solution)/shard_map/ppermute | solution.py:42
  16.2 0.7 shard_map.124
  16.8 0.7 collective-permute-start.5
  17.5 1.3 %collective-permute-done.2.refs_0_ = bf16[448,512]{1,0:T(8,128)(2,1)S(1)} collective-permute-done((bf16[448,512]{1,0:T(8,128)(2,1)}, bf16[448,512]{1,0:T(8,128)(2,1)S(1)}, u32[]{:S(2)}, u32[]{:S(2)}) %collective-permute-start.2) | collective-permute-done | bytes 458784 | tf_op jit(solution)/shard_map/ppermute | solution.py:38
  18.8 2.5 %collective-permute-done.refs_5_ = bf16[448,512]{1,0:T(8,128)(2,1)S(1)} collective-permute-done((bf16[448,512]{1,0:T(8,128)(2,1)}, bf16[448,512]{1,0:T(8,128)(2,1)S(1)}, u32[]{:S(2)}, u32[]{:S(2)}) %collective-permute-start) | collective-permute-done | bytes 458784 | tf_op jit(solution)/shard_map/ppermute | solution.py:34
  21.3 0.6 collective-permute-done.1.refs_6_
  21.9 0.8 collective-permute-done.5.got_ref
  22.7 3.0 %collective-permute-start.6 = (bf16[672,512]{1,0:T(8,128)(2,1)S(1)}, bf16[672,512]{1,0:T(8,128)(2,1)S(1)}, u32[]{:S(2)}, u32[]{:S(2)}) collective-permute-start(bf16[672,512]{1,0:T(8,128)(2,1)S(1)} %copy-done.11), channel_id=1, source_target_pairs={{0,112},{8,120},{16,96},{24,104},{32,80},{40,88},{48,64},{56,72},{... | collective-permute-start | bytes 2064392 | tf_op jit(solution)/shard_map/ppermute | solution.py:34
  25.7 0.2 collective-permute-start.7
  26.0 1.8 %collective-permute-start.8 = (bf16[448,512]{1,0:T(8,128)(2,1)S(1)}, bf16[448,512]{1,0:T(8,128)(2,1)S(1)}, u32[]{:S(2)}, u32[]{:S(2)}) collective-permute-start(bf16[448,512]{1,0:T(8,128)(2,1)S(1)} %collective-permute-done.1.refs_6_), channel_id=1, source_target_pairs={{0,16},{8,24},{16,0},{24,8},{32,48},{40,56},{48,32},{56,40},{64,80... | collective-permute-start | bytes 1376264 | tf_op jit(solution)/shard_map/ppermute | solution.py:38
  27.8 0.7 shard_map.125
  28.4 0.5 collective-permute-start.10
  29.0 1.2 %collective-permute-start.9 = (bf16[224,512]{1,0:T(8,128)(2,1)S(1)}, bf16[224,512]{1,0:T(8,128)(2,1)S(1)}, u32[]{:S(2)}, u32[]{:S(2)}) collective-permute-start(bf16[224,512]{1,0:T(8,128)(2,1)S(1)} %copy-done.12), channel_id=1, source_target_pairs={{0,48},{8,56},{16,32},{24,40},{32,16},{40,24},{48,0},{56,8},{64,11... | collective-permute-start | bytes 688136 | tf_op jit(solution)/shard_map/ppermute | solution.py:34
  30.2 16.2 %collective-permute-done.10.refs_2_ = bf16[224,512]{1,0:T(8,128)(2,1)S(1)} collective-permute-done((bf16[224,512]{1,0:T(8,128)(2,1)S(1)}, bf16[224,512]{1,0:T(8,128)(2,1)S(1)}, u32[]{:S(2)}, u32[]{:S(2)}) %collective-permute-start.10) | collective-permute-done | bytes 229408 | tf_op jit(solution)/shard_map/ppermute | solution.py:34
  46.4 0.0 collective-permute-done.9.refs_1_
  46.4 0.0 collective-permute-done.7.refs_1_
  46.4 0.9 collective-permute-done.8.refs_2_
  47.3 0.0 collective-permute-done.6.refs_3_.refs_7_
  47.3 0.0 collective-permute-start.15
  47.4 0.5 collective-permute-start.13
  47.9 0.0 collective-permute-start.14
  47.9 0.4 collective-permute-start.11
  48.3 2.9 %collective-permute-start.12 = (bf16[80,896]{1,0:T(8,128)(2,1)S(1)}, bf16[80,896]{1,0:T(8,128)(2,1)S(1)}, u32[]{:S(2)}, u32[]{:S(2)}) collective-permute-start(bf16[80,896]{1,0:T(8,128)(2,1)S(1)} %get-tuple-element.81), channel_id=1, source_target_pairs={{0,32},{8,40},{16,48},{24,56},{32,0},{40,8},{48,16},{56,24},{64,96... | collective-permute-start | bytes 430088 | tf_op jit(solution)/shard_map/ppermute | solution.py:46
  51.2 0.0 collective-permute-done.13.refs_9_
  51.2 0.0 collective-permute-start.17
  51.2 0.0 collective-permute-done.14.refs_10_
  51.2 0.5 collective-permute-start.18
  51.7 0.0 collective-permute-done.15.refs_11_
  51.7 0.3 collective-permute-start.19
  51.9 10.7 %shard_map.126 = (f32[4,224,512]{2,1,0:T(8,128)S(1)}, f32[4,16,512]{2,1,0:T(8,128)S(1)}, bf16[4,224,512]{2,1,0:T(8,128)(2,1)S(1)}, f32[8,128]{1,0:T(8,128)S(1)}) custom-call(s32[4]{0:T(128)S(1)} %copy-done.6, bf16[224,512]{1,0:T(8,128)(2,1)S(1)} %copy-done.2, bf16[224,512]{1,0:T(8,128)(2,1)S(1)} %collective-permute-done.9.refs_1_, ...), custom_call_target="tpu_custom_call" | custom-call | flops 1000 | bytes 1000 | tf_op jit(solution)/shard_map/pallas_call | solution.py:325
  62.7 2.4 %collective-permute-done.12.got_ref = bf16[80,896]{1,0:T(8,128)(2,1)S(1)} collective-permute-done((bf16[80,896]{1,0:T(8,128)(2,1)S(1)}, bf16[80,896]{1,0:T(8,128)(2,1)S(1)}, u32[]{:S(2)}, u32[]{:S(2)}) %collective-permute-start.12) | collective-permute-done | bytes 143392 | tf_op jit(solution)/shard_map/ppermute | solution.py:46
  65.1 0.0 collective-permute-done.11.refs_3_
  65.1 0.9 collective-permute-start.20
  66.0 0.7 shard_map.127
  66.6 1.5 %collective-permute-start.16 = (bf16[80,896]{1,0:T(8,128)(2,1)S(1)}, bf16[80,896]{1,0:T(8,128)(2,1)S(1)}, u32[]{:S(2)}, u32[]{:S(2)}) collective-permute-start(bf16[80,896]{1,0:T(8,128)(2,1)S(1)} %get-tuple-element.90), channel_id=1, source_target_pairs={{0,64},{8,72},{16,80},{24,88},{32,96},{40,104},{48,112},{56,120},{... | collective-permute-start | bytes 430088 | tf_op jit(solution)/shard_map/ppermute | solution.py:46
  68.1 0.0 collective-permute-done.17.refs_4_
  68.1 0.0 collective-permute-done.18.refs_5_
  68.1 0.0 collective-permute-done.19.refs_6_
  68.1 0.0 collective-permute-done.20.refs_7_
  68.2 10.1 %shard_map.128 = (bf16[224,512]{1,0:T(8,128)(2,1)S(1)}, bf16[224,512]{1,0:T(8,128)(2,1)S(1)}, bf16[224,512]{1,0:T(8,128)(2,1)S(1)}, bf16[224,512]{1,0:T(8,128)(2,1)S(1)}, f32[8,128]{1,0:T(8,128)S(1)}) custom-call(s32[4]{0:T(128)S(1)} %copy-done.6, bf16[448,512]{1,0:T(8,128)(2,1)S(1)} %collective-permute-done.2.refs_0_, ...), custom_call_target="tpu_custom_call" | custom-call | flops 1000 | bytes 1000 | tf_op jit(solution)/shard_map/pallas_call | solution.py:325
  78.2 0.0 collective-permute-done.16.got_ref
  78.2 1.0 collective-permute-start.21
  79.2 1.2 %collective-permute-start.22 = (bf16[224,512]{1,0:T(8,128)(2,1)S(1)}, bf16[224,512]{1,0:T(8,128)(2,1)S(1)}, u32[]{:S(2)}, u32[]{:S(2)}) collective-permute-start(bf16[224,512]{1,0:T(8,128)(2,1)S(1)} %get-tuple-element.103), channel_id=1, source_target_pairs={{0,64},{8,72},{16,80},{24,88},{32,96},{40,104},{48,112},{56,120},{... | collective-permute-start | bytes 688136 | tf_op jit(solution)/shard_map/ppermute | solution.py:34
  80.5 2.6 %collective-permute-start.23 = (bf16[224,512]{1,0:T(8,128)(2,1)S(1)}, bf16[224,512]{1,0:T(8,128)(2,1)S(1)}, u32[]{:S(2)}, u32[]{:S(2)}) collective-permute-start(bf16[224,512]{1,0:T(8,128)(2,1)S(1)} %get-tuple-element.104), channel_id=1, source_target_pairs={{0,112},{8,120},{16,96},{24,104},{32,80},{40,88},{48,64},{56,72},{... | collective-permute-start | bytes 688136 | tf_op jit(solution)/shard_map/ppermute | solution.py:34
  83.0 1.4 %shard_map.129 = (f32[72,896]{1,0:T(8,128)}, f32[72,896]{1,0:T(8,128)S(1)}, bf16[80,896]{1,0:T(8,128)(2,1)}) custom-call(s32[4]{0:T(128)S(1)} %copy-done.6, bf16[80,896]{1,0:T(8,128)(2,1)S(1)} %collective-permute-done.16.got_ref, f32[72,896]{1,0:T(8,128)S(1)} %get-tuple-element.106.total_ref, f32[72,896]{1,0:T(8,128)S(1)} %get-tuple-element.107.before_ref), custom_call_target="tpu_custom_call" | custom-call | flops 40000000000 | bytes 6291456 | tf_op jit(solution)/shard_map/pallas_call | solution.py:368
  84.4 1.4 %shard_map.130 = (f32[512,896]{1,0:T(8,128)S(1)}, f32[64,512]{1,0:T(8,128)S(1)}) custom-call(f32[72,896]{1,0:T(8,128)S(1)} %get-tuple-element.108.state_ref, f32[512,896]{1,0:T(8,128)S(1)} %get-tuple-element.109.mixed_ref, f32[512,14]{1,0:T(8,128)S(1)} %get-tuple-element.110.cum_ref, bf16[64,512]{1,0:T(8,128)(2,1)S(1)} %bitcast.13, ...), custom_call_target="tpu_custom_call" | custom-call | flops 40000000000 | bytes 6291456 | tf_op jit(solution)/shard_map/pallas_call | solution.py:380
  85.8 15.5 %all_to_all.9 = f32[8,8,512]{2,1,0:T(8,128)S(1)} all-to-all(f32[8,8,512]{2,1,0:T(8,128)S(1)} %bitcast.10), channel_id=1, replica_groups=mesh['ctx'=16,'tp'=8] {'tp'}, dimensions={0} | all-to-all | bytes 262144 | tf_op jit(solution)/shard_map/all_to_all | solution.py:447
  101.4 0.0 collective-permute-done.21.refs_1_
  101.4 0.0 collective-permute-done.22.refs_2_
  101.4 0.0 collective-permute-done.23.refs_3_
  101.4 1.1 %multiply_convert_fusion = bf16[512,896]{1,0:T(8,128)(2,1)} fusion(f32[512,896]{1,0:T(8,128)S(1)} %get-tuple-element.116, f32[896]{0:T(1024)S(1)} %copy-done.10, f32[512]{0:T(512)S(1)} %add_rsqrt_fusion), kind=kLoop, calls=%fused_computation | loop fusion | flops 1376256 | bytes 2758144 | tf_op jit(solution)/shard_map/convert_element_type | solution.py:450
  102.6 1.8 %shard_map.131 = bf16[512,896]{1,0:T(8,128)(2,1)} custom-call(s32[4]{0:T(128)S(1)} %copy-done.6, f32[8,128]{1,0:T(8,128)S(1)} %get-tuple-element.100._, bf16[224,512]{1,0:T(8,128)(2,1)S(1)} %get-tuple-element.112.refs_0_, bf16[224,512]{1,0:T(8,128)(2,1)S(1)} %collective-permute-done.21.refs_1_, bf16[224,512]{1,0:T(8,128)(2,1)S(1)} %collective-permute-done.22.refs_2_, ...), custom_call_target="tpu_custom_call" | custom-call | tf_op jit(solution)/shard_map/pallas_call | solution.py:338
  (29 shorter events, 0.1 us)
Async XLA Ops:
  0.6 10.4 %copy-start = (bf16[512,896]{1,0:T(8,128)(2,1)S(1)}, bf16[512,896]{1,0:T(8,128)(2,1)}, u32[]{:S(2)}) copy-start(bf16[512,896]{1,0:T(8,128)(2,1)} %x_ref) | copy-start | bytes 2752516
  0.6 10.3 %copy-start.4 = (bf16[512,64]{0,1:T(8,128)(2,1)S(1)}, bf16[512,64]{0,1:T(8,128)(2,1)}, u32[]{:S(2)}) copy-start(bf16[512,64]{0,1:T(8,128)(2,1)} %param.17) | copy-start | bytes 196612
  0.7 10.3 %copy-start.3 = (bf16[512,64]{0,1:T(8,128)(2,1)S(1)}, bf16[512,64]{0,1:T(8,128)(2,1)}, u32[]{:S(2)}) copy-start(bf16[512,64]{0,1:T(8,128)(2,1)} %param.16) | copy-start | bytes 196612
  0.7 10.3 %copy-start.5 = (f32[512,14]{0,1:T(8,128)S(1)}, f32[512,14]{0,1:T(8,128)}, u32[]{:S(2)}) copy-start(f32[512,14]{0,1:T(8,128)} %param.18) | copy-start | bytes 86020
  0.7 10.3 %copy-start.7 = (f32[14]{0:T(128)S(1)}, f32[14]{0:T(128)}, u32[]{:S(2)}) copy-start(f32[14]{0:T(128)} %param.19) | copy-start | bytes 172
  0.7 10.3 %copy-start.8 = (f32[14]{0:T(128)S(1)}, f32[14]{0:T(128)}, u32[]{:S(2)}) copy-start(f32[14]{0:T(128)} %param.20) | copy-start | bytes 172
  1.3 14.8 %copy-start.6 = (s32[4]{0:T(128)S(1)}, s32[4]{0:T(128)}, u32[]{:S(2)}) copy-start(s32[4]{0:T(128)} %pad_add_fusion.info) | copy-start | bytes 52
  5.5 17.2 %copy-start.11 = (bf16[672,512]{1,0:T(8,128)(2,1)S(1)}, bf16[672,512]{1,0:T(8,128)(2,1)}, u32[]{:S(2)}) copy-start(bf16[672,512]{1,0:T(8,128)(2,1)} %get-tuple-element.68) | copy-start | bytes 2064388
  5.5 22.9 %copy-start.13 = (bf16[224,512]{1,0:T(8,128)(2,1)S(1)}, bf16[224,512]{1,0:T(8,128)(2,1)}, u32[]{:S(2)}) copy-start(bf16[224,512]{1,0:T(8,128)(2,1)} %get-tuple-element.78) | copy-start | bytes 688132
  5.5 23.4 %copy-start.12 = (bf16[224,512]{1,0:T(8,128)(2,1)S(1)}, bf16[224,512]{1,0:T(8,128)(2,1)}, u32[]{:S(2)}) copy-start(bf16[224,512]{1,0:T(8,128)(2,1)} %get-tuple-element.77) | copy-start | bytes 688132
  5.5 46.4 %copy-start.1 = (bf16[448,512]{1,0:T(8,128)(2,1)S(1)}, bf16[448,512]{1,0:T(8,128)(2,1)}, u32[]{:S(2)}) copy-start(bf16[448,512]{1,0:T(8,128)(2,1)} %get-tuple-element.62.refs_4_) | copy-start | bytes 1376260
  5.6 46.4 %copy-start.2 = (bf16[224,512]{1,0:T(8,128)(2,1)S(1)}, bf16[224,512]{1,0:T(8,128)(2,1)}, u32[]{:S(2)}) copy-start(bf16[224,512]{1,0:T(8,128)(2,1)} %get-tuple-element.82.refs_0_) | copy-start | bytes 688132
  5.6 5.4 %collective-permute-start.3 = (bf16[448,512]{1,0:T(8,128)(2,1)}, bf16[448,512]{1,0:T(8,128)(2,1)S(1)}, u32[]{:S(2)}, u32[]{:S(2)}) collective-permute-start(bf16[448,512]{1,0:T(8,128)(2,1)} %get-tuple-element.62.refs_4_), channel_id=1, source_target_pairs={{0,8},{8,0},{16,24},{24,16},{32,40},{40,32},{48,56},{56,48},{64,72... | collective-permute-start | bytes 1376264 | tf_op jit(solution)/shard_map/ppermute | solution.py:42
  5.7 13.1 %collective-permute-start.2 = (bf16[448,512]{1,0:T(8,128)(2,1)}, bf16[448,512]{1,0:T(8,128)(2,1)S(1)}, u32[]{:S(2)}, u32[]{:S(2)}) collective-permute-start(bf16[448,512]{1,0:T(8,128)(2,1)} %get-tuple-element.62.refs_4_), channel_id=1, source_target_pairs={{0,16},{8,24},{16,0},{24,8},{32,48},{40,56},{48,32},{56,40},{64,80... | collective-permute-start | bytes 1376264 | tf_op jit(solution)/shard_map/ppermute | solution.py:38
  7.3 14.0 %collective-permute-start = (bf16[448,512]{1,0:T(8,128)(2,1)}, bf16[448,512]{1,0:T(8,128)(2,1)S(1)}, u32[]{:S(2)}, u32[]{:S(2)}) collective-permute-start(bf16[448,512]{1,0:T(8,128)(2,1)} %get-tuple-element.60), channel_id=1, source_target_pairs={{0,48},{8,56},{16,32},{24,40},{32,16},{40,24},{48,0},{56,8},{64,11... | collective-permute-start | bytes 1376264 | tf_op jit(solution)/shard_map/ppermute | solution.py:34
  9.4 12.5 %collective-permute-start.1 = (bf16[448,512]{1,0:T(8,128)(2,1)}, bf16[448,512]{1,0:T(8,128)(2,1)S(1)}, u32[]{:S(2)}, u32[]{:S(2)}) collective-permute-start(bf16[448,512]{1,0:T(8,128)(2,1)} %get-tuple-element.61), channel_id=1, source_target_pairs={{0,64},{8,72},{16,80},{24,88},{32,96},{40,104},{48,112},{56,120},{... | collective-permute-start | bytes 1376264 | tf_op jit(solution)/shard_map/ppermute | solution.py:34
  14.7 1.4 %collective-permute-start.4 = (bf16[80,896]{1,0:T(8,128)(2,1)S(1)}, bf16[80,896]{1,0:T(8,128)(2,1)S(1)}, u32[]{:S(2)}, u32[]{:S(2)}) collective-permute-start(bf16[80,896]{1,0:T(8,128)(2,1)S(1)} %get-tuple-element.65), channel_id=1, source_target_pairs={{0,8},{8,0},{16,24},{24,16},{32,40},{40,32},{48,56},{56,48},{64,72... | collective-permute-start | bytes 430088 | tf_op jit(solution)/shard_map/ppermute | solution.py:42
  16.8 5.9 %collective-permute-start.5 = (bf16[80,896]{1,0:T(8,128)(2,1)S(1)}, bf16[80,896]{1,0:T(8,128)(2,1)S(1)}, u32[]{:S(2)}, u32[]{:S(2)}) collective-permute-start(bf16[80,896]{1,0:T(8,128)(2,1)S(1)} %get-tuple-element.67), channel_id=1, source_target_pairs={{0,16},{8,24},{16,0},{24,8},{32,48},{40,56},{48,32},{56,40},{64,80... | collective-permute-start | bytes 430088 | tf_op jit(solution)/shard_map/ppermute | solution.py:38
  22.7 24.6 %collective-permute-start.6 = (bf16[672,512]{1,0:T(8,128)(2,1)S(1)}, bf16[672,512]{1,0:T(8,128)(2,1)S(1)}, u32[]{:S(2)}, u32[]{:S(2)}) collective-permute-start(bf16[672,512]{1,0:T(8,128)(2,1)S(1)} %copy-done.11), channel_id=1, source_target_pairs={{0,112},{8,120},{16,96},{24,104},{32,80},{40,88},{48,64},{56,72},{... | collective-permute-start | bytes 2064392 | tf_op jit(solution)/shard_map/ppermute | solution.py:34
  25.7 20.7 %collective-permute-start.7 = (bf16[448,512]{1,0:T(8,128)(2,1)S(1)}, bf16[448,512]{1,0:T(8,128)(2,1)S(1)}, u32[]{:S(2)}, u32[]{:S(2)}) collective-permute-start(bf16[448,512]{1,0:T(8,128)(2,1)S(1)} %collective-permute-done.refs_5_), channel_id=1, source_target_pairs={{0,16},{8,24},{16,0},{24,8},{32,48},{40,56},{48,32},{56,40},{64,80... | collective-permute-start | bytes 1376264 | tf_op jit(solution)/shard_map/ppermute | solution.py:38
  26.0 21.4 %collective-permute-start.8 = (bf16[448,512]{1,0:T(8,128)(2,1)S(1)}, bf16[448,512]{1,0:T(8,128)(2,1)S(1)}, u32[]{:S(2)}, u32[]{:S(2)}) collective-permute-start(bf16[448,512]{1,0:T(8,128)(2,1)S(1)} %collective-permute-done.1.refs_6_), channel_id=1, source_target_pairs={{0,16},{8,24},{16,0},{24,8},{32,48},{40,56},{48,32},{56,40},{64,80... | collective-permute-start | bytes 1376264 | tf_op jit(solution)/shard_map/ppermute | solution.py:38
  28.4 18.0 %collective-permute-start.10 = (bf16[224,512]{1,0:T(8,128)(2,1)S(1)}, bf16[224,512]{1,0:T(8,128)(2,1)S(1)}, u32[]{:S(2)}, u32[]{:S(2)}) collective-permute-start(bf16[224,512]{1,0:T(8,128)(2,1)S(1)} %copy-done.13), channel_id=1, source_target_pairs={{0,64},{8,72},{16,80},{24,88},{32,96},{40,104},{48,112},{56,120},{... | collective-permute-start | bytes 688136 | tf_op jit(solution)/shard_map/ppermute | solution.py:34
  29.0 17.4 %collective-permute-start.9 = (bf16[224,512]{1,0:T(8,128)(2,1)S(1)}, bf16[224,512]{1,0:T(8,128)(2,1)S(1)}, u32[]{:S(2)}, u32[]{:S(2)}) collective-permute-start(bf16[224,512]{1,0:T(8,128)(2,1)S(1)} %copy-done.12), channel_id=1, source_target_pairs={{0,48},{8,56},{16,32},{24,40},{32,16},{40,24},{48,0},{56,8},{64,11... | collective-permute-start | bytes 688136 | tf_op jit(solution)/shard_map/ppermute | solution.py:34
  47.3 4.3 %collective-permute-start.15 = (bf16[672,512]{1,0:T(8,128)(2,1)S(1)}, bf16[672,512]{1,0:T(8,128)(2,1)S(1)}, u32[]{:S(2)}, u32[]{:S(2)}) collective-permute-start(bf16[672,512]{1,0:T(8,128)(2,1)S(1)} %collective-permute-done.6.refs_3_.refs_7_), channel_id=1, source_target_pairs={{0,8},{8,0},{16,24},{24,16},{32,40},{40,32},{48,56},{56,48},{64,72... | collective-permute-start | bytes 2064392 | tf_op jit(solution)/shard_map/ppermute | solution.py:42
  47.4 3.8 %collective-permute-start.13 = (bf16[448,512]{1,0:T(8,128)(2,1)S(1)}, bf16[448,512]{1,0:T(8,128)(2,1)S(1)}, u32[]{:S(2)}, u32[]{:S(2)}) collective-permute-start(bf16[448,512]{1,0:T(8,128)(2,1)S(1)} %collective-permute-done.refs_5_), channel_id=1, source_target_pairs={{0,8},{8,0},{16,24},{24,16},{32,40},{40,32},{48,56},{56,48},{64,72... | collective-permute-start | bytes 1376264 | tf_op jit(solution)/shard_map/ppermute | solution.py:42
  47.9 3.3 %collective-permute-start.14 = (bf16[448,512]{1,0:T(8,128)(2,1)S(1)}, bf16[448,512]{1,0:T(8,128)(2,1)S(1)}, u32[]{:S(2)}, u32[]{:S(2)}) collective-permute-start(bf16[448,512]{1,0:T(8,128)(2,1)S(1)} %collective-permute-done.1.refs_6_), channel_id=1, source_target_pairs={{0,8},{8,0},{16,24},{24,16},{32,40},{40,32},{48,56},{56,48},{64,72... | collective-permute-start | bytes 1376264 | tf_op jit(solution)/shard_map/ppermute | solution.py:42
  47.9 17.2 %collective-permute-start.11 = (bf16[448,512]{1,0:T(8,128)(2,1)S(1)}, bf16[448,512]{1,0:T(8,128)(2,1)S(1)}, u32[]{:S(2)}, u32[]{:S(2)}) collective-permute-start(bf16[448,512]{1,0:T(8,128)(2,1)S(1)} %slice.6), channel_id=1, source_target_pairs={{0,16},{8,24},{16,0},{24,8},{32,48},{40,56},{48,32},{56,40},{64,80... | collective-permute-start | bytes 1376264 | tf_op jit(solution)/shard_map/ppermute | solution.py:38
  48.3 16.8 %collective-permute-start.12 = (bf16[80,896]{1,0:T(8,128)(2,1)S(1)}, bf16[80,896]{1,0:T(8,128)(2,1)S(1)}, u32[]{:S(2)}, u32[]{:S(2)}) collective-permute-start(bf16[80,896]{1,0:T(8,128)(2,1)S(1)} %get-tuple-element.81), channel_id=1, source_target_pairs={{0,32},{8,40},{16,48},{24,56},{32,0},{40,8},{48,16},{56,24},{64,96... | collective-permute-start | bytes 430088 | tf_op jit(solution)/shard_map/ppermute | solution.py:46
  51.2 17.0 %collective-permute-start.17 = (bf16[448,512]{1,0:T(8,128)(2,1)S(1)}, bf16[448,512]{1,0:T(8,128)(2,1)S(1)}, u32[]{:S(2)}, u32[]{:S(2)}) collective-permute-start(bf16[448,512]{1,0:T(8,128)(2,1)S(1)} %collective-permute-done.2.refs_0_), channel_id=1, source_target_pairs={{0,8},{8,0},{16,24},{24,16},{32,40},{40,32},{48,56},{56,48},{64,72... | collective-permute-start | bytes 1376264 | tf_op jit(solution)/shard_map/ppermute | solution.py:42
  51.2 17.0 %collective-permute-start.18 = (bf16[448,512]{1,0:T(8,128)(2,1)S(1)}, bf16[448,512]{1,0:T(8,128)(2,1)S(1)}, u32[]{:S(2)}, u32[]{:S(2)}) collective-permute-start(bf16[448,512]{1,0:T(8,128)(2,1)S(1)} %collective-permute-done.7.refs_1_), channel_id=1, source_target_pairs={{0,8},{8,0},{16,24},{24,16},{32,40},{40,32},{48,56},{56,48},{64,72... | collective-permute-start | bytes 1376264 | tf_op jit(solution)/shard_map/ppermute | solution.py:42
  51.7 16.5 %collective-permute-start.19 = (bf16[448,512]{1,0:T(8,128)(2,1)S(1)}, bf16[448,512]{1,0:T(8,128)(2,1)S(1)}, u32[]{:S(2)}, u32[]{:S(2)}) collective-permute-start(bf16[448,512]{1,0:T(8,128)(2,1)S(1)} %collective-permute-done.8.refs_2_), channel_id=1, source_target_pairs={{0,8},{8,0},{16,24},{24,16},{32,40},{40,32},{48,56},{56,48},{64,72... | collective-permute-start | bytes 1376264 | tf_op jit(solution)/shard_map/ppermute | solution.py:42
  65.1 3.1 %collective-permute-start.20 = (bf16[448,512]{1,0:T(8,128)(2,1)S(1)}, bf16[448,512]{1,0:T(8,128)(2,1)S(1)}, u32[]{:S(2)}, u32[]{:S(2)}) collective-permute-start(bf16[448,512]{1,0:T(8,128)(2,1)S(1)} %collective-permute-done.11.refs_3_), channel_id=1, source_target_pairs={{0,8},{8,0},{16,24},{24,16},{32,40},{40,32},{48,56},{56,48},{64,72... | collective-permute-start | bytes 1376264 | tf_op jit(solution)/shard_map/ppermute | solution.py:42
  66.6 11.6 %collective-permute-start.16 = (bf16[80,896]{1,0:T(8,128)(2,1)S(1)}, bf16[80,896]{1,0:T(8,128)(2,1)S(1)}, u32[]{:S(2)}, u32[]{:S(2)}) collective-permute-start(bf16[80,896]{1,0:T(8,128)(2,1)S(1)} %get-tuple-element.90), channel_id=1, source_target_pairs={{0,64},{8,72},{16,80},{24,88},{32,96},{40,104},{48,112},{56,120},{... | collective-permute-start | bytes 430088 | tf_op jit(solution)/shard_map/ppermute | solution.py:46
  78.2 23.1 %collective-permute-start.21 = (bf16[224,512]{1,0:T(8,128)(2,1)S(1)}, bf16[224,512]{1,0:T(8,128)(2,1)S(1)}, u32[]{:S(2)}, u32[]{:S(2)}) collective-permute-start(bf16[224,512]{1,0:T(8,128)(2,1)S(1)} %get-tuple-element.102), channel_id=1, source_target_pairs={{0,48},{8,56},{16,32},{24,40},{32,16},{40,24},{48,0},{56,8},{64,11... | collective-permute-start | bytes 688136 | tf_op jit(solution)/shard_map/ppermute | solution.py:34
  79.2 22.1 %collective-permute-start.22 = (bf16[224,512]{1,0:T(8,128)(2,1)S(1)}, bf16[224,512]{1,0:T(8,128)(2,1)S(1)}, u32[]{:S(2)}, u32[]{:S(2)}) collective-permute-start(bf16[224,512]{1,0:T(8,128)(2,1)S(1)} %get-tuple-element.103), channel_id=1, source_target_pairs={{0,64},{8,72},{16,80},{24,88},{32,96},{40,104},{48,112},{56,120},{... | collective-permute-start | bytes 688136 | tf_op jit(solution)/shard_map/ppermute | solution.py:34
  80.5 20.9 %collective-permute-start.23 = (bf16[224,512]{1,0:T(8,128)(2,1)S(1)}, bf16[224,512]{1,0:T(8,128)(2,1)S(1)}, u32[]{:S(2)}, u32[]{:S(2)}) collective-permute-start(bf16[224,512]{1,0:T(8,128)(2,1)S(1)} %get-tuple-element.104), channel_id=1, source_target_pairs={{0,112},{8,120},{16,96},{24,104},{32,80},{40,88},{48,64},{56,72},{... | collective-permute-start | bytes 688136 | tf_op jit(solution)/shard_map/ppermute | solution.py:34
  83.0 1.4 %copy-start.9 = (bf16[512,896]{1,0:T(8,128)(2,1)S(1)}, bf16[512,896]{1,0:T(8,128)(2,1)}, u32[]{:S(2)}) copy-start(bf16[512,896]{1,0:T(8,128)(2,1)} %gate_ref.1) | copy-start | bytes 2752516
  84.4 17.0 %copy-start.10 = (f32[896]{0:T(1024)S(1)}, f32[896]{0:T(1024)}, u32[]{:S(2)}) copy-start(f32[896]{0:T(1024)} %param.21) | copy-start | bytes 10756

commit v4 on v3

--- a/solution.py
+++ b/solution.py
@@ -55,16 +55,16 @@
 V_ROWS = slice(2 * ATT_DIM, 3 * ATT_DIM)
 
 
-def pack_kernel(info, q_in, k_in, v_in, q_own, q_1, q_2, kv_own, kv_1, kv_2, all_3, raw, rows_ref, sems):
-    copies = [pltpu.make_async_copy(src, raw.at[i], sems.at[i]) for i, src in enumerate((k_in, v_in, q_in))]
+def pack_kernel(info, q_in, k_in, v_in, q_own, kv_own, all_1, all_2, all_3, raw, rows_ref, sems):
+    copies = [pltpu.make_async_copy(src, raw.at[i], sems.at[i]) for i, src in enumerate((q_in, k_in, v_in))]
     for copy in copies:
         copy.start()
-    for i, (own, one, two, first) in enumerate(((kv_own, kv_1, kv_2, 0), (kv_own, kv_1, kv_2, ATT_DIM), (q_own, q_1, q_2, 0))):
+    for i, (out, first) in enumerate(((q_own, 0), (kv_own, 0), (kv_own, ATT_DIM))):
         copies[i].wait()
         rows_ref[i] = raw[i].T
-        for r, out in enumerate((own, one, two)):
-            out[first : first + ATT_DIM, :] = rows_ref[i, head_rows(info[0] ^ r), :]
-        all_3[(K_ROWS, V_ROWS, Q_ROWS)[i], :] = rows_ref[i, head_rows(info[0] ^ 3), :]
+        out[first : first + ATT_DIM, :] = rows_ref[i, head_rows(info[0]), :]
+        for r, away in ((1, all_1), (2, all_2), (3, all_3)):
+            away[i * ATT_DIM : (i + 1) * ATT_DIM, :] = rows_ref[i, head_rows(info[0] ^ r), :]
 
 
 def unpack_kernel(info, _, *refs):
@@ -74,24 +74,30 @@
     out_ref[...] = rows_ref[...].T
 
 
-def attend_kernel(own, info, *refs):
+def attend_kernel(stage, info, *refs):
     hid, kind, core = info[0], info[1], info[2]
     scale = ATT_DIM ** (-0.5) * LOG2E
-
-    if own:
-        queries, pieces, refs = refs[:4], refs[4:12], refs[12:]
-        acc, stats_out, qs, mark, ks, vs = refs
-        for r in range(4):
-            qs[r] = queries[r][Q_ROWS, :]
+    if stage == 0:
+        q_in, (kv_own, core_0, core_1, core_2, near_0, near_core_0), refs = refs[:3], refs[3:9], refs[9:]
+        acc, stats_ref, ks, vs, mark, qs = refs
+        pieces = [(0, 0, kv_own, 0), (1, 0, q_in[1], ATT_DIM), (2, 0, q_in[2], ATT_DIM)]
+        pieces += [(0, 1, core_0, 0), (1, 1, core_1, 0), (2, 1, core_2, 0)]
+        pieces += [(3, 0, near_0, 0), (3, 1, near_core_0, 0)]
+    elif stage == 1:
+        q_in, (core_3, near_1, near_core_1, near_2, near_core_2, _), refs = refs[:4], refs[4:10], refs[10:]
+        ks_early, vs_early, acc_in, stats_in, acc, stats_ref, mark, ks, vs, qs = refs
+        pieces = [(0, 0, q_in[3], ATT_DIM), (0, 1, core_3, 0)]
+        pieces += [(1, 0, near_1, 0), (1, 1, near_core_1, 0), (2, 0, near_2, 0), (2, 1, near_core_2, 0)]
     else:
-        pieces, refs = refs[:8], refs[8:]
-        _, qs, acc_in, stats_in, *o_out, mark, ks, vs, acc, os = refs
-    for i, piece in enumerate(pieces):
-        k_first = ATT_DIM if own and i & 3 == 3 else 0
-        v_first = k_first + ATT_DIM
-        start = pl.multiple_of((core ^ (i >> 2)) * TOK, TOK)
-        ks[hid ^ (i & 3), pl.ds(start, TOK), :] = piece[k_first:v_first, :].T
-        vs[hid ^ (i & 3), :, pl.ds(start, TOK)] = piece[v_first : v_first + ATT_DIM, :]
+        q_in, (near_3, near_core_3, _), refs = refs[:4], refs[4:7], refs[7:]
+        acc_in, stats_in, *o_out, mark, ks, vs, qs, acc, os = refs
+        pieces = [(0, 0, near_3, 0), (0, 1, near_core_3, 0)]
+    for slot, other, piece, first in pieces:
+        start = pl.multiple_of((core ^ other) * TOK, TOK)
+        ks[slot, pl.ds(start, TOK), :] = piece[first : first + ATT_DIM, :].T
+        vs[slot, :, pl.ds(start, TOK)] = piece[first + ATT_DIM : first + 2 * ATT_DIM, :]
+    for r, queries in enumerate(q_in):
+        qs[r] = queries[Q_ROWS, :]
     mark[...] = jnp.zeros_like(mark)
 
     def one_queries(r, carry):
@@ -122,25 +128,31 @@
                 )
             return tuple(new_stats)
 
-        def chip_block(j, stats):
-            return visit(ks[j], vs[j], stats, False)
-
-        def core_block(start, stats, masked):
-            start = pl.multiple_of(start, TOK)
-            return visit(
-                ks[chip, pl.ds(start, TOK), :], vs[chip, :, pl.ds(start, TOK)], stats, masked
-            )
-
-        if own:
+        def sweep(count, key_ref, value_ref, seen, stats):
+            def one(k, now):
+                times = jnp.where(seen(k), 1, 0)
+                return lax.fori_loop(
+                    0, times, lambda _, inner: visit(key_ref[k], value_ref[k], inner, False), now
+                )
+
+            return lax.fori_loop(0, count, one, stats)
+
+        def near_seen(k):
+            limit = jnp.where(kind == 0, ((chip + 1) >> 1) * 2, (chip >> 1) * 2 + 1)
+            return (hid ^ k) < limit
+
+        def diagonal(slot, stats):
+            def part(start, now, masked):
+                start = pl.multiple_of(start, TOK)
+                return visit(ks[slot, pl.ds(start, TOK), :], vs[slot, :, pl.ds(start, TOK)], now, masked)
+
+            stats = lax.fori_loop(0, core, lambda _, now: part(0, now, False), stats)
+            return part(core * TOK, stats, True)
+
+        if stage == 0:
             acc[r] = jnp.zeros((ATT_DIM, TOK), F32)
             first = (jnp.full((1, HALF), -1e30, F32), jnp.zeros((1, HALF), F32))
-            stats = lax.fori_loop(0, chip, chip_block, (first, first))
-            stats = lax.fori_loop(0, core, lambda k, now: core_block(0, now, False), stats)
-            stats = core_block(core * TOK, stats, True)
-            for half in range(2):
-                lanes = slice(half * HALF, (half + 1) * HALF)
-                stats_out[r, 0:8, lanes] = jnp.broadcast_to(stats[half][0], (8, HALF))
-                stats_out[r, 8:16, lanes] = jnp.broadcast_to(stats[half][1], (8, HALF))
+            stats = (first, first)
         else:
             acc[r] = acc_in[r]
             stats = tuple(
@@ -150,15 +162,35 @@
                 )
                 for half in range(2)
             )
-            count = jnp.where(kind == 0, ((chip + 1) >> 1) * 2, (chip >> 1) * 2 + 1)
-            stats = lax.fori_loop(0, count, chip_block, stats)
-            for half in range(2):
-                lanes = slice(half * HALF, (half + 1) * HALF)
+
+        if stage == 0:
+
+            def early(now):
+                now = sweep(4, ks, vs, lambda k: jnp.where(k == 3, near_seen(0), (hid ^ k) < chip), now)
+                return diagonal(r, now)
+
+            stats = lax.fori_loop(0, jnp.where(r == 3, 0, 1), lambda _, now: early(now), stats)
+        elif stage == 1:
+            last = jnp.where(r == 3, 1, 0)
+            stats = sweep(
+                4 * last, ks_early, vs_early, lambda k: jnp.where(k == 3, near_seen(0), (hid ^ k) < chip), stats
+            )
+            stats = sweep(3, ks, vs, lambda k: jnp.where(k == 0, (hid ^ 3) < chip, near_seen(k)), stats)
+            stats = lax.fori_loop(0, last, lambda _, now: diagonal(0, now), stats)
+        else:
+            stats = sweep(1, ks, vs, lambda k: near_seen(3), stats)
+
+        for half in range(2):
+            lanes = slice(half * HALF, (half + 1) * HALF)
+            if stage == 2:
                 os[r, :, lanes] = (acc[r, :, lanes] / stats[half][1]).astype(BF16)
+            else:
+                stats_ref[r, 0:8, lanes] = jnp.broadcast_to(stats[half][0], (8, HALF))
+                stats_ref[r, 8:16, lanes] = jnp.broadcast_to(stats[half][1], (8, HALF))
         return carry
 
     lax.fori_loop(0, 4, one_queries, 0)
-    if not own:
+    if stage == 2:
         for r in range(4):
             o_out[r][...] = os[r]
 
@@ -286,7 +318,6 @@
 
 
 SMALL = pl.CostEstimate(flops=1000, bytes_accessed=1000, transcendentals=0)
-LARGE = pl.CostEstimate(flops=4 * 10**10, bytes_accessed=6 * 2**20, transcendentals=10**6)
 
 
 def params(mib):
@@ -299,7 +330,7 @@
 
 def pack(info, query_rows, key_rows, value_rows):
     width = HEADS * ATT_DIM
-    rows = [ATT_DIM] * 3 + [2 * ATT_DIM] * 3 + [3 * ATT_DIM]
+    rows = [ATT_DIM, 2 * ATT_DIM] + [3 * ATT_DIM] * 3
     return pl.pallas_call(
         pack_kernel,
         out_shape=[shape((count, TOK), BF16) for count in rows],
@@ -314,16 +345,24 @@
     )(info, query_rows, key_rows, value_rows)
 
 
-def attend(own, info, *operands):
-    scratch = [pltpu.VMEM((4, 2 * TOK, ATT_DIM), BF16), pltpu.VMEM((4, ATT_DIM, 2 * TOK), BF16)]
-    if own:
-        out = [shape((4, ATT_DIM, TOK), F32), shape((4, 16, TOK), F32), shape((4, ATT_DIM, TOK), BF16)]
+def attend(stage, info, *operands):
+    slots = (4, 3, 1)[stage]
+    keys, values = (slots, 2 * TOK, ATT_DIM), (slots, ATT_DIM, 2 * TOK)
+    state = [shape((4, ATT_DIM, TOK), F32), shape((4, 16, TOK), F32)]
+    queries = pltpu.VMEM((4, ATT_DIM, TOK), BF16)
+    mark = [shape((8, 128), F32)]
+    if stage == 0:
+        out = state + [shape(keys, BF16), shape(values, BF16)] + mark
+        scratch = [queries]
+    elif stage == 1:
+        out = state + mark
+        scratch = [pltpu.VMEM(keys, BF16), pltpu.VMEM(values, BF16), queries]
     else:
-        out = [shape((ATT_DIM, TOK), BF16)] * 4
-        scratch += [pltpu.VMEM((4, ATT_DIM, TOK), F32), pltpu.VMEM((4, ATT_DIM, TOK), BF16)]
-    out = out + [shape((8, 128), F32)]
+        out = [shape((ATT_DIM, TOK), BF16)] * 4 + mark
+        scratch = [pltpu.VMEM(keys, BF16), pltpu.VMEM(values, BF16), queries]
+        scratch += [pltpu.VMEM((4, ATT_DIM, TOK), F32), queries]
     return pl.pallas_call(
-        functools.partial(attend_kernel, own),
+        functools.partial(attend_kernel, stage),
         out_shape=out,
         in_specs=[SMEM] + vmem(len(operands)),
         out_specs=vmem(len(out)),
@@ -371,7 +410,7 @@
         in_specs=[SMEM] + vmem(3),
         out_specs=vmem(3),
         compiler_params=params(40),
-        cost_estimate=LARGE if level == 3 else SMALL,
+        cost_estimate=SMALL,
     )(info, got, total, before)
 
 
@@ -383,7 +422,7 @@
         in_specs=vmem(5),
         out_specs=vmem(2),
         compiler_params=params(40),
-        cost_estimate=LARGE,
+        cost_estimate=SMALL,
     )(state, mixed, cum, read_t, gate)
 
 
@@ -405,9 +444,9 @@
     info = jnp.stack([y * 2 + (x >> 1), (x ^ (x >> 1)) & 1, core, me]).astype(jnp.int32)
     tie = lax.optimization_barrier
 
-    q_own, q_1, q_2, kv_own, kv_1, kv_2, all_3 = pack(info, query_rows, key_rows, value_rows)
-    here, near, from_core = [kv_own] + [None] * 3, [None] * 4, [None] * 4
-    here[1], here[2] = head_swap(kv_1, 1), head_swap(kv_2, 2)
+    q_own, kv_own, all_1, all_2, all_3 = pack(info, query_rows, key_rows, value_rows)
+    here, near, from_core, near_core = [None] * 4, [None] * 4, [None] * 4, [None] * 4
+    here[1], here[2] = head_swap(all_1, 1), head_swap(all_2, 2)
     near[0] = class_swap(kv_own)
     from_core[0] = core_swap(kv_own)
 
@@ -419,33 +458,44 @@
     before = jnp.zeros_like(total)
     total, before, sent = ssm_merge(0, info, core_swap(sent), total, before)
     got = class_swap(sent)
-
-    here[1], here[2], near[0], all_3, got = tie((here[1], here[2], near[0], all_3, got))
-    near[1], near[2] = class_swap(here[1]), class_swap(here[2])
-    here[3] = head_swap(all_3, 3)
+    near[0], sent = tie((near[0], sent))
+    near_core[0] = core_swap(near[0])
+
     total, before, sent = ssm_merge(1, info, got, total, before)
-    q_1, q_2, sent = tie((q_1, q_2, sent))
-    q_1, q_2 = head_swap(q_1, 1), head_swap(q_2, 2)
-
-    here[3], near[1], near[2], q_1, q_2, sent = tie((here[3], near[1], near[2], q_1, q_2, sent))
-    near[3] = class_swap(here[3][ATT_DIM:])
-    for r in range(1, 4):
-        from_core[r] = core_swap(here[r])
     got = block_swap(sent, 4)
-    partial, stats, queries, mark = attend(True, info, q_own, q_1, q_2, here[3], *here, *from_core)
-
-    near[3], got, mark = tie((near[3], got, mark))
-    near_core = [core_swap(piece) for piece in near]
+    here[1], here[2], near_core[0], got = tie((here[1], here[2], near_core[0], got))
+    for r in (1, 2):
+        kv = here[r][ATT_DIM:]
+        near[r] = class_swap(kv)
+        from_core[r] = core_swap(kv)
     total, before, sent = ssm_merge(2, info, got, total, before)
     got = block_swap(sent, 8)
-    *results, mark = attend(False, info, *near, *near_core, mark, queries, partial, stats)
-    back = [results[0]] + [head_swap(results[r], r) for r in range(1, 4)]
-    got, mark = tie((got, mark))
+    got, all_3 = tie((got, all_3))
+    here[3] = head_swap(all_3, 3)
     total, before, sent = ssm_merge(3, info, got, total, before)
     count = lax.axis_size("tp")
     gated, squares = ssm_carry(count, before, mixed, cum, read_t, ssm_gate)
+    *state, ks, vs, mark = attend(
+        0, info, q_own, here[1], here[2], kv_own, *from_core[:3], near[0], near_core[0]
+    )
+    squares, mark = tie((squares, mark))
     squares = lax.all_to_all(squares, "tp", 0, 0, tiled=True).reshape(count, 8, TOK)
-    *back, squares = tie((*back, squares))
+
+    here[3], near[1], near[2], squares, mark = tie((here[3], near[1], near[2], squares, mark))
+    kv = here[3][ATT_DIM:]
+    near[3] = class_swap(kv)
+    from_core[3] = core_swap(kv)
+    near_core[1], near_core[2] = core_swap(near[1]), core_swap(near[2])
+    queries = (q_own, here[1], here[2], here[3])
+    *state, mark = attend(
+        1, info, *queries, from_core[3], near[1], near_core[1], near[2], near_core[2], mark, ks, vs, *state
+    )
+
+    near[3], mark = tie((near[3], mark))
+    near_core[3] = core_swap(near[3])
+    *results, mark = attend(2, info, *queries, near[3], near_core[3], mark, *state)
+    back = [results[0]] + [head_swap(results[r], r) for r in range(1, 4)]
+    gated, mark = tie((gated, mark))
     factor = lax.rsqrt(jnp.sum(squares[:, 0], axis=0) / SSM_WIDTH + 1e-05)
     mixer_out = (gated * factor[:, None] * norm_gain[None, :]).astype(BF16)
     return (unpack(info, mark, back), mixer_out)

time: 105 us -> 118 us (1.12)
  blocking collectives: 15.5 us -> 0 us
  local copies, waits for them, and re-layouts: 0.11 us -> 10.2 us
  starting transfers between devices: 24.7 us -> 34.4 us
  waiting for transfers between devices: 26.1 us -> 33.1 us
  Pallas kernels: 35.2 us -> 37.2 us
    all_to_all x1 -> x0, blocking collectives: 15.5 us -> none  [on_device(): lax.all_to_all(squares, 'tp', 0, 0, tiled=True).reshape(count, 8, TOK)]
    ppermute x8 -> x6, waiting for transfers between devices: 19.3 us -> 7.61 us  [head_swap(): lax.ppermute(value, 'ctx', [(i, exchanged(i, r)) for i in range(CTX)])]
    unnamed x28 -> x38, local copies, waits for them, and re-layouts: 0.06 us -> 8.52 us
    all_to_all x0 -> x1, waiting for transfers between devices: none -> 8.13 us  [on_device(): lax.all_to_all(squares, 'tp', 0, 0, tiled=True).reshape(count, 8, TOK)]
    all_to_all x0 -> x1, starting transfers between devices: none -> 7.64 us  [on_device(): lax.all_to_all(squares, 'tp', 0, 0, tiled=True).reshape(count, 8, TOK)]
    ppermute x2, waiting for transfers between devices: 2.38 us -> 7.22 us  [block_swap(): return lax.ppermute(value, 'ctx', [(i, i ^ step) for i in range(CTX)])]
    ppermute x5, waiting for transfers between devices: 3.05 us -> 6.57 us  [class_swap(): return lax.ppermute(value, 'ctx', [(i, i ^ 2) for i in range(CTX)])]
    ppermute x9, waiting for transfers between devices: 1.37 us -> 3.58 us  [core_swap(): return lax.ppermute(value, 'ctx', [(i, i ^ 1) for i in range(CTX)])]
  transfers between devices with their start and end apart: 24 -> 23, of which waited for: 8 -> 11; matrix products, arithmetic and copies ran while one was open for 0% -> 2% of each run, Pallas kernels for 28% -> 24%
where the time goes in v4:
time: 118 us
  Pallas kernels  37.2 us (32%)
  starting transfers between devices  34.4 us (29%)
  waiting for transfers between devices  33.1 us (28%)
  local copies, waits for them, and re-layouts  10.2 us (9%)
  other arithmetic  1.85 us (2%)
    pallas_call x3, Pallas kernels, attend(): pl.pallas_call(functools.partial(attend_kernel, stage), out_shape=out, in...  21.9 us
    ppermute x6, starting transfers between devices, head_swap(): lax.ppermute(value, 'ctx', [(i, exchanged(i, r)) for i in range(CTX)])  12.3 us
    unnamed x38, local copies, waits for them, and re-layouts  8.52 us
    all_to_all x1, waiting for transfers between devices, on_device(): lax.all_to_all(squares, 'tp', 0, 0, tiled=True).reshape(count, 8, TOK)  8.13 us
    all_to_all x1, starting transfers between devices, on_device(): lax.all_to_all(squares, 'tp', 0, 0, tiled=True).reshape(count, 8, TOK)  7.64 us
    ppermute x6, waiting for transfers between devices, head_swap(): lax.ppermute(value, 'ctx', [(i, exchanged(i, r)) for i in range(CTX)])  7.61 us
    ppermute x2, waiting for transfers between devices, block_swap(): return lax.ppermute(value, 'ctx', [(i, i ^ step) for i in range(CTX)])  7.22 us
    ppermute x5, starting transfers between devices, class_swap(): return lax.ppermute(value, 'ctx', [(i, i ^ 2) for i in range(CTX)])  6.68 us
  transfers between devices with their start and end apart: 23, of which 11 were waited for; matrix products, arithmetic and copies ran while one was open for 2% of the time, Pallas kernels for 24%

profile of v4, /device:TPU:0, one launch (start us, length us, event | category | flops | bytes accessed | tf_op | source)
XLA Modules:
  0.0 117.6 jit_solution(9286890817443662491)
XLA Ops:
  0.7 0.7 pad_add_fusion.info
  1.4 4.5 %shard_map.122 = (bf16[224,512]{1,0:T(8,128)(2,1)}, bf16[448,512]{1,0:T(8,128)(2,1)}, bf16[672,512]{1,0:T(8,128)(2,1)}, bf16[672,512]{1,0:T(8,128)(2,1)}, bf16[672,512]{1,0:T(8,128)(2,1)}) custom-call(s32[4]{0:T(128)} %pad_add_fusion.info, bf16[512,896]{1,0:T(8,128)(2,1)} %q_in.1, bf16[512,896]{1,0:T(8,128)(2,1)} %k_in.1, bf16[512,896]{1,0:T(8,128)(2,1)} %v_in.1), custom_call_target="tpu_custom_call" | custom-call | tf_op jit(solution)/shard_map/pallas_call | solution.py:334
  5.8 0.1 collective-permute-start.3
  5.9 1.7 %collective-permute-start.2 = (bf16[448,512]{1,0:T(8,128)(2,1)}, bf16[448,512]{1,0:T(8,128)(2,1)S(1)}, u32[]{:S(2)}, u32[]{:S(2)}) collective-permute-start(bf16[448,512]{1,0:T(8,128)(2,1)} %get-tuple-element.58.refs_3_), channel_id=1, source_target_pairs={{0,16},{8,24},{16,0},{24,8},{32,48},{40,56},{48,32},{56,40},{64,80... | collective-permute-start | bytes 1376264 | tf_op jit(solution)/shard_map/ppermute | solution.py:38
  7.6 2.1 %collective-permute-start = (bf16[672,512]{1,0:T(8,128)(2,1)}, bf16[672,512]{1,0:T(8,128)(2,1)S(1)}, u32[]{:S(2)}, u32[]{:S(2)}) collective-permute-start(bf16[672,512]{1,0:T(8,128)(2,1)} %get-tuple-element.56), channel_id=1, source_target_pairs={{0,48},{8,56},{16,32},{24,40},{32,16},{40,24},{48,0},{56,8},{64,11... | collective-permute-start | bytes 2064392 | tf_op jit(solution)/shard_map/ppermute | solution.py:34
  9.7 1.6 %collective-permute-start.1 = (bf16[672,512]{1,0:T(8,128)(2,1)}, bf16[672,512]{1,0:T(8,128)(2,1)S(1)}, u32[]{:S(2)}, u32[]{:S(2)}) collective-permute-start(bf16[672,512]{1,0:T(8,128)(2,1)} %get-tuple-element.57), channel_id=1, source_target_pairs={{0,64},{8,72},{16,80},{24,88},{32,96},{40,104},{48,112},{56,120},{... | collective-permute-start | bytes 2064392 | tf_op jit(solution)/shard_map/ppermute | solution.py:34
  11.3 0.0 collective-permute-done.3.refs_4_
  11.3 3.6 %shard_map.123 = (f32[512,896]{1,0:T(8,128)S(1)}, f32[72,896]{1,0:T(8,128)S(1)}, bf16[80,896]{1,0:T(8,128)(2,1)S(1)}, f32[512,14]{1,0:T(8,128)S(1)}) custom-call(bf16[512,896]{1,0:T(8,128)(2,1)S(1)} %copy-done.9, bf16[64,512]{1,0:T(8,128)(2,1)S(1)} %bitcast.12, bf16[64,512]{1,0:T(8,128)(2,1)S(1)} %bitcast.10, f32[14,512]{1,0:T(8,128)S(1)} %bitcast.13, ...), custom_call_target="tpu_custom_call" | custom-call | flops 1000 | bytes 1000 | tf_op jit(solution)/shard_map/pallas_call | solution.py:390
  15.0 0.1 collective-permute-start.4
  15.1 1.4 %collective-permute-done.4.got_ref = bf16[80,896]{1,0:T(8,128)(2,1)S(1)} collective-permute-done((bf16[80,896]{1,0:T(8,128)(2,1)S(1)}, bf16[80,896]{1,0:T(8,128)(2,1)S(1)}, u32[]{:S(2)}, u32[]{:S(2)}) %collective-permute-start.4) | collective-permute-done | bytes 143392 | tf_op jit(solution)/shard_map/ppermute | solution.py:42
  16.4 0.7 shard_map.124
  17.1 2.0 %collective-permute-done.2.refs_7_ = bf16[448,512]{1,0:T(8,128)(2,1)S(1)} collective-permute-done((bf16[448,512]{1,0:T(8,128)(2,1)}, bf16[448,512]{1,0:T(8,128)(2,1)S(1)}, u32[]{:S(2)}, u32[]{:S(2)}) %collective-permute-start.2) | collective-permute-done | bytes 458784 | tf_op jit(solution)/shard_map/ppermute | solution.py:38
  19.1 0.0 collective-permute-start.5
  19.1 1.6 %collective-permute-start.6 = (bf16[80,896]{1,0:T(8,128)(2,1)S(1)}, bf16[80,896]{1,0:T(8,128)(2,1)S(1)}, u32[]{:S(2)}, u32[]{:S(2)}) collective-permute-start(bf16[80,896]{1,0:T(8,128)(2,1)S(1)} %get-tuple-element.62), channel_id=1, source_target_pairs={{0,16},{8,24},{16,0},{24,8},{32,48},{40,56},{48,32},{56,40},{64,80... | collective-permute-start | bytes 430088 | tf_op jit(solution)/shard_map/ppermute | solution.py:38
  20.7 4.6 %collective-permute-done.6.got_ref = bf16[80,896]{1,0:T(8,128)(2,1)S(1)} collective-permute-done((bf16[80,896]{1,0:T(8,128)(2,1)S(1)}, bf16[80,896]{1,0:T(8,128)(2,1)S(1)}, u32[]{:S(2)}, u32[]{:S(2)}) %collective-permute-start.6) | collective-permute-done | bytes 143392 | tf_op jit(solution)/shard_map/ppermute | solution.py:38
  25.3 0.7 shard_map.125
  25.9 3.2 %collective-permute-start.7 = (bf16[80,896]{1,0:T(8,128)(2,1)S(1)}, bf16[80,896]{1,0:T(8,128)(2,1)S(1)}, u32[]{:S(2)}, u32[]{:S(2)}) collective-permute-start(bf16[80,896]{1,0:T(8,128)(2,1)S(1)} %get-tuple-element.66), channel_id=1, source_target_pairs={{0,32},{8,40},{16,48},{24,56},{32,0},{40,8},{48,16},{56,24},{64,96... | collective-permute-start | bytes 430088 | tf_op jit(solution)/shard_map/ppermute | solution.py:46
  29.1 0.0 collective-permute-done.refs_1_
  29.1 3.8 %collective-permute-done.7.got_ref = bf16[80,896]{1,0:T(8,128)(2,1)S(1)} collective-permute-done((bf16[80,896]{1,0:T(8,128)(2,1)S(1)}, bf16[80,896]{1,0:T(8,128)(2,1)S(1)}, u32[]{:S(2)}, u32[]{:S(2)}) %collective-permute-start.7) | collective-permute-done | bytes 143392 | tf_op jit(solution)/shard_map/ppermute | solution.py:46
  32.9 0.0 collective-permute-done.5.refs_8_
  32.9 0.7 shard_map.126
  33.6 1.7 %collective-permute-start.8 = (bf16[80,896]{1,0:T(8,128)(2,1)S(1)}, bf16[80,896]{1,0:T(8,128)(2,1)S(1)}, u32[]{:S(2)}, u32[]{:S(2)}) collective-permute-start(bf16[80,896]{1,0:T(8,128)(2,1)S(1)} %get-tuple-element.70), channel_id=1, source_target_pairs={{0,64},{8,72},{16,80},{24,88},{32,96},{40,104},{48,112},{56,120},{... | collective-permute-start | bytes 430088 | tf_op jit(solution)/shard_map/ppermute | solution.py:46
  35.3 3.4 %collective-permute-done.8.got_ref = bf16[80,896]{1,0:T(8,128)(2,1)S(1)} collective-permute-done((bf16[80,896]{1,0:T(8,128)(2,1)S(1)}, bf16[80,896]{1,0:T(8,128)(2,1)S(1)}, u32[]{:S(2)}, u32[]{:S(2)}) %collective-permute-start.8) | collective-permute-done | bytes 143392 | tf_op jit(solution)/shard_map/ppermute | solution.py:46
  38.7 3.9 %collective-permute-start.9 = (bf16[672,512]{1,0:T(8,128)(2,1)}, bf16[672,512]{1,0:T(8,128)(2,1)S(1)}, u32[]{:S(2)}, u32[]{:S(2)}) collective-permute-start(bf16[672,512]{1,0:T(8,128)(2,1)} %get-tuple-element.82), channel_id=1, source_target_pairs={{0,112},{8,120},{16,96},{24,104},{32,80},{40,88},{48,64},{56,72},{... | collective-permute-start | bytes 2064392 | tf_op jit(solution)/shard_map/ppermute | solution.py:34
  42.6 0.8 slice.12
  43.4 0.8 slice.13
  44.2 0.0 collective-permute-start.13
  44.2 0.5 collective-permute-start.12
  44.7 0.2 collective-permute-start.11
  44.9 1.8 %collective-permute-start.10 = (bf16[448,512]{1,0:T(8,128)(2,1)}, bf16[448,512]{1,0:T(8,128)(2,1)S(1)}, u32[]{:S(2)}, u32[]{:S(2)}) collective-permute-start(bf16[448,512]{1,0:T(8,128)(2,1)} %slice.12), channel_id=1, source_target_pairs={{0,16},{8,24},{16,0},{24,8},{32,48},{40,56},{48,32},{56,40},{64,80... | collective-permute-start | bytes 1376264 | tf_op jit(solution)/shard_map/ppermute | solution.py:38
  46.7 1.4 %shard_map.127 = (f32[72,896]{1,0:T(8,128)}, f32[72,896]{1,0:T(8,128)S(1)}, bf16[80,896]{1,0:T(8,128)(2,1)}) custom-call(s32[4]{0:T(128)S(1)} %copy-done.14, bf16[80,896]{1,0:T(8,128)(2,1)S(1)} %collective-permute-done.8.got_ref, f32[72,896]{1,0:T(8,128)S(1)} %get-tuple-element.73.total_ref, f32[72,896]{1,0:T(8,128)S(1)} %get-tuple-element.74.before_ref), custom_call_target="tpu_custom_call" | custom-call | flops 1000 | bytes 1000 | tf_op jit(solution)/shard_map/pallas_call | solution.py:407
  48.1 2.1 %shard_map.128 = (f32[512,896]{1,0:T(8,128)S(1)}, f32[64,512]{1,0:T(8,128)}) custom-call(f32[72,896]{1,0:T(8,128)S(1)} %get-tuple-element.75.state_ref, f32[512,896]{1,0:T(8,128)S(1)} %get-tuple-element.76.mixed_ref, f32[512,14]{1,0:T(8,128)S(1)} %get-tuple-element.77.cum_ref, bf16[64,512]{1,0:T(8,128)(2,1)S(1)} %bitcast.11, bf16[512,896]{1,0:T(8,128)(2,1)S(1)} %copy-done.10), custom_call_target="tpu_custom_call" | custom-call | flops 1000 | bytes 1000 | tf_op jit(solution)/shard_map/pallas_call | solution.py:419
  50.2 0.0 collective-permute-done.13.refs_6_
  50.2 0.0 collective-permute-done.12.refs_5_
  50.2 9.2 %shard_map.129 = (f32[4,224,512]{2,1,0:T(8,128)S(1)}, f32[4,16,512]{2,1,0:T(8,128)S(1)}, bf16[4,1024,224]{2,1,0:T(8,128)(2,1)S(1)}, bf16[4,224,1024]{2,1,0:T(8,128)(2,1)S(1)}, f32[8,128]{1,0:T(8,128)S(1)}) custom-call(s32[4]{0:T(128)S(1)} %copy-done.14, bf16[224,512]{1,0:T(8,128)(2,1)S(1)} %copy-done.2, bf16[672,512]{1,0:T(8,128)(2,1)S(1)} %collective-permute-done.refs_1_, ...), custom_call_target="tpu_custom_call" | custom-call | flops 1000 | bytes 1000 | tf_op jit(solution)/shard_map/pallas_call | solution.py:364
  59.4 1.3 %copy-done = bf16[4,1024,224]{2,1,0:T(8,128)(2,1)} copy-done((bf16[4,1024,224]{2,1,0:T(8,128)(2,1)}, bf16[4,1024,224]{2,1,0:T(8,128)(2,1)S(1)}, u32[]{:S(2)}) %copy-start) | copy-done | bytes 1835032
  60.8 1.3 %copy-done.3 = f32[4,224,512]{2,1,0:T(8,128)} copy-done((f32[4,224,512]{2,1,0:T(8,128)}, f32[4,224,512]{2,1,0:T(8,128)S(1)}, u32[]{:S(2)}) %copy-start.3) | copy-done | bytes 1835032
  62.0 1.3 %copy-done.5 = bf16[4,224,1024]{2,1,0:T(8,128)(2,1)} copy-done((bf16[4,224,1024]{2,1,0:T(8,128)(2,1)}, bf16[4,224,1024]{2,1,0:T(8,128)(2,1)S(1)}, u32[]{:S(2)}) %copy-start.5) | copy-done | bytes 1835032
  63.3 7.6 %all-to-all-start = ((f32[8,8,512]{2,1,0:T(8,128)}), f32[8,8,512]{2,1,0:T(8,128)S(1)}, u32[]{:S(2)}, u32[]{:S(2)}) async-start(f32[8,8,512]{2,1,0:T(8,128)} %bitcast.9), calls=%async_computation | async-start | bytes 262144 | tf_op jit(solution)/shard_map/all_to_all | solution.py:482
  71.0 0.0 collective-permute-done.10.refs_5_
  71.0 8.1 %all-to-all-done = f32[8,8,512]{2,1,0:T(8,128)S(1)} async-done(((f32[8,8,512]{2,1,0:T(8,128)}), f32[8,8,512]{2,1,0:T(8,128)S(1)}, u32[]{:S(2)}, u32[]{:S(2)}) %all-to-all-start) | async-done | bytes 131104 | tf_op jit(solution)/shard_map/all_to_all | solution.py:482
  79.1 0.0 collective-permute-done.9.refs_3_
  79.1 0.5 collective-permute-start.15
  79.6 0.1 collective-permute-start.16
  79.7 0.4 collective-permute-start.17
  80.1 1.4 %collective-permute-start.14 = (bf16[448,512]{1,0:T(8,128)(2,1)S(1)}, bf16[448,512]{1,0:T(8,128)(2,1)S(1)}, u32[]{:S(2)}, u32[]{:S(2)}) collective-permute-start(bf16[448,512]{1,0:T(8,128)(2,1)S(1)} %slice.14), channel_id=1, source_target_pairs={{0,16},{8,24},{16,0},{24,8},{32,48},{40,56},{48,32},{56,40},{64,80... | collective-permute-start | bytes 1376264 | tf_op jit(solution)/shard_map/ppermute | solution.py:38
  81.6 0.0 collective-permute-done.15.refs_4_
  81.6 0.2 collective-permute-done.16.refs_6_
  81.7 0.7 collective-permute-done.17.refs_8_
  82.4 1.6 %copy-done.1 = bf16[4,1024,224]{2,1,0:T(8,128)(2,1)S(1)} copy-done((bf16[4,1024,224]{2,1,0:T(8,128)(2,1)S(1)}, bf16[4,1024,224]{2,1,0:T(8,128)(2,1)}, u32[]{:S(2)}) %copy-start.1) | copy-done | bytes 1835032
  84.0 1.5 %copy-done.4 = f32[4,224,512]{2,1,0:T(8,128)S(1)} copy-done((f32[4,224,512]{2,1,0:T(8,128)S(1)}, f32[4,224,512]{2,1,0:T(8,128)}, u32[]{:S(2)}) %copy-start.4) | copy-done | bytes 1835032
  85.5 1.5 %copy-done.6 = bf16[4,224,1024]{2,1,0:T(8,128)(2,1)S(1)} copy-done((bf16[4,224,1024]{2,1,0:T(8,128)(2,1)S(1)}, bf16[4,224,1024]{2,1,0:T(8,128)(2,1)}, u32[]{:S(2)}) %copy-start.6) | copy-done | bytes 1835032
  87.0 10.6 %shard_map.130 = (f32[4,224,512]{2,1,0:T(8,128)S(1)}, f32[4,16,512]{2,1,0:T(8,128)S(1)}, f32[8,128]{1,0:T(8,128)S(1)}) custom-call(s32[4]{0:T(128)S(1)} %copy-done.14, bf16[224,512]{1,0:T(8,128)(2,1)S(1)} %copy-done.2, bf16[672,512]{1,0:T(8,128)(2,1)S(1)} %collective-permute-done.refs_1_, bf16[672,512]{1,0:T(8,128)(2,1)S(1)} %collective-permute-done.1.refs_2_, ...), custom_call_target="tpu_custom_call" | custom-call | flops 1000 | bytes 1000 | tf_op jit(solution)/shard_map/pallas_call | solution.py:364
  97.5 1.2 collective-permute-start.18
  98.7 1.4 %collective-permute-done.18.refs_5_ = bf16[448,512]{1,0:T(8,128)(2,1)S(1)} collective-permute-done((bf16[448,512]{1,0:T(8,128)(2,1)S(1)}, bf16[448,512]{1,0:T(8,128)(2,1)S(1)}, u32[]{:S(2)}, u32[]{:S(2)}) %collective-permute-start.18) | collective-permute-done | bytes 458784 | tf_op jit(solution)/shard_map/ppermute | solution.py:42
  100.1 2.1 %shard_map.131 = (bf16[224,512]{1,0:T(8,128)(2,1)S(1)}, bf16[224,512]{1,0:T(8,128)(2,1)S(1)}, bf16[224,512]{1,0:T(8,128)(2,1)S(1)}, bf16[224,512]{1,0:T(8,128)(2,1)S(1)}, f32[8,128]{1,0:T(8,128)S(1)}) custom-call(s32[4]{0:T(128)S(1)} %copy-done.14, bf16[224,512]{1,0:T(8,128)(2,1)S(1)} %copy-done.2, bf16[672,512]{1,0:T(8,128)(2,1)S(1)} %collective-permute-done.refs_1_, ...), custom_call_target="tpu_custom_call" | custom-call | flops 1000 | bytes 1000 | tf_op jit(solution)/shard_map/pallas_call | solution.py:364
  102.3 0.6 collective-permute-start.19
  102.8 0.0 collective-permute-start.20
  102.9 4.2 %collective-permute-start.21 = (bf16[224,512]{1,0:T(8,128)(2,1)S(1)}, bf16[224,512]{1,0:T(8,128)(2,1)S(1)}, u32[]{:S(2)}, u32[]{:S(2)}) collective-permute-start(bf16[224,512]{1,0:T(8,128)(2,1)S(1)} %get-tuple-element.107), channel_id=1, source_target_pairs={{0,112},{8,120},{16,96},{24,104},{32,80},{40,88},{48,64},{56,72},{... | collective-permute-start | bytes 688136 | tf_op jit(solution)/shard_map/ppermute | solution.py:34
  107.1 1.1 multiply_convert_fusion
  108.2 3.8 %collective-permute-done.19.refs_1_ = bf16[224,512]{1,0:T(8,128)(2,1)S(1)} collective-permute-done((bf16[224,512]{1,0:T(8,128)(2,1)S(1)}, bf16[224,512]{1,0:T(8,128)(2,1)S(1)}, u32[]{:S(2)}, u32[]{:S(2)}) %collective-permute-start.19) | collective-permute-done | bytes 229408 | tf_op jit(solution)/shard_map/ppermute | solution.py:34
  112.0 0.0 collective-permute-done.20.refs_2_
  112.0 3.8 %collective-permute-done.21.refs_3_ = bf16[224,512]{1,0:T(8,128)(2,1)S(1)} collective-permute-done((bf16[224,512]{1,0:T(8,128)(2,1)S(1)}, bf16[224,512]{1,0:T(8,128)(2,1)S(1)}, u32[]{:S(2)}, u32[]{:S(2)}) %collective-permute-start.21) | collective-permute-done | bytes 229408 | tf_op jit(solution)/shard_map/ppermute | solution.py:34
  115.8 1.8 %shard_map.132 = bf16[512,896]{1,0:T(8,128)(2,1)} custom-call(s32[4]{0:T(128)S(1)} %copy-done.14, f32[8,128]{1,0:T(8,128)S(1)} %get-tuple-element.103._, bf16[224,512]{1,0:T(8,128)(2,1)S(1)} %get-tuple-element.104.refs_0_, bf16[224,512]{1,0:T(8,128)(2,1)S(1)} %collective-permute-done.19.refs_1_, bf16[224,512]{1,0:T(8,128)(2,1)S(1)} %collective-permute-done.20.refs_2_, ...), custom_call_target="tpu_custom_call" | custom-call | tf_op jit(solution)/shard_map/pallas_call | solution.py:377
  (39 shorter events, 0.2 us)
Async XLA Ops:
  0.6 10.6 %copy-start.9 = (bf16[512,896]{1,0:T(8,128)(2,1)S(1)}, bf16[512,896]{1,0:T(8,128)(2,1)}, u32[]{:S(2)}) copy-start(bf16[512,896]{1,0:T(8,128)(2,1)} %x_ref) | copy-start | bytes 2752516
  0.6 10.6 %copy-start.17 = (f32[14]{0:T(128)S(1)}, f32[14]{0:T(128)}, u32[]{:S(2)}) copy-start(f32[14]{0:T(128)} %param.20) | copy-start | bytes 172
  0.7 10.6 %copy-start.16 = (f32[14]{0:T(128)S(1)}, f32[14]{0:T(128)}, u32[]{:S(2)}) copy-start(f32[14]{0:T(128)} %param.19) | copy-start | bytes 172
  0.7 10.6 %copy-start.15 = (f32[512,14]{0,1:T(8,128)S(1)}, f32[512,14]{0,1:T(8,128)}, u32[]{:S(2)}) copy-start(f32[512,14]{0,1:T(8,128)} %param.18) | copy-start | bytes 86020
  0.7 10.6 %copy-start.12 = (bf16[512,64]{0,1:T(8,128)(2,1)S(1)}, bf16[512,64]{0,1:T(8,128)(2,1)}, u32[]{:S(2)}) copy-start(bf16[512,64]{0,1:T(8,128)(2,1)} %param.17) | copy-start | bytes 196612
  0.7 10.6 %copy-start.13 = (bf16[512,64]{0,1:T(8,128)(2,1)S(1)}, bf16[512,64]{0,1:T(8,128)(2,1)}, u32[]{:S(2)}) copy-start(bf16[512,64]{0,1:T(8,128)(2,1)} %param.16) | copy-start | bytes 196612
  1.4 15.1 %copy-start.14 = (s32[4]{0:T(128)S(1)}, s32[4]{0:T(128)}, u32[]{:S(2)}) copy-start(s32[4]{0:T(128)} %pad_add_fusion.info) | copy-start | bytes 52
  5.8 5.4 %collective-permute-start.3 = (bf16[448,512]{1,0:T(8,128)(2,1)}, bf16[448,512]{1,0:T(8,128)(2,1)S(1)}, u32[]{:S(2)}, u32[]{:S(2)}) collective-permute-start(bf16[448,512]{1,0:T(8,128)(2,1)} %get-tuple-element.58.refs_3_), channel_id=1, source_target_pairs={{0,8},{8,0},{16,24},{24,16},{32,40},{40,32},{48,56},{56,48},{64,72... | collective-permute-start | bytes 1376264 | tf_op jit(solution)/shard_map/ppermute | solution.py:42
  5.9 13.1 %collective-permute-start.2 = (bf16[448,512]{1,0:T(8,128)(2,1)}, bf16[448,512]{1,0:T(8,128)(2,1)S(1)}, u32[]{:S(2)}, u32[]{:S(2)}) collective-permute-start(bf16[448,512]{1,0:T(8,128)(2,1)} %get-tuple-element.58.refs_3_), channel_id=1, source_target_pairs={{0,16},{8,24},{16,0},{24,8},{32,48},{40,56},{48,32},{56,40},{64,80... | collective-permute-start | bytes 1376264 | tf_op jit(solution)/shard_map/ppermute | solution.py:38
  7.6 21.5 %collective-permute-start = (bf16[672,512]{1,0:T(8,128)(2,1)}, bf16[672,512]{1,0:T(8,128)(2,1)S(1)}, u32[]{:S(2)}, u32[]{:S(2)}) collective-permute-start(bf16[672,512]{1,0:T(8,128)(2,1)} %get-tuple-element.56), channel_id=1, source_target_pairs={{0,48},{8,56},{16,32},{24,40},{32,16},{40,24},{48,0},{56,8},{64,11... | collective-permute-start | bytes 2064392 | tf_op jit(solution)/shard_map/ppermute | solution.py:34
  9.7 19.4 %collective-permute-start.1 = (bf16[672,512]{1,0:T(8,128)(2,1)}, bf16[672,512]{1,0:T(8,128)(2,1)S(1)}, u32[]{:S(2)}, u32[]{:S(2)}) collective-permute-start(bf16[672,512]{1,0:T(8,128)(2,1)} %get-tuple-element.57), channel_id=1, source_target_pairs={{0,64},{8,72},{16,80},{24,88},{32,96},{40,104},{48,112},{56,120},{... | collective-permute-start | bytes 2064392 | tf_op jit(solution)/shard_map/ppermute | solution.py:34
  15.0 1.4 %collective-permute-start.4 = (bf16[80,896]{1,0:T(8,128)(2,1)S(1)}, bf16[80,896]{1,0:T(8,128)(2,1)S(1)}, u32[]{:S(2)}, u32[]{:S(2)}) collective-permute-start(bf16[80,896]{1,0:T(8,128)(2,1)S(1)} %get-tuple-element.60), channel_id=1, source_target_pairs={{0,8},{8,0},{16,24},{24,16},{32,40},{40,32},{48,56},{56,48},{64,72... | collective-permute-start | bytes 430088 | tf_op jit(solution)/shard_map/ppermute | solution.py:42
  19.1 13.8 %collective-permute-start.5 = (bf16[448,512]{1,0:T(8,128)(2,1)S(1)}, bf16[448,512]{1,0:T(8,128)(2,1)S(1)}, u32[]{:S(2)}, u32[]{:S(2)}) collective-permute-start(bf16[448,512]{1,0:T(8,128)(2,1)S(1)} %collective-permute-done.2.refs_7_), channel_id=1, source_target_pairs={{0,8},{8,0},{16,24},{24,16},{32,40},{40,32},{48,56},{56,48},{64,72... | collective-permute-start | bytes 1376264 | tf_op jit(solution)/shard_map/ppermute | solution.py:42
  19.1 6.2 %collective-permute-start.6 = (bf16[80,896]{1,0:T(8,128)(2,1)S(1)}, bf16[80,896]{1,0:T(8,128)(2,1)S(1)}, u32[]{:S(2)}, u32[]{:S(2)}) collective-permute-start(bf16[80,896]{1,0:T(8,128)(2,1)S(1)} %get-tuple-element.62), channel_id=1, source_target_pairs={{0,16},{8,24},{16,0},{24,8},{32,48},{40,56},{48,32},{56,40},{64,80... | collective-permute-start | bytes 430088 | tf_op jit(solution)/shard_map/ppermute | solution.py:38
  25.3 22.9 %copy-start.10 = (bf16[512,896]{1,0:T(8,128)(2,1)S(1)}, bf16[512,896]{1,0:T(8,128)(2,1)}, u32[]{:S(2)}) copy-start(bf16[512,896]{1,0:T(8,128)(2,1)} %gate_ref.1) | copy-start | bytes 2752516
  25.9 7.0 %collective-permute-start.7 = (bf16[80,896]{1,0:T(8,128)(2,1)S(1)}, bf16[80,896]{1,0:T(8,128)(2,1)S(1)}, u32[]{:S(2)}, u32[]{:S(2)}) collective-permute-start(bf16[80,896]{1,0:T(8,128)(2,1)S(1)} %get-tuple-element.66), channel_id=1, source_target_pairs={{0,32},{8,40},{16,48},{24,56},{32,0},{40,8},{48,16},{56,24},{64,96... | collective-permute-start | bytes 430088 | tf_op jit(solution)/shard_map/ppermute | solution.py:46
  33.6 5.2 %collective-permute-start.8 = (bf16[80,896]{1,0:T(8,128)(2,1)S(1)}, bf16[80,896]{1,0:T(8,128)(2,1)S(1)}, u32[]{:S(2)}, u32[]{:S(2)}) collective-permute-start(bf16[80,896]{1,0:T(8,128)(2,1)S(1)} %get-tuple-element.70), channel_id=1, source_target_pairs={{0,64},{8,72},{16,80},{24,88},{32,96},{40,104},{48,112},{56,120},{... | collective-permute-start | bytes 430088 | tf_op jit(solution)/shard_map/ppermute | solution.py:46
  38.7 40.4 %collective-permute-start.9 = (bf16[672,512]{1,0:T(8,128)(2,1)}, bf16[672,512]{1,0:T(8,128)(2,1)S(1)}, u32[]{:S(2)}, u32[]{:S(2)}) collective-permute-start(bf16[672,512]{1,0:T(8,128)(2,1)} %get-tuple-element.82), channel_id=1, source_target_pairs={{0,112},{8,120},{16,96},{24,104},{32,80},{40,88},{48,64},{56,72},{... | collective-permute-start | bytes 2064392 | tf_op jit(solution)/shard_map/ppermute | solution.py:34
  44.2 6.0 %collective-permute-start.13 = (bf16[448,512]{1,0:T(8,128)(2,1)}, bf16[448,512]{1,0:T(8,128)(2,1)S(1)}, u32[]{:S(2)}, u32[]{:S(2)}) collective-permute-start(bf16[448,512]{1,0:T(8,128)(2,1)} %slice.13), channel_id=1, source_target_pairs={{0,8},{8,0},{16,24},{24,16},{32,40},{40,32},{48,56},{56,48},{64,72... | collective-permute-start | bytes 1376264 | tf_op jit(solution)/shard_map/ppermute | solution.py:42
  44.2 6.0 %collective-permute-start.12 = (bf16[448,512]{1,0:T(8,128)(2,1)}, bf16[448,512]{1,0:T(8,128)(2,1)S(1)}, u32[]{:S(2)}, u32[]{:S(2)}) collective-permute-start(bf16[448,512]{1,0:T(8,128)(2,1)} %slice.12), channel_id=1, source_target_pairs={{0,8},{8,0},{16,24},{24,16},{32,40},{40,32},{48,56},{56,48},{64,72... | collective-permute-start | bytes 1376264 | tf_op jit(solution)/shard_map/ppermute | solution.py:42
  44.7 26.3 %collective-permute-start.11 = (bf16[448,512]{1,0:T(8,128)(2,1)}, bf16[448,512]{1,0:T(8,128)(2,1)S(1)}, u32[]{:S(2)}, u32[]{:S(2)}) collective-permute-start(bf16[448,512]{1,0:T(8,128)(2,1)} %slice.13), channel_id=1, source_target_pairs={{0,16},{8,24},{16,0},{24,8},{32,48},{40,56},{48,32},{56,40},{64,80... | collective-permute-start | bytes 1376264 | tf_op jit(solution)/shard_map/ppermute | solution.py:38
  44.9 26.0 %collective-permute-start.10 = (bf16[448,512]{1,0:T(8,128)(2,1)}, bf16[448,512]{1,0:T(8,128)(2,1)S(1)}, u32[]{:S(2)}, u32[]{:S(2)}) collective-permute-start(bf16[448,512]{1,0:T(8,128)(2,1)} %slice.12), channel_id=1, source_target_pairs={{0,16},{8,24},{16,0},{24,8},{32,48},{40,56},{48,32},{56,40},{64,80... | collective-permute-start | bytes 1376264 | tf_op jit(solution)/shard_map/ppermute | solution.py:38
  48.1 2.1 %copy-start.2 = (bf16[224,512]{1,0:T(8,128)(2,1)S(1)}, bf16[224,512]{1,0:T(8,128)(2,1)}, u32[]{:S(2)}) copy-start(bf16[224,512]{1,0:T(8,128)(2,1)} %get-tuple-element.79.refs_0_) | copy-start | bytes 688132
  48.1 2.1 %copy-start.11 = (bf16[448,512]{1,0:T(8,128)(2,1)S(1)}, bf16[448,512]{1,0:T(8,128)(2,1)}, u32[]{:S(2)}) copy-start(bf16[448,512]{1,0:T(8,128)(2,1)} %get-tuple-element.58.refs_3_) | copy-start | bytes 1376260
  50.2 9.2 %copy-start.7 = (f32[512,896]{1,0:T(8,128)}, f32[512,896]{1,0:T(8,128)S(1)}, u32[]{:S(2)}) copy-start(f32[512,896]{1,0:T(8,128)S(1)} %get-tuple-element.108) | copy-start | bytes 5505028
  59.4 1.3 %copy-start = (bf16[4,1024,224]{2,1,0:T(8,128)(2,1)}, bf16[4,1024,224]{2,1,0:T(8,128)(2,1)S(1)}, u32[]{:S(2)}) copy-start(bf16[4,1024,224]{2,1,0:T(8,128)(2,1)S(1)} %get-tuple-element.93.refs_10_) | copy-start | bytes 5505028
  60.8 1.3 %copy-start.3 = (f32[4,224,512]{2,1,0:T(8,128)}, f32[4,224,512]{2,1,0:T(8,128)S(1)}, u32[]{:S(2)}) copy-start(f32[4,224,512]{2,1,0:T(8,128)S(1)} %get-tuple-element.95.refs_12_) | copy-start | bytes 5505028
  62.0 1.3 %copy-start.5 = (bf16[4,224,1024]{2,1,0:T(8,128)(2,1)}, bf16[4,224,1024]{2,1,0:T(8,128)(2,1)S(1)}, u32[]{:S(2)}) copy-start(bf16[4,224,1024]{2,1,0:T(8,128)(2,1)S(1)} %get-tuple-element.94.refs_11_) | copy-start | bytes 5505028
  63.3 15.8 %all-to-all-start = ((f32[8,8,512]{2,1,0:T(8,128)}), f32[8,8,512]{2,1,0:T(8,128)S(1)}, u32[]{:S(2)}, u32[]{:S(2)}) async-start(f32[8,8,512]{2,1,0:T(8,128)} %bitcast.9), calls=%async_computation | async-start | bytes 262144 | tf_op jit(solution)/shard_map/all_to_all | solution.py:482
  79.1 2.4 %collective-permute-start.15 = (bf16[448,512]{1,0:T(8,128)(2,1)S(1)}, bf16[448,512]{1,0:T(8,128)(2,1)S(1)}, u32[]{:S(2)}, u32[]{:S(2)}) collective-permute-start(bf16[448,512]{1,0:T(8,128)(2,1)S(1)} %slice.14), channel_id=1, source_target_pairs={{0,8},{8,0},{16,24},{24,16},{32,40},{40,32},{48,56},{56,48},{64,72... | collective-permute-start | bytes 1376264 | tf_op jit(solution)/shard_map/ppermute | solution.py:42
  79.6 2.1 %collective-permute-start.16 = (bf16[448,512]{1,0:T(8,128)(2,1)S(1)}, bf16[448,512]{1,0:T(8,128)(2,1)S(1)}, u32[]{:S(2)}, u32[]{:S(2)}) collective-permute-start(bf16[448,512]{1,0:T(8,128)(2,1)S(1)} %collective-permute-done.10.refs_5_), channel_id=1, source_target_pairs={{0,8},{8,0},{16,24},{24,16},{32,40},{40,32},{48,56},{56,48},{64,72... | collective-permute-start | bytes 1376264 | tf_op jit(solution)/shard_map/ppermute | solution.py:42
  79.7 2.7 %collective-permute-start.17 = (bf16[448,512]{1,0:T(8,128)(2,1)S(1)}, bf16[448,512]{1,0:T(8,128)(2,1)S(1)}, u32[]{:S(2)}, u32[]{:S(2)}) collective-permute-start(bf16[448,512]{1,0:T(8,128)(2,1)S(1)} %collective-permute-done.11.refs_7_), channel_id=1, source_target_pairs={{0,8},{8,0},{16,24},{24,16},{32,40},{40,32},{48,56},{56,48},{64,72... | collective-permute-start | bytes 1376264 | tf_op jit(solution)/shard_map/ppermute | solution.py:42
  80.1 17.4 %collective-permute-start.14 = (bf16[448,512]{1,0:T(8,128)(2,1)S(1)}, bf16[448,512]{1,0:T(8,128)(2,1)S(1)}, u32[]{:S(2)}, u32[]{:S(2)}) collective-permute-start(bf16[448,512]{1,0:T(8,128)(2,1)S(1)} %slice.14), channel_id=1, source_target_pairs={{0,16},{8,24},{16,0},{24,8},{32,48},{40,56},{48,32},{56,40},{64,80... | collective-permute-start | bytes 1376264 | tf_op jit(solution)/shard_map/ppermute | solution.py:38
  82.4 1.6 %copy-start.1 = (bf16[4,1024,224]{2,1,0:T(8,128)(2,1)S(1)}, bf16[4,1024,224]{2,1,0:T(8,128)(2,1)}, u32[]{:S(2)}) copy-start(bf16[4,1024,224]{2,1,0:T(8,128)(2,1)} %copy-done) | copy-start | bytes 5505028
  84.0 1.5 %copy-start.4 = (f32[4,224,512]{2,1,0:T(8,128)S(1)}, f32[4,224,512]{2,1,0:T(8,128)}, u32[]{:S(2)}) copy-start(f32[4,224,512]{2,1,0:T(8,128)} %copy-done.3) | copy-start | bytes 5505028
  85.5 1.5 %copy-start.6 = (bf16[4,224,1024]{2,1,0:T(8,128)(2,1)S(1)}, bf16[4,224,1024]{2,1,0:T(8,128)(2,1)}, u32[]{:S(2)}) copy-start(bf16[4,224,1024]{2,1,0:T(8,128)(2,1)} %copy-done.5) | copy-start | bytes 5505028
  97.5 2.6 %collective-permute-start.18 = (bf16[448,512]{1,0:T(8,128)(2,1)S(1)}, bf16[448,512]{1,0:T(8,128)(2,1)S(1)}, u32[]{:S(2)}, u32[]{:S(2)}) collective-permute-start(bf16[448,512]{1,0:T(8,128)(2,1)S(1)} %collective-permute-done.14.refs_4_), channel_id=1, source_target_pairs={{0,8},{8,0},{16,24},{24,16},{32,40},{40,32},{48,56},{56,48},{64,72... | collective-permute-start | bytes 1376264 | tf_op jit(solution)/shard_map/ppermute | solution.py:42
  100.1 6.9 %copy-start.8 = (f32[512,896]{1,0:T(8,128)S(1)}, f32[512,896]{1,0:T(8,128)}, u32[]{:S(2)}) copy-start(f32[512,896]{1,0:T(8,128)} %copy-done.7) | copy-start | bytes 5505028
  100.1 6.9 %copy-start.18 = (f32[896]{0:T(1024)S(1)}, f32[896]{0:T(1024)}, u32[]{:S(2)}) copy-start(f32[896]{0:T(1024)} %param.21) | copy-start | bytes 10756
  102.3 9.7 %collective-permute-start.19 = (bf16[224,512]{1,0:T(8,128)(2,1)S(1)}, bf16[224,512]{1,0:T(8,128)(2,1)S(1)}, u32[]{:S(2)}, u32[]{:S(2)}) collective-permute-start(bf16[224,512]{1,0:T(8,128)(2,1)S(1)} %get-tuple-element.105), channel_id=1, source_target_pairs={{0,48},{8,56},{16,32},{24,40},{32,16},{40,24},{48,0},{56,8},{64,11... | collective-permute-start | bytes 688136 | tf_op jit(solution)/shard_map/ppermute | solution.py:34
  102.8 9.2 %collective-permute-start.20 = (bf16[224,512]{1,0:T(8,128)(2,1)S(1)}, bf16[224,512]{1,0:T(8,128)(2,1)S(1)}, u32[]{:S(2)}, u32[]{:S(2)}) collective-permute-start(bf16[224,512]{1,0:T(8,128)(2,1)S(1)} %get-tuple-element.106), channel_id=1, source_target_pairs={{0,64},{8,72},{16,80},{24,88},{32,96},{40,104},{48,112},{56,120},{... | collective-permute-start | bytes 688136 | tf_op jit(solution)/shard_map/ppermute | solution.py:34
  102.9 12.9 %collective-permute-start.21 = (bf16[224,512]{1,0:T(8,128)(2,1)S(1)}, bf16[224,512]{1,0:T(8,128)(2,1)S(1)}, u32[]{:S(2)}, u32[]{:S(2)}) collective-permute-start(bf16[224,512]{1,0:T(8,128)(2,1)S(1)} %get-tuple-element.107), channel_id=1, source_target_pairs={{0,112},{8,120},{16,96},{24,104},{32,80},{40,88},{48,64},{56,72},{... | collective-permute-start | bytes 688136 | tf_op jit(solution)/shard_map/ppermute | solution.py:34

commit v5 on v4

--- a/solution.py
+++ b/solution.py
@@ -44,6 +44,10 @@
 
 def block_swap(value, step):
     return lax.ppermute(value, "ctx", [(i, i ^ step) for i in range(CTX)])
+
+
+def step_swap(value, step):
+    return lax.ppermute(value, "tp", [(i, i ^ step) for i in range(8)])
 
 
 def head_rows(head):
@@ -306,7 +310,7 @@
         gated = mixed * (gate / (1.0 + jnp.exp(-gate)))
         gated_ref[:, lanes] = gated
         squares = squares + gated * gated
-    square_ref[...] = jnp.broadcast_to(jnp.sum(squares.T, axis=0, keepdims=True), square_ref.shape)
+    square_ref[...] = jnp.sum(squares.T, axis=0, keepdims=True)
 
 
 def vmem(count):
@@ -414,11 +418,11 @@
     )(info, got, total, before)
 
 
-def ssm_carry(count, state, mixed, cum, read_t, gate):
+def ssm_carry(state, mixed, cum, read_t, gate):
     tokens, width = mixed.shape
     return pl.pallas_call(
         ssm_carry_kernel,
-        out_shape=[shape((tokens, width), F32), shape((8 * count, tokens), F32)],
+        out_shape=[shape((tokens, width), F32), shape((1, tokens), F32)],
         in_specs=vmem(5),
         out_specs=vmem(2),
         compiler_params=params(40),
@@ -458,45 +462,49 @@
     before = jnp.zeros_like(total)
     total, before, sent = ssm_merge(0, info, core_swap(sent), total, before)
     got = class_swap(sent)
+
     near[0], sent = tie((near[0], sent))
     near_core[0] = core_swap(near[0])
 
-    total, before, sent = ssm_merge(1, info, got, total, before)
-    got = block_swap(sent, 4)
     here[1], here[2], near_core[0], got = tie((here[1], here[2], near_core[0], got))
     for r in (1, 2):
         kv = here[r][ATT_DIM:]
         near[r] = class_swap(kv)
         from_core[r] = core_swap(kv)
+    total, before, sent = ssm_merge(1, info, got, total, before)
+    got, all_3 = tie((block_swap(sent, 4), all_3))
+    here[3] = head_swap(all_3, 3)
     total, before, sent = ssm_merge(2, info, got, total, before)
     got = block_swap(sent, 8)
-    got, all_3 = tie((got, all_3))
-    here[3] = head_swap(all_3, 3)
-    total, before, sent = ssm_merge(3, info, got, total, before)
-    count = lax.axis_size("tp")
-    gated, squares = ssm_carry(count, before, mixed, cum, read_t, ssm_gate)
     *state, ks, vs, mark = attend(
         0, info, q_own, here[1], here[2], kv_own, *from_core[:3], near[0], near_core[0]
     )
-    squares, mark = tie((squares, mark))
-    squares = lax.all_to_all(squares, "tp", 0, 0, tiled=True).reshape(count, 8, TOK)
-
-    here[3], near[1], near[2], squares, mark = tie((here[3], near[1], near[2], squares, mark))
+
+    here[3], mark = tie((here[3], mark))
     kv = here[3][ATT_DIM:]
     near[3] = class_swap(kv)
     from_core[3] = core_swap(kv)
+    from_core[3], near[1], near[2], got, mark = tie((from_core[3], near[1], near[2], got, mark))
     near_core[1], near_core[2] = core_swap(near[1]), core_swap(near[2])
     queries = (q_own, here[1], here[2], here[3])
     *state, mark = attend(
         1, info, *queries, from_core[3], near[1], near_core[1], near[2], near_core[2], mark, ks, vs, *state
     )
 
-    near[3], mark = tie((near[3], mark))
+    near[3], got, mark = tie((near[3], got, mark))
     near_core[3] = core_swap(near[3])
+    total, before, sent = ssm_merge(3, info, got, total, before)
+    gated, squares = ssm_carry(before, mixed, cum, read_t, ssm_gate)
+    gated, squares, mark = tie((gated, squares, mark))
+    others = step_swap(squares, 4)
     *results, mark = attend(2, info, *queries, near[3], near_core[3], mark, *state)
     back = [results[0]] + [head_swap(results[r], r) for r in range(1, 4)]
-    gated, mark = tie((gated, mark))
-    factor = lax.rsqrt(jnp.sum(squares[:, 0], axis=0) / SSM_WIDTH + 1e-05)
+    others, mark = tie((others, mark))
+    squares = squares + others
+    for step in (1, 2):
+        squares = squares + step_swap(squares, step)
+    *back, squares = tie((*back, squares))
+    factor = lax.rsqrt(squares.reshape(TOK) / SSM_WIDTH + 1e-05)
     mixer_out = (gated * factor[:, None] * norm_gain[None, :]).astype(BF16)
     return (unpack(info, mark, back), mixer_out)
 

time: 118 us -> 108 us (0.915)
  local copies, waits for them, and re-layouts: 10.2 us -> 0.16 us
  waiting for transfers between devices: 33.1 us -> 38.5 us
  starting transfers between devices: 34.4 us -> 30.5 us
    ppermute x0 -> x3, waiting for transfers between devices: none -> 12.9 us  [step_swap(): return lax.ppermute(value, 'tp', [(i, i ^ step) for i in range(8)])]
    ppermute x0 -> x3, starting transfers between devices: none -> 8.69 us  [step_swap(): return lax.ppermute(value, 'tp', [(i, i ^ step) for i in range(8)])]
    unnamed x38 -> x24, local copies, waits for them, and re-layouts: 8.52 us -> 0.05 us
    all_to_all x1 -> x0, waiting for transfers between devices: 8.13 us -> none  [on_device(): lax.all_to_all(squares, 'tp', 0, 0, tiled=True).reshape(count, 8, TOK)]
    all_to_all x1 -> x0, starting transfers between devices: 7.64 us -> none  [on_device(): lax.all_to_all(squares, 'tp', 0, 0, tiled=True).reshape(count, 8, TOK)]
    ppermute x5, waiting for transfers between devices: 6.57 us -> 3.15 us  [class_swap(): return lax.ppermute(value, 'ctx', [(i, i ^ 2) for i in range(CTX)])]
    ppermute x2, waiting for transfers between devices: 7.22 us -> 9.93 us  [block_swap(): return lax.ppermute(value, 'ctx', [(i, i ^ step) for i in range(CTX)])]
    ppermute x2, starting transfers between devices: 4.93 us -> 2.99 us  [block_swap(): return lax.ppermute(value, 'ctx', [(i, i ^ step) for i in range(CTX)])]
  transfers between devices with their start and end apart: 23 -> 25, of which waited for: 11 -> 13; matrix products, arithmetic and copies ran while one was open for 2% -> 0% of each run, Pallas kernels for 24% -> 25%
where the time goes in v5:
time: 108 us
  waiting for transfers between devices  38.5 us (36%)
  Pallas kernels  36.3 us (34%)
  starting transfers between devices  30.5 us (28%)
  other arithmetic  1.73 us (2%)
    pallas_call x3, Pallas kernels, attend(): pl.pallas_call(functools.partial(attend_kernel, stage), out_shape=out, in...  21.7 us
    ppermute x3, waiting for transfers between devices, step_swap(): return lax.ppermute(value, 'tp', [(i, i ^ step) for i in range(8)])  12.9 us
    ppermute x6, starting transfers between devices, head_swap(): lax.ppermute(value, 'ctx', [(i, exchanged(i, r)) for i in range(CTX)])  11 us
    ppermute x2, waiting for transfers between devices, block_swap(): return lax.ppermute(value, 'ctx', [(i, i ^ step) for i in range(CTX)])  9.93 us
    ppermute x6, waiting for transfers between devices, head_swap(): lax.ppermute(value, 'ctx', [(i, exchanged(i, r)) for i in range(CTX)])  9.44 us
    ppermute x3, starting transfers between devices, step_swap(): return lax.ppermute(value, 'tp', [(i, i ^ step) for i in range(8)])  8.69 us
    ppermute x5, starting transfers between devices, class_swap(): return lax.ppermute(value, 'ctx', [(i, i ^ 2) for i in range(CTX)])  5.54 us
    pallas_call x1, Pallas kernels, pack(): pl.pallas_call(pack_kernel, out_shape=[shape((count, TOK), BF16) for coun...  4.41 us
  transfers between devices with their start and end apart: 25, of which 13 were waited for; matrix products, arithmetic and copies ran while one was open for 0% of the time, Pallas kernels for 25%

profile of v5, /device:TPU:0, one launch (start us, length us, event | category | flops | bytes accessed | tf_op | source)
XLA Modules:
  0.0 108.0 jit_solution(7592375127146635416)
XLA Ops:
  0.7 0.6 pad_add_fusion.info
  1.3 4.4 %shard_map.122 = (bf16[224,512]{1,0:T(8,128)(2,1)}, bf16[448,512]{1,0:T(8,128)(2,1)}, bf16[672,512]{1,0:T(8,128)(2,1)}, bf16[672,512]{1,0:T(8,128)(2,1)}, bf16[672,512]{1,0:T(8,128)(2,1)}) custom-call(s32[4]{0:T(128)} %pad_add_fusion.info, bf16[512,896]{1,0:T(8,128)(2,1)} %q_in.1, bf16[512,896]{1,0:T(8,128)(2,1)} %k_in.1, bf16[512,896]{1,0:T(8,128)(2,1)} %v_in.1), custom_call_target="tpu_custom_call" | custom-call | tf_op jit(solution)/shard_map/pallas_call | solution.py:338
  5.7 0.1 collective-permute-start.3
  5.8 1.7 %collective-permute-start.2 = (bf16[448,512]{1,0:T(8,128)(2,1)}, bf16[448,512]{1,0:T(8,128)(2,1)S(1)}, u32[]{:S(2)}, u32[]{:S(2)}) collective-permute-start(bf16[448,512]{1,0:T(8,128)(2,1)} %get-tuple-element.67.refs_3_), channel_id=1, source_target_pairs={{0,16},{8,24},{16,0},{24,8},{32,48},{40,56},{48,32},{56,40},{64,80... | collective-permute-start | bytes 1376264 | tf_op jit(solution)/shard_map/ppermute | solution.py:38
  7.4 2.1 %collective-permute-start = (bf16[672,512]{1,0:T(8,128)(2,1)}, bf16[672,512]{1,0:T(8,128)(2,1)S(1)}, u32[]{:S(2)}, u32[]{:S(2)}) collective-permute-start(bf16[672,512]{1,0:T(8,128)(2,1)} %get-tuple-element.65), channel_id=1, source_target_pairs={{0,48},{8,56},{16,32},{24,40},{32,16},{40,24},{48,0},{56,8},{64,11... | collective-permute-start | bytes 2064392 | tf_op jit(solution)/shard_map/ppermute | solution.py:34
  9.5 1.6 %collective-permute-start.1 = (bf16[672,512]{1,0:T(8,128)(2,1)}, bf16[672,512]{1,0:T(8,128)(2,1)S(1)}, u32[]{:S(2)}, u32[]{:S(2)}) collective-permute-start(bf16[672,512]{1,0:T(8,128)(2,1)} %get-tuple-element.66), channel_id=1, source_target_pairs={{0,64},{8,72},{16,80},{24,88},{32,96},{40,104},{48,112},{56,120},{... | collective-permute-start | bytes 2064392 | tf_op jit(solution)/shard_map/ppermute | solution.py:34
  11.1 0.0 collective-permute-done.3.refs_4_
  11.2 3.6 %shard_map.123 = (f32[512,896]{1,0:T(8,128)S(1)}, f32[72,896]{1,0:T(8,128)S(1)}, bf16[80,896]{1,0:T(8,128)(2,1)S(1)}, f32[512,14]{1,0:T(8,128)S(1)}) custom-call(bf16[512,896]{1,0:T(8,128)(2,1)S(1)} %copy-done.1, bf16[64,512]{1,0:T(8,128)(2,1)S(1)} %bitcast.12, bf16[64,512]{1,0:T(8,128)(2,1)S(1)} %bitcast.10, f32[14,512]{1,0:T(8,128)S(1)} %bitcast.13, ...), custom_call_target="tpu_custom_call" | custom-call | flops 1000 | bytes 1000 | tf_op jit(solution)/shard_map/pallas_call | solution.py:394
  14.8 0.1 collective-permute-start.4
  14.9 1.4 %collective-permute-done.4.got_ref = bf16[80,896]{1,0:T(8,128)(2,1)S(1)} collective-permute-done((bf16[80,896]{1,0:T(8,128)(2,1)S(1)}, bf16[80,896]{1,0:T(8,128)(2,1)S(1)}, u32[]{:S(2)}, u32[]{:S(2)}) %collective-permute-start.4) | collective-permute-done | bytes 143392 | tf_op jit(solution)/shard_map/ppermute | solution.py:42
  16.3 0.7 shard_map.124
  17.0 1.9 %collective-permute-done.2.refs_7_ = bf16[448,512]{1,0:T(8,128)(2,1)S(1)} collective-permute-done((bf16[448,512]{1,0:T(8,128)(2,1)}, bf16[448,512]{1,0:T(8,128)(2,1)S(1)}, u32[]{:S(2)}, u32[]{:S(2)}) %collective-permute-start.2) | collective-permute-done | bytes 458784 | tf_op jit(solution)/shard_map/ppermute | solution.py:38
  18.9 0.0 collective-permute-start.5
  18.9 1.6 %collective-permute-start.6 = (bf16[80,896]{1,0:T(8,128)(2,1)S(1)}, bf16[80,896]{1,0:T(8,128)(2,1)S(1)}, u32[]{:S(2)}, u32[]{:S(2)}) collective-permute-start(bf16[80,896]{1,0:T(8,128)(2,1)S(1)} %get-tuple-element.71), channel_id=1, source_target_pairs={{0,16},{8,24},{16,0},{24,8},{32,48},{40,56},{48,32},{56,40},{64,80... | collective-permute-start | bytes 430088 | tf_op jit(solution)/shard_map/ppermute | solution.py:38
  20.5 5.8 %collective-permute-done.refs_1_ = bf16[672,512]{1,0:T(8,128)(2,1)S(1)} collective-permute-done((bf16[672,512]{1,0:T(8,128)(2,1)}, bf16[672,512]{1,0:T(8,128)(2,1)S(1)}, u32[]{:S(2)}, u32[]{:S(2)}) %collective-permute-start) | collective-permute-done | bytes 688160 | tf_op jit(solution)/shard_map/ppermute | solution.py:34
  26.3 0.6 collective-permute-done.1.refs_2_
  27.0 0.0 collective-permute-done.6.got_ref
  27.0 0.0 collective-permute-done.5.refs_8_
  27.0 0.7 shard_map.125
  27.6 1.3 %collective-permute-start.7 = (bf16[80,896]{1,0:T(8,128)(2,1)S(1)}, bf16[80,896]{1,0:T(8,128)(2,1)S(1)}, u32[]{:S(2)}, u32[]{:S(2)}) collective-permute-start(bf16[80,896]{1,0:T(8,128)(2,1)S(1)} %get-tuple-element.76), channel_id=1, source_target_pairs={{0,32},{8,40},{16,48},{24,56},{32,0},{40,8},{48,16},{56,24},{64,96... | collective-permute-start | bytes 430088 | tf_op jit(solution)/shard_map/ppermute | solution.py:46
  29.0 5.4 %collective-permute-done.7.got_ref = bf16[80,896]{1,0:T(8,128)(2,1)S(1)} collective-permute-done((bf16[80,896]{1,0:T(8,128)(2,1)S(1)}, bf16[80,896]{1,0:T(8,128)(2,1)S(1)}, u32[]{:S(2)}, u32[]{:S(2)}) %collective-permute-start.7) | collective-permute-done | bytes 143392 | tf_op jit(solution)/shard_map/ppermute | solution.py:46
  34.3 2.5 %collective-permute-start.8 = (bf16[672,512]{1,0:T(8,128)(2,1)S(1)}, bf16[672,512]{1,0:T(8,128)(2,1)S(1)}, u32[]{:S(2)}, u32[]{:S(2)}) collective-permute-start(bf16[672,512]{1,0:T(8,128)(2,1)S(1)} %copy-done.11), channel_id=1, source_target_pairs={{0,112},{8,120},{16,96},{24,104},{32,80},{40,88},{48,64},{56,72},{... | collective-permute-start | bytes 2064392 | tf_op jit(solution)/shard_map/ppermute | solution.py:34
  36.9 0.1 collective-permute-start.10
  37.0 0.5 collective-permute-start.9
  37.5 0.0 collective-permute-start.14
  37.5 2.0 %collective-permute-start.13 = (bf16[448,512]{1,0:T(8,128)(2,1)S(1)}, bf16[448,512]{1,0:T(8,128)(2,1)S(1)}, u32[]{:S(2)}, u32[]{:S(2)}) collective-permute-start(bf16[448,512]{1,0:T(8,128)(2,1)S(1)} %slice.9), channel_id=1, source_target_pairs={{0,16},{8,24},{16,0},{24,8},{32,48},{40,56},{48,32},{56,40},{64,80... | collective-permute-start | bytes 1376264 | tf_op jit(solution)/shard_map/ppermute | solution.py:38
  39.5 0.0 collective-permute-done.10.refs_6_
  39.5 0.0 collective-permute-done.9.refs_5_
  39.5 9.1 %shard_map.126 = (f32[4,224,512]{2,1,0:T(8,128)S(1)}, f32[4,16,512]{2,1,0:T(8,128)S(1)}, bf16[4,1024,224]{2,1,0:T(8,128)(2,1)S(1)}, bf16[4,224,1024]{2,1,0:T(8,128)(2,1)S(1)}, f32[8,128]{1,0:T(8,128)S(1)}) custom-call(s32[4]{0:T(128)S(1)} %copy-done.6, bf16[224,512]{1,0:T(8,128)(2,1)S(1)} %copy-done, bf16[672,512]{1,0:T(8,128)(2,1)S(1)} %collective-permute-done.refs_1_, ...), custom_call_target="tpu_custom_call" | custom-call | flops 1000 | bytes 1000 | tf_op jit(solution)/shard_map/pallas_call | solution.py:368
  48.6 3.0 %collective-permute-done.8.refs_3_ = bf16[672,512]{1,0:T(8,128)(2,1)S(1)} collective-permute-done((bf16[672,512]{1,0:T(8,128)(2,1)S(1)}, bf16[672,512]{1,0:T(8,128)(2,1)S(1)}, u32[]{:S(2)}, u32[]{:S(2)}) %collective-permute-start.8) | collective-permute-done | bytes 688160 | tf_op jit(solution)/shard_map/ppermute | solution.py:34
  51.6 0.1 collective-permute-start.12
  51.7 0.7 shard_map.127
  52.4 1.7 %collective-permute-start.15 = (bf16[80,896]{1,0:T(8,128)(2,1)S(1)}, bf16[80,896]{1,0:T(8,128)(2,1)S(1)}, u32[]{:S(2)}, u32[]{:S(2)}) collective-permute-start(bf16[80,896]{1,0:T(8,128)(2,1)S(1)} %get-tuple-element.89), channel_id=1, source_target_pairs={{0,64},{8,72},{16,80},{24,88},{32,96},{40,104},{48,112},{56,120},{... | collective-permute-start | bytes 430088 | tf_op jit(solution)/shard_map/ppermute | solution.py:46
  54.1 4.6 %collective-permute-done.15.got_ref = bf16[80,896]{1,0:T(8,128)(2,1)S(1)} collective-permute-done((bf16[80,896]{1,0:T(8,128)(2,1)S(1)}, bf16[80,896]{1,0:T(8,128)(2,1)S(1)}, u32[]{:S(2)}, u32[]{:S(2)}) %collective-permute-start.15) | collective-permute-done | bytes 143392 | tf_op jit(solution)/shard_map/ppermute | solution.py:46
  58.6 0.0 collective-permute-done.14.refs_7_
  58.6 1.2 %collective-permute-done.13.refs_5_ = bf16[448,512]{1,0:T(8,128)(2,1)S(1)} collective-permute-done((bf16[448,512]{1,0:T(8,128)(2,1)S(1)}, bf16[448,512]{1,0:T(8,128)(2,1)S(1)}, u32[]{:S(2)}, u32[]{:S(2)}) %collective-permute-start.13) | collective-permute-done | bytes 458784 | tf_op jit(solution)/shard_map/ppermute | solution.py:38
  59.8 0.0 collective-permute-done.12.refs_4_
  59.8 0.0 collective-permute-start.16
  59.8 0.5 collective-permute-start.17
  60.3 0.3 collective-permute-start.11
  60.6 1.0 collective-permute-done.16.refs_6_
  61.7 0.7 collective-permute-done.17.refs_8_
  62.3 10.5 %shard_map.128 = (f32[4,224,512]{2,1,0:T(8,128)S(1)}, f32[4,16,512]{2,1,0:T(8,128)S(1)}, f32[8,128]{1,0:T(8,128)S(1)}) custom-call(s32[4]{0:T(128)S(1)} %copy-done.6, bf16[224,512]{1,0:T(8,128)(2,1)S(1)} %copy-done, bf16[672,512]{1,0:T(8,128)(2,1)S(1)} %collective-permute-done.refs_1_, bf16[672,512]{1,0:T(8,128)(2,1)S(1)} %collective-permute-done.1.refs_2_, ...), custom_call_target="tpu_custom_call" | custom-call | flops 1000 | bytes 1000 | tf_op jit(solution)/shard_map/pallas_call | solution.py:368
  72.8 0.0 collective-permute-done.11.refs_4_
  72.8 0.9 collective-permute-start.19
  73.8 1.4 %shard_map.129 = (f32[72,896]{1,0:T(8,128)}, f32[72,896]{1,0:T(8,128)S(1)}, bf16[80,896]{1,0:T(8,128)(2,1)}) custom-call(s32[4]{0:T(128)S(1)} %copy-done.6, bf16[80,896]{1,0:T(8,128)(2,1)S(1)} %collective-permute-done.15.got_ref, f32[72,896]{1,0:T(8,128)S(1)} %get-tuple-element.102.total_ref, f32[72,896]{1,0:T(8,128)S(1)} %get-tuple-element.103.before_ref), custom_call_target="tpu_custom_call" | custom-call | flops 1000 | bytes 1000 | tf_op jit(solution)/shard_map/pallas_call | solution.py:411
  75.1 1.3 %shard_map.130 = (f32[512,896]{1,0:T(8,128)S(1)}, f32[1,512]{1,0:T(1,128)S(1)}) custom-call(f32[72,896]{1,0:T(8,128)S(1)} %get-tuple-element.104.state_ref, f32[512,896]{1,0:T(8,128)S(1)} %get-tuple-element.105.mixed_ref, f32[512,14]{1,0:T(8,128)S(1)} %get-tuple-element.106.cum_ref, bf16[64,512]{1,0:T(8,128)(2,1)S(1)} %bitcast.11, bf16[512,896]{1,0:T(8,128)(2,1)S(1)} %copy-done.2), custom_call_target="tpu_custom_call" | custom-call | flops 1000 | bytes 1000 | tf_op jit(solution)/shard_map/pallas_call | solution.py:423
  76.5 0.0 collective-permute-done.19.refs_5_
  76.5 0.0 copy-start.10
  76.5 2.1 %shard_map.131 = (bf16[224,512]{1,0:T(8,128)(2,1)S(1)}, bf16[224,512]{1,0:T(8,128)(2,1)S(1)}, bf16[224,512]{1,0:T(8,128)(2,1)S(1)}, bf16[224,512]{1,0:T(8,128)(2,1)S(1)}, f32[8,128]{1,0:T(8,128)S(1)}) custom-call(s32[4]{0:T(128)S(1)} %copy-done.6, bf16[224,512]{1,0:T(8,128)(2,1)S(1)} %copy-done, bf16[672,512]{1,0:T(8,128)(2,1)S(1)} %collective-permute-done.refs_1_, ...), custom_call_target="tpu_custom_call" | custom-call | flops 1000 | bytes 1000 | tf_op jit(solution)/shard_map/pallas_call | solution.py:368
  78.6 1.8 %collective-permute-start.20 = (bf16[224,512]{1,0:T(8,128)(2,1)S(1)}, bf16[224,512]{1,0:T(8,128)(2,1)S(1)}, u32[]{:S(2)}, u32[]{:S(2)}) collective-permute-start(bf16[224,512]{1,0:T(8,128)(2,1)S(1)} %get-tuple-element.118), channel_id=1, source_target_pairs={{0,48},{8,56},{16,32},{24,40},{32,16},{40,24},{48,0},{56,8},{64,11... | collective-permute-start | bytes 688136 | tf_op jit(solution)/shard_map/ppermute | solution.py:34
  80.4 2.0 %collective-permute-start.21 = (bf16[224,512]{1,0:T(8,128)(2,1)S(1)}, bf16[224,512]{1,0:T(8,128)(2,1)S(1)}, u32[]{:S(2)}, u32[]{:S(2)}) collective-permute-start(bf16[224,512]{1,0:T(8,128)(2,1)S(1)} %get-tuple-element.119), channel_id=1, source_target_pairs={{0,64},{8,72},{16,80},{24,88},{32,96},{40,104},{48,112},{56,120},{... | collective-permute-start | bytes 688136 | tf_op jit(solution)/shard_map/ppermute | solution.py:34
  82.4 1.0 collective-permute-start.22
  83.4 2.9 %collective-permute-start.18 = (f32[1,512]{1,0:T(1,128)S(1)}, f32[1,512]{1,0:T(1,128)S(1)}, u32[]{:S(2)}, u32[]{:S(2)}) collective-permute-start(f32[1,512]{1,0:T(1,128)S(1)} %get-tuple-element.110), channel_id=1, source_target_pairs={{0,4},{1,5},{2,6},{3,7},{4,0},{5,1},{6,2},{7,3},{8,12},{9,13},{10,... | collective-permute-start | bytes 6152 | tf_op jit(solution)/shard_map/ppermute | solution.py:50
  86.3 9.7 %collective-permute-done.18 = f32[1,512]{1,0:T(1,128)S(1)} collective-permute-done((f32[1,512]{1,0:T(1,128)S(1)}, f32[1,512]{1,0:T(1,128)S(1)}, u32[]{:S(2)}, u32[]{:S(2)}) %collective-permute-start.18) | collective-permute-done | bytes 2080 | tf_op jit(solution)/shard_map/ppermute | solution.py:50
  96.0 1.9 %collective-permute-start.23 = (f32[1,512]{1,0:T(1,128)S(1)}, f32[1,512]{1,0:T(1,128)S(1)}, u32[]{:S(2)}, u32[]{:S(2)}) collective-permute-start(f32[1,512]{1,0:T(1,128)S(1)} %add.24), channel_id=1, source_target_pairs={{0,1},{1,0},{2,3},{3,2},{4,5},{5,4},{6,7},{7,6},{8,9},{9,8},{10,11... | collective-permute-start | bytes 6152 | tf_op jit(solution)/shard_map/ppermute | solution.py:50
  97.9 1.7 %collective-permute-done.23 = f32[1,512]{1,0:T(1,128)S(1)} collective-permute-done((f32[1,512]{1,0:T(1,128)S(1)}, f32[1,512]{1,0:T(1,128)S(1)}, u32[]{:S(2)}, u32[]{:S(2)}) %collective-permute-start.23) | collective-permute-done | bytes 2080 | tf_op jit(solution)/shard_map/ppermute | solution.py:50
  99.6 3.9 %collective-permute-start.24 = (f32[1,512]{1,0:T(1,128)S(1)}, f32[1,512]{1,0:T(1,128)S(1)}, u32[]{:S(2)}, u32[]{:S(2)}) collective-permute-start(f32[1,512]{1,0:T(1,128)S(1)} %add.25), channel_id=1, source_target_pairs={{0,2},{1,3},{2,0},{3,1},{4,6},{5,7},{6,4},{7,5},{8,10},{9,11},{10,... | collective-permute-start | bytes 6152 | tf_op jit(solution)/shard_map/ppermute | solution.py:50
  103.4 1.6 %collective-permute-done.24 = f32[1,512]{1,0:T(1,128)S(1)} collective-permute-done((f32[1,512]{1,0:T(1,128)S(1)}, f32[1,512]{1,0:T(1,128)S(1)}, u32[]{:S(2)}, u32[]{:S(2)}) %collective-permute-start.24) | collective-permute-done | bytes 2080 | tf_op jit(solution)/shard_map/ppermute | solution.py:50
  105.0 0.0 collective-permute-done.20.refs_1_
  105.0 0.0 collective-permute-done.21.refs_2_
  105.0 0.0 collective-permute-done.22.refs_3_
  105.1 1.1 %multiply_convert_fusion = bf16[512,896]{1,0:T(8,128)(2,1)} fusion(f32[512,896]{1,0:T(8,128)S(1)} %get-tuple-element.126, f32[896]{0:T(1024)S(1)} %copy-done.10, f32[512]{0:T(512)S(1)} %bitcast.16), kind=kLoop, calls=%fused_computation | loop fusion | flops 1376256 | bytes 2758144 | tf_op jit(solution)/shard_map/convert_element_type | solution.py:508
  106.2 1.8 %shard_map.132 = bf16[512,896]{1,0:T(8,128)(2,1)} custom-call(s32[4]{0:T(128)S(1)} %copy-done.6, f32[8,128]{1,0:T(8,128)S(1)} %get-tuple-element.116._, bf16[224,512]{1,0:T(8,128)(2,1)S(1)} %get-tuple-element.122.refs_0_, bf16[224,512]{1,0:T(8,128)(2,1)S(1)} %collective-permute-done.20.refs_1_, bf16[224,512]{1,0:T(8,128)(2,1)S(1)} %collective-permute-done.21.refs_2_, ...), custom_call_target="tpu_custom_call" | custom-call | tf_op jit(solution)/shard_map/pallas_call | solution.py:381
  (31 shorter events, 0.2 us)
Async XLA Ops:
  0.6 10.5 %copy-start.1 = (bf16[512,896]{1,0:T(8,128)(2,1)S(1)}, bf16[512,896]{1,0:T(8,128)(2,1)}, u32[]{:S(2)}) copy-start(bf16[512,896]{1,0:T(8,128)(2,1)} %x_ref) | copy-start | bytes 2752516
  0.6 10.5 %copy-start.9 = (f32[14]{0:T(128)S(1)}, f32[14]{0:T(128)}, u32[]{:S(2)}) copy-start(f32[14]{0:T(128)} %param.20) | copy-start | bytes 172
  0.7 10.5 %copy-start.8 = (f32[14]{0:T(128)S(1)}, f32[14]{0:T(128)}, u32[]{:S(2)}) copy-start(f32[14]{0:T(128)} %param.19) | copy-start | bytes 172
  0.7 10.5 %copy-start.7 = (f32[512,14]{0,1:T(8,128)S(1)}, f32[512,14]{0,1:T(8,128)}, u32[]{:S(2)}) copy-start(f32[512,14]{0,1:T(8,128)} %param.18) | copy-start | bytes 86020
  0.7 10.5 %copy-start.4 = (bf16[512,64]{0,1:T(8,128)(2,1)S(1)}, bf16[512,64]{0,1:T(8,128)(2,1)}, u32[]{:S(2)}) copy-start(bf16[512,64]{0,1:T(8,128)(2,1)} %param.17) | copy-start | bytes 196612
  0.7 10.5 %copy-start.5 = (bf16[512,64]{0,1:T(8,128)(2,1)S(1)}, bf16[512,64]{0,1:T(8,128)(2,1)}, u32[]{:S(2)}) copy-start(bf16[512,64]{0,1:T(8,128)(2,1)} %param.16) | copy-start | bytes 196612
  1.3 15.0 %copy-start.6 = (s32[4]{0:T(128)S(1)}, s32[4]{0:T(128)}, u32[]{:S(2)}) copy-start(s32[4]{0:T(128)} %pad_add_fusion.info) | copy-start | bytes 52
  5.7 28.6 %copy-start.11 = (bf16[672,512]{1,0:T(8,128)(2,1)S(1)}, bf16[672,512]{1,0:T(8,128)(2,1)}, u32[]{:S(2)}) copy-start(bf16[672,512]{1,0:T(8,128)(2,1)} %get-tuple-element.78) | copy-start | bytes 2064388
  5.7 5.4 %collective-permute-start.3 = (bf16[448,512]{1,0:T(8,128)(2,1)}, bf16[448,512]{1,0:T(8,128)(2,1)S(1)}, u32[]{:S(2)}, u32[]{:S(2)}) collective-permute-start(bf16[448,512]{1,0:T(8,128)(2,1)} %get-tuple-element.67.refs_3_), channel_id=1, source_target_pairs={{0,8},{8,0},{16,24},{24,16},{32,40},{40,32},{48,56},{56,48},{64,72... | collective-permute-start | bytes 1376264 | tf_op jit(solution)/shard_map/ppermute | solution.py:42
  5.8 13.1 %collective-permute-start.2 = (bf16[448,512]{1,0:T(8,128)(2,1)}, bf16[448,512]{1,0:T(8,128)(2,1)S(1)}, u32[]{:S(2)}, u32[]{:S(2)}) collective-permute-start(bf16[448,512]{1,0:T(8,128)(2,1)} %get-tuple-element.67.refs_3_), channel_id=1, source_target_pairs={{0,16},{8,24},{16,0},{24,8},{32,48},{40,56},{48,32},{56,40},{64,80... | collective-permute-start | bytes 1376264 | tf_op jit(solution)/shard_map/ppermute | solution.py:38
  7.4 18.9 %collective-permute-start = (bf16[672,512]{1,0:T(8,128)(2,1)}, bf16[672,512]{1,0:T(8,128)(2,1)S(1)}, u32[]{:S(2)}, u32[]{:S(2)}) collective-permute-start(bf16[672,512]{1,0:T(8,128)(2,1)} %get-tuple-element.65), channel_id=1, source_target_pairs={{0,48},{8,56},{16,32},{24,40},{32,16},{40,24},{48,0},{56,8},{64,11... | collective-permute-start | bytes 2064392 | tf_op jit(solution)/shard_map/ppermute | solution.py:34
  9.5 17.4 %collective-permute-start.1 = (bf16[672,512]{1,0:T(8,128)(2,1)}, bf16[672,512]{1,0:T(8,128)(2,1)S(1)}, u32[]{:S(2)}, u32[]{:S(2)}) collective-permute-start(bf16[672,512]{1,0:T(8,128)(2,1)} %get-tuple-element.66), channel_id=1, source_target_pairs={{0,64},{8,72},{16,80},{24,88},{32,96},{40,104},{48,112},{56,120},{... | collective-permute-start | bytes 2064392 | tf_op jit(solution)/shard_map/ppermute | solution.py:34
  14.8 24.7 %copy-start = (bf16[224,512]{1,0:T(8,128)(2,1)S(1)}, bf16[224,512]{1,0:T(8,128)(2,1)}, u32[]{:S(2)}) copy-start(bf16[224,512]{1,0:T(8,128)(2,1)} %get-tuple-element.79.refs_0_) | copy-start | bytes 688132
  14.8 24.7 %copy-start.3 = (bf16[448,512]{1,0:T(8,128)(2,1)S(1)}, bf16[448,512]{1,0:T(8,128)(2,1)}, u32[]{:S(2)}) copy-start(bf16[448,512]{1,0:T(8,128)(2,1)} %get-tuple-element.67.refs_3_) | copy-start | bytes 1376260
  14.8 1.4 %collective-permute-start.4 = (bf16[80,896]{1,0:T(8,128)(2,1)S(1)}, bf16[80,896]{1,0:T(8,128)(2,1)S(1)}, u32[]{:S(2)}, u32[]{:S(2)}) collective-permute-start(bf16[80,896]{1,0:T(8,128)(2,1)S(1)} %get-tuple-element.69), channel_id=1, source_target_pairs={{0,8},{8,0},{16,24},{24,16},{32,40},{40,32},{48,56},{56,48},{64,72... | collective-permute-start | bytes 430088 | tf_op jit(solution)/shard_map/ppermute | solution.py:42
  18.9 8.0 %collective-permute-start.5 = (bf16[448,512]{1,0:T(8,128)(2,1)S(1)}, bf16[448,512]{1,0:T(8,128)(2,1)S(1)}, u32[]{:S(2)}, u32[]{:S(2)}) collective-permute-start(bf16[448,512]{1,0:T(8,128)(2,1)S(1)} %collective-permute-done.2.refs_7_), channel_id=1, source_target_pairs={{0,8},{8,0},{16,24},{24,16},{32,40},{40,32},{48,56},{56,48},{64,72... | collective-permute-start | bytes 1376264 | tf_op jit(solution)/shard_map/ppermute | solution.py:42
  18.9 8.0 %collective-permute-start.6 = (bf16[80,896]{1,0:T(8,128)(2,1)S(1)}, bf16[80,896]{1,0:T(8,128)(2,1)S(1)}, u32[]{:S(2)}, u32[]{:S(2)}) collective-permute-start(bf16[80,896]{1,0:T(8,128)(2,1)S(1)} %get-tuple-element.71), channel_id=1, source_target_pairs={{0,16},{8,24},{16,0},{24,8},{32,48},{40,56},{48,32},{56,40},{64,80... | collective-permute-start | bytes 430088 | tf_op jit(solution)/shard_map/ppermute | solution.py:38
  27.6 6.7 %collective-permute-start.7 = (bf16[80,896]{1,0:T(8,128)(2,1)S(1)}, bf16[80,896]{1,0:T(8,128)(2,1)S(1)}, u32[]{:S(2)}, u32[]{:S(2)}) collective-permute-start(bf16[80,896]{1,0:T(8,128)(2,1)S(1)} %get-tuple-element.76), channel_id=1, source_target_pairs={{0,32},{8,40},{16,48},{24,56},{32,0},{40,8},{48,16},{56,24},{64,96... | collective-permute-start | bytes 430088 | tf_op jit(solution)/shard_map/ppermute | solution.py:46
  34.3 17.3 %collective-permute-start.8 = (bf16[672,512]{1,0:T(8,128)(2,1)S(1)}, bf16[672,512]{1,0:T(8,128)(2,1)S(1)}, u32[]{:S(2)}, u32[]{:S(2)}) collective-permute-start(bf16[672,512]{1,0:T(8,128)(2,1)S(1)} %copy-done.11), channel_id=1, source_target_pairs={{0,112},{8,120},{16,96},{24,104},{32,80},{40,88},{48,64},{56,72},{... | collective-permute-start | bytes 2064392 | tf_op jit(solution)/shard_map/ppermute | solution.py:34
  36.9 2.6 %collective-permute-start.10 = (bf16[448,512]{1,0:T(8,128)(2,1)S(1)}, bf16[448,512]{1,0:T(8,128)(2,1)S(1)}, u32[]{:S(2)}, u32[]{:S(2)}) collective-permute-start(bf16[448,512]{1,0:T(8,128)(2,1)S(1)} %slice.10), channel_id=1, source_target_pairs={{0,8},{8,0},{16,24},{24,16},{32,40},{40,32},{48,56},{56,48},{64,72... | collective-permute-start | bytes 1376264 | tf_op jit(solution)/shard_map/ppermute | solution.py:42
  37.0 2.5 %collective-permute-start.9 = (bf16[448,512]{1,0:T(8,128)(2,1)S(1)}, bf16[448,512]{1,0:T(8,128)(2,1)S(1)}, u32[]{:S(2)}, u32[]{:S(2)}) collective-permute-start(bf16[448,512]{1,0:T(8,128)(2,1)S(1)} %slice.9), channel_id=1, source_target_pairs={{0,8},{8,0},{16,24},{24,16},{32,40},{40,32},{48,56},{56,48},{64,72... | collective-permute-start | bytes 1376264 | tf_op jit(solution)/shard_map/ppermute | solution.py:42
  37.5 21.2 %collective-permute-start.14 = (bf16[448,512]{1,0:T(8,128)(2,1)S(1)}, bf16[448,512]{1,0:T(8,128)(2,1)S(1)}, u32[]{:S(2)}, u32[]{:S(2)}) collective-permute-start(bf16[448,512]{1,0:T(8,128)(2,1)S(1)} %slice.10), channel_id=1, source_target_pairs={{0,16},{8,24},{16,0},{24,8},{32,48},{40,56},{48,32},{56,40},{64,80... | collective-permute-start | bytes 1376264 | tf_op jit(solution)/shard_map/ppermute | solution.py:38
  37.5 22.3 %collective-permute-start.13 = (bf16[448,512]{1,0:T(8,128)(2,1)S(1)}, bf16[448,512]{1,0:T(8,128)(2,1)S(1)}, u32[]{:S(2)}, u32[]{:S(2)}) collective-permute-start(bf16[448,512]{1,0:T(8,128)(2,1)S(1)} %slice.9), channel_id=1, source_target_pairs={{0,16},{8,24},{16,0},{24,8},{32,48},{40,56},{48,32},{56,40},{64,80... | collective-permute-start | bytes 1376264 | tf_op jit(solution)/shard_map/ppermute | solution.py:38
  51.6 8.2 %collective-permute-start.12 = (bf16[448,512]{1,0:T(8,128)(2,1)S(1)}, bf16[448,512]{1,0:T(8,128)(2,1)S(1)}, u32[]{:S(2)}, u32[]{:S(2)}) collective-permute-start(bf16[448,512]{1,0:T(8,128)(2,1)S(1)} %slice.11), channel_id=1, source_target_pairs={{0,8},{8,0},{16,24},{24,16},{32,40},{40,32},{48,56},{56,48},{64,72... | collective-permute-start | bytes 1376264 | tf_op jit(solution)/shard_map/ppermute | solution.py:42
  52.4 6.2 %collective-permute-start.15 = (bf16[80,896]{1,0:T(8,128)(2,1)S(1)}, bf16[80,896]{1,0:T(8,128)(2,1)S(1)}, u32[]{:S(2)}, u32[]{:S(2)}) collective-permute-start(bf16[80,896]{1,0:T(8,128)(2,1)S(1)} %get-tuple-element.89), channel_id=1, source_target_pairs={{0,64},{8,72},{16,80},{24,88},{32,96},{40,104},{48,112},{56,120},{... | collective-permute-start | bytes 430088 | tf_op jit(solution)/shard_map/ppermute | solution.py:46
  59.8 1.8 %collective-permute-start.16 = (bf16[448,512]{1,0:T(8,128)(2,1)S(1)}, bf16[448,512]{1,0:T(8,128)(2,1)S(1)}, u32[]{:S(2)}, u32[]{:S(2)}) collective-permute-start(bf16[448,512]{1,0:T(8,128)(2,1)S(1)} %collective-permute-done.13.refs_5_), channel_id=1, source_target_pairs={{0,8},{8,0},{16,24},{24,16},{32,40},{40,32},{48,56},{56,48},{64,72... | collective-permute-start | bytes 1376264 | tf_op jit(solution)/shard_map/ppermute | solution.py:42
  59.8 2.5 %collective-permute-start.17 = (bf16[448,512]{1,0:T(8,128)(2,1)S(1)}, bf16[448,512]{1,0:T(8,128)(2,1)S(1)}, u32[]{:S(2)}, u32[]{:S(2)}) collective-permute-start(bf16[448,512]{1,0:T(8,128)(2,1)S(1)} %collective-permute-done.14.refs_7_), channel_id=1, source_target_pairs={{0,8},{8,0},{16,24},{24,16},{32,40},{40,32},{48,56},{56,48},{64,72... | collective-permute-start | bytes 1376264 | tf_op jit(solution)/shard_map/ppermute | solution.py:42
  60.3 12.5 %collective-permute-start.11 = (bf16[448,512]{1,0:T(8,128)(2,1)S(1)}, bf16[448,512]{1,0:T(8,128)(2,1)S(1)}, u32[]{:S(2)}, u32[]{:S(2)}) collective-permute-start(bf16[448,512]{1,0:T(8,128)(2,1)S(1)} %slice.11), channel_id=1, source_target_pairs={{0,16},{8,24},{16,0},{24,8},{32,48},{40,56},{48,32},{56,40},{64,80... | collective-permute-start | bytes 1376264 | tf_op jit(solution)/shard_map/ppermute | solution.py:38
  62.3 12.8 %copy-start.2 = (bf16[512,896]{1,0:T(8,128)(2,1)S(1)}, bf16[512,896]{1,0:T(8,128)(2,1)}, u32[]{:S(2)}) copy-start(bf16[512,896]{1,0:T(8,128)(2,1)} %gate_ref.1) | copy-start | bytes 2752516
  72.8 3.6 %collective-permute-start.19 = (bf16[448,512]{1,0:T(8,128)(2,1)S(1)}, bf16[448,512]{1,0:T(8,128)(2,1)S(1)}, u32[]{:S(2)}, u32[]{:S(2)}) collective-permute-start(bf16[448,512]{1,0:T(8,128)(2,1)S(1)} %collective-permute-done.11.refs_4_), channel_id=1, source_target_pairs={{0,8},{8,0},{16,24},{24,16},{32,40},{40,32},{48,56},{56,48},{64,72... | collective-permute-start | bytes 1376264 | tf_op jit(solution)/shard_map/ppermute | solution.py:42
  76.5 28.6 %copy-start.10 = (f32[896]{0:T(1024)S(1)}, f32[896]{0:T(1024)}, u32[]{:S(2)}) copy-start(f32[896]{0:T(1024)} %param.21) | copy-start | bytes 10756
  78.6 26.4 %collective-permute-start.20 = (bf16[224,512]{1,0:T(8,128)(2,1)S(1)}, bf16[224,512]{1,0:T(8,128)(2,1)S(1)}, u32[]{:S(2)}, u32[]{:S(2)}) collective-permute-start(bf16[224,512]{1,0:T(8,128)(2,1)S(1)} %get-tuple-element.118), channel_id=1, source_target_pairs={{0,48},{8,56},{16,32},{24,40},{32,16},{40,24},{48,0},{56,8},{64,11... | collective-permute-start | bytes 688136 | tf_op jit(solution)/shard_map/ppermute | solution.py:34
  80.4 24.6 %collective-permute-start.21 = (bf16[224,512]{1,0:T(8,128)(2,1)S(1)}, bf16[224,512]{1,0:T(8,128)(2,1)S(1)}, u32[]{:S(2)}, u32[]{:S(2)}) collective-permute-start(bf16[224,512]{1,0:T(8,128)(2,1)S(1)} %get-tuple-element.119), channel_id=1, source_target_pairs={{0,64},{8,72},{16,80},{24,88},{32,96},{40,104},{48,112},{56,120},{... | collective-permute-start | bytes 688136 | tf_op jit(solution)/shard_map/ppermute | solution.py:34
  82.4 22.6 %collective-permute-start.22 = (bf16[224,512]{1,0:T(8,128)(2,1)S(1)}, bf16[224,512]{1,0:T(8,128)(2,1)S(1)}, u32[]{:S(2)}, u32[]{:S(2)}) collective-permute-start(bf16[224,512]{1,0:T(8,128)(2,1)S(1)} %get-tuple-element.120), channel_id=1, source_target_pairs={{0,112},{8,120},{16,96},{24,104},{32,80},{40,88},{48,64},{56,72},{... | collective-permute-start | bytes 688136 | tf_op jit(solution)/shard_map/ppermute | solution.py:34
  83.4 12.6 %collective-permute-start.18 = (f32[1,512]{1,0:T(1,128)S(1)}, f32[1,512]{1,0:T(1,128)S(1)}, u32[]{:S(2)}, u32[]{:S(2)}) collective-permute-start(f32[1,512]{1,0:T(1,128)S(1)} %get-tuple-element.110), channel_id=1, source_target_pairs={{0,4},{1,5},{2,6},{3,7},{4,0},{5,1},{6,2},{7,3},{8,12},{9,13},{10,... | collective-permute-start | bytes 6152 | tf_op jit(solution)/shard_map/ppermute | solution.py:50
  96.0 3.6 %collective-permute-start.23 = (f32[1,512]{1,0:T(1,128)S(1)}, f32[1,512]{1,0:T(1,128)S(1)}, u32[]{:S(2)}, u32[]{:S(2)}) collective-permute-start(f32[1,512]{1,0:T(1,128)S(1)} %add.24), channel_id=1, source_target_pairs={{0,1},{1,0},{2,3},{3,2},{4,5},{5,4},{6,7},{7,6},{8,9},{9,8},{10,11... | collective-permute-start | bytes 6152 | tf_op jit(solution)/shard_map/ppermute | solution.py:50
  99.6 5.4 %collective-permute-start.24 = (f32[1,512]{1,0:T(1,128)S(1)}, f32[1,512]{1,0:T(1,128)S(1)}, u32[]{:S(2)}, u32[]{:S(2)}) collective-permute-start(f32[1,512]{1,0:T(1,128)S(1)} %add.25), channel_id=1, source_target_pairs={{0,2},{1,3},{2,0},{3,1},{4,6},{5,7},{6,4},{7,5},{8,10},{9,11},{10,... | collective-permute-start | bytes 6152 | tf_op jit(solution)/shard_map/ppermute | solution.py:50

commit v6 on v5

--- a/solution.py
+++ b/solution.py
@@ -466,26 +466,28 @@
     near[0], sent = tie((near[0], sent))
     near_core[0] = core_swap(near[0])
 
-    here[1], here[2], near_core[0], got = tie((here[1], here[2], near_core[0], got))
-    for r in (1, 2):
-        kv = here[r][ATT_DIM:]
-        near[r] = class_swap(kv)
-        from_core[r] = core_swap(kv)
+    here[1], here[2], near_core[0], all_3, got = tie((here[1], here[2], near_core[0], all_3, got))
+    kv = [piece[ATT_DIM:] for piece in here[1:3]]
+    near[1], near[2] = class_swap(kv[0]), class_swap(kv[1])
+    here[3] = head_swap(all_3, 3)
     total, before, sent = ssm_merge(1, info, got, total, before)
-    got, all_3 = tie((block_swap(sent, 4), all_3))
-    here[3] = head_swap(all_3, 3)
-    total, before, sent = ssm_merge(2, info, got, total, before)
-    got = block_swap(sent, 8)
+    *kv, sent = tie((*kv, sent))
+    from_core[1], from_core[2] = core_swap(kv[0]), core_swap(kv[1])
+    from_core[1], from_core[2], sent = tie((from_core[1], from_core[2], sent))
+    got = block_swap(sent, 4)
     *state, ks, vs, mark = attend(
         0, info, q_own, here[1], here[2], kv_own, *from_core[:3], near[0], near_core[0]
     )
 
-    here[3], mark = tie((here[3], mark))
+    here[3], near[1], near[2], mark = tie((here[3], near[1], near[2], mark))
     kv = here[3][ATT_DIM:]
+    from_core[3] = core_swap(kv)
+    near_core[1], near_core[2] = core_swap(near[1]), core_swap(near[2])
+    kv, got = tie((kv, got))
     near[3] = class_swap(kv)
-    from_core[3] = core_swap(kv)
-    from_core[3], near[1], near[2], got, mark = tie((from_core[3], near[1], near[2], got, mark))
-    near_core[1], near_core[2] = core_swap(near[1]), core_swap(near[2])
+    total, before, sent = ssm_merge(2, info, got, total, before)
+    sent, mark = tie((sent, mark))
+    got = block_swap(sent, 8)
     queries = (q_own, here[1], here[2], here[3])
     *state, mark = attend(
         1, info, *queries, from_core[3], near[1], near_core[1], near[2], near_core[2], mark, ks, vs, *state
@@ -496,12 +498,10 @@
     total, before, sent = ssm_merge(3, info, got, total, before)
     gated, squares = ssm_carry(before, mixed, cum, read_t, ssm_gate)
     gated, squares, mark = tie((gated, squares, mark))
-    others = step_swap(squares, 4)
     *results, mark = attend(2, info, *queries, near[3], near_core[3], mark, *state)
     back = [results[0]] + [head_swap(results[r], r) for r in range(1, 4)]
-    others, mark = tie((others, mark))
-    squares = squares + others
-    for step in (1, 2):
+    squares, mark = tie((squares, mark))
+    for step in (1, 2, 4):
         squares = squares + step_swap(squares, step)
     *back, squares = tie((*back, squares))
     factor = lax.rsqrt(squares.reshape(TOK) / SSM_WIDTH + 1e-05)

time: 108 us -> 97.3 us (0.901)
  waiting for transfers between devices: 38.5 us -> 28.7 us
  starting transfers between devices: 30.5 us -> 29 us
    ppermute x5, waiting for transfers between devices: 3.15 us -> 12.8 us  [class_swap(): return lax.ppermute(value, 'ctx', [(i, i ^ 2) for i in range(CTX)])]
    ppermute x3, waiting for transfers between devices: 12.9 us -> 5.4 us  [step_swap(): return lax.ppermute(value, 'tp', [(i, i ^ step) for i in range(8)])]
    ppermute x2, waiting for transfers between devices: 9.93 us -> 2.67 us  [block_swap(): return lax.ppermute(value, 'ctx', [(i, i ^ step) for i in range(CTX)])]
    ppermute x6, waiting for transfers between devices: 9.44 us -> 6.46 us  [head_swap(): lax.ppermute(value, 'ctx', [(i, exchanged(i, r)) for i in range(CTX)])]
    ppermute x9, waiting for transfers between devices: 3.05 us -> 1.37 us  [core_swap(): return lax.ppermute(value, 'ctx', [(i, i ^ 1) for i in range(CTX)])]
    ppermute x2, starting transfers between devices: 2.99 us -> 1.79 us  [block_swap(): return lax.ppermute(value, 'ctx', [(i, i ^ step) for i in range(CTX)])]
  transfers between devices with their start and end apart: 25 -> 25, of which waited for: 13 -> 10; matrix products, arithmetic and copies ran while one was open for 0% -> 0% of each run, Pallas kernels for 25% -> 29%
where the time goes in v6:
time: 97.3 us; the launch traced here: 96.8 us
  Pallas kernels  36.3 us (37%)
  starting transfers between devices  29 us (30%)
  waiting for transfers between devices  28.7 us (29%)
  other arithmetic  1.73 us (2%)
  between operations  0.98 us (1%)
    pallas_call x3, Pallas kernels, attend(): pl.pallas_call(functools.partial(attend_kernel, stage), out_shape=out, in...  21.7 us
    ppermute x5, waiting for transfers between devices, class_swap(): return lax.ppermute(value, 'ctx', [(i, i ^ 2) for i in range(CTX)])  12.8 us
    ppermute x6, starting transfers between devices, head_swap(): lax.ppermute(value, 'ctx', [(i, exchanged(i, r)) for i in range(CTX)])  11.7 us
    ppermute x3, starting transfers between devices, step_swap(): return lax.ppermute(value, 'tp', [(i, i ^ step) for i in range(8)])  8.74 us
    ppermute x6, waiting for transfers between devices, head_swap(): lax.ppermute(value, 'ctx', [(i, exchanged(i, r)) for i in range(CTX)])  6.46 us
    ppermute x3, waiting for transfers between devices, step_swap(): return lax.ppermute(value, 'tp', [(i, i ^ step) for i in range(8)])  5.4 us
    ppermute x5, starting transfers between devices, class_swap(): return lax.ppermute(value, 'ctx', [(i, i ^ 2) for i in range(CTX)])  5.26 us
    pallas_call x1, Pallas kernels, pack(): pl.pallas_call(pack_kernel, out_shape=[shape((count, TOK), BF16) for coun...  4.41 us
  transfers between devices with their start and end apart: 25, of which 10 were waited for; matrix products, arithmetic and copies ran while one was open for 0% of the time, Pallas kernels for 29%

profile of v6, /device:TPU:0, one launch (start us, length us, event | category | flops | bytes accessed | tf_op | source)
XLA Modules:
  0.0 96.8 jit_solution(17309737455541086874)
XLA Ops:
  0.7 0.6 pad_add_fusion.info
  1.3 4.4 %shard_map.122 = (bf16[224,512]{1,0:T(8,128)(2,1)}, bf16[448,512]{1,0:T(8,128)(2,1)}, bf16[672,512]{1,0:T(8,128)(2,1)}, bf16[672,512]{1,0:T(8,128)(2,1)}, bf16[672,512]{1,0:T(8,128)(2,1)}) custom-call(s32[4]{0:T(128)} %pad_add_fusion.info, bf16[512,896]{1,0:T(8,128)(2,1)} %q_in.1, bf16[512,896]{1,0:T(8,128)(2,1)} %k_in.1, bf16[512,896]{1,0:T(8,128)(2,1)} %v_in.1), custom_call_target="tpu_custom_call" | custom-call | tf_op jit(solution)/shard_map/pallas_call | solution.py:338
  5.7 0.1 collective-permute-start.3
  5.8 1.7 %collective-permute-start.2 = (bf16[448,512]{1,0:T(8,128)(2,1)}, bf16[448,512]{1,0:T(8,128)(2,1)S(1)}, u32[]{:S(2)}, u32[]{:S(2)}) collective-permute-start(bf16[448,512]{1,0:T(8,128)(2,1)} %get-tuple-element.73.refs_3_), channel_id=1, source_target_pairs={{0,16},{8,24},{16,0},{24,8},{32,48},{40,56},{48,32},{56,40},{64,80... | collective-permute-start | bytes 1376264 | tf_op jit(solution)/shard_map/ppermute | solution.py:38
  7.4 2.1 %collective-permute-start = (bf16[672,512]{1,0:T(8,128)(2,1)}, bf16[672,512]{1,0:T(8,128)(2,1)S(1)}, u32[]{:S(2)}, u32[]{:S(2)}) collective-permute-start(bf16[672,512]{1,0:T(8,128)(2,1)} %get-tuple-element.71), channel_id=1, source_target_pairs={{0,48},{8,56},{16,32},{24,40},{32,16},{40,24},{48,0},{56,8},{64,11... | collective-permute-start | bytes 2064392 | tf_op jit(solution)/shard_map/ppermute | solution.py:34
  9.5 1.6 %collective-permute-start.1 = (bf16[672,512]{1,0:T(8,128)(2,1)}, bf16[672,512]{1,0:T(8,128)(2,1)S(1)}, u32[]{:S(2)}, u32[]{:S(2)}) collective-permute-start(bf16[672,512]{1,0:T(8,128)(2,1)} %get-tuple-element.72), channel_id=1, source_target_pairs={{0,64},{8,72},{16,80},{24,88},{32,96},{40,104},{48,112},{56,120},{... | collective-permute-start | bytes 2064392 | tf_op jit(solution)/shard_map/ppermute | solution.py:34
  11.1 0.0 collective-permute-done.3.refs_4_
  11.2 3.6 %shard_map.123 = (f32[512,896]{1,0:T(8,128)S(1)}, f32[72,896]{1,0:T(8,128)S(1)}, bf16[80,896]{1,0:T(8,128)(2,1)S(1)}, f32[512,14]{1,0:T(8,128)S(1)}) custom-call(bf16[512,896]{1,0:T(8,128)(2,1)S(1)} %copy-done.1, bf16[64,512]{1,0:T(8,128)(2,1)S(1)} %bitcast.12, bf16[64,512]{1,0:T(8,128)(2,1)S(1)} %bitcast.10, f32[14,512]{1,0:T(8,128)S(1)} %bitcast.13, ...), custom_call_target="tpu_custom_call" | custom-call | flops 1000 | bytes 1000 | tf_op jit(solution)/shard_map/pallas_call | solution.py:394
  14.8 0.1 collective-permute-start.4
  14.9 1.4 %collective-permute-done.4.got_ref = bf16[80,896]{1,0:T(8,128)(2,1)S(1)} collective-permute-done((bf16[80,896]{1,0:T(8,128)(2,1)S(1)}, bf16[80,896]{1,0:T(8,128)(2,1)S(1)}, u32[]{:S(2)}, u32[]{:S(2)}) %collective-permute-start.4) | collective-permute-done | bytes 143392 | tf_op jit(solution)/shard_map/ppermute | solution.py:42
  16.3 0.7 shard_map.124
  17.0 1.9 %collective-permute-done.2.refs_7_ = bf16[448,512]{1,0:T(8,128)(2,1)S(1)} collective-permute-done((bf16[448,512]{1,0:T(8,128)(2,1)}, bf16[448,512]{1,0:T(8,128)(2,1)S(1)}, u32[]{:S(2)}, u32[]{:S(2)}) %collective-permute-start.2) | collective-permute-done | bytes 458784 | tf_op jit(solution)/shard_map/ppermute | solution.py:38
  18.9 0.0 collective-permute-start.5
  18.9 1.6 %collective-permute-start.6 = (bf16[80,896]{1,0:T(8,128)(2,1)S(1)}, bf16[80,896]{1,0:T(8,128)(2,1)S(1)}, u32[]{:S(2)}, u32[]{:S(2)}) collective-permute-start(bf16[80,896]{1,0:T(8,128)(2,1)S(1)} %get-tuple-element.77), channel_id=1, source_target_pairs={{0,16},{8,24},{16,0},{24,8},{32,48},{40,56},{48,32},{56,40},{64,80... | collective-permute-start | bytes 430088 | tf_op jit(solution)/shard_map/ppermute | solution.py:38
  20.5 5.8 %collective-permute-done.refs_1_ = bf16[672,512]{1,0:T(8,128)(2,1)S(1)} collective-permute-done((bf16[672,512]{1,0:T(8,128)(2,1)}, bf16[672,512]{1,0:T(8,128)(2,1)S(1)}, u32[]{:S(2)}, u32[]{:S(2)}) %collective-permute-start) | collective-permute-done | bytes 688160 | tf_op jit(solution)/shard_map/ppermute | solution.py:34
  26.3 0.6 collective-permute-done.1.refs_2_
  27.0 0.0 collective-permute-done.6.got_ref
  27.0 0.0 collective-permute-done.5.refs_8_
  27.0 2.6 %collective-permute-start.7 = (bf16[672,512]{1,0:T(8,128)(2,1)S(1)}, bf16[672,512]{1,0:T(8,128)(2,1)S(1)}, u32[]{:S(2)}, u32[]{:S(2)}) collective-permute-start(bf16[672,512]{1,0:T(8,128)(2,1)S(1)} %copy-done.11), channel_id=1, source_target_pairs={{0,112},{8,120},{16,96},{24,104},{32,80},{40,88},{48,64},{56,72},{... | collective-permute-start | bytes 2064392 | tf_op jit(solution)/shard_map/ppermute | solution.py:34
  29.6 0.7 shard_map.125
  30.3 0.1 collective-permute-start.10
  30.4 0.5 collective-permute-start.11
  30.9 0.0 collective-permute-start.9
  30.9 2.0 %collective-permute-start.8 = (bf16[448,512]{1,0:T(8,128)(2,1)S(1)}, bf16[448,512]{1,0:T(8,128)(2,1)S(1)}, u32[]{:S(2)}, u32[]{:S(2)}) collective-permute-start(bf16[448,512]{1,0:T(8,128)(2,1)S(1)} %slice.9), channel_id=1, source_target_pairs={{0,16},{8,24},{16,0},{24,8},{32,48},{40,56},{48,32},{56,40},{64,80... | collective-permute-start | bytes 1376264 | tf_op jit(solution)/shard_map/ppermute | solution.py:38
  32.9 0.0 collective-permute-done.10.refs_5_
  32.9 0.0 collective-permute-done.11.refs_6_
  32.9 1.3 %collective-permute-start.12 = (bf16[80,896]{1,0:T(8,128)(2,1)S(1)}, bf16[80,896]{1,0:T(8,128)(2,1)S(1)}, u32[]{:S(2)}, u32[]{:S(2)}) collective-permute-start(bf16[80,896]{1,0:T(8,128)(2,1)S(1)} %get-tuple-element.97), channel_id=1, source_target_pairs={{0,32},{8,40},{16,48},{24,56},{32,0},{40,8},{48,16},{56,24},{64,96... | collective-permute-start | bytes 430088 | tf_op jit(solution)/shard_map/ppermute | solution.py:46
  34.2 9.1 %shard_map.126 = (f32[4,224,512]{2,1,0:T(8,128)S(1)}, f32[4,16,512]{2,1,0:T(8,128)S(1)}, bf16[4,1024,224]{2,1,0:T(8,128)(2,1)S(1)}, bf16[4,224,1024]{2,1,0:T(8,128)(2,1)S(1)}, f32[8,128]{1,0:T(8,128)S(1)}) custom-call(s32[4]{0:T(128)S(1)} %copy-done.6, bf16[224,512]{1,0:T(8,128)(2,1)S(1)} %copy-done, bf16[672,512]{1,0:T(8,128)(2,1)S(1)} %collective-permute-done.refs_1_, ...), custom_call_target="tpu_custom_call" | custom-call | flops 1000 | bytes 1000 | tf_op jit(solution)/shard_map/pallas_call | solution.py:368
  43.3 1.0 %collective-permute-done.9.refs_7_ = bf16[448,512]{1,0:T(8,128)(2,1)S(1)} collective-permute-done((bf16[448,512]{1,0:T(8,128)(2,1)S(1)}, bf16[448,512]{1,0:T(8,128)(2,1)S(1)}, u32[]{:S(2)}, u32[]{:S(2)}) %collective-permute-start.9) | collective-permute-done | bytes 458784 | tf_op jit(solution)/shard_map/ppermute | solution.py:38
  44.3 9.8 %collective-permute-done.8.refs_5_ = bf16[448,512]{1,0:T(8,128)(2,1)S(1)} collective-permute-done((bf16[448,512]{1,0:T(8,128)(2,1)S(1)}, bf16[448,512]{1,0:T(8,128)(2,1)S(1)}, u32[]{:S(2)}, u32[]{:S(2)}) %collective-permute-start.8) | collective-permute-done | bytes 458784 | tf_op jit(solution)/shard_map/ppermute | solution.py:38
  54.1 0.0 collective-permute-done.7.refs_3_
  54.1 0.1 collective-permute-start.15
  54.2 0.5 collective-permute-start.16
  54.7 0.1 collective-permute-start.17
  54.8 2.7 %collective-permute-done.12.got_ref = bf16[80,896]{1,0:T(8,128)(2,1)S(1)} collective-permute-done((bf16[80,896]{1,0:T(8,128)(2,1)S(1)}, bf16[80,896]{1,0:T(8,128)(2,1)S(1)}, u32[]{:S(2)}, u32[]{:S(2)}) %collective-permute-start.12) | collective-permute-done | bytes 143392 | tf_op jit(solution)/shard_map/ppermute | solution.py:46
  57.5 0.0 collective-permute-start.13
  57.5 0.7 shard_map.127
  58.1 0.5 collective-permute-start.14
  58.7 0.0 collective-permute-done.15.refs_4_
  58.7 0.0 collective-permute-done.16.refs_6_
  58.7 0.0 collective-permute-done.17.refs_8_
  58.7 0.0 copy-start.2
  58.7 10.5 %shard_map.128 = (f32[4,224,512]{2,1,0:T(8,128)S(1)}, f32[4,16,512]{2,1,0:T(8,128)S(1)}, f32[8,128]{1,0:T(8,128)S(1)}) custom-call(s32[4]{0:T(128)S(1)} %copy-done.6, bf16[224,512]{1,0:T(8,128)(2,1)S(1)} %copy-done, bf16[672,512]{1,0:T(8,128)(2,1)S(1)} %collective-permute-done.refs_1_, bf16[672,512]{1,0:T(8,128)(2,1)S(1)} %collective-permute-done.1.refs_2_, ...), custom_call_target="tpu_custom_call" | custom-call | flops 1000 | bytes 1000 | tf_op jit(solution)/shard_map/pallas_call | solution.py:368
  69.2 0.0 collective-permute-done.14.got_ref
  69.2 0.0 collective-permute-done.13.refs_4_
  69.2 0.1 collective-permute-start.18
  69.3 1.4 %shard_map.129 = (f32[72,896]{1,0:T(8,128)}, f32[72,896]{1,0:T(8,128)S(1)}, bf16[80,896]{1,0:T(8,128)(2,1)}) custom-call(s32[4]{0:T(128)S(1)} %copy-done.6, bf16[80,896]{1,0:T(8,128)(2,1)S(1)} %collective-permute-done.14.got_ref, f32[72,896]{1,0:T(8,128)S(1)} %get-tuple-element.114.total_ref, f32[72,896]{1,0:T(8,128)S(1)} %get-tuple-element.115.before_ref), custom_call_target="tpu_custom_call" | custom-call | flops 1000 | bytes 1000 | tf_op jit(solution)/shard_map/pallas_call | solution.py:411
  70.7 1.3 %shard_map.130 = (f32[512,896]{1,0:T(8,128)S(1)}, f32[1,512]{1,0:T(1,128)S(1)}) custom-call(f32[72,896]{1,0:T(8,128)S(1)} %get-tuple-element.116.state_ref, f32[512,896]{1,0:T(8,128)S(1)} %get-tuple-element.117.mixed_ref, f32[512,14]{1,0:T(8,128)S(1)} %get-tuple-element.118.cum_ref, bf16[64,512]{1,0:T(8,128)(2,1)S(1)} %bitcast.11, bf16[512,896]{1,0:T(8,128)(2,1)S(1)} %copy-done.2), custom_call_target="tpu_custom_call" | custom-call | flops 1000 | bytes 1000 | tf_op jit(solution)/shard_map/pallas_call | solution.py:423
  72.0 0.0 collective-permute-done.18.refs_5_
  72.1 0.0 copy-start.10
  72.1 2.1 %shard_map.131 = (bf16[224,512]{1,0:T(8,128)(2,1)S(1)}, bf16[224,512]{1,0:T(8,128)(2,1)S(1)}, bf16[224,512]{1,0:T(8,128)(2,1)S(1)}, bf16[224,512]{1,0:T(8,128)(2,1)S(1)}, f32[8,128]{1,0:T(8,128)S(1)}) custom-call(s32[4]{0:T(128)S(1)} %copy-done.6, bf16[224,512]{1,0:T(8,128)(2,1)S(1)} %copy-done, bf16[672,512]{1,0:T(8,128)(2,1)S(1)} %collective-permute-done.refs_1_, ...), custom_call_target="tpu_custom_call" | custom-call | flops 1000 | bytes 1000 | tf_op jit(solution)/shard_map/pallas_call | solution.py:368
  74.2 1.6 %collective-permute-start.19 = (bf16[224,512]{1,0:T(8,128)(2,1)S(1)}, bf16[224,512]{1,0:T(8,128)(2,1)S(1)}, u32[]{:S(2)}, u32[]{:S(2)}) collective-permute-start(bf16[224,512]{1,0:T(8,128)(2,1)S(1)} %get-tuple-element.130), channel_id=1, source_target_pairs={{0,48},{8,56},{16,32},{24,40},{32,16},{40,24},{48,0},{56,8},{64,11... | collective-permute-start | bytes 688136 | tf_op jit(solution)/shard_map/ppermute | solution.py:34
  75.8 2.6 %collective-permute-start.20 = (bf16[224,512]{1,0:T(8,128)(2,1)S(1)}, bf16[224,512]{1,0:T(8,128)(2,1)S(1)}, u32[]{:S(2)}, u32[]{:S(2)}) collective-permute-start(bf16[224,512]{1,0:T(8,128)(2,1)S(1)} %get-tuple-element.131), channel_id=1, source_target_pairs={{0,64},{8,72},{16,80},{24,88},{32,96},{40,104},{48,112},{56,120},{... | collective-permute-start | bytes 688136 | tf_op jit(solution)/shard_map/ppermute | solution.py:34
  78.4 1.2 %collective-permute-start.21 = (bf16[224,512]{1,0:T(8,128)(2,1)S(1)}, bf16[224,512]{1,0:T(8,128)(2,1)S(1)}, u32[]{:S(2)}, u32[]{:S(2)}) collective-permute-start(bf16[224,512]{1,0:T(8,128)(2,1)S(1)} %get-tuple-element.132), channel_id=1, source_target_pairs={{0,112},{8,120},{16,96},{24,104},{32,80},{40,88},{48,64},{56,72},{... | collective-permute-start | bytes 688136 | tf_op jit(solution)/shard_map/ppermute | solution.py:34
  79.6 1.9 %collective-permute-start.22 = (f32[1,512]{1,0:T(1,128)S(1)}, f32[1,512]{1,0:T(1,128)S(1)}, u32[]{:S(2)}, u32[]{:S(2)}) collective-permute-start(f32[1,512]{1,0:T(1,128)S(1)} %get-tuple-element.133), channel_id=1, source_target_pairs={{0,1},{1,0},{2,3},{3,2},{4,5},{5,4},{6,7},{7,6},{8,9},{9,8},{10,11... | collective-permute-start | bytes 6152 | tf_op jit(solution)/shard_map/ppermute | solution.py:50
  81.5 1.7 %collective-permute-done.22 = f32[1,512]{1,0:T(1,128)S(1)} collective-permute-done((f32[1,512]{1,0:T(1,128)S(1)}, f32[1,512]{1,0:T(1,128)S(1)}, u32[]{:S(2)}, u32[]{:S(2)}) %collective-permute-start.22) | collective-permute-done | bytes 2080 | tf_op jit(solution)/shard_map/ppermute | solution.py:50
  83.2 3.9 %collective-permute-start.23 = (f32[1,512]{1,0:T(1,128)S(1)}, f32[1,512]{1,0:T(1,128)S(1)}, u32[]{:S(2)}, u32[]{:S(2)}) collective-permute-start(f32[1,512]{1,0:T(1,128)S(1)} %add.24), channel_id=1, source_target_pairs={{0,2},{1,3},{2,0},{3,1},{4,6},{5,7},{6,4},{7,5},{8,10},{9,11},{10,... | collective-permute-start | bytes 6152 | tf_op jit(solution)/shard_map/ppermute | solution.py:50
  87.1 1.6 %collective-permute-done.23 = f32[1,512]{1,0:T(1,128)S(1)} collective-permute-done((f32[1,512]{1,0:T(1,128)S(1)}, f32[1,512]{1,0:T(1,128)S(1)}, u32[]{:S(2)}, u32[]{:S(2)}) %collective-permute-start.23) | collective-permute-done | bytes 2080 | tf_op jit(solution)/shard_map/ppermute | solution.py:50
  88.7 2.9 %collective-permute-start.24 = (f32[1,512]{1,0:T(1,128)S(1)}, f32[1,512]{1,0:T(1,128)S(1)}, u32[]{:S(2)}, u32[]{:S(2)}) collective-permute-start(f32[1,512]{1,0:T(1,128)S(1)} %add.25), channel_id=1, source_target_pairs={{0,4},{1,5},{2,6},{3,7},{4,0},{5,1},{6,2},{7,3},{8,12},{9,13},{10,... | collective-permute-start | bytes 6152 | tf_op jit(solution)/shard_map/ppermute | solution.py:50
  91.6 2.2 %collective-permute-done.24 = f32[1,512]{1,0:T(1,128)S(1)} collective-permute-done((f32[1,512]{1,0:T(1,128)S(1)}, f32[1,512]{1,0:T(1,128)S(1)}, u32[]{:S(2)}, u32[]{:S(2)}) %collective-permute-start.24) | collective-permute-done | bytes 2080 | tf_op jit(solution)/shard_map/ppermute | solution.py:50
  93.8 0.0 collective-permute-done.19.refs_1_
  93.8 0.0 collective-permute-done.21.refs_3_
  93.8 1.1 %multiply_convert_fusion = bf16[512,896]{1,0:T(8,128)(2,1)} fusion(f32[512,896]{1,0:T(8,128)S(1)} %get-tuple-element.138, f32[896]{0:T(1024)S(1)} %copy-done.10, f32[512]{0:T(512)S(1)} %bitcast.16), kind=kLoop, calls=%fused_computation | loop fusion | flops 1376256 | bytes 2758144 | tf_op jit(solution)/shard_map/convert_element_type | solution.py:508
  95.0 1.8 %shard_map.132 = bf16[512,896]{1,0:T(8,128)(2,1)} custom-call(s32[4]{0:T(128)S(1)} %copy-done.6, f32[8,128]{1,0:T(8,128)S(1)} %get-tuple-element.128._, bf16[224,512]{1,0:T(8,128)(2,1)S(1)} %get-tuple-element.134.refs_0_, bf16[224,512]{1,0:T(8,128)(2,1)S(1)} %collective-permute-done.19.refs_1_, bf16[224,512]{1,0:T(8,128)(2,1)S(1)} %collective-permute-done.20.refs_2_, ...), custom_call_target="tpu_custom_call" | custom-call | tf_op jit(solution)/shard_map/pallas_call | solution.py:381
  (31 shorter events, 0.2 us)
Async XLA Ops:
  0.6 10.5 %copy-start.1 = (bf16[512,896]{1,0:T(8,128)(2,1)S(1)}, bf16[512,896]{1,0:T(8,128)(2,1)}, u32[]{:S(2)}) copy-start(bf16[512,896]{1,0:T(8,128)(2,1)} %x_ref) | copy-start | bytes 2752516
  0.6 10.5 %copy-start.9 = (f32[14]{0:T(128)S(1)}, f32[14]{0:T(128)}, u32[]{:S(2)}) copy-start(f32[14]{0:T(128)} %param.20) | copy-start | bytes 172
  0.7 10.5 %copy-start.8 = (f32[14]{0:T(128)S(1)}, f32[14]{0:T(128)}, u32[]{:S(2)}) copy-start(f32[14]{0:T(128)} %param.19) | copy-start | bytes 172
  0.7 10.5 %copy-start.7 = (f32[512,14]{0,1:T(8,128)S(1)}, f32[512,14]{0,1:T(8,128)}, u32[]{:S(2)}) copy-start(f32[512,14]{0,1:T(8,128)} %param.18) | copy-start | bytes 86020
  0.7 10.5 %copy-start.4 = (bf16[512,64]{0,1:T(8,128)(2,1)S(1)}, bf16[512,64]{0,1:T(8,128)(2,1)}, u32[]{:S(2)}) copy-start(bf16[512,64]{0,1:T(8,128)(2,1)} %param.17) | copy-start | bytes 196612
  0.7 10.5 %copy-start.5 = (bf16[512,64]{0,1:T(8,128)(2,1)S(1)}, bf16[512,64]{0,1:T(8,128)(2,1)}, u32[]{:S(2)}) copy-start(bf16[512,64]{0,1:T(8,128)(2,1)} %param.16) | copy-start | bytes 196612
  1.3 15.0 %copy-start.6 = (s32[4]{0:T(128)S(1)}, s32[4]{0:T(128)}, u32[]{:S(2)}) copy-start(s32[4]{0:T(128)} %pad_add_fusion.info) | copy-start | bytes 52
  5.7 21.3 %copy-start.11 = (bf16[672,512]{1,0:T(8,128)(2,1)S(1)}, bf16[672,512]{1,0:T(8,128)(2,1)}, u32[]{:S(2)}) copy-start(bf16[672,512]{1,0:T(8,128)(2,1)} %get-tuple-element.80) | copy-start | bytes 2064388
  5.7 5.4 %collective-permute-start.3 = (bf16[448,512]{1,0:T(8,128)(2,1)}, bf16[448,512]{1,0:T(8,128)(2,1)S(1)}, u32[]{:S(2)}, u32[]{:S(2)}) collective-permute-start(bf16[448,512]{1,0:T(8,128)(2,1)} %get-tuple-element.73.refs_3_), channel_id=1, source_target_pairs={{0,8},{8,0},{16,24},{24,16},{32,40},{40,32},{48,56},{56,48},{64,72... | collective-permute-start | bytes 1376264 | tf_op jit(solution)/shard_map/ppermute | solution.py:42
  5.8 13.1 %collective-permute-start.2 = (bf16[448,512]{1,0:T(8,128)(2,1)}, bf16[448,512]{1,0:T(8,128)(2,1)S(1)}, u32[]{:S(2)}, u32[]{:S(2)}) collective-permute-start(bf16[448,512]{1,0:T(8,128)(2,1)} %get-tuple-element.73.refs_3_), channel_id=1, source_target_pairs={{0,16},{8,24},{16,0},{24,8},{32,48},{40,56},{48,32},{56,40},{64,80... | collective-permute-start | bytes 1376264 | tf_op jit(solution)/shard_map/ppermute | solution.py:38
  7.4 18.9 %collective-permute-start = (bf16[672,512]{1,0:T(8,128)(2,1)}, bf16[672,512]{1,0:T(8,128)(2,1)S(1)}, u32[]{:S(2)}, u32[]{:S(2)}) collective-permute-start(bf16[672,512]{1,0:T(8,128)(2,1)} %get-tuple-element.71), channel_id=1, source_target_pairs={{0,48},{8,56},{16,32},{24,40},{32,16},{40,24},{48,0},{56,8},{64,11... | collective-permute-start | bytes 2064392 | tf_op jit(solution)/shard_map/ppermute | solution.py:34
  9.5 17.4 %collective-permute-start.1 = (bf16[672,512]{1,0:T(8,128)(2,1)}, bf16[672,512]{1,0:T(8,128)(2,1)S(1)}, u32[]{:S(2)}, u32[]{:S(2)}) collective-permute-start(bf16[672,512]{1,0:T(8,128)(2,1)} %get-tuple-element.72), channel_id=1, source_target_pairs={{0,64},{8,72},{16,80},{24,88},{32,96},{40,104},{48,112},{56,120},{... | collective-permute-start | bytes 2064392 | tf_op jit(solution)/shard_map/ppermute | solution.py:34
  14.8 19.4 %copy-start = (bf16[224,512]{1,0:T(8,128)(2,1)S(1)}, bf16[224,512]{1,0:T(8,128)(2,1)}, u32[]{:S(2)}) copy-start(bf16[224,512]{1,0:T(8,128)(2,1)} %get-tuple-element.83.refs_0_) | copy-start | bytes 688132
  14.8 19.4 %copy-start.3 = (bf16[448,512]{1,0:T(8,128)(2,1)S(1)}, bf16[448,512]{1,0:T(8,128)(2,1)}, u32[]{:S(2)}) copy-start(bf16[448,512]{1,0:T(8,128)(2,1)} %get-tuple-element.73.refs_3_) | copy-start | bytes 1376260
  14.8 1.4 %collective-permute-start.4 = (bf16[80,896]{1,0:T(8,128)(2,1)S(1)}, bf16[80,896]{1,0:T(8,128)(2,1)S(1)}, u32[]{:S(2)}, u32[]{:S(2)}) collective-permute-start(bf16[80,896]{1,0:T(8,128)(2,1)S(1)} %get-tuple-element.75), channel_id=1, source_target_pairs={{0,8},{8,0},{16,24},{24,16},{32,40},{40,32},{48,56},{56,48},{64,72... | collective-permute-start | bytes 430088 | tf_op jit(solution)/shard_map/ppermute | solution.py:42
  18.9 8.0 %collective-permute-start.5 = (bf16[448,512]{1,0:T(8,128)(2,1)S(1)}, bf16[448,512]{1,0:T(8,128)(2,1)S(1)}, u32[]{:S(2)}, u32[]{:S(2)}) collective-permute-start(bf16[448,512]{1,0:T(8,128)(2,1)S(1)} %collective-permute-done.2.refs_7_), channel_id=1, source_target_pairs={{0,8},{8,0},{16,24},{24,16},{32,40},{40,32},{48,56},{56,48},{64,72... | collective-permute-start | bytes 1376264 | tf_op jit(solution)/shard_map/ppermute | solution.py:42
  18.9 8.0 %collective-permute-start.6 = (bf16[80,896]{1,0:T(8,128)(2,1)S(1)}, bf16[80,896]{1,0:T(8,128)(2,1)S(1)}, u32[]{:S(2)}, u32[]{:S(2)}) collective-permute-start(bf16[80,896]{1,0:T(8,128)(2,1)S(1)} %get-tuple-element.77), channel_id=1, source_target_pairs={{0,16},{8,24},{16,0},{24,8},{32,48},{40,56},{48,32},{56,40},{64,80... | collective-permute-start | bytes 430088 | tf_op jit(solution)/shard_map/ppermute | solution.py:38
  27.0 27.1 %collective-permute-start.7 = (bf16[672,512]{1,0:T(8,128)(2,1)S(1)}, bf16[672,512]{1,0:T(8,128)(2,1)S(1)}, u32[]{:S(2)}, u32[]{:S(2)}) collective-permute-start(bf16[672,512]{1,0:T(8,128)(2,1)S(1)} %copy-done.11), channel_id=1, source_target_pairs={{0,112},{8,120},{16,96},{24,104},{32,80},{40,88},{48,64},{56,72},{... | collective-permute-start | bytes 2064392 | tf_op jit(solution)/shard_map/ppermute | solution.py:34
  30.3 2.6 %collective-permute-start.10 = (bf16[448,512]{1,0:T(8,128)(2,1)S(1)}, bf16[448,512]{1,0:T(8,128)(2,1)S(1)}, u32[]{:S(2)}, u32[]{:S(2)}) collective-permute-start(bf16[448,512]{1,0:T(8,128)(2,1)S(1)} %slice.9), channel_id=1, source_target_pairs={{0,8},{8,0},{16,24},{24,16},{32,40},{40,32},{48,56},{56,48},{64,72... | collective-permute-start | bytes 1376264 | tf_op jit(solution)/shard_map/ppermute | solution.py:42
  30.4 2.5 %collective-permute-start.11 = (bf16[448,512]{1,0:T(8,128)(2,1)S(1)}, bf16[448,512]{1,0:T(8,128)(2,1)S(1)}, u32[]{:S(2)}, u32[]{:S(2)}) collective-permute-start(bf16[448,512]{1,0:T(8,128)(2,1)S(1)} %slice.10), channel_id=1, source_target_pairs={{0,8},{8,0},{16,24},{24,16},{32,40},{40,32},{48,56},{56,48},{64,72... | collective-permute-start | bytes 1376264 | tf_op jit(solution)/shard_map/ppermute | solution.py:42
  30.9 13.4 %collective-permute-start.9 = (bf16[448,512]{1,0:T(8,128)(2,1)S(1)}, bf16[448,512]{1,0:T(8,128)(2,1)S(1)}, u32[]{:S(2)}, u32[]{:S(2)}) collective-permute-start(bf16[448,512]{1,0:T(8,128)(2,1)S(1)} %slice.10), channel_id=1, source_target_pairs={{0,16},{8,24},{16,0},{24,8},{32,48},{40,56},{48,32},{56,40},{64,80... | collective-permute-start | bytes 1376264 | tf_op jit(solution)/shard_map/ppermute | solution.py:38
  30.9 23.2 %collective-permute-start.8 = (bf16[448,512]{1,0:T(8,128)(2,1)S(1)}, bf16[448,512]{1,0:T(8,128)(2,1)S(1)}, u32[]{:S(2)}, u32[]{:S(2)}) collective-permute-start(bf16[448,512]{1,0:T(8,128)(2,1)S(1)} %slice.9), channel_id=1, source_target_pairs={{0,16},{8,24},{16,0},{24,8},{32,48},{40,56},{48,32},{56,40},{64,80... | collective-permute-start | bytes 1376264 | tf_op jit(solution)/shard_map/ppermute | solution.py:38
  32.9 24.6 %collective-permute-start.12 = (bf16[80,896]{1,0:T(8,128)(2,1)S(1)}, bf16[80,896]{1,0:T(8,128)(2,1)S(1)}, u32[]{:S(2)}, u32[]{:S(2)}) collective-permute-start(bf16[80,896]{1,0:T(8,128)(2,1)S(1)} %get-tuple-element.97), channel_id=1, source_target_pairs={{0,32},{8,40},{16,48},{24,56},{32,0},{40,8},{48,16},{56,24},{64,96... | collective-permute-start | bytes 430088 | tf_op jit(solution)/shard_map/ppermute | solution.py:46
  54.1 4.5 %collective-permute-start.15 = (bf16[448,512]{1,0:T(8,128)(2,1)S(1)}, bf16[448,512]{1,0:T(8,128)(2,1)S(1)}, u32[]{:S(2)}, u32[]{:S(2)}) collective-permute-start(bf16[448,512]{1,0:T(8,128)(2,1)S(1)} %slice.11), channel_id=1, source_target_pairs={{0,8},{8,0},{16,24},{24,16},{32,40},{40,32},{48,56},{56,48},{64,72... | collective-permute-start | bytes 1376264 | tf_op jit(solution)/shard_map/ppermute | solution.py:42
  54.2 4.5 %collective-permute-start.16 = (bf16[448,512]{1,0:T(8,128)(2,1)S(1)}, bf16[448,512]{1,0:T(8,128)(2,1)S(1)}, u32[]{:S(2)}, u32[]{:S(2)}) collective-permute-start(bf16[448,512]{1,0:T(8,128)(2,1)S(1)} %collective-permute-done.8.refs_5_), channel_id=1, source_target_pairs={{0,8},{8,0},{16,24},{24,16},{32,40},{40,32},{48,56},{56,48},{64,72... | collective-permute-start | bytes 1376264 | tf_op jit(solution)/shard_map/ppermute | solution.py:42
  54.7 4.0 %collective-permute-start.17 = (bf16[448,512]{1,0:T(8,128)(2,1)S(1)}, bf16[448,512]{1,0:T(8,128)(2,1)S(1)}, u32[]{:S(2)}, u32[]{:S(2)}) collective-permute-start(bf16[448,512]{1,0:T(8,128)(2,1)S(1)} %collective-permute-done.9.refs_7_), channel_id=1, source_target_pairs={{0,8},{8,0},{16,24},{24,16},{32,40},{40,32},{48,56},{56,48},{64,72... | collective-permute-start | bytes 1376264 | tf_op jit(solution)/shard_map/ppermute | solution.py:42
  57.5 11.8 %collective-permute-start.13 = (bf16[448,512]{1,0:T(8,128)(2,1)S(1)}, bf16[448,512]{1,0:T(8,128)(2,1)S(1)}, u32[]{:S(2)}, u32[]{:S(2)}) collective-permute-start(bf16[448,512]{1,0:T(8,128)(2,1)S(1)} %slice.11), channel_id=1, source_target_pairs={{0,16},{8,24},{16,0},{24,8},{32,48},{40,56},{48,32},{56,40},{64,80... | collective-permute-start | bytes 1376264 | tf_op jit(solution)/shard_map/ppermute | solution.py:38
  58.1 11.1 %collective-permute-start.14 = (bf16[80,896]{1,0:T(8,128)(2,1)S(1)}, bf16[80,896]{1,0:T(8,128)(2,1)S(1)}, u32[]{:S(2)}, u32[]{:S(2)}) collective-permute-start(bf16[80,896]{1,0:T(8,128)(2,1)S(1)} %get-tuple-element.104), channel_id=1, source_target_pairs={{0,64},{8,72},{16,80},{24,88},{32,96},{40,104},{48,112},{56,120},{... | collective-permute-start | bytes 430088 | tf_op jit(solution)/shard_map/ppermute | solution.py:46
  58.7 12.0 %copy-start.2 = (bf16[512,896]{1,0:T(8,128)(2,1)S(1)}, bf16[512,896]{1,0:T(8,128)(2,1)}, u32[]{:S(2)}) copy-start(bf16[512,896]{1,0:T(8,128)(2,1)} %gate_ref.1) | copy-start | bytes 2752516
  69.2 2.8 %collective-permute-start.18 = (bf16[448,512]{1,0:T(8,128)(2,1)S(1)}, bf16[448,512]{1,0:T(8,128)(2,1)S(1)}, u32[]{:S(2)}, u32[]{:S(2)}) collective-permute-start(bf16[448,512]{1,0:T(8,128)(2,1)S(1)} %collective-permute-done.13.refs_4_), channel_id=1, source_target_pairs={{0,8},{8,0},{16,24},{24,16},{32,40},{40,32},{48,56},{56,48},{64,72... | collective-permute-start | bytes 1376264 | tf_op jit(solution)/shard_map/ppermute | solution.py:42
  72.1 21.7 %copy-start.10 = (f32[896]{0:T(1024)S(1)}, f32[896]{0:T(1024)}, u32[]{:S(2)}) copy-start(f32[896]{0:T(1024)} %param.21) | copy-start | bytes 10756
  74.2 19.6 %collective-permute-start.19 = (bf16[224,512]{1,0:T(8,128)(2,1)S(1)}, bf16[224,512]{1,0:T(8,128)(2,1)S(1)}, u32[]{:S(2)}, u32[]{:S(2)}) collective-permute-start(bf16[224,512]{1,0:T(8,128)(2,1)S(1)} %get-tuple-element.130), channel_id=1, source_target_pairs={{0,48},{8,56},{16,32},{24,40},{32,16},{40,24},{48,0},{56,8},{64,11... | collective-permute-start | bytes 688136 | tf_op jit(solution)/shard_map/ppermute | solution.py:34
  75.8 18.0 %collective-permute-start.20 = (bf16[224,512]{1,0:T(8,128)(2,1)S(1)}, bf16[224,512]{1,0:T(8,128)(2,1)S(1)}, u32[]{:S(2)}, u32[]{:S(2)}) collective-permute-start(bf16[224,512]{1,0:T(8,128)(2,1)S(1)} %get-tuple-element.131), channel_id=1, source_target_pairs={{0,64},{8,72},{16,80},{24,88},{32,96},{40,104},{48,112},{56,120},{... | collective-permute-start | bytes 688136 | tf_op jit(solution)/shard_map/ppermute | solution.py:34
  78.4 15.3 %collective-permute-start.21 = (bf16[224,512]{1,0:T(8,128)(2,1)S(1)}, bf16[224,512]{1,0:T(8,128)(2,1)S(1)}, u32[]{:S(2)}, u32[]{:S(2)}) collective-permute-start(bf16[224,512]{1,0:T(8,128)(2,1)S(1)} %get-tuple-element.132), channel_id=1, source_target_pairs={{0,112},{8,120},{16,96},{24,104},{32,80},{40,88},{48,64},{56,72},{... | collective-permute-start | bytes 688136 | tf_op jit(solution)/shard_map/ppermute | solution.py:34
  79.6 3.6 %collective-permute-start.22 = (f32[1,512]{1,0:T(1,128)S(1)}, f32[1,512]{1,0:T(1,128)S(1)}, u32[]{:S(2)}, u32[]{:S(2)}) collective-permute-start(f32[1,512]{1,0:T(1,128)S(1)} %get-tuple-element.133), channel_id=1, source_target_pairs={{0,1},{1,0},{2,3},{3,2},{4,5},{5,4},{6,7},{7,6},{8,9},{9,8},{10,11... | collective-permute-start | bytes 6152 | tf_op jit(solution)/shard_map/ppermute | solution.py:50
  83.2 5.5 %collective-permute-start.23 = (f32[1,512]{1,0:T(1,128)S(1)}, f32[1,512]{1,0:T(1,128)S(1)}, u32[]{:S(2)}, u32[]{:S(2)}) collective-permute-start(f32[1,512]{1,0:T(1,128)S(1)} %add.24), channel_id=1, source_target_pairs={{0,2},{1,3},{2,0},{3,1},{4,6},{5,7},{6,4},{7,5},{8,10},{9,11},{10,... | collective-permute-start | bytes 6152 | tf_op jit(solution)/shard_map/ppermute | solution.py:50
  88.7 5.1 %collective-permute-start.24 = (f32[1,512]{1,0:T(1,128)S(1)}, f32[1,512]{1,0:T(1,128)S(1)}, u32[]{:S(2)}, u32[]{:S(2)}) collective-permute-start(f32[1,512]{1,0:T(1,128)S(1)} %add.25), channel_id=1, source_target_pairs={{0,4},{1,5},{2,6},{3,7},{4,0},{5,1},{6,2},{7,3},{8,12},{9,13},{10,... | collective-permute-start | bytes 6152 | tf_op jit(solution)/shard_map/ppermute | solution.py:50

commit v7 on v6

--- a/solution.py
+++ b/solution.py
@@ -88,16 +88,23 @@
         pieces += [(0, 1, core_0, 0), (1, 1, core_1, 0), (2, 1, core_2, 0)]
         pieces += [(3, 0, near_0, 0), (3, 1, near_core_0, 0)]
     elif stage == 1:
-        q_in, (core_3, near_1, near_core_1, near_2, near_core_2, _), refs = refs[:4], refs[4:10], refs[10:]
+        q_in, (core_keys_3, core_values_3, _), refs = refs[:4], refs[4:7], refs[7:]
         ks_early, vs_early, acc_in, stats_in, acc, stats_ref, mark, ks, vs, qs = refs
-        pieces = [(0, 0, q_in[3], ATT_DIM), (0, 1, core_3, 0)]
-        pieces += [(1, 0, near_1, 0), (1, 1, near_core_1, 0), (2, 0, near_2, 0), (2, 1, near_core_2, 0)]
+        pieces = [(0, 0, q_in[3], ATT_DIM), (0, 1, (core_keys_3, core_values_3), 0)]
+    elif stage == 2:
+        q_in, (near_1, near_core_1, near_2, near_core_2, _), refs = refs[:4], refs[4:9], refs[9:]
+        acc_in, stats_in, acc, stats_ref, mark, ks, vs, qs = refs
+        pieces = [(0, 0, near_1, 0), (0, 1, near_core_1, 0), (1, 0, near_2, 0), (1, 1, near_core_2, 0)]
     else:
         q_in, (near_3, near_core_3, _), refs = refs[:4], refs[4:7], refs[7:]
         acc_in, stats_in, *o_out, mark, ks, vs, qs, acc, os = refs
         pieces = [(0, 0, near_3, 0), (0, 1, near_core_3, 0)]
     for slot, other, piece, first in pieces:
         start = pl.multiple_of((core ^ other) * TOK, TOK)
+        if isinstance(piece, tuple):
+            ks[slot, pl.ds(start, TOK), :] = piece[0][...].T
+            vs[slot, :, pl.ds(start, TOK)] = piece[1][...]
+            continue
         ks[slot, pl.ds(start, TOK), :] = piece[first : first + ATT_DIM, :].T
         vs[slot, :, pl.ds(start, TOK)] = piece[first + ATT_DIM : first + 2 * ATT_DIM, :]
     for r, queries in enumerate(q_in):
@@ -179,14 +186,16 @@
             stats = sweep(
                 4 * last, ks_early, vs_early, lambda k: jnp.where(k == 3, near_seen(0), (hid ^ k) < chip), stats
             )
-            stats = sweep(3, ks, vs, lambda k: jnp.where(k == 0, (hid ^ 3) < chip, near_seen(k)), stats)
+            stats = sweep(1, ks, vs, lambda k: (hid ^ 3) < chip, stats)
             stats = lax.fori_loop(0, last, lambda _, now: diagonal(0, now), stats)
+        elif stage == 2:
+            stats = sweep(2, ks, vs, lambda k: near_seen(k + 1), stats)
         else:
             stats = sweep(1, ks, vs, lambda k: near_seen(3), stats)
 
         for half in range(2):
             lanes = slice(half * HALF, (half + 1) * HALF)
-            if stage == 2:
+            if stage == 3:
                 os[r, :, lanes] = (acc[r, :, lanes] / stats[half][1]).astype(BF16)
             else:
                 stats_ref[r, 0:8, lanes] = jnp.broadcast_to(stats[half][0], (8, HALF))
@@ -194,7 +203,7 @@
         return carry
 
     lax.fori_loop(0, 4, one_queries, 0)
-    if stage == 2:
+    if stage == 3:
         for r in range(4):
             o_out[r][...] = os[r]
 
@@ -350,7 +359,7 @@
 
 
 def attend(stage, info, *operands):
-    slots = (4, 3, 1)[stage]
+    slots = (4, 1, 2, 1)[stage]
     keys, values = (slots, 2 * TOK, ATT_DIM), (slots, ATT_DIM, 2 * TOK)
     state = [shape((4, ATT_DIM, TOK), F32), shape((4, 16, TOK), F32)]
     queries = pltpu.VMEM((4, ATT_DIM, TOK), BF16)
@@ -358,7 +367,7 @@
     if stage == 0:
         out = state + [shape(keys, BF16), shape(values, BF16)] + mark
         scratch = [queries]
-    elif stage == 1:
+    elif stage < 3:
         out = state + mark
         scratch = [pltpu.VMEM(keys, BF16), pltpu.VMEM(values, BF16), queries]
     else:
@@ -479,29 +488,31 @@
         0, info, q_own, here[1], here[2], kv_own, *from_core[:3], near[0], near_core[0]
     )
 
-    here[3], near[1], near[2], mark = tie((here[3], near[1], near[2], mark))
+    here[3], mark = tie((here[3], mark))
     kv = here[3][ATT_DIM:]
-    from_core[3] = core_swap(kv)
+    from_core[3] = (core_swap(here[3][K_ROWS]), core_swap(here[3][V_ROWS]))
+    queries = (q_own, here[1], here[2], here[3])
+    *state, mark = attend(1, info, *queries, *from_core[3], mark, ks, vs, *state)
+
+    near[1], near[2], mark = tie((near[1], near[2], mark))
     near_core[1], near_core[2] = core_swap(near[1]), core_swap(near[2])
     kv, got = tie((kv, got))
     near[3] = class_swap(kv)
     total, before, sent = ssm_merge(2, info, got, total, before)
     sent, mark = tie((sent, mark))
     got = block_swap(sent, 8)
-    queries = (q_own, here[1], here[2], here[3])
-    *state, mark = attend(
-        1, info, *queries, from_core[3], near[1], near_core[1], near[2], near_core[2], mark, ks, vs, *state
-    )
-
-    near[3], got, mark = tie((near[3], got, mark))
-    near_core[3] = core_swap(near[3])
+    *state, mark = attend(2, info, *queries, near[1], near_core[1], near[2], near_core[2], mark, *state)
+
+    got, mark = tie((got, mark))
     total, before, sent = ssm_merge(3, info, got, total, before)
     gated, squares = ssm_carry(before, mixed, cum, read_t, ssm_gate)
-    gated, squares, mark = tie((gated, squares, mark))
-    *results, mark = attend(2, info, *queries, near[3], near_core[3], mark, *state)
+    squares = squares + step_swap(squares, 1)
+    near[3], gated, squares, mark = tie((near[3], gated, squares, mark))
+    near_core[3] = core_swap(near[3])
+    *results, mark = attend(3, info, *queries, near[3], near_core[3], mark, *state)
     back = [results[0]] + [head_swap(results[r], r) for r in range(1, 4)]
     squares, mark = tie((squares, mark))
-    for step in (1, 2, 4):
+    for step in (2, 4):
         squares = squares + step_swap(squares, step)
     *back, squares = tie((*back, squares))
     factor = lax.rsqrt(squares.reshape(TOK) / SSM_WIDTH + 1e-05)

time: 97.3 us -> 97 us (level)
  waiting for transfers between devices: 28.7 us -> 26.1 us
    ppermute x5, waiting for transfers between devices: 12.8 us -> 2.73 us  [class_swap(): return lax.ppermute(value, 'ctx', [(i, i ^ 2) for i in range(CTX)])]
    ppermute x6, waiting for transfers between devices: 6.46 us -> 9.81 us  [head_swap(): lax.ppermute(value, 'ctx', [(i, exchanged(i, r)) for i in range(CTX)])]
    ppermute x9 -> x10, waiting for transfers between devices: 1.37 us -> 3.79 us  [core_swap(): return lax.ppermute(value, 'ctx', [(i, i ^ 1) for i in range(CTX)])]
    ppermute x3, waiting for transfers between devices: 5.4 us -> 6.91 us  [step_swap(): return lax.ppermute(value, 'tp', [(i, i ^ step) for i in range(8)])]
    ppermute x6, starting transfers between devices: 11.7 us -> 12.7 us  [head_swap(): lax.ppermute(value, 'ctx', [(i, exchanged(i, r)) for i in range(CTX)])]
    pallas_call x3 -> x4, Pallas kernels: 21.7 us -> 22.5 us  [attend(): pl.pallas_call(functools.partial(attend_kernel, stage), out_shape=out, in...]
  transfers between devices with their start and end apart: 25 -> 26, of which waited for: 10 -> 13; matrix products, arithmetic and copies ran while one was open for 0% -> 0% of each run, Pallas kernels for 29% -> 30%
where the time goes in v7:
time: 97 us; the launch traced here: 96 us
  Pallas kernels  37.1 us (38%)
  starting transfers between devices  29.9 us (31%)
  waiting for transfers between devices  26.1 us (27%)
  other arithmetic  1.75 us (2%)
  between operations  0.99 us (1%)
    pallas_call x4, Pallas kernels, attend(): pl.pallas_call(functools.partial(attend_kernel, stage), out_shape=out, in...  22.5 us
    ppermute x6, starting transfers between devices, head_swap(): lax.ppermute(value, 'ctx', [(i, exchanged(i, r)) for i in range(CTX)])  12.7 us
    ppermute x6, waiting for transfers between devices, head_swap(): lax.ppermute(value, 'ctx', [(i, exchanged(i, r)) for i in range(CTX)])  9.81 us
    ppermute x3, starting transfers between devices, step_swap(): return lax.ppermute(value, 'tp', [(i, i ^ step) for i in range(8)])  8.75 us
    ppermute x3, waiting for transfers between devices, step_swap(): return lax.ppermute(value, 'tp', [(i, i ^ step) for i in range(8)])  6.91 us
    ppermute x5, starting transfers between devices, class_swap(): return lax.ppermute(value, 'ctx', [(i, i ^ 2) for i in range(CTX)])  5.26 us
    pallas_call x1, Pallas kernels, pack(): pl.pallas_call(pack_kernel, out_shape=[shape((count, TOK), BF16) for coun...  4.42 us
    ppermute x10, waiting for transfers between devices, core_swap(): return lax.ppermute(value, 'ctx', [(i, i ^ 1) for i in range(CTX)])  3.79 us
  transfers between devices with their start and end apart: 26, of which 13 were waited for; matrix products, arithmetic and copies ran while one was open for 0% of the time, Pallas kernels for 30%

profile of v7, /device:TPU:0, one launch (start us, length us, event | category | flops | bytes accessed | tf_op | source)
XLA Modules:
  0.0 96.0 jit_solution(5613552367209743204)
XLA Ops:
  0.7 0.6 pad_add_fusion.info
  1.3 4.4 %shard_map.122 = (bf16[224,512]{1,0:T(8,128)(2,1)}, bf16[448,512]{1,0:T(8,128)(2,1)}, bf16[672,512]{1,0:T(8,128)(2,1)}, bf16[672,512]{1,0:T(8,128)(2,1)}, bf16[672,512]{1,0:T(8,128)(2,1)}) custom-call(s32[4]{0:T(128)} %pad_add_fusion.info, bf16[512,896]{1,0:T(8,128)(2,1)} %q_in.1, bf16[512,896]{1,0:T(8,128)(2,1)} %k_in.1, bf16[512,896]{1,0:T(8,128)(2,1)} %v_in.1), custom_call_target="tpu_custom_call" | custom-call | tf_op jit(solution)/shard_map/pallas_call | solution.py:347
  5.7 0.1 collective-permute-start.3
  5.8 1.7 %collective-permute-start.2 = (bf16[448,512]{1,0:T(8,128)(2,1)}, bf16[448,512]{1,0:T(8,128)(2,1)S(1)}, u32[]{:S(2)}, u32[]{:S(2)}) collective-permute-start(bf16[448,512]{1,0:T(8,128)(2,1)} %get-tuple-element.77.refs_3_), channel_id=1, source_target_pairs={{0,16},{8,24},{16,0},{24,8},{32,48},{40,56},{48,32},{56,40},{64,80... | collective-permute-start | bytes 1376264 | tf_op jit(solution)/shard_map/ppermute | solution.py:38
  7.5 2.1 %collective-permute-start = (bf16[672,512]{1,0:T(8,128)(2,1)}, bf16[672,512]{1,0:T(8,128)(2,1)S(1)}, u32[]{:S(2)}, u32[]{:S(2)}) collective-permute-start(bf16[672,512]{1,0:T(8,128)(2,1)} %get-tuple-element.75), channel_id=1, source_target_pairs={{0,48},{8,56},{16,32},{24,40},{32,16},{40,24},{48,0},{56,8},{64,11... | collective-permute-start | bytes 2064392 | tf_op jit(solution)/shard_map/ppermute | solution.py:34
  9.6 1.6 %collective-permute-start.1 = (bf16[672,512]{1,0:T(8,128)(2,1)}, bf16[672,512]{1,0:T(8,128)(2,1)S(1)}, u32[]{:S(2)}, u32[]{:S(2)}) collective-permute-start(bf16[672,512]{1,0:T(8,128)(2,1)} %get-tuple-element.76), channel_id=1, source_target_pairs={{0,64},{8,72},{16,80},{24,88},{32,96},{40,104},{48,112},{56,120},{... | collective-permute-start | bytes 2064392 | tf_op jit(solution)/shard_map/ppermute | solution.py:34
  11.1 0.0 collective-permute-done.3.refs_4_
  11.2 3.6 %shard_map.123 = (f32[512,896]{1,0:T(8,128)S(1)}, f32[72,896]{1,0:T(8,128)S(1)}, bf16[80,896]{1,0:T(8,128)(2,1)S(1)}, f32[512,14]{1,0:T(8,128)S(1)}) custom-call(bf16[512,896]{1,0:T(8,128)(2,1)S(1)} %copy-done.1, bf16[64,512]{1,0:T(8,128)(2,1)S(1)} %bitcast.12, bf16[64,512]{1,0:T(8,128)(2,1)S(1)} %bitcast.10, f32[14,512]{1,0:T(8,128)S(1)} %bitcast.13, ...), custom_call_target="tpu_custom_call" | custom-call | flops 1000 | bytes 1000 | tf_op jit(solution)/shard_map/pallas_call | solution.py:403
  14.9 0.1 collective-permute-start.4
  15.0 1.4 %collective-permute-done.4.got_ref = bf16[80,896]{1,0:T(8,128)(2,1)S(1)} collective-permute-done((bf16[80,896]{1,0:T(8,128)(2,1)S(1)}, bf16[80,896]{1,0:T(8,128)(2,1)S(1)}, u32[]{:S(2)}, u32[]{:S(2)}) %collective-permute-start.4) | collective-permute-done | bytes 143392 | tf_op jit(solution)/shard_map/ppermute | solution.py:42
  16.3 0.7 shard_map.124
  17.0 1.9 %collective-permute-done.2.refs_7_ = bf16[448,512]{1,0:T(8,128)(2,1)S(1)} collective-permute-done((bf16[448,512]{1,0:T(8,128)(2,1)}, bf16[448,512]{1,0:T(8,128)(2,1)S(1)}, u32[]{:S(2)}, u32[]{:S(2)}) %collective-permute-start.2) | collective-permute-done | bytes 458784 | tf_op jit(solution)/shard_map/ppermute | solution.py:38
  19.0 0.0 collective-permute-start.5
  19.0 1.6 %collective-permute-start.6 = (bf16[80,896]{1,0:T(8,128)(2,1)S(1)}, bf16[80,896]{1,0:T(8,128)(2,1)S(1)}, u32[]{:S(2)}, u32[]{:S(2)}) collective-permute-start(bf16[80,896]{1,0:T(8,128)(2,1)S(1)} %get-tuple-element.81), channel_id=1, source_target_pairs={{0,16},{8,24},{16,0},{24,8},{32,48},{40,56},{48,32},{56,40},{64,80... | collective-permute-start | bytes 430088 | tf_op jit(solution)/shard_map/ppermute | solution.py:38
  20.5 5.8 %collective-permute-done.refs_1_ = bf16[672,512]{1,0:T(8,128)(2,1)S(1)} collective-permute-done((bf16[672,512]{1,0:T(8,128)(2,1)}, bf16[672,512]{1,0:T(8,128)(2,1)S(1)}, u32[]{:S(2)}, u32[]{:S(2)}) %collective-permute-start) | collective-permute-done | bytes 688160 | tf_op jit(solution)/shard_map/ppermute | solution.py:34
  26.4 0.6 collective-permute-done.1.refs_2_
  27.0 0.0 collective-permute-done.6.got_ref
  27.0 0.0 collective-permute-done.5.refs_8_
  27.0 2.6 %collective-permute-start.7 = (bf16[672,512]{1,0:T(8,128)(2,1)S(1)}, bf16[672,512]{1,0:T(8,128)(2,1)S(1)}, u32[]{:S(2)}, u32[]{:S(2)}) collective-permute-start(bf16[672,512]{1,0:T(8,128)(2,1)S(1)} %copy-done.11), channel_id=1, source_target_pairs={{0,112},{8,120},{16,96},{24,104},{32,80},{40,88},{48,64},{56,72},{... | collective-permute-start | bytes 2064392 | tf_op jit(solution)/shard_map/ppermute | solution.py:34
  29.6 0.7 shard_map.125
  30.3 0.1 collective-permute-start.8
  30.4 0.5 collective-permute-start.9
  30.9 0.0 collective-permute-start.12
  30.9 2.0 %collective-permute-start.13 = (bf16[448,512]{1,0:T(8,128)(2,1)S(1)}, bf16[448,512]{1,0:T(8,128)(2,1)S(1)}, u32[]{:S(2)}, u32[]{:S(2)}) collective-permute-start(bf16[448,512]{1,0:T(8,128)(2,1)S(1)} %slice.16), channel_id=1, source_target_pairs={{0,16},{8,24},{16,0},{24,8},{32,48},{40,56},{48,32},{56,40},{64,80... | collective-permute-start | bytes 1376264 | tf_op jit(solution)/shard_map/ppermute | solution.py:38
  33.0 0.0 collective-permute-done.8.refs_5_
  33.0 0.0 collective-permute-done.9.refs_6_
  33.0 9.2 %shard_map.126 = (f32[4,224,512]{2,1,0:T(8,128)S(1)}, f32[4,16,512]{2,1,0:T(8,128)S(1)}, bf16[4,1024,224]{2,1,0:T(8,128)(2,1)S(1)}, bf16[4,224,1024]{2,1,0:T(8,128)(2,1)S(1)}, f32[8,128]{1,0:T(8,128)S(1)}) custom-call(s32[4]{0:T(128)S(1)} %copy-done.6, bf16[224,512]{1,0:T(8,128)(2,1)S(1)} %copy-done, bf16[672,512]{1,0:T(8,128)(2,1)S(1)} %collective-permute-done.refs_1_, ...), custom_call_target="tpu_custom_call" | custom-call | flops 1000 | bytes 1000 | tf_op jit(solution)/shard_map/pallas_call | solution.py:377
  42.2 3.4 %collective-permute-done.7.refs_3_ = bf16[672,512]{1,0:T(8,128)(2,1)S(1)} collective-permute-done((bf16[672,512]{1,0:T(8,128)(2,1)S(1)}, bf16[672,512]{1,0:T(8,128)(2,1)S(1)}, u32[]{:S(2)}, u32[]{:S(2)}) %collective-permute-start.7) | collective-permute-done | bytes 688160 | tf_op jit(solution)/shard_map/ppermute | solution.py:34
  45.6 0.1 collective-permute-start.14
  45.7 0.5 collective-permute-start.15
  46.2 0.7 collective-permute-start.10
  46.8 0.3 collective-permute-done.14.refs_4_
  47.1 0.3 collective-permute-done.15.refs_5_
  47.5 5.9 %shard_map.128 = (f32[4,224,512]{2,1,0:T(8,128)S(1)}, f32[4,16,512]{2,1,0:T(8,128)S(1)}, f32[8,128]{1,0:T(8,128)S(1)}) custom-call(s32[4]{0:T(128)S(1)} %copy-done.6, bf16[224,512]{1,0:T(8,128)(2,1)S(1)} %copy-done, bf16[672,512]{1,0:T(8,128)(2,1)S(1)} %collective-permute-done.refs_1_, bf16[672,512]{1,0:T(8,128)(2,1)S(1)} %collective-permute-done.1.refs_2_, ...), custom_call_target="tpu_custom_call" | custom-call | flops 1000 | bytes 1000 | tf_op jit(solution)/shard_map/pallas_call | solution.py:377
  53.3 0.0 collective-permute-done.12.refs_4_
  53.3 0.8 collective-permute-done.13.refs_6_
  54.1 0.2 collective-permute-start.17
  54.3 0.3 collective-permute-start.18
  54.7 2.8 %collective-permute-done.10.got_ref = bf16[80,896]{1,0:T(8,128)(2,1)S(1)} collective-permute-done((bf16[80,896]{1,0:T(8,128)(2,1)S(1)}, bf16[80,896]{1,0:T(8,128)(2,1)S(1)}, u32[]{:S(2)}, u32[]{:S(2)}) %collective-permute-start.10) | collective-permute-done | bytes 143392 | tf_op jit(solution)/shard_map/ppermute | solution.py:46
  57.5 0.0 collective-permute-start.11
  57.5 0.7 shard_map.127
  58.2 0.5 collective-permute-start.16
  58.7 0.0 collective-permute-done.17.refs_5_
  58.7 5.4 %shard_map.129 = (f32[4,224,512]{2,1,0:T(8,128)S(1)}, f32[4,16,512]{2,1,0:T(8,128)S(1)}, f32[8,128]{1,0:T(8,128)S(1)}) custom-call(s32[4]{0:T(128)S(1)} %copy-done.6, bf16[224,512]{1,0:T(8,128)(2,1)S(1)} %copy-done, bf16[672,512]{1,0:T(8,128)(2,1)S(1)} %collective-permute-done.refs_1_, bf16[672,512]{1,0:T(8,128)(2,1)S(1)} %collective-permute-done.1.refs_2_, ...), custom_call_target="tpu_custom_call" | custom-call | flops 1000 | bytes 1000 | tf_op jit(solution)/shard_map/pallas_call | solution.py:377
  64.1 0.0 collective-permute-done.16.got_ref
  64.1 1.4 %shard_map.130 = (f32[72,896]{1,0:T(8,128)}, f32[72,896]{1,0:T(8,128)S(1)}, bf16[80,896]{1,0:T(8,128)(2,1)}) custom-call(s32[4]{0:T(128)S(1)} %copy-done.6, bf16[80,896]{1,0:T(8,128)(2,1)S(1)} %collective-permute-done.16.got_ref, f32[72,896]{1,0:T(8,128)S(1)} %get-tuple-element.122.total_ref, f32[72,896]{1,0:T(8,128)S(1)} %get-tuple-element.123.before_ref), custom_call_target="tpu_custom_call" | custom-call | flops 1000 | bytes 1000 | tf_op jit(solution)/shard_map/pallas_call | solution.py:420
  65.5 1.3 %shard_map.131 = (f32[512,896]{1,0:T(8,128)S(1)}, f32[1,512]{1,0:T(1,128)S(1)}) custom-call(f32[72,896]{1,0:T(8,128)S(1)} %get-tuple-element.124.state_ref, f32[512,896]{1,0:T(8,128)S(1)} %get-tuple-element.125.mixed_ref, f32[512,14]{1,0:T(8,128)S(1)} %get-tuple-element.126.cum_ref, bf16[64,512]{1,0:T(8,128)(2,1)S(1)} %bitcast.11, bf16[512,896]{1,0:T(8,128)(2,1)S(1)} %copy-done.2), custom_call_target="tpu_custom_call" | custom-call | flops 1000 | bytes 1000 | tf_op jit(solution)/shard_map/pallas_call | solution.py:432
  66.8 2.0 %collective-permute-start.19 = (f32[1,512]{1,0:T(1,128)S(1)}, f32[1,512]{1,0:T(1,128)S(1)}, u32[]{:S(2)}, u32[]{:S(2)}) collective-permute-start(f32[1,512]{1,0:T(1,128)S(1)} %get-tuple-element.128), channel_id=1, source_target_pairs={{0,1},{1,0},{2,3},{3,2},{4,5},{5,4},{6,7},{7,6},{8,9},{9,8},{10,11... | collective-permute-start | bytes 6152 | tf_op jit(solution)/shard_map/ppermute | solution.py:50
  68.8 1.7 %collective-permute-done.19 = f32[1,512]{1,0:T(1,128)S(1)} collective-permute-done((f32[1,512]{1,0:T(1,128)S(1)}, f32[1,512]{1,0:T(1,128)S(1)}, u32[]{:S(2)}, u32[]{:S(2)}) %collective-permute-start.19) | collective-permute-done | bytes 2080 | tf_op jit(solution)/shard_map/ppermute | solution.py:50
  70.5 0.0 collective-permute-done.11.refs_4_
  70.5 0.1 collective-permute-start.20
  70.6 1.8 %collective-permute-done.20.refs_5_ = bf16[448,512]{1,0:T(8,128)(2,1)S(1)} collective-permute-done((bf16[448,512]{1,0:T(8,128)(2,1)S(1)}, bf16[448,512]{1,0:T(8,128)(2,1)S(1)}, u32[]{:S(2)}, u32[]{:S(2)}) %collective-permute-start.20) | collective-permute-done | bytes 458784 | tf_op jit(solution)/shard_map/ppermute | solution.py:42
  72.4 2.1 %shard_map.132 = (bf16[224,512]{1,0:T(8,128)(2,1)S(1)}, bf16[224,512]{1,0:T(8,128)(2,1)S(1)}, bf16[224,512]{1,0:T(8,128)(2,1)S(1)}, bf16[224,512]{1,0:T(8,128)(2,1)S(1)}, f32[8,128]{1,0:T(8,128)S(1)}) custom-call(s32[4]{0:T(128)S(1)} %copy-done.6, bf16[224,512]{1,0:T(8,128)(2,1)S(1)} %copy-done, bf16[672,512]{1,0:T(8,128)(2,1)S(1)} %collective-permute-done.refs_1_, ...), custom_call_target="tpu_custom_call" | custom-call | flops 1000 | bytes 1000 | tf_op jit(solution)/shard_map/pallas_call | solution.py:377
  74.5 1.6 %collective-permute-start.21 = (bf16[224,512]{1,0:T(8,128)(2,1)S(1)}, bf16[224,512]{1,0:T(8,128)(2,1)S(1)}, u32[]{:S(2)}, u32[]{:S(2)}) collective-permute-start(bf16[224,512]{1,0:T(8,128)(2,1)S(1)} %get-tuple-element.138), channel_id=1, source_target_pairs={{0,48},{8,56},{16,32},{24,40},{32,16},{40,24},{48,0},{56,8},{64,11... | collective-permute-start | bytes 688136 | tf_op jit(solution)/shard_map/ppermute | solution.py:34
  76.1 3.7 %collective-permute-start.22 = (bf16[224,512]{1,0:T(8,128)(2,1)S(1)}, bf16[224,512]{1,0:T(8,128)(2,1)S(1)}, u32[]{:S(2)}, u32[]{:S(2)}) collective-permute-start(bf16[224,512]{1,0:T(8,128)(2,1)S(1)} %get-tuple-element.139), channel_id=1, source_target_pairs={{0,64},{8,72},{16,80},{24,88},{32,96},{40,104},{48,112},{56,120},{... | collective-permute-start | bytes 688136 | tf_op jit(solution)/shard_map/ppermute | solution.py:34
  79.8 1.2 %collective-permute-start.23 = (bf16[224,512]{1,0:T(8,128)(2,1)S(1)}, bf16[224,512]{1,0:T(8,128)(2,1)S(1)}, u32[]{:S(2)}, u32[]{:S(2)}) collective-permute-start(bf16[224,512]{1,0:T(8,128)(2,1)S(1)} %get-tuple-element.140), channel_id=1, source_target_pairs={{0,112},{8,120},{16,96},{24,104},{32,80},{40,88},{48,64},{56,72},{... | collective-permute-start | bytes 688136 | tf_op jit(solution)/shard_map/ppermute | solution.py:34
  80.9 3.9 %collective-permute-start.24 = (f32[1,512]{1,0:T(1,128)S(1)}, f32[1,512]{1,0:T(1,128)S(1)}, u32[]{:S(2)}, u32[]{:S(2)}) collective-permute-start(f32[1,512]{1,0:T(1,128)S(1)} %add.24), channel_id=1, source_target_pairs={{0,2},{1,3},{2,0},{3,1},{4,6},{5,7},{6,4},{7,5},{8,10},{9,11},{10,... | collective-permute-start | bytes 6152 | tf_op jit(solution)/shard_map/ppermute | solution.py:50
  84.8 1.6 %collective-permute-done.24 = f32[1,512]{1,0:T(1,128)S(1)} collective-permute-done((f32[1,512]{1,0:T(1,128)S(1)}, f32[1,512]{1,0:T(1,128)S(1)}, u32[]{:S(2)}, u32[]{:S(2)}) %collective-permute-start.24) | collective-permute-done | bytes 2080 | tf_op jit(solution)/shard_map/ppermute | solution.py:50
  86.4 2.9 %collective-permute-start.25 = (f32[1,512]{1,0:T(1,128)S(1)}, f32[1,512]{1,0:T(1,128)S(1)}, u32[]{:S(2)}, u32[]{:S(2)}) collective-permute-start(f32[1,512]{1,0:T(1,128)S(1)} %add.25), channel_id=1, source_target_pairs={{0,4},{1,5},{2,6},{3,7},{4,0},{5,1},{6,2},{7,3},{8,12},{9,13},{10,... | collective-permute-start | bytes 6152 | tf_op jit(solution)/shard_map/ppermute | solution.py:50
  89.3 3.7 %collective-permute-done.25 = f32[1,512]{1,0:T(1,128)S(1)} collective-permute-done((f32[1,512]{1,0:T(1,128)S(1)}, f32[1,512]{1,0:T(1,128)S(1)}, u32[]{:S(2)}, u32[]{:S(2)}) %collective-permute-start.25) | collective-permute-done | bytes 2080 | tf_op jit(solution)/shard_map/ppermute | solution.py:50
  92.9 0.0 collective-permute-done.21.refs_1_
  93.0 0.0 collective-permute-done.23.refs_3_
  93.0 1.1 %multiply_convert_fusion = bf16[512,896]{1,0:T(8,128)(2,1)} fusion(f32[512,896]{1,0:T(8,128)S(1)} %get-tuple-element.146, f32[896]{0:T(1024)S(1)} %copy-done.10, f32[512]{0:T(512)S(1)} %bitcast.16), kind=kLoop, calls=%fused_computation | loop fusion | flops 1376256 | bytes 2758144 | tf_op jit(solution)/shard_map/convert_element_type | solution.py:519
  94.1 1.8 %shard_map.133 = bf16[512,896]{1,0:T(8,128)(2,1)} custom-call(s32[4]{0:T(128)S(1)} %copy-done.6, f32[8,128]{1,0:T(8,128)S(1)} %get-tuple-element.136._, bf16[224,512]{1,0:T(8,128)(2,1)S(1)} %get-tuple-element.142.refs_0_, bf16[224,512]{1,0:T(8,128)(2,1)S(1)} %collective-permute-done.21.refs_1_, bf16[224,512]{1,0:T(8,128)(2,1)S(1)} %collective-permute-done.22.refs_2_, ...), custom_call_target="tpu_custom_call" | custom-call | tf_op jit(solution)/shard_map/pallas_call | solution.py:390
  (35 shorter events, 0.2 us)
Async XLA Ops:
  0.6 10.5 %copy-start.1 = (bf16[512,896]{1,0:T(8,128)(2,1)S(1)}, bf16[512,896]{1,0:T(8,128)(2,1)}, u32[]{:S(2)}) copy-start(bf16[512,896]{1,0:T(8,128)(2,1)} %x_ref) | copy-start | bytes 2752516
  0.6 10.5 %copy-start.4 = (bf16[512,64]{0,1:T(8,128)(2,1)S(1)}, bf16[512,64]{0,1:T(8,128)(2,1)}, u32[]{:S(2)}) copy-start(bf16[512,64]{0,1:T(8,128)(2,1)} %param.17) | copy-start | bytes 196612
  0.7 10.5 %copy-start.5 = (bf16[512,64]{0,1:T(8,128)(2,1)S(1)}, bf16[512,64]{0,1:T(8,128)(2,1)}, u32[]{:S(2)}) copy-start(bf16[512,64]{0,1:T(8,128)(2,1)} %param.16) | copy-start | bytes 196612
  0.7 10.5 %copy-start.7 = (f32[512,14]{0,1:T(8,128)S(1)}, f32[512,14]{0,1:T(8,128)}, u32[]{:S(2)}) copy-start(f32[512,14]{0,1:T(8,128)} %param.18) | copy-start | bytes 86020
  0.7 10.5 %copy-start.8 = (f32[14]{0:T(128)S(1)}, f32[14]{0:T(128)}, u32[]{:S(2)}) copy-start(f32[14]{0:T(128)} %param.19) | copy-start | bytes 172
  0.7 10.5 %copy-start.9 = (f32[14]{0:T(128)S(1)}, f32[14]{0:T(128)}, u32[]{:S(2)}) copy-start(f32[14]{0:T(128)} %param.20) | copy-start | bytes 172
  1.3 15.1 %copy-start.6 = (s32[4]{0:T(128)S(1)}, s32[4]{0:T(128)}, u32[]{:S(2)}) copy-start(s32[4]{0:T(128)} %pad_add_fusion.info) | copy-start | bytes 52
  5.7 21.3 %copy-start.11 = (bf16[672,512]{1,0:T(8,128)(2,1)S(1)}, bf16[672,512]{1,0:T(8,128)(2,1)}, u32[]{:S(2)}) copy-start(bf16[672,512]{1,0:T(8,128)(2,1)} %get-tuple-element.84) | copy-start | bytes 2064388
  5.7 5.4 %collective-permute-start.3 = (bf16[448,512]{1,0:T(8,128)(2,1)}, bf16[448,512]{1,0:T(8,128)(2,1)S(1)}, u32[]{:S(2)}, u32[]{:S(2)}) collective-permute-start(bf16[448,512]{1,0:T(8,128)(2,1)} %get-tuple-element.77.refs_3_), channel_id=1, source_target_pairs={{0,8},{8,0},{16,24},{24,16},{32,40},{40,32},{48,56},{56,48},{64,72... | collective-permute-start | bytes 1376264 | tf_op jit(solution)/shard_map/ppermute | solution.py:42
  5.8 13.1 %collective-permute-start.2 = (bf16[448,512]{1,0:T(8,128)(2,1)}, bf16[448,512]{1,0:T(8,128)(2,1)S(1)}, u32[]{:S(2)}, u32[]{:S(2)}) collective-permute-start(bf16[448,512]{1,0:T(8,128)(2,1)} %get-tuple-element.77.refs_3_), channel_id=1, source_target_pairs={{0,16},{8,24},{16,0},{24,8},{32,48},{40,56},{48,32},{56,40},{64,80... | collective-permute-start | bytes 1376264 | tf_op jit(solution)/shard_map/ppermute | solution.py:38
  7.5 18.9 %collective-permute-start = (bf16[672,512]{1,0:T(8,128)(2,1)}, bf16[672,512]{1,0:T(8,128)(2,1)S(1)}, u32[]{:S(2)}, u32[]{:S(2)}) collective-permute-start(bf16[672,512]{1,0:T(8,128)(2,1)} %get-tuple-element.75), channel_id=1, source_target_pairs={{0,48},{8,56},{16,32},{24,40},{32,16},{40,24},{48,0},{56,8},{64,11... | collective-permute-start | bytes 2064392 | tf_op jit(solution)/shard_map/ppermute | solution.py:34
  9.6 17.4 %collective-permute-start.1 = (bf16[672,512]{1,0:T(8,128)(2,1)}, bf16[672,512]{1,0:T(8,128)(2,1)S(1)}, u32[]{:S(2)}, u32[]{:S(2)}) collective-permute-start(bf16[672,512]{1,0:T(8,128)(2,1)} %get-tuple-element.76), channel_id=1, source_target_pairs={{0,64},{8,72},{16,80},{24,88},{32,96},{40,104},{48,112},{56,120},{... | collective-permute-start | bytes 2064392 | tf_op jit(solution)/shard_map/ppermute | solution.py:34
  14.8 18.1 %copy-start = (bf16[224,512]{1,0:T(8,128)(2,1)S(1)}, bf16[224,512]{1,0:T(8,128)(2,1)}, u32[]{:S(2)}) copy-start(bf16[224,512]{1,0:T(8,128)(2,1)} %get-tuple-element.85.refs_0_) | copy-start | bytes 688132
  14.9 18.1 %copy-start.3 = (bf16[448,512]{1,0:T(8,128)(2,1)S(1)}, bf16[448,512]{1,0:T(8,128)(2,1)}, u32[]{:S(2)}) copy-start(bf16[448,512]{1,0:T(8,128)(2,1)} %get-tuple-element.77.refs_3_) | copy-start | bytes 1376260
  14.9 1.4 %collective-permute-start.4 = (bf16[80,896]{1,0:T(8,128)(2,1)S(1)}, bf16[80,896]{1,0:T(8,128)(2,1)S(1)}, u32[]{:S(2)}, u32[]{:S(2)}) collective-permute-start(bf16[80,896]{1,0:T(8,128)(2,1)S(1)} %get-tuple-element.79), channel_id=1, source_target_pairs={{0,8},{8,0},{16,24},{24,16},{32,40},{40,32},{48,56},{56,48},{64,72... | collective-permute-start | bytes 430088 | tf_op jit(solution)/shard_map/ppermute | solution.py:42
  19.0 8.0 %collective-permute-start.5 = (bf16[448,512]{1,0:T(8,128)(2,1)S(1)}, bf16[448,512]{1,0:T(8,128)(2,1)S(1)}, u32[]{:S(2)}, u32[]{:S(2)}) collective-permute-start(bf16[448,512]{1,0:T(8,128)(2,1)S(1)} %collective-permute-done.2.refs_7_), channel_id=1, source_target_pairs={{0,8},{8,0},{16,24},{24,16},{32,40},{40,32},{48,56},{56,48},{64,72... | collective-permute-start | bytes 1376264 | tf_op jit(solution)/shard_map/ppermute | solution.py:42
  19.0 8.0 %collective-permute-start.6 = (bf16[80,896]{1,0:T(8,128)(2,1)S(1)}, bf16[80,896]{1,0:T(8,128)(2,1)S(1)}, u32[]{:S(2)}, u32[]{:S(2)}) collective-permute-start(bf16[80,896]{1,0:T(8,128)(2,1)S(1)} %get-tuple-element.81), channel_id=1, source_target_pairs={{0,16},{8,24},{16,0},{24,8},{32,48},{40,56},{48,32},{56,40},{64,80... | collective-permute-start | bytes 430088 | tf_op jit(solution)/shard_map/ppermute | solution.py:38
  27.0 18.5 %collective-permute-start.7 = (bf16[672,512]{1,0:T(8,128)(2,1)S(1)}, bf16[672,512]{1,0:T(8,128)(2,1)S(1)}, u32[]{:S(2)}, u32[]{:S(2)}) collective-permute-start(bf16[672,512]{1,0:T(8,128)(2,1)S(1)} %copy-done.11), channel_id=1, source_target_pairs={{0,112},{8,120},{16,96},{24,104},{32,80},{40,88},{48,64},{56,72},{... | collective-permute-start | bytes 2064392 | tf_op jit(solution)/shard_map/ppermute | solution.py:34
  30.3 2.6 %collective-permute-start.8 = (bf16[448,512]{1,0:T(8,128)(2,1)S(1)}, bf16[448,512]{1,0:T(8,128)(2,1)S(1)}, u32[]{:S(2)}, u32[]{:S(2)}) collective-permute-start(bf16[448,512]{1,0:T(8,128)(2,1)S(1)} %slice.15), channel_id=1, source_target_pairs={{0,8},{8,0},{16,24},{24,16},{32,40},{40,32},{48,56},{56,48},{64,72... | collective-permute-start | bytes 1376264 | tf_op jit(solution)/shard_map/ppermute | solution.py:42
  30.4 2.5 %collective-permute-start.9 = (bf16[448,512]{1,0:T(8,128)(2,1)S(1)}, bf16[448,512]{1,0:T(8,128)(2,1)S(1)}, u32[]{:S(2)}, u32[]{:S(2)}) collective-permute-start(bf16[448,512]{1,0:T(8,128)(2,1)S(1)} %slice.16), channel_id=1, source_target_pairs={{0,8},{8,0},{16,24},{24,16},{32,40},{40,32},{48,56},{56,48},{64,72... | collective-permute-start | bytes 1376264 | tf_op jit(solution)/shard_map/ppermute | solution.py:42
  30.9 22.4 %collective-permute-start.12 = (bf16[448,512]{1,0:T(8,128)(2,1)S(1)}, bf16[448,512]{1,0:T(8,128)(2,1)S(1)}, u32[]{:S(2)}, u32[]{:S(2)}) collective-permute-start(bf16[448,512]{1,0:T(8,128)(2,1)S(1)} %slice.15), channel_id=1, source_target_pairs={{0,16},{8,24},{16,0},{24,8},{32,48},{40,56},{48,32},{56,40},{64,80... | collective-permute-start | bytes 1376264 | tf_op jit(solution)/shard_map/ppermute | solution.py:38
  30.9 23.2 %collective-permute-start.13 = (bf16[448,512]{1,0:T(8,128)(2,1)S(1)}, bf16[448,512]{1,0:T(8,128)(2,1)S(1)}, u32[]{:S(2)}, u32[]{:S(2)}) collective-permute-start(bf16[448,512]{1,0:T(8,128)(2,1)S(1)} %slice.16), channel_id=1, source_target_pairs={{0,16},{8,24},{16,0},{24,8},{32,48},{40,56},{48,32},{56,40},{64,80... | collective-permute-start | bytes 1376264 | tf_op jit(solution)/shard_map/ppermute | solution.py:38
  45.6 1.6 %collective-permute-start.14 = (bf16[224,512]{1,0:T(8,128)(2,1)S(1)}, bf16[224,512]{1,0:T(8,128)(2,1)S(1)}, u32[]{:S(2)}, u32[]{:S(2)}) collective-permute-start(bf16[224,512]{1,0:T(8,128)(2,1)S(1)} %get-tuple-element.149), channel_id=1, source_target_pairs={{0,8},{8,0},{16,24},{24,16},{32,40},{40,32},{48,56},{56,48},{64,72... | collective-permute-start | bytes 688136 | tf_op jit(solution)/shard_map/ppermute | solution.py:42
  45.7 1.8 %collective-permute-start.15 = (bf16[224,512]{1,0:T(8,128)(2,1)S(1)}, bf16[224,512]{1,0:T(8,128)(2,1)S(1)}, u32[]{:S(2)}, u32[]{:S(2)}) collective-permute-start(bf16[224,512]{1,0:T(8,128)(2,1)S(1)} %get-tuple-element.148), channel_id=1, source_target_pairs={{0,8},{8,0},{16,24},{24,16},{32,40},{40,32},{48,56},{56,48},{64,72... | collective-permute-start | bytes 688136 | tf_op jit(solution)/shard_map/ppermute | solution.py:42
  46.2 11.4 %collective-permute-start.10 = (bf16[80,896]{1,0:T(8,128)(2,1)S(1)}, bf16[80,896]{1,0:T(8,128)(2,1)S(1)}, u32[]{:S(2)}, u32[]{:S(2)}) collective-permute-start(bf16[80,896]{1,0:T(8,128)(2,1)S(1)} %get-tuple-element.101), channel_id=1, source_target_pairs={{0,32},{8,40},{16,48},{24,56},{32,0},{40,8},{48,16},{56,24},{64,96... | collective-permute-start | bytes 430088 | tf_op jit(solution)/shard_map/ppermute | solution.py:46
  54.1 4.6 %collective-permute-start.17 = (bf16[448,512]{1,0:T(8,128)(2,1)S(1)}, bf16[448,512]{1,0:T(8,128)(2,1)S(1)}, u32[]{:S(2)}, u32[]{:S(2)}) collective-permute-start(bf16[448,512]{1,0:T(8,128)(2,1)S(1)} %collective-permute-done.12.refs_4_), channel_id=1, source_target_pairs={{0,8},{8,0},{16,24},{24,16},{32,40},{40,32},{48,56},{56,48},{64,72... | collective-permute-start | bytes 1376264 | tf_op jit(solution)/shard_map/ppermute | solution.py:42
  54.3 4.4 %collective-permute-start.18 = (bf16[448,512]{1,0:T(8,128)(2,1)S(1)}, bf16[448,512]{1,0:T(8,128)(2,1)S(1)}, u32[]{:S(2)}, u32[]{:S(2)}) collective-permute-start(bf16[448,512]{1,0:T(8,128)(2,1)S(1)} %collective-permute-done.13.refs_6_), channel_id=1, source_target_pairs={{0,8},{8,0},{16,24},{24,16},{32,40},{40,32},{48,56},{56,48},{64,72... | collective-permute-start | bytes 1376264 | tf_op jit(solution)/shard_map/ppermute | solution.py:42
  57.5 12.9 %collective-permute-start.11 = (bf16[448,512]{1,0:T(8,128)(2,1)S(1)}, bf16[448,512]{1,0:T(8,128)(2,1)S(1)}, u32[]{:S(2)}, u32[]{:S(2)}) collective-permute-start(bf16[448,512]{1,0:T(8,128)(2,1)S(1)} %slice.17), channel_id=1, source_target_pairs={{0,16},{8,24},{16,0},{24,8},{32,48},{40,56},{48,32},{56,40},{64,80... | collective-permute-start | bytes 1376264 | tf_op jit(solution)/shard_map/ppermute | solution.py:38
  58.2 5.9 %collective-permute-start.16 = (bf16[80,896]{1,0:T(8,128)(2,1)S(1)}, bf16[80,896]{1,0:T(8,128)(2,1)S(1)}, u32[]{:S(2)}, u32[]{:S(2)}) collective-permute-start(bf16[80,896]{1,0:T(8,128)(2,1)S(1)} %get-tuple-element.114), channel_id=1, source_target_pairs={{0,64},{8,72},{16,80},{24,88},{32,96},{40,104},{48,112},{56,120},{... | collective-permute-start | bytes 430088 | tf_op jit(solution)/shard_map/ppermute | solution.py:46
  58.7 6.8 %copy-start.2 = (bf16[512,896]{1,0:T(8,128)(2,1)S(1)}, bf16[512,896]{1,0:T(8,128)(2,1)}, u32[]{:S(2)}) copy-start(bf16[512,896]{1,0:T(8,128)(2,1)} %gate_ref.1) | copy-start | bytes 2752516
  66.8 3.7 %collective-permute-start.19 = (f32[1,512]{1,0:T(1,128)S(1)}, f32[1,512]{1,0:T(1,128)S(1)}, u32[]{:S(2)}, u32[]{:S(2)}) collective-permute-start(f32[1,512]{1,0:T(1,128)S(1)} %get-tuple-element.128), channel_id=1, source_target_pairs={{0,1},{1,0},{2,3},{3,2},{4,5},{5,4},{6,7},{7,6},{8,9},{9,8},{10,11... | collective-permute-start | bytes 6152 | tf_op jit(solution)/shard_map/ppermute | solution.py:50
  70.5 1.9 %collective-permute-start.20 = (bf16[448,512]{1,0:T(8,128)(2,1)S(1)}, bf16[448,512]{1,0:T(8,128)(2,1)S(1)}, u32[]{:S(2)}, u32[]{:S(2)}) collective-permute-start(bf16[448,512]{1,0:T(8,128)(2,1)S(1)} %collective-permute-done.11.refs_4_), channel_id=1, source_target_pairs={{0,8},{8,0},{16,24},{24,16},{32,40},{40,32},{48,56},{56,48},{64,72... | collective-permute-start | bytes 1376264 | tf_op jit(solution)/shard_map/ppermute | solution.py:42
  72.4 20.6 %copy-start.10 = (f32[896]{0:T(1024)S(1)}, f32[896]{0:T(1024)}, u32[]{:S(2)}) copy-start(f32[896]{0:T(1024)} %param.21) | copy-start | bytes 10756
  74.5 18.5 %collective-permute-start.21 = (bf16[224,512]{1,0:T(8,128)(2,1)S(1)}, bf16[224,512]{1,0:T(8,128)(2,1)S(1)}, u32[]{:S(2)}, u32[]{:S(2)}) collective-permute-start(bf16[224,512]{1,0:T(8,128)(2,1)S(1)} %get-tuple-element.138), channel_id=1, source_target_pairs={{0,48},{8,56},{16,32},{24,40},{32,16},{40,24},{48,0},{56,8},{64,11... | collective-permute-start | bytes 688136 | tf_op jit(solution)/shard_map/ppermute | solution.py:34
  76.1 16.9 %collective-permute-start.22 = (bf16[224,512]{1,0:T(8,128)(2,1)S(1)}, bf16[224,512]{1,0:T(8,128)(2,1)S(1)}, u32[]{:S(2)}, u32[]{:S(2)}) collective-permute-start(bf16[224,512]{1,0:T(8,128)(2,1)S(1)} %get-tuple-element.139), channel_id=1, source_target_pairs={{0,64},{8,72},{16,80},{24,88},{32,96},{40,104},{48,112},{56,120},{... | collective-permute-start | bytes 688136 | tf_op jit(solution)/shard_map/ppermute | solution.py:34
  79.8 13.2 %collective-permute-start.23 = (bf16[224,512]{1,0:T(8,128)(2,1)S(1)}, bf16[224,512]{1,0:T(8,128)(2,1)S(1)}, u32[]{:S(2)}, u32[]{:S(2)}) collective-permute-start(bf16[224,512]{1,0:T(8,128)(2,1)S(1)} %get-tuple-element.140), channel_id=1, source_target_pairs={{0,112},{8,120},{16,96},{24,104},{32,80},{40,88},{48,64},{56,72},{... | collective-permute-start | bytes 688136 | tf_op jit(solution)/shard_map/ppermute | solution.py:34
  80.9 5.4 %collective-permute-start.24 = (f32[1,512]{1,0:T(1,128)S(1)}, f32[1,512]{1,0:T(1,128)S(1)}, u32[]{:S(2)}, u32[]{:S(2)}) collective-permute-start(f32[1,512]{1,0:T(1,128)S(1)} %add.24), channel_id=1, source_target_pairs={{0,2},{1,3},{2,0},{3,1},{4,6},{5,7},{6,4},{7,5},{8,10},{9,11},{10,... | collective-permute-start | bytes 6152 | tf_op jit(solution)/shard_map/ppermute | solution.py:50
  86.4 6.6 %collective-permute-start.25 = (f32[1,512]{1,0:T(1,128)S(1)}, f32[1,512]{1,0:T(1,128)S(1)}, u32[]{:S(2)}, u32[]{:S(2)}) collective-permute-start(f32[1,512]{1,0:T(1,128)S(1)} %add.25), channel_id=1, source_target_pairs={{0,4},{1,5},{2,6},{3,7},{4,0},{5,1},{6,2},{7,3},{8,12},{9,13},{10,... | collective-permute-start | bytes 6152 | tf_op jit(solution)/shard_map/ppermute | solution.py:50

commit v8 on v7

--- a/solution.py
+++ b/solution.py
@@ -506,13 +506,14 @@
     got, mark = tie((got, mark))
     total, before, sent = ssm_merge(3, info, got, total, before)
     gated, squares = ssm_carry(before, mixed, cum, read_t, ssm_gate)
-    squares = squares + step_swap(squares, 1)
     near[3], gated, squares, mark = tie((near[3], gated, squares, mark))
     near_core[3] = core_swap(near[3])
+    squares = squares + step_swap(squares, 4)
+    near_core[3], squares = tie((near_core[3], squares))
     *results, mark = attend(3, info, *queries, near[3], near_core[3], mark, *state)
     back = [results[0]] + [head_swap(results[r], r) for r in range(1, 4)]
     squares, mark = tie((squares, mark))
-    for step in (2, 4):
+    for step in (1, 2):
         squares = squares + step_swap(squares, step)
     *back, squares = tie((*back, squares))
     factor = lax.rsqrt(squares.reshape(TOK) / SSM_WIDTH + 1e-05)

time: 97 us -> 94.7 us (0.976)
  starting transfers between devices: 29.9 us -> 28.6 us
    ppermute x5, waiting for transfers between devices: 2.73 us -> 5.14 us  [class_swap(): return lax.ppermute(value, 'ctx', [(i, i ^ 2) for i in range(CTX)])]
    ppermute x10, waiting for transfers between devices: 3.79 us -> 1.99 us  [core_swap(): return lax.ppermute(value, 'ctx', [(i, i ^ 1) for i in range(CTX)])]
    ppermute x3, waiting for transfers between devices: 6.91 us -> 5.41 us  [step_swap(): return lax.ppermute(value, 'tp', [(i, i ^ step) for i in range(8)])]
    ppermute x6, starting transfers between devices: 12.7 us -> 11.6 us  [head_swap(): lax.ppermute(value, 'ctx', [(i, exchanged(i, r)) for i in range(CTX)])]
  transfers between devices with their start and end apart: 26 -> 26, of which waited for: 13 -> 14; matrix products, arithmetic and copies ran while one was open for 0% -> 0% of each run, Pallas kernels for 30% -> 30%
where the time goes in v8:
time: 94.7 us; the launch traced here: 94.5 us
  Pallas kernels  37.1 us (39%)
  starting transfers between devices  28.6 us (30%)
  waiting for transfers between devices  25.9 us (27%)
  other arithmetic  1.75 us (2%)
  between operations  0.98 us (1%)
    pallas_call x4, Pallas kernels, attend(): pl.pallas_call(functools.partial(attend_kernel, stage), out_shape=out, in...  22.6 us
    ppermute x6, starting transfers between devices, head_swap(): lax.ppermute(value, 'ctx', [(i, exchanged(i, r)) for i in range(CTX)])  11.6 us
    ppermute x6, waiting for transfers between devices, head_swap(): lax.ppermute(value, 'ctx', [(i, exchanged(i, r)) for i in range(CTX)])  10.5 us
    ppermute x3, starting transfers between devices, step_swap(): return lax.ppermute(value, 'tp', [(i, i ^ step) for i in range(8)])  8.7 us
    ppermute x3, waiting for transfers between devices, step_swap(): return lax.ppermute(value, 'tp', [(i, i ^ step) for i in range(8)])  5.41 us
    ppermute x5, starting transfers between devices, class_swap(): return lax.ppermute(value, 'ctx', [(i, i ^ 2) for i in range(CTX)])  5.26 us
    ppermute x5, waiting for transfers between devices, class_swap(): return lax.ppermute(value, 'ctx', [(i, i ^ 2) for i in range(CTX)])  5.14 us
    pallas_call x1, Pallas kernels, pack(): pl.pallas_call(pack_kernel, out_shape=[shape((count, TOK), BF16) for coun...  4.42 us
  transfers between devices with their start and end apart: 26, of which 14 were waited for; matrix products, arithmetic and copies ran while one was open for 0% of the time, Pallas kernels for 30%

profile of v8, /device:TPU:0, one launch (start us, length us, event | category | flops | bytes accessed | tf_op | source)
XLA Modules:
  0.0 94.5 jit_solution(349954170032208389)
XLA Ops:
  0.7 0.6 pad_add_fusion.info
  1.3 4.4 %shard_map.122 = (bf16[224,512]{1,0:T(8,128)(2,1)}, bf16[448,512]{1,0:T(8,128)(2,1)}, bf16[672,512]{1,0:T(8,128)(2,1)}, bf16[672,512]{1,0:T(8,128)(2,1)}, bf16[672,512]{1,0:T(8,128)(2,1)}) custom-call(s32[4]{0:T(128)} %pad_add_fusion.info, bf16[512,896]{1,0:T(8,128)(2,1)} %q_in.1, bf16[512,896]{1,0:T(8,128)(2,1)} %k_in.1, bf16[512,896]{1,0:T(8,128)(2,1)} %v_in.1), custom_call_target="tpu_custom_call" | custom-call | tf_op jit(solution)/shard_map/pallas_call | solution.py:347
  5.7 0.1 collective-permute-start.3
  5.8 1.7 %collective-permute-start.2 = (bf16[448,512]{1,0:T(8,128)(2,1)}, bf16[448,512]{1,0:T(8,128)(2,1)S(1)}, u32[]{:S(2)}, u32[]{:S(2)}) collective-permute-start(bf16[448,512]{1,0:T(8,128)(2,1)} %get-tuple-element.79.refs_3_), channel_id=1, source_target_pairs={{0,16},{8,24},{16,0},{24,8},{32,48},{40,56},{48,32},{56,40},{64,80... | collective-permute-start | bytes 1376264 | tf_op jit(solution)/shard_map/ppermute | solution.py:38
  7.5 2.1 %collective-permute-start = (bf16[672,512]{1,0:T(8,128)(2,1)}, bf16[672,512]{1,0:T(8,128)(2,1)S(1)}, u32[]{:S(2)}, u32[]{:S(2)}) collective-permute-start(bf16[672,512]{1,0:T(8,128)(2,1)} %get-tuple-element.77), channel_id=1, source_target_pairs={{0,48},{8,56},{16,32},{24,40},{32,16},{40,24},{48,0},{56,8},{64,11... | collective-permute-start | bytes 2064392 | tf_op jit(solution)/shard_map/ppermute | solution.py:34
  9.6 1.6 %collective-permute-start.1 = (bf16[672,512]{1,0:T(8,128)(2,1)}, bf16[672,512]{1,0:T(8,128)(2,1)S(1)}, u32[]{:S(2)}, u32[]{:S(2)}) collective-permute-start(bf16[672,512]{1,0:T(8,128)(2,1)} %get-tuple-element.78), channel_id=1, source_target_pairs={{0,64},{8,72},{16,80},{24,88},{32,96},{40,104},{48,112},{56,120},{... | collective-permute-start | bytes 2064392 | tf_op jit(solution)/shard_map/ppermute | solution.py:34
  11.1 0.0 collective-permute-done.3.refs_4_
  11.2 3.6 %shard_map.123 = (f32[512,896]{1,0:T(8,128)S(1)}, f32[72,896]{1,0:T(8,128)S(1)}, bf16[80,896]{1,0:T(8,128)(2,1)S(1)}, f32[512,14]{1,0:T(8,128)S(1)}) custom-call(bf16[512,896]{1,0:T(8,128)(2,1)S(1)} %copy-done.1, bf16[64,512]{1,0:T(8,128)(2,1)S(1)} %bitcast.12, bf16[64,512]{1,0:T(8,128)(2,1)S(1)} %bitcast.10, f32[14,512]{1,0:T(8,128)S(1)} %bitcast.13, ...), custom_call_target="tpu_custom_call" | custom-call | flops 1000 | bytes 1000 | tf_op jit(solution)/shard_map/pallas_call | solution.py:403
  14.9 0.1 collective-permute-start.4
  15.0 1.4 %collective-permute-done.4.got_ref = bf16[80,896]{1,0:T(8,128)(2,1)S(1)} collective-permute-done((bf16[80,896]{1,0:T(8,128)(2,1)S(1)}, bf16[80,896]{1,0:T(8,128)(2,1)S(1)}, u32[]{:S(2)}, u32[]{:S(2)}) %collective-permute-start.4) | collective-permute-done | bytes 143392 | tf_op jit(solution)/shard_map/ppermute | solution.py:42
  16.3 0.7 shard_map.124
  17.0 1.9 %collective-permute-done.2.refs_7_ = bf16[448,512]{1,0:T(8,128)(2,1)S(1)} collective-permute-done((bf16[448,512]{1,0:T(8,128)(2,1)}, bf16[448,512]{1,0:T(8,128)(2,1)S(1)}, u32[]{:S(2)}, u32[]{:S(2)}) %collective-permute-start.2) | collective-permute-done | bytes 458784 | tf_op jit(solution)/shard_map/ppermute | solution.py:38
  19.0 0.0 collective-permute-start.5
  19.0 1.6 %collective-permute-start.6 = (bf16[80,896]{1,0:T(8,128)(2,1)S(1)}, bf16[80,896]{1,0:T(8,128)(2,1)S(1)}, u32[]{:S(2)}, u32[]{:S(2)}) collective-permute-start(bf16[80,896]{1,0:T(8,128)(2,1)S(1)} %get-tuple-element.83), channel_id=1, source_target_pairs={{0,16},{8,24},{16,0},{24,8},{32,48},{40,56},{48,32},{56,40},{64,80... | collective-permute-start | bytes 430088 | tf_op jit(solution)/shard_map/ppermute | solution.py:38
  20.5 5.8 %collective-permute-done.refs_1_ = bf16[672,512]{1,0:T(8,128)(2,1)S(1)} collective-permute-done((bf16[672,512]{1,0:T(8,128)(2,1)}, bf16[672,512]{1,0:T(8,128)(2,1)S(1)}, u32[]{:S(2)}, u32[]{:S(2)}) %collective-permute-start) | collective-permute-done | bytes 688160 | tf_op jit(solution)/shard_map/ppermute | solution.py:34
  26.4 0.6 collective-permute-done.1.refs_2_
  27.0 0.0 collective-permute-done.6.got_ref
  27.0 0.0 collective-permute-done.5.refs_8_
  27.0 2.6 %collective-permute-start.7 = (bf16[672,512]{1,0:T(8,128)(2,1)S(1)}, bf16[672,512]{1,0:T(8,128)(2,1)S(1)}, u32[]{:S(2)}, u32[]{:S(2)}) collective-permute-start(bf16[672,512]{1,0:T(8,128)(2,1)S(1)} %copy-done.11), channel_id=1, source_target_pairs={{0,112},{8,120},{16,96},{24,104},{32,80},{40,88},{48,64},{56,72},{... | collective-permute-start | bytes 2064392 | tf_op jit(solution)/shard_map/ppermute | solution.py:34
  29.6 0.7 shard_map.125
  30.3 0.1 collective-permute-start.8
  30.4 0.5 collective-permute-start.9
  30.9 0.0 collective-permute-start.12
  30.9 2.0 %collective-permute-start.13 = (bf16[448,512]{1,0:T(8,128)(2,1)S(1)}, bf16[448,512]{1,0:T(8,128)(2,1)S(1)}, u32[]{:S(2)}, u32[]{:S(2)}) collective-permute-start(bf16[448,512]{1,0:T(8,128)(2,1)S(1)} %slice.16), channel_id=1, source_target_pairs={{0,16},{8,24},{16,0},{24,8},{32,48},{40,56},{48,32},{56,40},{64,80... | collective-permute-start | bytes 1376264 | tf_op jit(solution)/shard_map/ppermute | solution.py:38
  33.0 0.0 collective-permute-done.8.refs_5_
  33.0 0.0 collective-permute-done.9.refs_6_
  33.0 9.2 %shard_map.126 = (f32[4,224,512]{2,1,0:T(8,128)S(1)}, f32[4,16,512]{2,1,0:T(8,128)S(1)}, bf16[4,1024,224]{2,1,0:T(8,128)(2,1)S(1)}, bf16[4,224,1024]{2,1,0:T(8,128)(2,1)S(1)}, f32[8,128]{1,0:T(8,128)S(1)}) custom-call(s32[4]{0:T(128)S(1)} %copy-done.6, bf16[224,512]{1,0:T(8,128)(2,1)S(1)} %copy-done, bf16[672,512]{1,0:T(8,128)(2,1)S(1)} %collective-permute-done.refs_1_, ...), custom_call_target="tpu_custom_call" | custom-call | flops 1000 | bytes 1000 | tf_op jit(solution)/shard_map/pallas_call | solution.py:377
  42.2 3.4 %collective-permute-done.7.refs_3_ = bf16[672,512]{1,0:T(8,128)(2,1)S(1)} collective-permute-done((bf16[672,512]{1,0:T(8,128)(2,1)S(1)}, bf16[672,512]{1,0:T(8,128)(2,1)S(1)}, u32[]{:S(2)}, u32[]{:S(2)}) %collective-permute-start.7) | collective-permute-done | bytes 688160 | tf_op jit(solution)/shard_map/ppermute | solution.py:34
  45.6 0.1 collective-permute-start.14
  45.7 0.5 collective-permute-start.15
  46.2 0.7 collective-permute-start.10
  46.8 0.3 collective-permute-done.14.refs_4_
  47.1 0.3 collective-permute-done.15.refs_5_
  47.5 5.9 %shard_map.128 = (f32[4,224,512]{2,1,0:T(8,128)S(1)}, f32[4,16,512]{2,1,0:T(8,128)S(1)}, f32[8,128]{1,0:T(8,128)S(1)}) custom-call(s32[4]{0:T(128)S(1)} %copy-done.6, bf16[224,512]{1,0:T(8,128)(2,1)S(1)} %copy-done, bf16[672,512]{1,0:T(8,128)(2,1)S(1)} %collective-permute-done.refs_1_, bf16[672,512]{1,0:T(8,128)(2,1)S(1)} %collective-permute-done.1.refs_2_, ...), custom_call_target="tpu_custom_call" | custom-call | flops 1000 | bytes 1000 | tf_op jit(solution)/shard_map/pallas_call | solution.py:377
  53.3 0.0 collective-permute-done.12.refs_4_
  53.3 0.8 collective-permute-done.13.refs_6_
  54.1 0.2 collective-permute-start.17
  54.3 0.3 collective-permute-start.18
  54.7 2.8 %collective-permute-done.10.got_ref = bf16[80,896]{1,0:T(8,128)(2,1)S(1)} collective-permute-done((bf16[80,896]{1,0:T(8,128)(2,1)S(1)}, bf16[80,896]{1,0:T(8,128)(2,1)S(1)}, u32[]{:S(2)}, u32[]{:S(2)}) %collective-permute-start.10) | collective-permute-done | bytes 143392 | tf_op jit(solution)/shard_map/ppermute | solution.py:46
  57.5 0.0 collective-permute-start.11
  57.5 0.7 shard_map.127
  58.2 0.5 collective-permute-start.16
  58.7 0.0 collective-permute-done.17.refs_5_
  58.7 0.0 collective-permute-done.18.refs_7_
  58.7 5.4 %shard_map.129 = (f32[4,224,512]{2,1,0:T(8,128)S(1)}, f32[4,16,512]{2,1,0:T(8,128)S(1)}, f32[8,128]{1,0:T(8,128)S(1)}) custom-call(s32[4]{0:T(128)S(1)} %copy-done.6, bf16[224,512]{1,0:T(8,128)(2,1)S(1)} %copy-done, bf16[672,512]{1,0:T(8,128)(2,1)S(1)} %collective-permute-done.refs_1_, bf16[672,512]{1,0:T(8,128)(2,1)S(1)} %collective-permute-done.1.refs_2_, ...), custom_call_target="tpu_custom_call" | custom-call | flops 1000 | bytes 1000 | tf_op jit(solution)/shard_map/pallas_call | solution.py:377
  64.1 1.4 %shard_map.130 = (f32[72,896]{1,0:T(8,128)}, f32[72,896]{1,0:T(8,128)S(1)}, bf16[80,896]{1,0:T(8,128)(2,1)}) custom-call(s32[4]{0:T(128)S(1)} %copy-done.6, bf16[80,896]{1,0:T(8,128)(2,1)S(1)} %collective-permute-done.16.got_ref, f32[72,896]{1,0:T(8,128)S(1)} %get-tuple-element.124.total_ref, f32[72,896]{1,0:T(8,128)S(1)} %get-tuple-element.125.before_ref), custom_call_target="tpu_custom_call" | custom-call | flops 1000 | bytes 1000 | tf_op jit(solution)/shard_map/pallas_call | solution.py:420
  65.5 1.3 %shard_map.131 = (f32[512,896]{1,0:T(8,128)S(1)}, f32[1,512]{1,0:T(1,128)S(1)}) custom-call(f32[72,896]{1,0:T(8,128)S(1)} %get-tuple-element.126.state_ref, f32[512,896]{1,0:T(8,128)S(1)} %get-tuple-element.127.mixed_ref, f32[512,14]{1,0:T(8,128)S(1)} %get-tuple-element.128.cum_ref, bf16[64,512]{1,0:T(8,128)(2,1)S(1)} %bitcast.11, bf16[512,896]{1,0:T(8,128)(2,1)S(1)} %copy-done.2), custom_call_target="tpu_custom_call" | custom-call | flops 1000 | bytes 1000 | tf_op jit(solution)/shard_map/pallas_call | solution.py:432
  66.8 2.4 %collective-permute-done.11.refs_4_ = bf16[448,512]{1,0:T(8,128)(2,1)S(1)} collective-permute-done((bf16[448,512]{1,0:T(8,128)(2,1)S(1)}, bf16[448,512]{1,0:T(8,128)(2,1)S(1)}, u32[]{:S(2)}, u32[]{:S(2)}) %collective-permute-start.11) | collective-permute-done | bytes 458784 | tf_op jit(solution)/shard_map/ppermute | solution.py:38
  69.2 2.9 %collective-permute-start.20 = (f32[1,512]{1,0:T(1,128)S(1)}, f32[1,512]{1,0:T(1,128)S(1)}, u32[]{:S(2)}, u32[]{:S(2)}) collective-permute-start(f32[1,512]{1,0:T(1,128)S(1)} %get-tuple-element.133), channel_id=1, source_target_pairs={{0,4},{1,5},{2,6},{3,7},{4,0},{5,1},{6,2},{7,3},{8,12},{9,13},{10,... | collective-permute-start | bytes 6152 | tf_op jit(solution)/shard_map/ppermute | solution.py:50
  72.1 2.2 %collective-permute-done.20 = f32[1,512]{1,0:T(1,128)S(1)} collective-permute-done((f32[1,512]{1,0:T(1,128)S(1)}, f32[1,512]{1,0:T(1,128)S(1)}, u32[]{:S(2)}, u32[]{:S(2)}) %collective-permute-start.20) | collective-permute-done | bytes 2080 | tf_op jit(solution)/shard_map/ppermute | solution.py:50
  74.3 0.0 collective-permute-done.19.refs_5_
  74.3 0.0 copy-start.10
  74.3 2.1 %shard_map.132 = (bf16[224,512]{1,0:T(8,128)(2,1)S(1)}, bf16[224,512]{1,0:T(8,128)(2,1)S(1)}, bf16[224,512]{1,0:T(8,128)(2,1)S(1)}, bf16[224,512]{1,0:T(8,128)(2,1)S(1)}, f32[8,128]{1,0:T(8,128)S(1)}) custom-call(s32[4]{0:T(128)S(1)} %copy-done.6, bf16[224,512]{1,0:T(8,128)(2,1)S(1)} %copy-done, bf16[672,512]{1,0:T(8,128)(2,1)S(1)} %collective-permute-done.refs_1_, ...), custom_call_target="tpu_custom_call" | custom-call | flops 1000 | bytes 1000 | tf_op jit(solution)/shard_map/pallas_call | solution.py:377
  76.4 1.6 %collective-permute-start.21 = (bf16[224,512]{1,0:T(8,128)(2,1)S(1)}, bf16[224,512]{1,0:T(8,128)(2,1)S(1)}, u32[]{:S(2)}, u32[]{:S(2)}) collective-permute-start(bf16[224,512]{1,0:T(8,128)(2,1)S(1)} %get-tuple-element.142), channel_id=1, source_target_pairs={{0,48},{8,56},{16,32},{24,40},{32,16},{40,24},{48,0},{56,8},{64,11... | collective-permute-start | bytes 688136 | tf_op jit(solution)/shard_map/ppermute | solution.py:34
  78.0 2.6 %collective-permute-start.22 = (bf16[224,512]{1,0:T(8,128)(2,1)S(1)}, bf16[224,512]{1,0:T(8,128)(2,1)S(1)}, u32[]{:S(2)}, u32[]{:S(2)}) collective-permute-start(bf16[224,512]{1,0:T(8,128)(2,1)S(1)} %get-tuple-element.143), channel_id=1, source_target_pairs={{0,64},{8,72},{16,80},{24,88},{32,96},{40,104},{48,112},{56,120},{... | collective-permute-start | bytes 688136 | tf_op jit(solution)/shard_map/ppermute | solution.py:34
  80.6 1.2 %collective-permute-start.23 = (bf16[224,512]{1,0:T(8,128)(2,1)S(1)}, bf16[224,512]{1,0:T(8,128)(2,1)S(1)}, u32[]{:S(2)}, u32[]{:S(2)}) collective-permute-start(bf16[224,512]{1,0:T(8,128)(2,1)S(1)} %get-tuple-element.144), channel_id=1, source_target_pairs={{0,112},{8,120},{16,96},{24,104},{32,80},{40,88},{48,64},{56,72},{... | collective-permute-start | bytes 688136 | tf_op jit(solution)/shard_map/ppermute | solution.py:34
  81.8 1.9 %collective-permute-start.24 = (f32[1,512]{1,0:T(1,128)S(1)}, f32[1,512]{1,0:T(1,128)S(1)}, u32[]{:S(2)}, u32[]{:S(2)}) collective-permute-start(f32[1,512]{1,0:T(1,128)S(1)} %add.24), channel_id=1, source_target_pairs={{0,1},{1,0},{2,3},{3,2},{4,5},{5,4},{6,7},{7,6},{8,9},{9,8},{10,11... | collective-permute-start | bytes 6152 | tf_op jit(solution)/shard_map/ppermute | solution.py:50
  83.7 1.7 %collective-permute-done.24 = f32[1,512]{1,0:T(1,128)S(1)} collective-permute-done((f32[1,512]{1,0:T(1,128)S(1)}, f32[1,512]{1,0:T(1,128)S(1)}, u32[]{:S(2)}, u32[]{:S(2)}) %collective-permute-start.24) | collective-permute-done | bytes 2080 | tf_op jit(solution)/shard_map/ppermute | solution.py:50
  85.3 3.9 %collective-permute-start.25 = (f32[1,512]{1,0:T(1,128)S(1)}, f32[1,512]{1,0:T(1,128)S(1)}, u32[]{:S(2)}, u32[]{:S(2)}) collective-permute-start(f32[1,512]{1,0:T(1,128)S(1)} %add.25), channel_id=1, source_target_pairs={{0,2},{1,3},{2,0},{3,1},{4,6},{5,7},{6,4},{7,5},{8,10},{9,11},{10,... | collective-permute-start | bytes 6152 | tf_op jit(solution)/shard_map/ppermute | solution.py:50
  89.2 1.6 %collective-permute-done.25 = f32[1,512]{1,0:T(1,128)S(1)} collective-permute-done((f32[1,512]{1,0:T(1,128)S(1)}, f32[1,512]{1,0:T(1,128)S(1)}, u32[]{:S(2)}, u32[]{:S(2)}) %collective-permute-start.25) | collective-permute-done | bytes 2080 | tf_op jit(solution)/shard_map/ppermute | solution.py:50
  90.8 0.0 collective-permute-done.21.refs_1_
  90.8 0.7 collective-permute-done.23.refs_3_
  91.5 1.1 %multiply_convert_fusion = bf16[512,896]{1,0:T(8,128)(2,1)} fusion(f32[512,896]{1,0:T(8,128)S(1)} %get-tuple-element.150, f32[896]{0:T(1024)S(1)} %copy-done.10, f32[512]{0:T(512)S(1)} %bitcast.16), kind=kLoop, calls=%fused_computation | loop fusion | flops 1376256 | bytes 2758144 | tf_op jit(solution)/shard_map/convert_element_type | solution.py:520
  92.7 1.8 %shard_map.133 = bf16[512,896]{1,0:T(8,128)(2,1)} custom-call(s32[4]{0:T(128)S(1)} %copy-done.6, f32[8,128]{1,0:T(8,128)S(1)} %get-tuple-element.140._, bf16[224,512]{1,0:T(8,128)(2,1)S(1)} %get-tuple-element.146.refs_0_, bf16[224,512]{1,0:T(8,128)(2,1)S(1)} %collective-permute-done.21.refs_1_, bf16[224,512]{1,0:T(8,128)(2,1)S(1)} %collective-permute-done.22.refs_2_, ...), custom_call_target="tpu_custom_call" | custom-call | tf_op jit(solution)/shard_map/pallas_call | solution.py:390
  (35 shorter events, 0.2 us)
Async XLA Ops:
  0.6 10.5 %copy-start.1 = (bf16[512,896]{1,0:T(8,128)(2,1)S(1)}, bf16[512,896]{1,0:T(8,128)(2,1)}, u32[]{:S(2)}) copy-start(bf16[512,896]{1,0:T(8,128)(2,1)} %x_ref) | copy-start | bytes 2752516
  0.6 10.5 %copy-start.4 = (bf16[512,64]{0,1:T(8,128)(2,1)S(1)}, bf16[512,64]{0,1:T(8,128)(2,1)}, u32[]{:S(2)}) copy-start(bf16[512,64]{0,1:T(8,128)(2,1)} %param.17) | copy-start | bytes 196612
  0.7 10.5 %copy-start.5 = (bf16[512,64]{0,1:T(8,128)(2,1)S(1)}, bf16[512,64]{0,1:T(8,128)(2,1)}, u32[]{:S(2)}) copy-start(bf16[512,64]{0,1:T(8,128)(2,1)} %param.16) | copy-start | bytes 196612
  0.7 10.5 %copy-start.7 = (f32[512,14]{0,1:T(8,128)S(1)}, f32[512,14]{0,1:T(8,128)}, u32[]{:S(2)}) copy-start(f32[512,14]{0,1:T(8,128)} %param.18) | copy-start | bytes 86020
  0.7 10.5 %copy-start.8 = (f32[14]{0:T(128)S(1)}, f32[14]{0:T(128)}, u32[]{:S(2)}) copy-start(f32[14]{0:T(128)} %param.19) | copy-start | bytes 172
  0.7 10.5 %copy-start.9 = (f32[14]{0:T(128)S(1)}, f32[14]{0:T(128)}, u32[]{:S(2)}) copy-start(f32[14]{0:T(128)} %param.20) | copy-start | bytes 172
  1.3 15.1 %copy-start.6 = (s32[4]{0:T(128)S(1)}, s32[4]{0:T(128)}, u32[]{:S(2)}) copy-start(s32[4]{0:T(128)} %pad_add_fusion.info) | copy-start | bytes 52
  5.7 21.3 %copy-start.11 = (bf16[672,512]{1,0:T(8,128)(2,1)S(1)}, bf16[672,512]{1,0:T(8,128)(2,1)}, u32[]{:S(2)}) copy-start(bf16[672,512]{1,0:T(8,128)(2,1)} %get-tuple-element.86) | copy-start | bytes 2064388
  5.7 5.4 %collective-permute-start.3 = (bf16[448,512]{1,0:T(8,128)(2,1)}, bf16[448,512]{1,0:T(8,128)(2,1)S(1)}, u32[]{:S(2)}, u32[]{:S(2)}) collective-permute-start(bf16[448,512]{1,0:T(8,128)(2,1)} %get-tuple-element.79.refs_3_), channel_id=1, source_target_pairs={{0,8},{8,0},{16,24},{24,16},{32,40},{40,32},{48,56},{56,48},{64,72... | collective-permute-start | bytes 1376264 | tf_op jit(solution)/shard_map/ppermute | solution.py:42
  5.8 13.1 %collective-permute-start.2 = (bf16[448,512]{1,0:T(8,128)(2,1)}, bf16[448,512]{1,0:T(8,128)(2,1)S(1)}, u32[]{:S(2)}, u32[]{:S(2)}) collective-permute-start(bf16[448,512]{1,0:T(8,128)(2,1)} %get-tuple-element.79.refs_3_), channel_id=1, source_target_pairs={{0,16},{8,24},{16,0},{24,8},{32,48},{40,56},{48,32},{56,40},{64,80... | collective-permute-start | bytes 1376264 | tf_op jit(solution)/shard_map/ppermute | solution.py:38
  7.5 18.9 %collective-permute-start = (bf16[672,512]{1,0:T(8,128)(2,1)}, bf16[672,512]{1,0:T(8,128)(2,1)S(1)}, u32[]{:S(2)}, u32[]{:S(2)}) collective-permute-start(bf16[672,512]{1,0:T(8,128)(2,1)} %get-tuple-element.77), channel_id=1, source_target_pairs={{0,48},{8,56},{16,32},{24,40},{32,16},{40,24},{48,0},{56,8},{64,11... | collective-permute-start | bytes 2064392 | tf_op jit(solution)/shard_map/ppermute | solution.py:34
  9.6 17.4 %collective-permute-start.1 = (bf16[672,512]{1,0:T(8,128)(2,1)}, bf16[672,512]{1,0:T(8,128)(2,1)S(1)}, u32[]{:S(2)}, u32[]{:S(2)}) collective-permute-start(bf16[672,512]{1,0:T(8,128)(2,1)} %get-tuple-element.78), channel_id=1, source_target_pairs={{0,64},{8,72},{16,80},{24,88},{32,96},{40,104},{48,112},{56,120},{... | collective-permute-start | bytes 2064392 | tf_op jit(solution)/shard_map/ppermute | solution.py:34
  14.8 18.1 %copy-start = (bf16[224,512]{1,0:T(8,128)(2,1)S(1)}, bf16[224,512]{1,0:T(8,128)(2,1)}, u32[]{:S(2)}) copy-start(bf16[224,512]{1,0:T(8,128)(2,1)} %get-tuple-element.87.refs_0_) | copy-start | bytes 688132
  14.9 18.1 %copy-start.3 = (bf16[448,512]{1,0:T(8,128)(2,1)S(1)}, bf16[448,512]{1,0:T(8,128)(2,1)}, u32[]{:S(2)}) copy-start(bf16[448,512]{1,0:T(8,128)(2,1)} %get-tuple-element.79.refs_3_) | copy-start | bytes 1376260
  14.9 1.4 %collective-permute-start.4 = (bf16[80,896]{1,0:T(8,128)(2,1)S(1)}, bf16[80,896]{1,0:T(8,128)(2,1)S(1)}, u32[]{:S(2)}, u32[]{:S(2)}) collective-permute-start(bf16[80,896]{1,0:T(8,128)(2,1)S(1)} %get-tuple-element.81), channel_id=1, source_target_pairs={{0,8},{8,0},{16,24},{24,16},{32,40},{40,32},{48,56},{56,48},{64,72... | collective-permute-start | bytes 430088 | tf_op jit(solution)/shard_map/ppermute | solution.py:42
  19.0 8.0 %collective-permute-start.5 = (bf16[448,512]{1,0:T(8,128)(2,1)S(1)}, bf16[448,512]{1,0:T(8,128)(2,1)S(1)}, u32[]{:S(2)}, u32[]{:S(2)}) collective-permute-start(bf16[448,512]{1,0:T(8,128)(2,1)S(1)} %collective-permute-done.2.refs_7_), channel_id=1, source_target_pairs={{0,8},{8,0},{16,24},{24,16},{32,40},{40,32},{48,56},{56,48},{64,72... | collective-permute-start | bytes 1376264 | tf_op jit(solution)/shard_map/ppermute | solution.py:42
  19.0 8.0 %collective-permute-start.6 = (bf16[80,896]{1,0:T(8,128)(2,1)S(1)}, bf16[80,896]{1,0:T(8,128)(2,1)S(1)}, u32[]{:S(2)}, u32[]{:S(2)}) collective-permute-start(bf16[80,896]{1,0:T(8,128)(2,1)S(1)} %get-tuple-element.83), channel_id=1, source_target_pairs={{0,16},{8,24},{16,0},{24,8},{32,48},{40,56},{48,32},{56,40},{64,80... | collective-permute-start | bytes 430088 | tf_op jit(solution)/shard_map/ppermute | solution.py:38
  27.0 18.5 %collective-permute-start.7 = (bf16[672,512]{1,0:T(8,128)(2,1)S(1)}, bf16[672,512]{1,0:T(8,128)(2,1)S(1)}, u32[]{:S(2)}, u32[]{:S(2)}) collective-permute-start(bf16[672,512]{1,0:T(8,128)(2,1)S(1)} %copy-done.11), channel_id=1, source_target_pairs={{0,112},{8,120},{16,96},{24,104},{32,80},{40,88},{48,64},{56,72},{... | collective-permute-start | bytes 2064392 | tf_op jit(solution)/shard_map/ppermute | solution.py:34
  30.3 2.6 %collective-permute-start.8 = (bf16[448,512]{1,0:T(8,128)(2,1)S(1)}, bf16[448,512]{1,0:T(8,128)(2,1)S(1)}, u32[]{:S(2)}, u32[]{:S(2)}) collective-permute-start(bf16[448,512]{1,0:T(8,128)(2,1)S(1)} %slice.15), channel_id=1, source_target_pairs={{0,8},{8,0},{16,24},{24,16},{32,40},{40,32},{48,56},{56,48},{64,72... | collective-permute-start | bytes 1376264 | tf_op jit(solution)/shard_map/ppermute | solution.py:42
  30.4 2.5 %collective-permute-start.9 = (bf16[448,512]{1,0:T(8,128)(2,1)S(1)}, bf16[448,512]{1,0:T(8,128)(2,1)S(1)}, u32[]{:S(2)}, u32[]{:S(2)}) collective-permute-start(bf16[448,512]{1,0:T(8,128)(2,1)S(1)} %slice.16), channel_id=1, source_target_pairs={{0,8},{8,0},{16,24},{24,16},{32,40},{40,32},{48,56},{56,48},{64,72... | collective-permute-start | bytes 1376264 | tf_op jit(solution)/shard_map/ppermute | solution.py:42
  30.9 22.4 %collective-permute-start.12 = (bf16[448,512]{1,0:T(8,128)(2,1)S(1)}, bf16[448,512]{1,0:T(8,128)(2,1)S(1)}, u32[]{:S(2)}, u32[]{:S(2)}) collective-permute-start(bf16[448,512]{1,0:T(8,128)(2,1)S(1)} %slice.15), channel_id=1, source_target_pairs={{0,16},{8,24},{16,0},{24,8},{32,48},{40,56},{48,32},{56,40},{64,80... | collective-permute-start | bytes 1376264 | tf_op jit(solution)/shard_map/ppermute | solution.py:38
  30.9 23.2 %collective-permute-start.13 = (bf16[448,512]{1,0:T(8,128)(2,1)S(1)}, bf16[448,512]{1,0:T(8,128)(2,1)S(1)}, u32[]{:S(2)}, u32[]{:S(2)}) collective-permute-start(bf16[448,512]{1,0:T(8,128)(2,1)S(1)} %slice.16), channel_id=1, source_target_pairs={{0,16},{8,24},{16,0},{24,8},{32,48},{40,56},{48,32},{56,40},{64,80... | collective-permute-start | bytes 1376264 | tf_op jit(solution)/shard_map/ppermute | solution.py:38
  45.6 1.6 %collective-permute-start.14 = (bf16[224,512]{1,0:T(8,128)(2,1)S(1)}, bf16[224,512]{1,0:T(8,128)(2,1)S(1)}, u32[]{:S(2)}, u32[]{:S(2)}) collective-permute-start(bf16[224,512]{1,0:T(8,128)(2,1)S(1)} %get-tuple-element.153), channel_id=1, source_target_pairs={{0,8},{8,0},{16,24},{24,16},{32,40},{40,32},{48,56},{56,48},{64,72... | collective-permute-start | bytes 688136 | tf_op jit(solution)/shard_map/ppermute | solution.py:42
  45.7 1.8 %collective-permute-start.15 = (bf16[224,512]{1,0:T(8,128)(2,1)S(1)}, bf16[224,512]{1,0:T(8,128)(2,1)S(1)}, u32[]{:S(2)}, u32[]{:S(2)}) collective-permute-start(bf16[224,512]{1,0:T(8,128)(2,1)S(1)} %get-tuple-element.152), channel_id=1, source_target_pairs={{0,8},{8,0},{16,24},{24,16},{32,40},{40,32},{48,56},{56,48},{64,72... | collective-permute-start | bytes 688136 | tf_op jit(solution)/shard_map/ppermute | solution.py:42
  46.2 11.4 %collective-permute-start.10 = (bf16[80,896]{1,0:T(8,128)(2,1)S(1)}, bf16[80,896]{1,0:T(8,128)(2,1)S(1)}, u32[]{:S(2)}, u32[]{:S(2)}) collective-permute-start(bf16[80,896]{1,0:T(8,128)(2,1)S(1)} %get-tuple-element.103), channel_id=1, source_target_pairs={{0,32},{8,40},{16,48},{24,56},{32,0},{40,8},{48,16},{56,24},{64,96... | collective-permute-start | bytes 430088 | tf_op jit(solution)/shard_map/ppermute | solution.py:46
  54.1 4.6 %collective-permute-start.17 = (bf16[448,512]{1,0:T(8,128)(2,1)S(1)}, bf16[448,512]{1,0:T(8,128)(2,1)S(1)}, u32[]{:S(2)}, u32[]{:S(2)}) collective-permute-start(bf16[448,512]{1,0:T(8,128)(2,1)S(1)} %collective-permute-done.12.refs_4_), channel_id=1, source_target_pairs={{0,8},{8,0},{16,24},{24,16},{32,40},{40,32},{48,56},{56,48},{64,72... | collective-permute-start | bytes 1376264 | tf_op jit(solution)/shard_map/ppermute | solution.py:42
  54.3 4.4 %collective-permute-start.18 = (bf16[448,512]{1,0:T(8,128)(2,1)S(1)}, bf16[448,512]{1,0:T(8,128)(2,1)S(1)}, u32[]{:S(2)}, u32[]{:S(2)}) collective-permute-start(bf16[448,512]{1,0:T(8,128)(2,1)S(1)} %collective-permute-done.13.refs_6_), channel_id=1, source_target_pairs={{0,8},{8,0},{16,24},{24,16},{32,40},{40,32},{48,56},{56,48},{64,72... | collective-permute-start | bytes 1376264 | tf_op jit(solution)/shard_map/ppermute | solution.py:42
  57.5 11.7 %collective-permute-start.11 = (bf16[448,512]{1,0:T(8,128)(2,1)S(1)}, bf16[448,512]{1,0:T(8,128)(2,1)S(1)}, u32[]{:S(2)}, u32[]{:S(2)}) collective-permute-start(bf16[448,512]{1,0:T(8,128)(2,1)S(1)} %slice.17), channel_id=1, source_target_pairs={{0,16},{8,24},{16,0},{24,8},{32,48},{40,56},{48,32},{56,40},{64,80... | collective-permute-start | bytes 1376264 | tf_op jit(solution)/shard_map/ppermute | solution.py:38
  58.2 5.9 %collective-permute-start.16 = (bf16[80,896]{1,0:T(8,128)(2,1)S(1)}, bf16[80,896]{1,0:T(8,128)(2,1)S(1)}, u32[]{:S(2)}, u32[]{:S(2)}) collective-permute-start(bf16[80,896]{1,0:T(8,128)(2,1)S(1)} %get-tuple-element.116), channel_id=1, source_target_pairs={{0,64},{8,72},{16,80},{24,88},{32,96},{40,104},{48,112},{56,120},{... | collective-permute-start | bytes 430088 | tf_op jit(solution)/shard_map/ppermute | solution.py:46
  58.7 6.8 %copy-start.2 = (bf16[512,896]{1,0:T(8,128)(2,1)S(1)}, bf16[512,896]{1,0:T(8,128)(2,1)}, u32[]{:S(2)}) copy-start(bf16[512,896]{1,0:T(8,128)(2,1)} %gate_ref.1) | copy-start | bytes 2752516
  69.2 5.1 %collective-permute-start.19 = (bf16[448,512]{1,0:T(8,128)(2,1)S(1)}, bf16[448,512]{1,0:T(8,128)(2,1)S(1)}, u32[]{:S(2)}, u32[]{:S(2)}) collective-permute-start(bf16[448,512]{1,0:T(8,128)(2,1)S(1)} %collective-permute-done.11.refs_4_), channel_id=1, source_target_pairs={{0,8},{8,0},{16,24},{24,16},{32,40},{40,32},{48,56},{56,48},{64,72... | collective-permute-start | bytes 1376264 | tf_op jit(solution)/shard_map/ppermute | solution.py:42
  69.2 5.1 %collective-permute-start.20 = (f32[1,512]{1,0:T(1,128)S(1)}, f32[1,512]{1,0:T(1,128)S(1)}, u32[]{:S(2)}, u32[]{:S(2)}) collective-permute-start(f32[1,512]{1,0:T(1,128)S(1)} %get-tuple-element.133), channel_id=1, source_target_pairs={{0,4},{1,5},{2,6},{3,7},{4,0},{5,1},{6,2},{7,3},{8,12},{9,13},{10,... | collective-permute-start | bytes 6152 | tf_op jit(solution)/shard_map/ppermute | solution.py:50
  74.3 17.2 %copy-start.10 = (f32[896]{0:T(1024)S(1)}, f32[896]{0:T(1024)}, u32[]{:S(2)}) copy-start(f32[896]{0:T(1024)} %param.21) | copy-start | bytes 10756
  76.4 14.4 %collective-permute-start.21 = (bf16[224,512]{1,0:T(8,128)(2,1)S(1)}, bf16[224,512]{1,0:T(8,128)(2,1)S(1)}, u32[]{:S(2)}, u32[]{:S(2)}) collective-permute-start(bf16[224,512]{1,0:T(8,128)(2,1)S(1)} %get-tuple-element.142), channel_id=1, source_target_pairs={{0,48},{8,56},{16,32},{24,40},{32,16},{40,24},{48,0},{56,8},{64,11... | collective-permute-start | bytes 688136 | tf_op jit(solution)/shard_map/ppermute | solution.py:34
  78.0 12.8 %collective-permute-start.22 = (bf16[224,512]{1,0:T(8,128)(2,1)S(1)}, bf16[224,512]{1,0:T(8,128)(2,1)S(1)}, u32[]{:S(2)}, u32[]{:S(2)}) collective-permute-start(bf16[224,512]{1,0:T(8,128)(2,1)S(1)} %get-tuple-element.143), channel_id=1, source_target_pairs={{0,64},{8,72},{16,80},{24,88},{32,96},{40,104},{48,112},{56,120},{... | collective-permute-start | bytes 688136 | tf_op jit(solution)/shard_map/ppermute | solution.py:34
  80.6 10.9 %collective-permute-start.23 = (bf16[224,512]{1,0:T(8,128)(2,1)S(1)}, bf16[224,512]{1,0:T(8,128)(2,1)S(1)}, u32[]{:S(2)}, u32[]{:S(2)}) collective-permute-start(bf16[224,512]{1,0:T(8,128)(2,1)S(1)} %get-tuple-element.144), channel_id=1, source_target_pairs={{0,112},{8,120},{16,96},{24,104},{32,80},{40,88},{48,64},{56,72},{... | collective-permute-start | bytes 688136 | tf_op jit(solution)/shard_map/ppermute | solution.py:34
  81.8 3.6 %collective-permute-start.24 = (f32[1,512]{1,0:T(1,128)S(1)}, f32[1,512]{1,0:T(1,128)S(1)}, u32[]{:S(2)}, u32[]{:S(2)}) collective-permute-start(f32[1,512]{1,0:T(1,128)S(1)} %add.24), channel_id=1, source_target_pairs={{0,1},{1,0},{2,3},{3,2},{4,5},{5,4},{6,7},{7,6},{8,9},{9,8},{10,11... | collective-permute-start | bytes 6152 | tf_op jit(solution)/shard_map/ppermute | solution.py:50
  85.3 5.4 %collective-permute-start.25 = (f32[1,512]{1,0:T(1,128)S(1)}, f32[1,512]{1,0:T(1,128)S(1)}, u32[]{:S(2)}, u32[]{:S(2)}) collective-permute-start(f32[1,512]{1,0:T(1,128)S(1)} %add.25), channel_id=1, source_target_pairs={{0,2},{1,3},{2,0},{3,1},{4,6},{5,7},{6,4},{7,5},{8,10},{9,11},{10,... | collective-permute-start | bytes 6152 | tf_op jit(solution)/shard_map/ppermute | solution.py:50

commit v9 on v8

--- a/solution.py
+++ b/solution.py
@@ -119,7 +119,7 @@
             scores = [
                 jnp.dot(keys, qs[r, :, lanes[half]], preferred_element_type=F32) for half in range(2)
             ]
-            new_stats, low, shrinks = [], [], []
+            new_stats = []
             for half in range(2):
                 (top, total), s = stats[half], scores[half]
                 if masked:
@@ -131,11 +131,8 @@
                 shrink = jnp.exp2((top - new_top) * scale)
                 total = total * shrink + jnp.sum(p, axis=0, keepdims=True)
                 new_stats.append((new_top, total))
-                low.append(p.astype(BF16))
-                shrinks.append(shrink)
-            for half in range(2):
-                acc[r, :, lanes[half]] = acc[r, :, lanes[half]] * shrinks[half] + jnp.dot(
-                    values, low[half], preferred_element_type=F32
+                acc[r, :, lanes[half]] = acc[r, :, lanes[half]] * shrink + jnp.dot(
+                    values, p.astype(BF16), preferred_element_type=F32
                 )
             return tuple(new_stats)
 

time: 94.7 us -> 94.7 us (level)
  no operation moved by 1% of the time
where the time goes in v9:
time: 94.7 us; the launch traced here: 94.5 us
  Pallas kernels  37.1 us (39%)
  starting transfers between devices  28.6 us (30%)
  waiting for transfers between devices  25.9 us (27%)
  other arithmetic  1.75 us (2%)
  between operations  0.98 us (1%)
    pallas_call x4, Pallas kernels, attend(): pl.pallas_call(functools.partial(attend_kernel, stage), out_shape=out, in...  22.6 us
    ppermute x6, starting transfers between devices, head_swap(): lax.ppermute(value, 'ctx', [(i, exchanged(i, r)) for i in range(CTX)])  11.6 us
    ppermute x6, waiting for transfers between devices, head_swap(): lax.ppermute(value, 'ctx', [(i, exchanged(i, r)) for i in range(CTX)])  10.5 us
    ppermute x3, starting transfers between devices, step_swap(): return lax.ppermute(value, 'tp', [(i, i ^ step) for i in range(8)])  8.7 us
    ppermute x3, waiting for transfers between devices, step_swap(): return lax.ppermute(value, 'tp', [(i, i ^ step) for i in range(8)])  5.41 us
    ppermute x5, starting transfers between devices, class_swap(): return lax.ppermute(value, 'ctx', [(i, i ^ 2) for i in range(CTX)])  5.26 us
    ppermute x5, waiting for transfers between devices, class_swap(): return lax.ppermute(value, 'ctx', [(i, i ^ 2) for i in range(CTX)])  5.14 us
    pallas_call x1, Pallas kernels, pack(): pl.pallas_call(pack_kernel, out_shape=[shape((count, TOK), BF16) for coun...  4.42 us
  transfers between devices with their start and end apart: 26, of which 14 were waited for; matrix products, arithmetic and copies ran while one was open for 0% of the time, Pallas kernels for 30%

profile of v9, /device:TPU:0, one launch (start us, length us, event | category | flops | bytes accessed | tf_op | source)
XLA Modules:
  0.0 94.5 jit_solution(349954170032208389)
XLA Ops:
  0.7 0.6 pad_add_fusion.info
  1.3 4.4 %shard_map.122 = (bf16[224,512]{1,0:T(8,128)(2,1)}, bf16[448,512]{1,0:T(8,128)(2,1)}, bf16[672,512]{1,0:T(8,128)(2,1)}, bf16[672,512]{1,0:T(8,128)(2,1)}, bf16[672,512]{1,0:T(8,128)(2,1)}) custom-call(s32[4]{0:T(128)} %pad_add_fusion.info, bf16[512,896]{1,0:T(8,128)(2,1)} %q_in.1, bf16[512,896]{1,0:T(8,128)(2,1)} %k_in.1, bf16[512,896]{1,0:T(8,128)(2,1)} %v_in.1), custom_call_target="tpu_custom_call" | custom-call | tf_op jit(solution)/shard_map/pallas_call | solution.py:344
  5.7 0.1 collective-permute-start.3
  5.8 1.7 %collective-permute-start.2 = (bf16[448,512]{1,0:T(8,128)(2,1)}, bf16[448,512]{1,0:T(8,128)(2,1)S(1)}, u32[]{:S(2)}, u32[]{:S(2)}) collective-permute-start(bf16[448,512]{1,0:T(8,128)(2,1)} %get-tuple-element.79.refs_3_), channel_id=1, source_target_pairs={{0,16},{8,24},{16,0},{24,8},{32,48},{40,56},{48,32},{56,40},{64,80... | collective-permute-start | bytes 1376264 | tf_op jit(solution)/shard_map/ppermute | solution.py:38
  7.5 2.1 %collective-permute-start = (bf16[672,512]{1,0:T(8,128)(2,1)}, bf16[672,512]{1,0:T(8,128)(2,1)S(1)}, u32[]{:S(2)}, u32[]{:S(2)}) collective-permute-start(bf16[672,512]{1,0:T(8,128)(2,1)} %get-tuple-element.77), channel_id=1, source_target_pairs={{0,48},{8,56},{16,32},{24,40},{32,16},{40,24},{48,0},{56,8},{64,11... | collective-permute-start | bytes 2064392 | tf_op jit(solution)/shard_map/ppermute | solution.py:34
  9.6 1.6 %collective-permute-start.1 = (bf16[672,512]{1,0:T(8,128)(2,1)}, bf16[672,512]{1,0:T(8,128)(2,1)S(1)}, u32[]{:S(2)}, u32[]{:S(2)}) collective-permute-start(bf16[672,512]{1,0:T(8,128)(2,1)} %get-tuple-element.78), channel_id=1, source_target_pairs={{0,64},{8,72},{16,80},{24,88},{32,96},{40,104},{48,112},{56,120},{... | collective-permute-start | bytes 2064392 | tf_op jit(solution)/shard_map/ppermute | solution.py:34
  11.1 0.0 collective-permute-done.3.refs_4_
  11.2 3.6 %shard_map.123 = (f32[512,896]{1,0:T(8,128)S(1)}, f32[72,896]{1,0:T(8,128)S(1)}, bf16[80,896]{1,0:T(8,128)(2,1)S(1)}, f32[512,14]{1,0:T(8,128)S(1)}) custom-call(bf16[512,896]{1,0:T(8,128)(2,1)S(1)} %copy-done.1, bf16[64,512]{1,0:T(8,128)(2,1)S(1)} %bitcast.12, bf16[64,512]{1,0:T(8,128)(2,1)S(1)} %bitcast.10, f32[14,512]{1,0:T(8,128)S(1)} %bitcast.13, ...), custom_call_target="tpu_custom_call" | custom-call | flops 1000 | bytes 1000 | tf_op jit(solution)/shard_map/pallas_call | solution.py:400
  14.9 0.1 collective-permute-start.4
  15.0 1.4 %collective-permute-done.4.got_ref = bf16[80,896]{1,0:T(8,128)(2,1)S(1)} collective-permute-done((bf16[80,896]{1,0:T(8,128)(2,1)S(1)}, bf16[80,896]{1,0:T(8,128)(2,1)S(1)}, u32[]{:S(2)}, u32[]{:S(2)}) %collective-permute-start.4) | collective-permute-done | bytes 143392 | tf_op jit(solution)/shard_map/ppermute | solution.py:42
  16.3 0.7 shard_map.124
  17.0 1.9 %collective-permute-done.2.refs_7_ = bf16[448,512]{1,0:T(8,128)(2,1)S(1)} collective-permute-done((bf16[448,512]{1,0:T(8,128)(2,1)}, bf16[448,512]{1,0:T(8,128)(2,1)S(1)}, u32[]{:S(2)}, u32[]{:S(2)}) %collective-permute-start.2) | collective-permute-done | bytes 458784 | tf_op jit(solution)/shard_map/ppermute | solution.py:38
  19.0 0.0 collective-permute-start.5
  19.0 1.6 %collective-permute-start.6 = (bf16[80,896]{1,0:T(8,128)(2,1)S(1)}, bf16[80,896]{1,0:T(8,128)(2,1)S(1)}, u32[]{:S(2)}, u32[]{:S(2)}) collective-permute-start(bf16[80,896]{1,0:T(8,128)(2,1)S(1)} %get-tuple-element.83), channel_id=1, source_target_pairs={{0,16},{8,24},{16,0},{24,8},{32,48},{40,56},{48,32},{56,40},{64,80... | collective-permute-start | bytes 430088 | tf_op jit(solution)/shard_map/ppermute | solution.py:38
  20.5 5.8 %collective-permute-done.refs_1_ = bf16[672,512]{1,0:T(8,128)(2,1)S(1)} collective-permute-done((bf16[672,512]{1,0:T(8,128)(2,1)}, bf16[672,512]{1,0:T(8,128)(2,1)S(1)}, u32[]{:S(2)}, u32[]{:S(2)}) %collective-permute-start) | collective-permute-done | bytes 688160 | tf_op jit(solution)/shard_map/ppermute | solution.py:34
  26.4 0.6 collective-permute-done.1.refs_2_
  27.0 0.0 collective-permute-done.6.got_ref
  27.0 0.0 collective-permute-done.5.refs_8_
  27.0 2.6 %collective-permute-start.7 = (bf16[672,512]{1,0:T(8,128)(2,1)S(1)}, bf16[672,512]{1,0:T(8,128)(2,1)S(1)}, u32[]{:S(2)}, u32[]{:S(2)}) collective-permute-start(bf16[672,512]{1,0:T(8,128)(2,1)S(1)} %copy-done.11), channel_id=1, source_target_pairs={{0,112},{8,120},{16,96},{24,104},{32,80},{40,88},{48,64},{56,72},{... | collective-permute-start | bytes 2064392 | tf_op jit(solution)/shard_map/ppermute | solution.py:34
  29.6 0.7 shard_map.125
  30.3 0.1 collective-permute-start.8
  30.4 0.5 collective-permute-start.9
  30.9 0.0 collective-permute-start.12
  30.9 2.0 %collective-permute-start.13 = (bf16[448,512]{1,0:T(8,128)(2,1)S(1)}, bf16[448,512]{1,0:T(8,128)(2,1)S(1)}, u32[]{:S(2)}, u32[]{:S(2)}) collective-permute-start(bf16[448,512]{1,0:T(8,128)(2,1)S(1)} %slice.16), channel_id=1, source_target_pairs={{0,16},{8,24},{16,0},{24,8},{32,48},{40,56},{48,32},{56,40},{64,80... | collective-permute-start | bytes 1376264 | tf_op jit(solution)/shard_map/ppermute | solution.py:38
  33.0 0.0 collective-permute-done.8.refs_5_
  33.0 0.0 collective-permute-done.9.refs_6_
  33.0 9.2 %shard_map.126 = (f32[4,224,512]{2,1,0:T(8,128)S(1)}, f32[4,16,512]{2,1,0:T(8,128)S(1)}, bf16[4,1024,224]{2,1,0:T(8,128)(2,1)S(1)}, bf16[4,224,1024]{2,1,0:T(8,128)(2,1)S(1)}, f32[8,128]{1,0:T(8,128)S(1)}) custom-call(s32[4]{0:T(128)S(1)} %copy-done.6, bf16[224,512]{1,0:T(8,128)(2,1)S(1)} %copy-done, bf16[672,512]{1,0:T(8,128)(2,1)S(1)} %collective-permute-done.refs_1_, ...), custom_call_target="tpu_custom_call" | custom-call | flops 1000 | bytes 1000 | tf_op jit(solution)/shard_map/pallas_call | solution.py:374
  42.2 3.4 %collective-permute-done.7.refs_3_ = bf16[672,512]{1,0:T(8,128)(2,1)S(1)} collective-permute-done((bf16[672,512]{1,0:T(8,128)(2,1)S(1)}, bf16[672,512]{1,0:T(8,128)(2,1)S(1)}, u32[]{:S(2)}, u32[]{:S(2)}) %collective-permute-start.7) | collective-permute-done | bytes 688160 | tf_op jit(solution)/shard_map/ppermute | solution.py:34
  45.6 0.1 collective-permute-start.14
  45.7 0.5 collective-permute-start.15
  46.2 0.7 collective-permute-start.10
  46.8 0.3 collective-permute-done.14.refs_4_
  47.1 0.3 collective-permute-done.15.refs_5_
  47.5 5.9 %shard_map.128 = (f32[4,224,512]{2,1,0:T(8,128)S(1)}, f32[4,16,512]{2,1,0:T(8,128)S(1)}, f32[8,128]{1,0:T(8,128)S(1)}) custom-call(s32[4]{0:T(128)S(1)} %copy-done.6, bf16[224,512]{1,0:T(8,128)(2,1)S(1)} %copy-done, bf16[672,512]{1,0:T(8,128)(2,1)S(1)} %collective-permute-done.refs_1_, bf16[672,512]{1,0:T(8,128)(2,1)S(1)} %collective-permute-done.1.refs_2_, ...), custom_call_target="tpu_custom_call" | custom-call | flops 1000 | bytes 1000 | tf_op jit(solution)/shard_map/pallas_call | solution.py:374
  53.3 0.0 collective-permute-done.12.refs_4_
  53.3 0.8 collective-permute-done.13.refs_6_
  54.1 0.2 collective-permute-start.17
  54.3 0.3 collective-permute-start.18
  54.7 2.8 %collective-permute-done.10.got_ref = bf16[80,896]{1,0:T(8,128)(2,1)S(1)} collective-permute-done((bf16[80,896]{1,0:T(8,128)(2,1)S(1)}, bf16[80,896]{1,0:T(8,128)(2,1)S(1)}, u32[]{:S(2)}, u32[]{:S(2)}) %collective-permute-start.10) | collective-permute-done | bytes 143392 | tf_op jit(solution)/shard_map/ppermute | solution.py:46
  57.5 0.0 collective-permute-start.11
  57.5 0.7 shard_map.127
  58.2 0.5 collective-permute-start.16
  58.7 0.0 collective-permute-done.17.refs_5_
  58.7 0.0 collective-permute-done.18.refs_7_
  58.7 5.4 %shard_map.129 = (f32[4,224,512]{2,1,0:T(8,128)S(1)}, f32[4,16,512]{2,1,0:T(8,128)S(1)}, f32[8,128]{1,0:T(8,128)S(1)}) custom-call(s32[4]{0:T(128)S(1)} %copy-done.6, bf16[224,512]{1,0:T(8,128)(2,1)S(1)} %copy-done, bf16[672,512]{1,0:T(8,128)(2,1)S(1)} %collective-permute-done.refs_1_, bf16[672,512]{1,0:T(8,128)(2,1)S(1)} %collective-permute-done.1.refs_2_, ...), custom_call_target="tpu_custom_call" | custom-call | flops 1000 | bytes 1000 | tf_op jit(solution)/shard_map/pallas_call | solution.py:374
  64.1 1.4 %shard_map.130 = (f32[72,896]{1,0:T(8,128)}, f32[72,896]{1,0:T(8,128)S(1)}, bf16[80,896]{1,0:T(8,128)(2,1)}) custom-call(s32[4]{0:T(128)S(1)} %copy-done.6, bf16[80,896]{1,0:T(8,128)(2,1)S(1)} %collective-permute-done.16.got_ref, f32[72,896]{1,0:T(8,128)S(1)} %get-tuple-element.124.total_ref, f32[72,896]{1,0:T(8,128)S(1)} %get-tuple-element.125.before_ref), custom_call_target="tpu_custom_call" | custom-call | flops 1000 | bytes 1000 | tf_op jit(solution)/shard_map/pallas_call | solution.py:417
  65.5 1.3 %shard_map.131 = (f32[512,896]{1,0:T(8,128)S(1)}, f32[1,512]{1,0:T(1,128)S(1)}) custom-call(f32[72,896]{1,0:T(8,128)S(1)} %get-tuple-element.126.state_ref, f32[512,896]{1,0:T(8,128)S(1)} %get-tuple-element.127.mixed_ref, f32[512,14]{1,0:T(8,128)S(1)} %get-tuple-element.128.cum_ref, bf16[64,512]{1,0:T(8,128)(2,1)S(1)} %bitcast.11, bf16[512,896]{1,0:T(8,128)(2,1)S(1)} %copy-done.2), custom_call_target="tpu_custom_call" | custom-call | flops 1000 | bytes 1000 | tf_op jit(solution)/shard_map/pallas_call | solution.py:429
  66.8 2.4 %collective-permute-done.11.refs_4_ = bf16[448,512]{1,0:T(8,128)(2,1)S(1)} collective-permute-done((bf16[448,512]{1,0:T(8,128)(2,1)S(1)}, bf16[448,512]{1,0:T(8,128)(2,1)S(1)}, u32[]{:S(2)}, u32[]{:S(2)}) %collective-permute-start.11) | collective-permute-done | bytes 458784 | tf_op jit(solution)/shard_map/ppermute | solution.py:38
  69.2 2.9 %collective-permute-start.20 = (f32[1,512]{1,0:T(1,128)S(1)}, f32[1,512]{1,0:T(1,128)S(1)}, u32[]{:S(2)}, u32[]{:S(2)}) collective-permute-start(f32[1,512]{1,0:T(1,128)S(1)} %get-tuple-element.133), channel_id=1, source_target_pairs={{0,4},{1,5},{2,6},{3,7},{4,0},{5,1},{6,2},{7,3},{8,12},{9,13},{10,... | collective-permute-start | bytes 6152 | tf_op jit(solution)/shard_map/ppermute | solution.py:50
  72.1 2.2 %collective-permute-done.20 = f32[1,512]{1,0:T(1,128)S(1)} collective-permute-done((f32[1,512]{1,0:T(1,128)S(1)}, f32[1,512]{1,0:T(1,128)S(1)}, u32[]{:S(2)}, u32[]{:S(2)}) %collective-permute-start.20) | collective-permute-done | bytes 2080 | tf_op jit(solution)/shard_map/ppermute | solution.py:50
  74.3 0.0 collective-permute-done.19.refs_5_
  74.3 0.0 copy-start.10
  74.3 2.1 %shard_map.132 = (bf16[224,512]{1,0:T(8,128)(2,1)S(1)}, bf16[224,512]{1,0:T(8,128)(2,1)S(1)}, bf16[224,512]{1,0:T(8,128)(2,1)S(1)}, bf16[224,512]{1,0:T(8,128)(2,1)S(1)}, f32[8,128]{1,0:T(8,128)S(1)}) custom-call(s32[4]{0:T(128)S(1)} %copy-done.6, bf16[224,512]{1,0:T(8,128)(2,1)S(1)} %copy-done, bf16[672,512]{1,0:T(8,128)(2,1)S(1)} %collective-permute-done.refs_1_, ...), custom_call_target="tpu_custom_call" | custom-call | flops 1000 | bytes 1000 | tf_op jit(solution)/shard_map/pallas_call | solution.py:374
  76.4 1.6 %collective-permute-start.21 = (bf16[224,512]{1,0:T(8,128)(2,1)S(1)}, bf16[224,512]{1,0:T(8,128)(2,1)S(1)}, u32[]{:S(2)}, u32[]{:S(2)}) collective-permute-start(bf16[224,512]{1,0:T(8,128)(2,1)S(1)} %get-tuple-element.142), channel_id=1, source_target_pairs={{0,48},{8,56},{16,32},{24,40},{32,16},{40,24},{48,0},{56,8},{64,11... | collective-permute-start | bytes 688136 | tf_op jit(solution)/shard_map/ppermute | solution.py:34
  78.0 2.6 %collective-permute-start.22 = (bf16[224,512]{1,0:T(8,128)(2,1)S(1)}, bf16[224,512]{1,0:T(8,128)(2,1)S(1)}, u32[]{:S(2)}, u32[]{:S(2)}) collective-permute-start(bf16[224,512]{1,0:T(8,128)(2,1)S(1)} %get-tuple-element.143), channel_id=1, source_target_pairs={{0,64},{8,72},{16,80},{24,88},{32,96},{40,104},{48,112},{56,120},{... | collective-permute-start | bytes 688136 | tf_op jit(solution)/shard_map/ppermute | solution.py:34
  80.6 1.2 %collective-permute-start.23 = (bf16[224,512]{1,0:T(8,128)(2,1)S(1)}, bf16[224,512]{1,0:T(8,128)(2,1)S(1)}, u32[]{:S(2)}, u32[]{:S(2)}) collective-permute-start(bf16[224,512]{1,0:T(8,128)(2,1)S(1)} %get-tuple-element.144), channel_id=1, source_target_pairs={{0,112},{8,120},{16,96},{24,104},{32,80},{40,88},{48,64},{56,72},{... | collective-permute-start | bytes 688136 | tf_op jit(solution)/shard_map/ppermute | solution.py:34
  81.8 1.9 %collective-permute-start.24 = (f32[1,512]{1,0:T(1,128)S(1)}, f32[1,512]{1,0:T(1,128)S(1)}, u32[]{:S(2)}, u32[]{:S(2)}) collective-permute-start(f32[1,512]{1,0:T(1,128)S(1)} %add.24), channel_id=1, source_target_pairs={{0,1},{1,0},{2,3},{3,2},{4,5},{5,4},{6,7},{7,6},{8,9},{9,8},{10,11... | collective-permute-start | bytes 6152 | tf_op jit(solution)/shard_map/ppermute | solution.py:50
  83.7 1.7 %collective-permute-done.24 = f32[1,512]{1,0:T(1,128)S(1)} collective-permute-done((f32[1,512]{1,0:T(1,128)S(1)}, f32[1,512]{1,0:T(1,128)S(1)}, u32[]{:S(2)}, u32[]{:S(2)}) %collective-permute-start.24) | collective-permute-done | bytes 2080 | tf_op jit(solution)/shard_map/ppermute | solution.py:50
  85.3 3.9 %collective-permute-start.25 = (f32[1,512]{1,0:T(1,128)S(1)}, f32[1,512]{1,0:T(1,128)S(1)}, u32[]{:S(2)}, u32[]{:S(2)}) collective-permute-start(f32[1,512]{1,0:T(1,128)S(1)} %add.25), channel_id=1, source_target_pairs={{0,2},{1,3},{2,0},{3,1},{4,6},{5,7},{6,4},{7,5},{8,10},{9,11},{10,... | collective-permute-start | bytes 6152 | tf_op jit(solution)/shard_map/ppermute | solution.py:50
  89.2 1.6 %collective-permute-done.25 = f32[1,512]{1,0:T(1,128)S(1)} collective-permute-done((f32[1,512]{1,0:T(1,128)S(1)}, f32[1,512]{1,0:T(1,128)S(1)}, u32[]{:S(2)}, u32[]{:S(2)}) %collective-permute-start.25) | collective-permute-done | bytes 2080 | tf_op jit(solution)/shard_map/ppermute | solution.py:50
  90.8 0.0 collective-permute-done.21.refs_1_
  90.8 0.7 collective-permute-done.23.refs_3_
  91.5 1.1 %multiply_convert_fusion = bf16[512,896]{1,0:T(8,128)(2,1)} fusion(f32[512,896]{1,0:T(8,128)S(1)} %get-tuple-element.150, f32[896]{0:T(1024)S(1)} %copy-done.10, f32[512]{0:T(512)S(1)} %bitcast.16), kind=kLoop, calls=%fused_computation | loop fusion | flops 1376256 | bytes 2758144 | tf_op jit(solution)/shard_map/convert_element_type | solution.py:517
  92.7 1.8 %shard_map.133 = bf16[512,896]{1,0:T(8,128)(2,1)} custom-call(s32[4]{0:T(128)S(1)} %copy-done.6, f32[8,128]{1,0:T(8,128)S(1)} %get-tuple-element.140._, bf16[224,512]{1,0:T(8,128)(2,1)S(1)} %get-tuple-element.146.refs_0_, bf16[224,512]{1,0:T(8,128)(2,1)S(1)} %collective-permute-done.21.refs_1_, bf16[224,512]{1,0:T(8,128)(2,1)S(1)} %collective-permute-done.22.refs_2_, ...), custom_call_target="tpu_custom_call" | custom-call | tf_op jit(solution)/shard_map/pallas_call | solution.py:387
  (35 shorter events, 0.2 us)
Async XLA Ops:
  0.6 10.5 %copy-start.1 = (bf16[512,896]{1,0:T(8,128)(2,1)S(1)}, bf16[512,896]{1,0:T(8,128)(2,1)}, u32[]{:S(2)}) copy-start(bf16[512,896]{1,0:T(8,128)(2,1)} %x_ref) | copy-start | bytes 2752516
  0.6 10.5 %copy-start.4 = (bf16[512,64]{0,1:T(8,128)(2,1)S(1)}, bf16[512,64]{0,1:T(8,128)(2,1)}, u32[]{:S(2)}) copy-start(bf16[512,64]{0,1:T(8,128)(2,1)} %param.17) | copy-start | bytes 196612
  0.7 10.5 %copy-start.5 = (bf16[512,64]{0,1:T(8,128)(2,1)S(1)}, bf16[512,64]{0,1:T(8,128)(2,1)}, u32[]{:S(2)}) copy-start(bf16[512,64]{0,1:T(8,128)(2,1)} %param.16) | copy-start | bytes 196612
  0.7 10.5 %copy-start.7 = (f32[512,14]{0,1:T(8,128)S(1)}, f32[512,14]{0,1:T(8,128)}, u32[]{:S(2)}) copy-start(f32[512,14]{0,1:T(8,128)} %param.18) | copy-start | bytes 86020
  0.7 10.5 %copy-start.8 = (f32[14]{0:T(128)S(1)}, f32[14]{0:T(128)}, u32[]{:S(2)}) copy-start(f32[14]{0:T(128)} %param.19) | copy-start | bytes 172
  0.7 10.5 %copy-start.9 = (f32[14]{0:T(128)S(1)}, f32[14]{0:T(128)}, u32[]{:S(2)}) copy-start(f32[14]{0:T(128)} %param.20) | copy-start | bytes 172
  1.3 15.1 %copy-start.6 = (s32[4]{0:T(128)S(1)}, s32[4]{0:T(128)}, u32[]{:S(2)}) copy-start(s32[4]{0:T(128)} %pad_add_fusion.info) | copy-start | bytes 52
  5.7 21.3 %copy-start.11 = (bf16[672,512]{1,0:T(8,128)(2,1)S(1)}, bf16[672,512]{1,0:T(8,128)(2,1)}, u32[]{:S(2)}) copy-start(bf16[672,512]{1,0:T(8,128)(2,1)} %get-tuple-element.86) | copy-start | bytes 2064388
  5.7 5.4 %collective-permute-start.3 = (bf16[448,512]{1,0:T(8,128)(2,1)}, bf16[448,512]{1,0:T(8,128)(2,1)S(1)}, u32[]{:S(2)}, u32[]{:S(2)}) collective-permute-start(bf16[448,512]{1,0:T(8,128)(2,1)} %get-tuple-element.79.refs_3_), channel_id=1, source_target_pairs={{0,8},{8,0},{16,24},{24,16},{32,40},{40,32},{48,56},{56,48},{64,72... | collective-permute-start | bytes 1376264 | tf_op jit(solution)/shard_map/ppermute | solution.py:42
  5.8 13.1 %collective-permute-start.2 = (bf16[448,512]{1,0:T(8,128)(2,1)}, bf16[448,512]{1,0:T(8,128)(2,1)S(1)}, u32[]{:S(2)}, u32[]{:S(2)}) collective-permute-start(bf16[448,512]{1,0:T(8,128)(2,1)} %get-tuple-element.79.refs_3_), channel_id=1, source_target_pairs={{0,16},{8,24},{16,0},{24,8},{32,48},{40,56},{48,32},{56,40},{64,80... | collective-permute-start | bytes 1376264 | tf_op jit(solution)/shard_map/ppermute | solution.py:38
  7.5 18.9 %collective-permute-start = (bf16[672,512]{1,0:T(8,128)(2,1)}, bf16[672,512]{1,0:T(8,128)(2,1)S(1)}, u32[]{:S(2)}, u32[]{:S(2)}) collective-permute-start(bf16[672,512]{1,0:T(8,128)(2,1)} %get-tuple-element.77), channel_id=1, source_target_pairs={{0,48},{8,56},{16,32},{24,40},{32,16},{40,24},{48,0},{56,8},{64,11... | collective-permute-start | bytes 2064392 | tf_op jit(solution)/shard_map/ppermute | solution.py:34
  9.6 17.4 %collective-permute-start.1 = (bf16[672,512]{1,0:T(8,128)(2,1)}, bf16[672,512]{1,0:T(8,128)(2,1)S(1)}, u32[]{:S(2)}, u32[]{:S(2)}) collective-permute-start(bf16[672,512]{1,0:T(8,128)(2,1)} %get-tuple-element.78), channel_id=1, source_target_pairs={{0,64},{8,72},{16,80},{24,88},{32,96},{40,104},{48,112},{56,120},{... | collective-permute-start | bytes 2064392 | tf_op jit(solution)/shard_map/ppermute | solution.py:34
  14.8 18.1 %copy-start = (bf16[224,512]{1,0:T(8,128)(2,1)S(1)}, bf16[224,512]{1,0:T(8,128)(2,1)}, u32[]{:S(2)}) copy-start(bf16[224,512]{1,0:T(8,128)(2,1)} %get-tuple-element.87.refs_0_) | copy-start | bytes 688132
  14.9 18.1 %copy-start.3 = (bf16[448,512]{1,0:T(8,128)(2,1)S(1)}, bf16[448,512]{1,0:T(8,128)(2,1)}, u32[]{:S(2)}) copy-start(bf16[448,512]{1,0:T(8,128)(2,1)} %get-tuple-element.79.refs_3_) | copy-start | bytes 1376260
  14.9 1.4 %collective-permute-start.4 = (bf16[80,896]{1,0:T(8,128)(2,1)S(1)}, bf16[80,896]{1,0:T(8,128)(2,1)S(1)}, u32[]{:S(2)}, u32[]{:S(2)}) collective-permute-start(bf16[80,896]{1,0:T(8,128)(2,1)S(1)} %get-tuple-element.81), channel_id=1, source_target_pairs={{0,8},{8,0},{16,24},{24,16},{32,40},{40,32},{48,56},{56,48},{64,72... | collective-permute-start | bytes 430088 | tf_op jit(solution)/shard_map/ppermute | solution.py:42
  19.0 8.0 %collective-permute-start.5 = (bf16[448,512]{1,0:T(8,128)(2,1)S(1)}, bf16[448,512]{1,0:T(8,128)(2,1)S(1)}, u32[]{:S(2)}, u32[]{:S(2)}) collective-permute-start(bf16[448,512]{1,0:T(8,128)(2,1)S(1)} %collective-permute-done.2.refs_7_), channel_id=1, source_target_pairs={{0,8},{8,0},{16,24},{24,16},{32,40},{40,32},{48,56},{56,48},{64,72... | collective-permute-start | bytes 1376264 | tf_op jit(solution)/shard_map/ppermute | solution.py:42
  19.0 8.0 %collective-permute-start.6 = (bf16[80,896]{1,0:T(8,128)(2,1)S(1)}, bf16[80,896]{1,0:T(8,128)(2,1)S(1)}, u32[]{:S(2)}, u32[]{:S(2)}) collective-permute-start(bf16[80,896]{1,0:T(8,128)(2,1)S(1)} %get-tuple-element.83), channel_id=1, source_target_pairs={{0,16},{8,24},{16,0},{24,8},{32,48},{40,56},{48,32},{56,40},{64,80... | collective-permute-start | bytes 430088 | tf_op jit(solution)/shard_map/ppermute | solution.py:38
  27.0 18.5 %collective-permute-start.7 = (bf16[672,512]{1,0:T(8,128)(2,1)S(1)}, bf16[672,512]{1,0:T(8,128)(2,1)S(1)}, u32[]{:S(2)}, u32[]{:S(2)}) collective-permute-start(bf16[672,512]{1,0:T(8,128)(2,1)S(1)} %copy-done.11), channel_id=1, source_target_pairs={{0,112},{8,120},{16,96},{24,104},{32,80},{40,88},{48,64},{56,72},{... | collective-permute-start | bytes 2064392 | tf_op jit(solution)/shard_map/ppermute | solution.py:34
  30.3 2.6 %collective-permute-start.8 = (bf16[448,512]{1,0:T(8,128)(2,1)S(1)}, bf16[448,512]{1,0:T(8,128)(2,1)S(1)}, u32[]{:S(2)}, u32[]{:S(2)}) collective-permute-start(bf16[448,512]{1,0:T(8,128)(2,1)S(1)} %slice.15), channel_id=1, source_target_pairs={{0,8},{8,0},{16,24},{24,16},{32,40},{40,32},{48,56},{56,48},{64,72... | collective-permute-start | bytes 1376264 | tf_op jit(solution)/shard_map/ppermute | solution.py:42
  30.4 2.5 %collective-permute-start.9 = (bf16[448,512]{1,0:T(8,128)(2,1)S(1)}, bf16[448,512]{1,0:T(8,128)(2,1)S(1)}, u32[]{:S(2)}, u32[]{:S(2)}) collective-permute-start(bf16[448,512]{1,0:T(8,128)(2,1)S(1)} %slice.16), channel_id=1, source_target_pairs={{0,8},{8,0},{16,24},{24,16},{32,40},{40,32},{48,56},{56,48},{64,72... | collective-permute-start | bytes 1376264 | tf_op jit(solution)/shard_map/ppermute | solution.py:42
  30.9 22.4 %collective-permute-start.12 = (bf16[448,512]{1,0:T(8,128)(2,1)S(1)}, bf16[448,512]{1,0:T(8,128)(2,1)S(1)}, u32[]{:S(2)}, u32[]{:S(2)}) collective-permute-start(bf16[448,512]{1,0:T(8,128)(2,1)S(1)} %slice.15), channel_id=1, source_target_pairs={{0,16},{8,24},{16,0},{24,8},{32,48},{40,56},{48,32},{56,40},{64,80... | collective-permute-start | bytes 1376264 | tf_op jit(solution)/shard_map/ppermute | solution.py:38
  30.9 23.2 %collective-permute-start.13 = (bf16[448,512]{1,0:T(8,128)(2,1)S(1)}, bf16[448,512]{1,0:T(8,128)(2,1)S(1)}, u32[]{:S(2)}, u32[]{:S(2)}) collective-permute-start(bf16[448,512]{1,0:T(8,128)(2,1)S(1)} %slice.16), channel_id=1, source_target_pairs={{0,16},{8,24},{16,0},{24,8},{32,48},{40,56},{48,32},{56,40},{64,80... | collective-permute-start | bytes 1376264 | tf_op jit(solution)/shard_map/ppermute | solution.py:38
  45.6 1.6 %collective-permute-start.14 = (bf16[224,512]{1,0:T(8,128)(2,1)S(1)}, bf16[224,512]{1,0:T(8,128)(2,1)S(1)}, u32[]{:S(2)}, u32[]{:S(2)}) collective-permute-start(bf16[224,512]{1,0:T(8,128)(2,1)S(1)} %get-tuple-element.153), channel_id=1, source_target_pairs={{0,8},{8,0},{16,24},{24,16},{32,40},{40,32},{48,56},{56,48},{64,72... | collective-permute-start | bytes 688136 | tf_op jit(solution)/shard_map/ppermute | solution.py:42
  45.7 1.8 %collective-permute-start.15 = (bf16[224,512]{1,0:T(8,128)(2,1)S(1)}, bf16[224,512]{1,0:T(8,128)(2,1)S(1)}, u32[]{:S(2)}, u32[]{:S(2)}) collective-permute-start(bf16[224,512]{1,0:T(8,128)(2,1)S(1)} %get-tuple-element.152), channel_id=1, source_target_pairs={{0,8},{8,0},{16,24},{24,16},{32,40},{40,32},{48,56},{56,48},{64,72... | collective-permute-start | bytes 688136 | tf_op jit(solution)/shard_map/ppermute | solution.py:42
  46.2 11.4 %collective-permute-start.10 = (bf16[80,896]{1,0:T(8,128)(2,1)S(1)}, bf16[80,896]{1,0:T(8,128)(2,1)S(1)}, u32[]{:S(2)}, u32[]{:S(2)}) collective-permute-start(bf16[80,896]{1,0:T(8,128)(2,1)S(1)} %get-tuple-element.103), channel_id=1, source_target_pairs={{0,32},{8,40},{16,48},{24,56},{32,0},{40,8},{48,16},{56,24},{64,96... | collective-permute-start | bytes 430088 | tf_op jit(solution)/shard_map/ppermute | solution.py:46
  54.1 4.6 %collective-permute-start.17 = (bf16[448,512]{1,0:T(8,128)(2,1)S(1)}, bf16[448,512]{1,0:T(8,128)(2,1)S(1)}, u32[]{:S(2)}, u32[]{:S(2)}) collective-permute-start(bf16[448,512]{1,0:T(8,128)(2,1)S(1)} %collective-permute-done.12.refs_4_), channel_id=1, source_target_pairs={{0,8},{8,0},{16,24},{24,16},{32,40},{40,32},{48,56},{56,48},{64,72... | collective-permute-start | bytes 1376264 | tf_op jit(solution)/shard_map/ppermute | solution.py:42
  54.3 4.4 %collective-permute-start.18 = (bf16[448,512]{1,0:T(8,128)(2,1)S(1)}, bf16[448,512]{1,0:T(8,128)(2,1)S(1)}, u32[]{:S(2)}, u32[]{:S(2)}) collective-permute-start(bf16[448,512]{1,0:T(8,128)(2,1)S(1)} %collective-permute-done.13.refs_6_), channel_id=1, source_target_pairs={{0,8},{8,0},{16,24},{24,16},{32,40},{40,32},{48,56},{56,48},{64,72... | collective-permute-start | bytes 1376264 | tf_op jit(solution)/shard_map/ppermute | solution.py:42
  57.5 11.7 %collective-permute-start.11 = (bf16[448,512]{1,0:T(8,128)(2,1)S(1)}, bf16[448,512]{1,0:T(8,128)(2,1)S(1)}, u32[]{:S(2)}, u32[]{:S(2)}) collective-permute-start(bf16[448,512]{1,0:T(8,128)(2,1)S(1)} %slice.17), channel_id=1, source_target_pairs={{0,16},{8,24},{16,0},{24,8},{32,48},{40,56},{48,32},{56,40},{64,80... | collective-permute-start | bytes 1376264 | tf_op jit(solution)/shard_map/ppermute | solution.py:38
  58.2 5.9 %collective-permute-start.16 = (bf16[80,896]{1,0:T(8,128)(2,1)S(1)}, bf16[80,896]{1,0:T(8,128)(2,1)S(1)}, u32[]{:S(2)}, u32[]{:S(2)}) collective-permute-start(bf16[80,896]{1,0:T(8,128)(2,1)S(1)} %get-tuple-element.116), channel_id=1, source_target_pairs={{0,64},{8,72},{16,80},{24,88},{32,96},{40,104},{48,112},{56,120},{... | collective-permute-start | bytes 430088 | tf_op jit(solution)/shard_map/ppermute | solution.py:46
  58.7 6.8 %copy-start.2 = (bf16[512,896]{1,0:T(8,128)(2,1)S(1)}, bf16[512,896]{1,0:T(8,128)(2,1)}, u32[]{:S(2)}) copy-start(bf16[512,896]{1,0:T(8,128)(2,1)} %gate_ref.1) | copy-start | bytes 2752516
  69.2 5.1 %collective-permute-start.19 = (bf16[448,512]{1,0:T(8,128)(2,1)S(1)}, bf16[448,512]{1,0:T(8,128)(2,1)S(1)}, u32[]{:S(2)}, u32[]{:S(2)}) collective-permute-start(bf16[448,512]{1,0:T(8,128)(2,1)S(1)} %collective-permute-done.11.refs_4_), channel_id=1, source_target_pairs={{0,8},{8,0},{16,24},{24,16},{32,40},{40,32},{48,56},{56,48},{64,72... | collective-permute-start | bytes 1376264 | tf_op jit(solution)/shard_map/ppermute | solution.py:42
  69.2 5.1 %collective-permute-start.20 = (f32[1,512]{1,0:T(1,128)S(1)}, f32[1,512]{1,0:T(1,128)S(1)}, u32[]{:S(2)}, u32[]{:S(2)}) collective-permute-start(f32[1,512]{1,0:T(1,128)S(1)} %get-tuple-element.133), channel_id=1, source_target_pairs={{0,4},{1,5},{2,6},{3,7},{4,0},{5,1},{6,2},{7,3},{8,12},{9,13},{10,... | collective-permute-start | bytes 6152 | tf_op jit(solution)/shard_map/ppermute | solution.py:50
  74.3 17.2 %copy-start.10 = (f32[896]{0:T(1024)S(1)}, f32[896]{0:T(1024)}, u32[]{:S(2)}) copy-start(f32[896]{0:T(1024)} %param.21) | copy-start | bytes 10756
  76.4 14.4 %collective-permute-start.21 = (bf16[224,512]{1,0:T(8,128)(2,1)S(1)}, bf16[224,512]{1,0:T(8,128)(2,1)S(1)}, u32[]{:S(2)}, u32[]{:S(2)}) collective-permute-start(bf16[224,512]{1,0:T(8,128)(2,1)S(1)} %get-tuple-element.142), channel_id=1, source_target_pairs={{0,48},{8,56},{16,32},{24,40},{32,16},{40,24},{48,0},{56,8},{64,11... | collective-permute-start | bytes 688136 | tf_op jit(solution)/shard_map/ppermute | solution.py:34
  78.0 12.8 %collective-permute-start.22 = (bf16[224,512]{1,0:T(8,128)(2,1)S(1)}, bf16[224,512]{1,0:T(8,128)(2,1)S(1)}, u32[]{:S(2)}, u32[]{:S(2)}) collective-permute-start(bf16[224,512]{1,0:T(8,128)(2,1)S(1)} %get-tuple-element.143), channel_id=1, source_target_pairs={{0,64},{8,72},{16,80},{24,88},{32,96},{40,104},{48,112},{56,120},{... | collective-permute-start | bytes 688136 | tf_op jit(solution)/shard_map/ppermute | solution.py:34
  80.6 10.9 %collective-permute-start.23 = (bf16[224,512]{1,0:T(8,128)(2,1)S(1)}, bf16[224,512]{1,0:T(8,128)(2,1)S(1)}, u32[]{:S(2)}, u32[]{:S(2)}) collective-permute-start(bf16[224,512]{1,0:T(8,128)(2,1)S(1)} %get-tuple-element.144), channel_id=1, source_target_pairs={{0,112},{8,120},{16,96},{24,104},{32,80},{40,88},{48,64},{56,72},{... | collective-permute-start | bytes 688136 | tf_op jit(solution)/shard_map/ppermute | solution.py:34
  81.8 3.6 %collective-permute-start.24 = (f32[1,512]{1,0:T(1,128)S(1)}, f32[1,512]{1,0:T(1,128)S(1)}, u32[]{:S(2)}, u32[]{:S(2)}) collective-permute-start(f32[1,512]{1,0:T(1,128)S(1)} %add.24), channel_id=1, source_target_pairs={{0,1},{1,0},{2,3},{3,2},{4,5},{5,4},{6,7},{7,6},{8,9},{9,8},{10,11... | collective-permute-start | bytes 6152 | tf_op jit(solution)/shard_map/ppermute | solution.py:50
  85.3 5.4 %collective-permute-start.25 = (f32[1,512]{1,0:T(1,128)S(1)}, f32[1,512]{1,0:T(1,128)S(1)}, u32[]{:S(2)}, u32[]{:S(2)}) collective-permute-start(f32[1,512]{1,0:T(1,128)S(1)} %add.25), channel_id=1, source_target_pairs={{0,2},{1,3},{2,0},{3,1},{4,6},{5,7},{6,4},{7,5},{8,10},{9,11},{10,... | collective-permute-start | bytes 6152 | tf_op jit(solution)/shard_map/ppermute | solution.py:50

commit v10 on v8

--- a/solution.py
+++ b/solution.py
@@ -15,6 +15,7 @@
 TOK = 512
 HEADS = 4
 CTX = 16
+VALUE_ROWS = ATT_DIM + 16
 HALF = 256
 LOG2E = math.log2(math.e)
 F32 = jnp.float32
@@ -101,12 +102,13 @@
         pieces = [(0, 0, near_3, 0), (0, 1, near_core_3, 0)]
     for slot, other, piece, first in pieces:
         start = pl.multiple_of((core ^ other) * TOK, TOK)
+        vs[slot, ATT_DIM:VALUE_ROWS, pl.ds(start, TOK)] = jnp.ones((VALUE_ROWS - ATT_DIM, TOK), BF16)
         if isinstance(piece, tuple):
             ks[slot, pl.ds(start, TOK), :] = piece[0][...].T
-            vs[slot, :, pl.ds(start, TOK)] = piece[1][...]
+            vs[slot, 0:ATT_DIM, pl.ds(start, TOK)] = piece[1][...]
             continue
         ks[slot, pl.ds(start, TOK), :] = piece[first : first + ATT_DIM, :].T
-        vs[slot, :, pl.ds(start, TOK)] = piece[first + ATT_DIM : first + 2 * ATT_DIM, :]
+        vs[slot, 0:ATT_DIM, pl.ds(start, TOK)] = piece[first + ATT_DIM : first + 2 * ATT_DIM, :]
     for r, queries in enumerate(q_in):
         qs[r] = queries[Q_ROWS, :]
     mark[...] = jnp.zeros_like(mark)
@@ -121,7 +123,7 @@
             ]
             new_stats, low, shrinks = [], [], []
             for half in range(2):
-                (top, total), s = stats[half], scores[half]
+                top, s = stats[half], scores[half]
                 if masked:
                     k_pos = lax.broadcasted_iota(jnp.int32, s.shape, 0)
                     q_pos = lax.broadcasted_iota(jnp.int32, s.shape, 1) + half * HALF
@@ -129,8 +131,7 @@
                 new_top = jnp.maximum(top, jnp.max(s, axis=0, keepdims=True))
                 p = jnp.exp2((s - new_top) * scale)
                 shrink = jnp.exp2((top - new_top) * scale)
-                total = total * shrink + jnp.sum(p, axis=0, keepdims=True)
-                new_stats.append((new_top, total))
+                new_stats.append(new_top)
                 low.append(p.astype(BF16))
                 shrinks.append(shrink)
             for half in range(2):
@@ -161,18 +162,12 @@
             return part(core * TOK, stats, True)
 
         if stage == 0:
-            acc[r] = jnp.zeros((ATT_DIM, TOK), F32)
-            first = (jnp.full((1, HALF), -1e30, F32), jnp.zeros((1, HALF), F32))
+            acc[r] = jnp.zeros((VALUE_ROWS, TOK), F32)
+            first = jnp.full((1, HALF), -1e30, F32)
             stats = (first, first)
         else:
             acc[r] = acc_in[r]
-            stats = tuple(
-                (
-                    stats_in[r, 0:1, half * HALF : (half + 1) * HALF],
-                    stats_in[r, 8:9, half * HALF : (half + 1) * HALF],
-                )
-                for half in range(2)
-            )
+            stats = tuple(stats_in[r, 0:1, half * HALF : (half + 1) * HALF] for half in range(2))
 
         if stage == 0:
 
@@ -196,10 +191,10 @@
         for half in range(2):
             lanes = slice(half * HALF, (half + 1) * HALF)
             if stage == 3:
-                os[r, :, lanes] = (acc[r, :, lanes] / stats[half][1]).astype(BF16)
+                total = acc[r, ATT_DIM : ATT_DIM + 1, lanes]
+                os[r, :, lanes] = (acc[r, 0:ATT_DIM, lanes] / total).astype(BF16)
             else:
-                stats_ref[r, 0:8, lanes] = jnp.broadcast_to(stats[half][0], (8, HALF))
-                stats_ref[r, 8:16, lanes] = jnp.broadcast_to(stats[half][1], (8, HALF))
+                stats_ref[r, :, lanes] = jnp.broadcast_to(stats[half], (8, HALF))
         return carry
 
     lax.fori_loop(0, 4, one_queries, 0)
@@ -360,8 +355,8 @@
 
 def attend(stage, info, *operands):
     slots = (4, 1, 2, 1)[stage]
-    keys, values = (slots, 2 * TOK, ATT_DIM), (slots, ATT_DIM, 2 * TOK)
-    state = [shape((4, ATT_DIM, TOK), F32), shape((4, 16, TOK), F32)]
+    keys, values = (slots, 2 * TOK, ATT_DIM), (slots, VALUE_ROWS, 2 * TOK)
+    state = [shape((4, VALUE_ROWS, TOK), F32), shape((4, 8, TOK), F32)]
     queries = pltpu.VMEM((4, ATT_DIM, TOK), BF16)
     mark = [shape((8, 128), F32)]
     if stage == 0:
@@ -373,7 +368,7 @@
     else:
         out = [shape((ATT_DIM, TOK), BF16)] * 4 + mark
         scratch = [pltpu.VMEM(keys, BF16), pltpu.VMEM(values, BF16), queries]
-        scratch += [pltpu.VMEM((4, ATT_DIM, TOK), F32), queries]
+        scratch += [pltpu.VMEM((4, VALUE_ROWS, TOK), F32), queries]
     return pl.pallas_call(
         functools.partial(attend_kernel, stage),
         out_shape=out,

time: 94.7 us -> 94.9 us (level)
  transfers between devices with their start and end apart: 26 -> 26, of which waited for: 14 -> 14; matrix products, arithmetic and copies ran while one was open for 0% -> 0% of each run, Pallas kernels for 30% -> 31%
where the time goes in v10:
time: 94.9 us; the launch traced here: 94.7 us
  Pallas kernels  37.9 us (40%)
  starting transfers between devices  28.9 us (30%)
  waiting for transfers between devices  25.1 us (26%)
  other arithmetic  1.75 us (2%)
  between operations  0.97 us (1%)
    pallas_call x4, Pallas kernels, attend(): pl.pallas_call(functools.partial(attend_kernel, stage), out_shape=out, in...  23.3 us
    ppermute x6, starting transfers between devices, head_swap(): lax.ppermute(value, 'ctx', [(i, exchanged(i, r)) for i in range(CTX)])  11.7 us
    ppermute x6, waiting for transfers between devices, head_swap(): lax.ppermute(value, 'ctx', [(i, exchanged(i, r)) for i in range(CTX)])  10.5 us
    ppermute x3, starting transfers between devices, step_swap(): return lax.ppermute(value, 'tp', [(i, i ^ step) for i in range(8)])  8.71 us
    ppermute x3, waiting for transfers between devices, step_swap(): return lax.ppermute(value, 'tp', [(i, i ^ step) for i in range(8)])  5.4 us
    ppermute x5, starting transfers between devices, class_swap(): return lax.ppermute(value, 'ctx', [(i, i ^ 2) for i in range(CTX)])  5.26 us
    ppermute x5, waiting for transfers between devices, class_swap(): return lax.ppermute(value, 'ctx', [(i, i ^ 2) for i in range(CTX)])  4.46 us
    pallas_call x1, Pallas kernels, pack(): pl.pallas_call(pack_kernel, out_shape=[shape((count, TOK), BF16) for coun...  4.42 us
  transfers between devices with their start and end apart: 26, of which 14 were waited for; matrix products, arithmetic and copies ran while one was open for 0% of the time, Pallas kernels for 31%

profile of v10, /device:TPU:0, one launch (start us, length us, event | category | flops | bytes accessed | tf_op | source)
XLA Modules:
  0.0 94.7 jit_solution(5010894115630117260)
XLA Ops:
  0.7 0.6 pad_add_fusion.info
  1.3 4.4 %shard_map.122 = (bf16[224,512]{1,0:T(8,128)(2,1)}, bf16[448,512]{1,0:T(8,128)(2,1)}, bf16[672,512]{1,0:T(8,128)(2,1)}, bf16[672,512]{1,0:T(8,128)(2,1)}, bf16[672,512]{1,0:T(8,128)(2,1)}) custom-call(s32[4]{0:T(128)} %pad_add_fusion.info, bf16[512,896]{1,0:T(8,128)(2,1)} %q_in.1, bf16[512,896]{1,0:T(8,128)(2,1)} %k_in.1, bf16[512,896]{1,0:T(8,128)(2,1)} %v_in.1), custom_call_target="tpu_custom_call" | custom-call | tf_op jit(solution)/shard_map/pallas_call | solution.py:342
  5.7 0.1 collective-permute-start.3
  5.8 1.7 %collective-permute-start.2 = (bf16[448,512]{1,0:T(8,128)(2,1)}, bf16[448,512]{1,0:T(8,128)(2,1)S(1)}, u32[]{:S(2)}, u32[]{:S(2)}) collective-permute-start(bf16[448,512]{1,0:T(8,128)(2,1)} %get-tuple-element.79.refs_3_), channel_id=1, source_target_pairs={{0,16},{8,24},{16,0},{24,8},{32,48},{40,56},{48,32},{56,40},{64,80... | collective-permute-start | bytes 1376264 | tf_op jit(solution)/shard_map/ppermute | solution.py:39
  7.5 2.1 %collective-permute-start = (bf16[672,512]{1,0:T(8,128)(2,1)}, bf16[672,512]{1,0:T(8,128)(2,1)S(1)}, u32[]{:S(2)}, u32[]{:S(2)}) collective-permute-start(bf16[672,512]{1,0:T(8,128)(2,1)} %get-tuple-element.77), channel_id=1, source_target_pairs={{0,48},{8,56},{16,32},{24,40},{32,16},{40,24},{48,0},{56,8},{64,11... | collective-permute-start | bytes 2064392 | tf_op jit(solution)/shard_map/ppermute | solution.py:35
  9.6 1.6 %collective-permute-start.1 = (bf16[672,512]{1,0:T(8,128)(2,1)}, bf16[672,512]{1,0:T(8,128)(2,1)S(1)}, u32[]{:S(2)}, u32[]{:S(2)}) collective-permute-start(bf16[672,512]{1,0:T(8,128)(2,1)} %get-tuple-element.78), channel_id=1, source_target_pairs={{0,64},{8,72},{16,80},{24,88},{32,96},{40,104},{48,112},{56,120},{... | collective-permute-start | bytes 2064392 | tf_op jit(solution)/shard_map/ppermute | solution.py:35
  11.1 0.0 collective-permute-done.3.refs_4_
  11.2 3.6 %shard_map.123 = (f32[512,896]{1,0:T(8,128)S(1)}, f32[72,896]{1,0:T(8,128)S(1)}, bf16[80,896]{1,0:T(8,128)(2,1)S(1)}, f32[512,14]{1,0:T(8,128)S(1)}) custom-call(bf16[512,896]{1,0:T(8,128)(2,1)S(1)} %copy-done.1, bf16[64,512]{1,0:T(8,128)(2,1)S(1)} %bitcast.12, bf16[64,512]{1,0:T(8,128)(2,1)S(1)} %bitcast.10, f32[14,512]{1,0:T(8,128)S(1)} %bitcast.13, ...), custom_call_target="tpu_custom_call" | custom-call | flops 1000 | bytes 1000 | tf_op jit(solution)/shard_map/pallas_call | solution.py:398
  14.9 0.1 collective-permute-start.4
  15.0 1.4 %collective-permute-done.4.got_ref = bf16[80,896]{1,0:T(8,128)(2,1)S(1)} collective-permute-done((bf16[80,896]{1,0:T(8,128)(2,1)S(1)}, bf16[80,896]{1,0:T(8,128)(2,1)S(1)}, u32[]{:S(2)}, u32[]{:S(2)}) %collective-permute-start.4) | collective-permute-done | bytes 143392 | tf_op jit(solution)/shard_map/ppermute | solution.py:43
  16.3 0.7 shard_map.124
  17.0 1.9 %collective-permute-done.2.refs_7_ = bf16[448,512]{1,0:T(8,128)(2,1)S(1)} collective-permute-done((bf16[448,512]{1,0:T(8,128)(2,1)}, bf16[448,512]{1,0:T(8,128)(2,1)S(1)}, u32[]{:S(2)}, u32[]{:S(2)}) %collective-permute-start.2) | collective-permute-done | bytes 458784 | tf_op jit(solution)/shard_map/ppermute | solution.py:39
  19.0 0.0 collective-permute-start.5
  19.0 1.6 %collective-permute-start.6 = (bf16[80,896]{1,0:T(8,128)(2,1)S(1)}, bf16[80,896]{1,0:T(8,128)(2,1)S(1)}, u32[]{:S(2)}, u32[]{:S(2)}) collective-permute-start(bf16[80,896]{1,0:T(8,128)(2,1)S(1)} %get-tuple-element.83), channel_id=1, source_target_pairs={{0,16},{8,24},{16,0},{24,8},{32,48},{40,56},{48,32},{56,40},{64,80... | collective-permute-start | bytes 430088 | tf_op jit(solution)/shard_map/ppermute | solution.py:39
  20.5 5.8 %collective-permute-done.refs_1_ = bf16[672,512]{1,0:T(8,128)(2,1)S(1)} collective-permute-done((bf16[672,512]{1,0:T(8,128)(2,1)}, bf16[672,512]{1,0:T(8,128)(2,1)S(1)}, u32[]{:S(2)}, u32[]{:S(2)}) %collective-permute-start) | collective-permute-done | bytes 688160 | tf_op jit(solution)/shard_map/ppermute | solution.py:35
  26.4 0.6 collective-permute-done.1.refs_2_
  27.0 0.0 collective-permute-done.6.got_ref
  27.0 0.0 collective-permute-done.5.refs_8_
  27.0 2.6 %collective-permute-start.7 = (bf16[672,512]{1,0:T(8,128)(2,1)S(1)}, bf16[672,512]{1,0:T(8,128)(2,1)S(1)}, u32[]{:S(2)}, u32[]{:S(2)}) collective-permute-start(bf16[672,512]{1,0:T(8,128)(2,1)S(1)} %copy-done.11), channel_id=1, source_target_pairs={{0,112},{8,120},{16,96},{24,104},{32,80},{40,88},{48,64},{56,72},{... | collective-permute-start | bytes 2064392 | tf_op jit(solution)/shard_map/ppermute | solution.py:35
  29.6 0.7 shard_map.125
  30.3 0.1 collective-permute-start.8
  30.4 0.5 collective-permute-start.9
  30.9 0.0 collective-permute-start.12
  30.9 2.0 %collective-permute-start.13 = (bf16[448,512]{1,0:T(8,128)(2,1)S(1)}, bf16[448,512]{1,0:T(8,128)(2,1)S(1)}, u32[]{:S(2)}, u32[]{:S(2)}) collective-permute-start(bf16[448,512]{1,0:T(8,128)(2,1)S(1)} %slice.16), channel_id=1, source_target_pairs={{0,16},{8,24},{16,0},{24,8},{32,48},{40,56},{48,32},{56,40},{64,80... | collective-permute-start | bytes 1376264 | tf_op jit(solution)/shard_map/ppermute | solution.py:39
  33.0 0.0 collective-permute-done.8.refs_5_
  33.0 0.0 collective-permute-done.9.refs_6_
  33.0 9.2 %shard_map.126 = (f32[4,240,512]{2,1,0:T(8,128)S(1)}, f32[4,8,512]{2,1,0:T(8,128)S(1)}, bf16[4,1024,224]{2,1,0:T(8,128)(2,1)S(1)}, bf16[4,240,1024]{2,1,0:T(8,128)(2,1)S(1)}, f32[8,128]{1,0:T(8,128)S(1)}) custom-call(s32[4]{0:T(128)S(1)} %copy-done.6, bf16[224,512]{1,0:T(8,128)(2,1)S(1)} %copy-done, bf16[672,512]{1,0:T(8,128)(2,1)S(1)} %collective-permute-done.refs_1_, ...), custom_call_target="tpu_custom_call" | custom-call | flops 1000 | bytes 1000 | tf_op jit(solution)/shard_map/pallas_call | solution.py:372
  42.2 3.3 %collective-permute-done.7.refs_3_ = bf16[672,512]{1,0:T(8,128)(2,1)S(1)} collective-permute-done((bf16[672,512]{1,0:T(8,128)(2,1)S(1)}, bf16[672,512]{1,0:T(8,128)(2,1)S(1)}, u32[]{:S(2)}, u32[]{:S(2)}) %collective-permute-start.7) | collective-permute-done | bytes 688160 | tf_op jit(solution)/shard_map/ppermute | solution.py:35
  45.6 0.1 collective-permute-start.14
  45.7 0.5 collective-permute-start.15
  46.2 0.7 collective-permute-start.10
  46.8 0.3 collective-permute-done.14.refs_4_
  47.1 0.3 collective-permute-done.15.refs_5_
  47.5 6.2 %shard_map.128 = (f32[4,240,512]{2,1,0:T(8,128)S(1)}, f32[4,8,512]{2,1,0:T(8,128)S(1)}, f32[8,128]{1,0:T(8,128)S(1)}) custom-call(s32[4]{0:T(128)S(1)} %copy-done.6, bf16[224,512]{1,0:T(8,128)(2,1)S(1)} %copy-done, bf16[672,512]{1,0:T(8,128)(2,1)S(1)} %collective-permute-done.refs_1_, bf16[672,512]{1,0:T(8,128)(2,1)S(1)} %collective-permute-done.1.refs_2_, ...), custom_call_target="tpu_custom_call" | custom-call | flops 1000 | bytes 1000 | tf_op jit(solution)/shard_map/pallas_call | solution.py:372
  53.7 0.0 collective-permute-done.12.refs_4_
  53.7 0.4 collective-permute-done.13.refs_6_
  54.1 0.5 collective-permute-start.17
  54.7 0.1 collective-permute-start.18
  54.8 2.7 %collective-permute-done.10.got_ref = bf16[80,896]{1,0:T(8,128)(2,1)S(1)} collective-permute-done((bf16[80,896]{1,0:T(8,128)(2,1)S(1)}, bf16[80,896]{1,0:T(8,128)(2,1)S(1)}, u32[]{:S(2)}, u32[]{:S(2)}) %collective-permute-start.10) | collective-permute-done | bytes 143392 | tf_op jit(solution)/shard_map/ppermute | solution.py:47
  57.5 0.0 collective-permute-start.11
  57.5 0.7 shard_map.127
  58.2 0.5 collective-permute-start.16
  58.7 0.0 collective-permute-done.17.refs_5_
  58.7 0.0 collective-permute-done.18.refs_7_
  58.7 5.6 %shard_map.129 = (f32[4,240,512]{2,1,0:T(8,128)S(1)}, f32[4,8,512]{2,1,0:T(8,128)S(1)}, f32[8,128]{1,0:T(8,128)S(1)}) custom-call(s32[4]{0:T(128)S(1)} %copy-done.6, bf16[224,512]{1,0:T(8,128)(2,1)S(1)} %copy-done, bf16[672,512]{1,0:T(8,128)(2,1)S(1)} %collective-permute-done.refs_1_, bf16[672,512]{1,0:T(8,128)(2,1)S(1)} %collective-permute-done.1.refs_2_, ...), custom_call_target="tpu_custom_call" | custom-call | flops 1000 | bytes 1000 | tf_op jit(solution)/shard_map/pallas_call | solution.py:372
  64.4 0.0 collective-permute-done.16.got_ref
  64.4 1.4 %shard_map.130 = (f32[72,896]{1,0:T(8,128)}, f32[72,896]{1,0:T(8,128)S(1)}, bf16[80,896]{1,0:T(8,128)(2,1)}) custom-call(s32[4]{0:T(128)S(1)} %copy-done.6, bf16[80,896]{1,0:T(8,128)(2,1)S(1)} %collective-permute-done.16.got_ref, f32[72,896]{1,0:T(8,128)S(1)} %get-tuple-element.124.total_ref, f32[72,896]{1,0:T(8,128)S(1)} %get-tuple-element.125.before_ref), custom_call_target="tpu_custom_call" | custom-call | flops 1000 | bytes 1000 | tf_op jit(solution)/shard_map/pallas_call | solution.py:415
  65.7 1.3 %shard_map.131 = (f32[512,896]{1,0:T(8,128)S(1)}, f32[1,512]{1,0:T(1,128)S(1)}) custom-call(f32[72,896]{1,0:T(8,128)S(1)} %get-tuple-element.126.state_ref, f32[512,896]{1,0:T(8,128)S(1)} %get-tuple-element.127.mixed_ref, f32[512,14]{1,0:T(8,128)S(1)} %get-tuple-element.128.cum_ref, bf16[64,512]{1,0:T(8,128)(2,1)S(1)} %bitcast.11, bf16[512,896]{1,0:T(8,128)(2,1)S(1)} %copy-done.2), custom_call_target="tpu_custom_call" | custom-call | flops 1000 | bytes 1000 | tf_op jit(solution)/shard_map/pallas_call | solution.py:427
  67.1 2.1 %collective-permute-done.11.refs_4_ = bf16[448,512]{1,0:T(8,128)(2,1)S(1)} collective-permute-done((bf16[448,512]{1,0:T(8,128)(2,1)S(1)}, bf16[448,512]{1,0:T(8,128)(2,1)S(1)}, u32[]{:S(2)}, u32[]{:S(2)}) %collective-permute-start.11) | collective-permute-done | bytes 458784 | tf_op jit(solution)/shard_map/ppermute | solution.py:39
  69.2 2.9 %collective-permute-start.20 = (f32[1,512]{1,0:T(1,128)S(1)}, f32[1,512]{1,0:T(1,128)S(1)}, u32[]{:S(2)}, u32[]{:S(2)}) collective-permute-start(f32[1,512]{1,0:T(1,128)S(1)} %get-tuple-element.133), channel_id=1, source_target_pairs={{0,4},{1,5},{2,6},{3,7},{4,0},{5,1},{6,2},{7,3},{8,12},{9,13},{10,... | collective-permute-start | bytes 6152 | tf_op jit(solution)/shard_map/ppermute | solution.py:51
  72.1 2.2 %collective-permute-done.20 = f32[1,512]{1,0:T(1,128)S(1)} collective-permute-done((f32[1,512]{1,0:T(1,128)S(1)}, f32[1,512]{1,0:T(1,128)S(1)}, u32[]{:S(2)}, u32[]{:S(2)}) %collective-permute-start.20) | collective-permute-done | bytes 2080 | tf_op jit(solution)/shard_map/ppermute | solution.py:51
  74.3 0.0 collective-permute-done.19.refs_5_
  74.3 0.0 copy-start.10
  74.3 2.2 %shard_map.132 = (bf16[224,512]{1,0:T(8,128)(2,1)S(1)}, bf16[224,512]{1,0:T(8,128)(2,1)S(1)}, bf16[224,512]{1,0:T(8,128)(2,1)S(1)}, bf16[224,512]{1,0:T(8,128)(2,1)S(1)}, f32[8,128]{1,0:T(8,128)S(1)}) custom-call(s32[4]{0:T(128)S(1)} %copy-done.6, bf16[224,512]{1,0:T(8,128)(2,1)S(1)} %copy-done, bf16[672,512]{1,0:T(8,128)(2,1)S(1)} %collective-permute-done.refs_1_, ...), custom_call_target="tpu_custom_call" | custom-call | flops 1000 | bytes 1000 | tf_op jit(solution)/shard_map/pallas_call | solution.py:372
  76.5 1.6 %collective-permute-start.21 = (bf16[224,512]{1,0:T(8,128)(2,1)S(1)}, bf16[224,512]{1,0:T(8,128)(2,1)S(1)}, u32[]{:S(2)}, u32[]{:S(2)}) collective-permute-start(bf16[224,512]{1,0:T(8,128)(2,1)S(1)} %get-tuple-element.142), channel_id=1, source_target_pairs={{0,48},{8,56},{16,32},{24,40},{32,16},{40,24},{48,0},{56,8},{64,11... | collective-permute-start | bytes 688136 | tf_op jit(solution)/shard_map/ppermute | solution.py:35
  78.1 2.7 %collective-permute-start.22 = (bf16[224,512]{1,0:T(8,128)(2,1)S(1)}, bf16[224,512]{1,0:T(8,128)(2,1)S(1)}, u32[]{:S(2)}, u32[]{:S(2)}) collective-permute-start(bf16[224,512]{1,0:T(8,128)(2,1)S(1)} %get-tuple-element.143), channel_id=1, source_target_pairs={{0,64},{8,72},{16,80},{24,88},{32,96},{40,104},{48,112},{56,120},{... | collective-permute-start | bytes 688136 | tf_op jit(solution)/shard_map/ppermute | solution.py:35
  80.8 1.2 %collective-permute-start.23 = (bf16[224,512]{1,0:T(8,128)(2,1)S(1)}, bf16[224,512]{1,0:T(8,128)(2,1)S(1)}, u32[]{:S(2)}, u32[]{:S(2)}) collective-permute-start(bf16[224,512]{1,0:T(8,128)(2,1)S(1)} %get-tuple-element.144), channel_id=1, source_target_pairs={{0,112},{8,120},{16,96},{24,104},{32,80},{40,88},{48,64},{56,72},{... | collective-permute-start | bytes 688136 | tf_op jit(solution)/shard_map/ppermute | solution.py:35
  82.0 1.9 %collective-permute-start.24 = (f32[1,512]{1,0:T(1,128)S(1)}, f32[1,512]{1,0:T(1,128)S(1)}, u32[]{:S(2)}, u32[]{:S(2)}) collective-permute-start(f32[1,512]{1,0:T(1,128)S(1)} %add.24), channel_id=1, source_target_pairs={{0,1},{1,0},{2,3},{3,2},{4,5},{5,4},{6,7},{7,6},{8,9},{9,8},{10,11... | collective-permute-start | bytes 6152 | tf_op jit(solution)/shard_map/ppermute | solution.py:51
  83.9 1.7 %collective-permute-done.24 = f32[1,512]{1,0:T(1,128)S(1)} collective-permute-done((f32[1,512]{1,0:T(1,128)S(1)}, f32[1,512]{1,0:T(1,128)S(1)}, u32[]{:S(2)}, u32[]{:S(2)}) %collective-permute-start.24) | collective-permute-done | bytes 2080 | tf_op jit(solution)/shard_map/ppermute | solution.py:51
  85.6 3.9 %collective-permute-start.25 = (f32[1,512]{1,0:T(1,128)S(1)}, f32[1,512]{1,0:T(1,128)S(1)}, u32[]{:S(2)}, u32[]{:S(2)}) collective-permute-start(f32[1,512]{1,0:T(1,128)S(1)} %add.25), channel_id=1, source_target_pairs={{0,2},{1,3},{2,0},{3,1},{4,6},{5,7},{6,4},{7,5},{8,10},{9,11},{10,... | collective-permute-start | bytes 6152 | tf_op jit(solution)/shard_map/ppermute | solution.py:51
  89.5 1.6 %collective-permute-done.25 = f32[1,512]{1,0:T(1,128)S(1)} collective-permute-done((f32[1,512]{1,0:T(1,128)S(1)}, f32[1,512]{1,0:T(1,128)S(1)}, u32[]{:S(2)}, u32[]{:S(2)}) %collective-permute-start.25) | collective-permute-done | bytes 2080 | tf_op jit(solution)/shard_map/ppermute | solution.py:51
  91.1 0.7 collective-permute-done.23.refs_3_
  91.8 1.1 %multiply_convert_fusion = bf16[512,896]{1,0:T(8,128)(2,1)} fusion(f32[512,896]{1,0:T(8,128)S(1)} %get-tuple-element.150, f32[896]{0:T(1024)S(1)} %copy-done.10, f32[512]{0:T(512)S(1)} %bitcast.16), kind=kLoop, calls=%fused_computation | loop fusion | flops 1376256 | bytes 2758144 | tf_op jit(solution)/shard_map/convert_element_type | solution.py:515
  92.9 1.8 %shard_map.133 = bf16[512,896]{1,0:T(8,128)(2,1)} custom-call(s32[4]{0:T(128)S(1)} %copy-done.6, f32[8,128]{1,0:T(8,128)S(1)} %get-tuple-element.140._, bf16[224,512]{1,0:T(8,128)(2,1)S(1)} %get-tuple-element.146.refs_0_, bf16[224,512]{1,0:T(8,128)(2,1)S(1)} %collective-permute-done.21.refs_1_, bf16[224,512]{1,0:T(8,128)(2,1)S(1)} %collective-permute-done.22.refs_2_, ...), custom_call_target="tpu_custom_call" | custom-call | tf_op jit(solution)/shard_map/pallas_call | solution.py:385
  (35 shorter events, 0.2 us)
Async XLA Ops:
  0.6 10.5 %copy-start.1 = (bf16[512,896]{1,0:T(8,128)(2,1)S(1)}, bf16[512,896]{1,0:T(8,128)(2,1)}, u32[]{:S(2)}) copy-start(bf16[512,896]{1,0:T(8,128)(2,1)} %x_ref) | copy-start | bytes 2752516
  0.6 10.5 %copy-start.4 = (bf16[512,64]{0,1:T(8,128)(2,1)S(1)}, bf16[512,64]{0,1:T(8,128)(2,1)}, u32[]{:S(2)}) copy-start(bf16[512,64]{0,1:T(8,128)(2,1)} %param.17) | copy-start | bytes 196612
  0.7 10.5 %copy-start.5 = (bf16[512,64]{0,1:T(8,128)(2,1)S(1)}, bf16[512,64]{0,1:T(8,128)(2,1)}, u32[]{:S(2)}) copy-start(bf16[512,64]{0,1:T(8,128)(2,1)} %param.16) | copy-start | bytes 196612
  0.7 10.5 %copy-start.7 = (f32[512,14]{0,1:T(8,128)S(1)}, f32[512,14]{0,1:T(8,128)}, u32[]{:S(2)}) copy-start(f32[512,14]{0,1:T(8,128)} %param.18) | copy-start | bytes 86020
  0.7 10.5 %copy-start.8 = (f32[14]{0:T(128)S(1)}, f32[14]{0:T(128)}, u32[]{:S(2)}) copy-start(f32[14]{0:T(128)} %param.19) | copy-start | bytes 172
  0.7 10.5 %copy-start.9 = (f32[14]{0:T(128)S(1)}, f32[14]{0:T(128)}, u32[]{:S(2)}) copy-start(f32[14]{0:T(128)} %param.20) | copy-start | bytes 172
  1.3 15.1 %copy-start.6 = (s32[4]{0:T(128)S(1)}, s32[4]{0:T(128)}, u32[]{:S(2)}) copy-start(s32[4]{0:T(128)} %pad_add_fusion.info) | copy-start | bytes 52
  5.7 21.3 %copy-start.11 = (bf16[672,512]{1,0:T(8,128)(2,1)S(1)}, bf16[672,512]{1,0:T(8,128)(2,1)}, u32[]{:S(2)}) copy-start(bf16[672,512]{1,0:T(8,128)(2,1)} %get-tuple-element.86) | copy-start | bytes 2064388
  5.7 5.4 %collective-permute-start.3 = (bf16[448,512]{1,0:T(8,128)(2,1)}, bf16[448,512]{1,0:T(8,128)(2,1)S(1)}, u32[]{:S(2)}, u32[]{:S(2)}) collective-permute-start(bf16[448,512]{1,0:T(8,128)(2,1)} %get-tuple-element.79.refs_3_), channel_id=1, source_target_pairs={{0,8},{8,0},{16,24},{24,16},{32,40},{40,32},{48,56},{56,48},{64,72... | collective-permute-start | bytes 1376264 | tf_op jit(solution)/shard_map/ppermute | solution.py:43
  5.8 13.1 %collective-permute-start.2 = (bf16[448,512]{1,0:T(8,128)(2,1)}, bf16[448,512]{1,0:T(8,128)(2,1)S(1)}, u32[]{:S(2)}, u32[]{:S(2)}) collective-permute-start(bf16[448,512]{1,0:T(8,128)(2,1)} %get-tuple-element.79.refs_3_), channel_id=1, source_target_pairs={{0,16},{8,24},{16,0},{24,8},{32,48},{40,56},{48,32},{56,40},{64,80... | collective-permute-start | bytes 1376264 | tf_op jit(solution)/shard_map/ppermute | solution.py:39
  7.5 18.9 %collective-permute-start = (bf16[672,512]{1,0:T(8,128)(2,1)}, bf16[672,512]{1,0:T(8,128)(2,1)S(1)}, u32[]{:S(2)}, u32[]{:S(2)}) collective-permute-start(bf16[672,512]{1,0:T(8,128)(2,1)} %get-tuple-element.77), channel_id=1, source_target_pairs={{0,48},{8,56},{16,32},{24,40},{32,16},{40,24},{48,0},{56,8},{64,11... | collective-permute-start | bytes 2064392 | tf_op jit(solution)/shard_map/ppermute | solution.py:35
  9.6 17.4 %collective-permute-start.1 = (bf16[672,512]{1,0:T(8,128)(2,1)}, bf16[672,512]{1,0:T(8,128)(2,1)S(1)}, u32[]{:S(2)}, u32[]{:S(2)}) collective-permute-start(bf16[672,512]{1,0:T(8,128)(2,1)} %get-tuple-element.78), channel_id=1, source_target_pairs={{0,64},{8,72},{16,80},{24,88},{32,96},{40,104},{48,112},{56,120},{... | collective-permute-start | bytes 2064392 | tf_op jit(solution)/shard_map/ppermute | solution.py:35
  14.8 18.1 %copy-start = (bf16[224,512]{1,0:T(8,128)(2,1)S(1)}, bf16[224,512]{1,0:T(8,128)(2,1)}, u32[]{:S(2)}) copy-start(bf16[224,512]{1,0:T(8,128)(2,1)} %get-tuple-element.87.refs_0_) | copy-start | bytes 688132
  14.9 18.1 %copy-start.3 = (bf16[448,512]{1,0:T(8,128)(2,1)S(1)}, bf16[448,512]{1,0:T(8,128)(2,1)}, u32[]{:S(2)}) copy-start(bf16[448,512]{1,0:T(8,128)(2,1)} %get-tuple-element.79.refs_3_) | copy-start | bytes 1376260
  14.9 1.4 %collective-permute-start.4 = (bf16[80,896]{1,0:T(8,128)(2,1)S(1)}, bf16[80,896]{1,0:T(8,128)(2,1)S(1)}, u32[]{:S(2)}, u32[]{:S(2)}) collective-permute-start(bf16[80,896]{1,0:T(8,128)(2,1)S(1)} %get-tuple-element.81), channel_id=1, source_target_pairs={{0,8},{8,0},{16,24},{24,16},{32,40},{40,32},{48,56},{56,48},{64,72... | collective-permute-start | bytes 430088 | tf_op jit(solution)/shard_map/ppermute | solution.py:43
  19.0 8.0 %collective-permute-start.5 = (bf16[448,512]{1,0:T(8,128)(2,1)S(1)}, bf16[448,512]{1,0:T(8,128)(2,1)S(1)}, u32[]{:S(2)}, u32[]{:S(2)}) collective-permute-start(bf16[448,512]{1,0:T(8,128)(2,1)S(1)} %collective-permute-done.2.refs_7_), channel_id=1, source_target_pairs={{0,8},{8,0},{16,24},{24,16},{32,40},{40,32},{48,56},{56,48},{64,72... | collective-permute-start | bytes 1376264 | tf_op jit(solution)/shard_map/ppermute | solution.py:43
  19.0 8.0 %collective-permute-start.6 = (bf16[80,896]{1,0:T(8,128)(2,1)S(1)}, bf16[80,896]{1,0:T(8,128)(2,1)S(1)}, u32[]{:S(2)}, u32[]{:S(2)}) collective-permute-start(bf16[80,896]{1,0:T(8,128)(2,1)S(1)} %get-tuple-element.83), channel_id=1, source_target_pairs={{0,16},{8,24},{16,0},{24,8},{32,48},{40,56},{48,32},{56,40},{64,80... | collective-permute-start | bytes 430088 | tf_op jit(solution)/shard_map/ppermute | solution.py:39
  27.0 18.5 %collective-permute-start.7 = (bf16[672,512]{1,0:T(8,128)(2,1)S(1)}, bf16[672,512]{1,0:T(8,128)(2,1)S(1)}, u32[]{:S(2)}, u32[]{:S(2)}) collective-permute-start(bf16[672,512]{1,0:T(8,128)(2,1)S(1)} %copy-done.11), channel_id=1, source_target_pairs={{0,112},{8,120},{16,96},{24,104},{32,80},{40,88},{48,64},{56,72},{... | collective-permute-start | bytes 2064392 | tf_op jit(solution)/shard_map/ppermute | solution.py:35
  30.3 2.6 %collective-permute-start.8 = (bf16[448,512]{1,0:T(8,128)(2,1)S(1)}, bf16[448,512]{1,0:T(8,128)(2,1)S(1)}, u32[]{:S(2)}, u32[]{:S(2)}) collective-permute-start(bf16[448,512]{1,0:T(8,128)(2,1)S(1)} %slice.15), channel_id=1, source_target_pairs={{0,8},{8,0},{16,24},{24,16},{32,40},{40,32},{48,56},{56,48},{64,72... | collective-permute-start | bytes 1376264 | tf_op jit(solution)/shard_map/ppermute | solution.py:43
  30.4 2.5 %collective-permute-start.9 = (bf16[448,512]{1,0:T(8,128)(2,1)S(1)}, bf16[448,512]{1,0:T(8,128)(2,1)S(1)}, u32[]{:S(2)}, u32[]{:S(2)}) collective-permute-start(bf16[448,512]{1,0:T(8,128)(2,1)S(1)} %slice.16), channel_id=1, source_target_pairs={{0,8},{8,0},{16,24},{24,16},{32,40},{40,32},{48,56},{56,48},{64,72... | collective-permute-start | bytes 1376264 | tf_op jit(solution)/shard_map/ppermute | solution.py:43
  30.9 22.8 %collective-permute-start.12 = (bf16[448,512]{1,0:T(8,128)(2,1)S(1)}, bf16[448,512]{1,0:T(8,128)(2,1)S(1)}, u32[]{:S(2)}, u32[]{:S(2)}) collective-permute-start(bf16[448,512]{1,0:T(8,128)(2,1)S(1)} %slice.15), channel_id=1, source_target_pairs={{0,16},{8,24},{16,0},{24,8},{32,48},{40,56},{48,32},{56,40},{64,80... | collective-permute-start | bytes 1376264 | tf_op jit(solution)/shard_map/ppermute | solution.py:39
  30.9 23.2 %collective-permute-start.13 = (bf16[448,512]{1,0:T(8,128)(2,1)S(1)}, bf16[448,512]{1,0:T(8,128)(2,1)S(1)}, u32[]{:S(2)}, u32[]{:S(2)}) collective-permute-start(bf16[448,512]{1,0:T(8,128)(2,1)S(1)} %slice.16), channel_id=1, source_target_pairs={{0,16},{8,24},{16,0},{24,8},{32,48},{40,56},{48,32},{56,40},{64,80... | collective-permute-start | bytes 1376264 | tf_op jit(solution)/shard_map/ppermute | solution.py:39
  45.6 1.6 %collective-permute-start.14 = (bf16[224,512]{1,0:T(8,128)(2,1)S(1)}, bf16[224,512]{1,0:T(8,128)(2,1)S(1)}, u32[]{:S(2)}, u32[]{:S(2)}) collective-permute-start(bf16[224,512]{1,0:T(8,128)(2,1)S(1)} %get-tuple-element.153), channel_id=1, source_target_pairs={{0,8},{8,0},{16,24},{24,16},{32,40},{40,32},{48,56},{56,48},{64,72... | collective-permute-start | bytes 688136 | tf_op jit(solution)/shard_map/ppermute | solution.py:43
  45.7 1.8 %collective-permute-start.15 = (bf16[224,512]{1,0:T(8,128)(2,1)S(1)}, bf16[224,512]{1,0:T(8,128)(2,1)S(1)}, u32[]{:S(2)}, u32[]{:S(2)}) collective-permute-start(bf16[224,512]{1,0:T(8,128)(2,1)S(1)} %get-tuple-element.152), channel_id=1, source_target_pairs={{0,8},{8,0},{16,24},{24,16},{32,40},{40,32},{48,56},{56,48},{64,72... | collective-permute-start | bytes 688136 | tf_op jit(solution)/shard_map/ppermute | solution.py:43
  46.2 11.4 %collective-permute-start.10 = (bf16[80,896]{1,0:T(8,128)(2,1)S(1)}, bf16[80,896]{1,0:T(8,128)(2,1)S(1)}, u32[]{:S(2)}, u32[]{:S(2)}) collective-permute-start(bf16[80,896]{1,0:T(8,128)(2,1)S(1)} %get-tuple-element.103), channel_id=1, source_target_pairs={{0,32},{8,40},{16,48},{24,56},{32,0},{40,8},{48,16},{56,24},{64,96... | collective-permute-start | bytes 430088 | tf_op jit(solution)/shard_map/ppermute | solution.py:47
  54.1 4.6 %collective-permute-start.17 = (bf16[448,512]{1,0:T(8,128)(2,1)S(1)}, bf16[448,512]{1,0:T(8,128)(2,1)S(1)}, u32[]{:S(2)}, u32[]{:S(2)}) collective-permute-start(bf16[448,512]{1,0:T(8,128)(2,1)S(1)} %collective-permute-done.12.refs_4_), channel_id=1, source_target_pairs={{0,8},{8,0},{16,24},{24,16},{32,40},{40,32},{48,56},{56,48},{64,72... | collective-permute-start | bytes 1376264 | tf_op jit(solution)/shard_map/ppermute | solution.py:43
  54.7 4.1 %collective-permute-start.18 = (bf16[448,512]{1,0:T(8,128)(2,1)S(1)}, bf16[448,512]{1,0:T(8,128)(2,1)S(1)}, u32[]{:S(2)}, u32[]{:S(2)}) collective-permute-start(bf16[448,512]{1,0:T(8,128)(2,1)S(1)} %collective-permute-done.13.refs_6_), channel_id=1, source_target_pairs={{0,8},{8,0},{16,24},{24,16},{32,40},{40,32},{48,56},{56,48},{64,72... | collective-permute-start | bytes 1376264 | tf_op jit(solution)/shard_map/ppermute | solution.py:43
  57.5 11.7 %collective-permute-start.11 = (bf16[448,512]{1,0:T(8,128)(2,1)S(1)}, bf16[448,512]{1,0:T(8,128)(2,1)S(1)}, u32[]{:S(2)}, u32[]{:S(2)}) collective-permute-start(bf16[448,512]{1,0:T(8,128)(2,1)S(1)} %slice.17), channel_id=1, source_target_pairs={{0,16},{8,24},{16,0},{24,8},{32,48},{40,56},{48,32},{56,40},{64,80... | collective-permute-start | bytes 1376264 | tf_op jit(solution)/shard_map/ppermute | solution.py:39
  58.2 6.2 %collective-permute-start.16 = (bf16[80,896]{1,0:T(8,128)(2,1)S(1)}, bf16[80,896]{1,0:T(8,128)(2,1)S(1)}, u32[]{:S(2)}, u32[]{:S(2)}) collective-permute-start(bf16[80,896]{1,0:T(8,128)(2,1)S(1)} %get-tuple-element.116), channel_id=1, source_target_pairs={{0,64},{8,72},{16,80},{24,88},{32,96},{40,104},{48,112},{56,120},{... | collective-permute-start | bytes 430088 | tf_op jit(solution)/shard_map/ppermute | solution.py:47
  58.7 7.0 %copy-start.2 = (bf16[512,896]{1,0:T(8,128)(2,1)S(1)}, bf16[512,896]{1,0:T(8,128)(2,1)}, u32[]{:S(2)}) copy-start(bf16[512,896]{1,0:T(8,128)(2,1)} %gate_ref.1) | copy-start | bytes 2752516
  69.2 5.1 %collective-permute-start.19 = (bf16[448,512]{1,0:T(8,128)(2,1)S(1)}, bf16[448,512]{1,0:T(8,128)(2,1)S(1)}, u32[]{:S(2)}, u32[]{:S(2)}) collective-permute-start(bf16[448,512]{1,0:T(8,128)(2,1)S(1)} %collective-permute-done.11.refs_4_), channel_id=1, source_target_pairs={{0,8},{8,0},{16,24},{24,16},{32,40},{40,32},{48,56},{56,48},{64,72... | collective-permute-start | bytes 1376264 | tf_op jit(solution)/shard_map/ppermute | solution.py:43
  69.2 5.1 %collective-permute-start.20 = (f32[1,512]{1,0:T(1,128)S(1)}, f32[1,512]{1,0:T(1,128)S(1)}, u32[]{:S(2)}, u32[]{:S(2)}) collective-permute-start(f32[1,512]{1,0:T(1,128)S(1)} %get-tuple-element.133), channel_id=1, source_target_pairs={{0,4},{1,5},{2,6},{3,7},{4,0},{5,1},{6,2},{7,3},{8,12},{9,13},{10,... | collective-permute-start | bytes 6152 | tf_op jit(solution)/shard_map/ppermute | solution.py:51
  74.3 17.5 %copy-start.10 = (f32[896]{0:T(1024)S(1)}, f32[896]{0:T(1024)}, u32[]{:S(2)}) copy-start(f32[896]{0:T(1024)} %param.21) | copy-start | bytes 10756
  76.5 14.5 %collective-permute-start.21 = (bf16[224,512]{1,0:T(8,128)(2,1)S(1)}, bf16[224,512]{1,0:T(8,128)(2,1)S(1)}, u32[]{:S(2)}, u32[]{:S(2)}) collective-permute-start(bf16[224,512]{1,0:T(8,128)(2,1)S(1)} %get-tuple-element.142), channel_id=1, source_target_pairs={{0,48},{8,56},{16,32},{24,40},{32,16},{40,24},{48,0},{56,8},{64,11... | collective-permute-start | bytes 688136 | tf_op jit(solution)/shard_map/ppermute | solution.py:35
  78.1 12.9 %collective-permute-start.22 = (bf16[224,512]{1,0:T(8,128)(2,1)S(1)}, bf16[224,512]{1,0:T(8,128)(2,1)S(1)}, u32[]{:S(2)}, u32[]{:S(2)}) collective-permute-start(bf16[224,512]{1,0:T(8,128)(2,1)S(1)} %get-tuple-element.143), channel_id=1, source_target_pairs={{0,64},{8,72},{16,80},{24,88},{32,96},{40,104},{48,112},{56,120},{... | collective-permute-start | bytes 688136 | tf_op jit(solution)/shard_map/ppermute | solution.py:35
  80.8 10.9 %collective-permute-start.23 = (bf16[224,512]{1,0:T(8,128)(2,1)S(1)}, bf16[224,512]{1,0:T(8,128)(2,1)S(1)}, u32[]{:S(2)}, u32[]{:S(2)}) collective-permute-start(bf16[224,512]{1,0:T(8,128)(2,1)S(1)} %get-tuple-element.144), channel_id=1, source_target_pairs={{0,112},{8,120},{16,96},{24,104},{32,80},{40,88},{48,64},{56,72},{... | collective-permute-start | bytes 688136 | tf_op jit(solution)/shard_map/ppermute | solution.py:35
  82.0 3.6 %collective-permute-start.24 = (f32[1,512]{1,0:T(1,128)S(1)}, f32[1,512]{1,0:T(1,128)S(1)}, u32[]{:S(2)}, u32[]{:S(2)}) collective-permute-start(f32[1,512]{1,0:T(1,128)S(1)} %add.24), channel_id=1, source_target_pairs={{0,1},{1,0},{2,3},{3,2},{4,5},{5,4},{6,7},{7,6},{8,9},{9,8},{10,11... | collective-permute-start | bytes 6152 | tf_op jit(solution)/shard_map/ppermute | solution.py:51
  85.6 5.4 %collective-permute-start.25 = (f32[1,512]{1,0:T(1,128)S(1)}, f32[1,512]{1,0:T(1,128)S(1)}, u32[]{:S(2)}, u32[]{:S(2)}) collective-permute-start(f32[1,512]{1,0:T(1,128)S(1)} %add.25), channel_id=1, source_target_pairs={{0,2},{1,3},{2,0},{3,1},{4,6},{5,7},{6,4},{7,5},{8,10},{9,11},{10,... | collective-permute-start | bytes 6152 | tf_op jit(solution)/shard_map/ppermute | solution.py:51

commit v11 on v8

--- a/solution.py
+++ b/solution.py
@@ -92,9 +92,9 @@
         ks_early, vs_early, acc_in, stats_in, acc, stats_ref, mark, ks, vs, qs = refs
         pieces = [(0, 0, q_in[3], ATT_DIM), (0, 1, (core_keys_3, core_values_3), 0)]
     elif stage == 2:
-        q_in, (near_1, near_core_1, near_2, near_core_2, _), refs = refs[:4], refs[4:9], refs[9:]
+        q_in, (near_both, core_both, _), refs = refs[:4], refs[4:7], refs[7:]
         acc_in, stats_in, acc, stats_ref, mark, ks, vs, qs = refs
-        pieces = [(0, 0, near_1, 0), (0, 1, near_core_1, 0), (1, 0, near_2, 0), (1, 1, near_core_2, 0)]
+        pieces = [(k, other, ref, k * 2 * ATT_DIM) for other, ref in enumerate((near_both, core_both)) for k in range(2)]
     else:
         q_in, (near_3, near_core_3, _), refs = refs[:4], refs[4:7], refs[7:]
         acc_in, stats_in, *o_out, mark, ks, vs, qs, acc, os = refs
@@ -477,7 +477,7 @@
 
     here[1], here[2], near_core[0], all_3, got = tie((here[1], here[2], near_core[0], all_3, got))
     kv = [piece[ATT_DIM:] for piece in here[1:3]]
-    near[1], near[2] = class_swap(kv[0]), class_swap(kv[1])
+    near_both = class_swap(jnp.concatenate(kv, axis=0))
     here[3] = head_swap(all_3, 3)
     total, before, sent = ssm_merge(1, info, got, total, before)
     *kv, sent = tie((*kv, sent))
@@ -494,14 +494,14 @@
     queries = (q_own, here[1], here[2], here[3])
     *state, mark = attend(1, info, *queries, *from_core[3], mark, ks, vs, *state)
 
-    near[1], near[2], mark = tie((near[1], near[2], mark))
-    near_core[1], near_core[2] = core_swap(near[1]), core_swap(near[2])
+    near_both, got, mark = tie((near_both, got, mark))
+    near_core_both = core_swap(near_both)
     kv, got = tie((kv, got))
     near[3] = class_swap(kv)
     total, before, sent = ssm_merge(2, info, got, total, before)
     sent, mark = tie((sent, mark))
     got = block_swap(sent, 8)
-    *state, mark = attend(2, info, *queries, near[1], near_core[1], near[2], near_core[2], mark, *state)
+    *state, mark = attend(2, info, *queries, near_both, near_core_both, mark, *state)
 
     got, mark = tie((got, mark))
     total, before, sent = ssm_merge(3, info, got, total, before)

time: 94.7 us -> 96.2 us (1.016)
  waiting for transfers between devices: 25.9 us -> 29.8 us
  starting transfers between devices: 28.6 us -> 26.2 us
    ppermute x10 -> x9, waiting for transfers between devices: 1.99 us -> 4.94 us  [core_swap(): return lax.ppermute(value, 'ctx', [(i, i ^ 1) for i in range(CTX)])]
    ppermute x5 -> x4, starting transfers between devices: 5.26 us -> 3.4 us  [class_swap(): return lax.ppermute(value, 'ctx', [(i, i ^ 2) for i in range(CTX)])]
    ppermute x2, waiting for transfers between devices: 2.85 us -> 4.35 us  [block_swap(): return lax.ppermute(value, 'ctx', [(i, i ^ step) for i in range(CTX)])]
    ppermute x5 -> x4, waiting for transfers between devices: 5.14 us -> 4.47 us  [class_swap(): return lax.ppermute(value, 'ctx', [(i, i ^ 2) for i in range(CTX)])]
  transfers between devices with their start and end apart: 26 -> 24, of which waited for: 14 -> 16; matrix products, arithmetic and copies ran while one was open for 0% -> 0% of each run, Pallas kernels for 30% -> 30%
where the time goes in v11:
time: 96.2 us; the launch traced here: 96.1 us
  Pallas kernels  37.1 us (39%)
  waiting for transfers between devices  29.8 us (31%)
  starting transfers between devices  26.2 us (27%)
  other arithmetic  1.87 us (2%)
  between operations  0.97 us (1%)
    pallas_call x4, Pallas kernels, attend(): pl.pallas_call(functools.partial(attend_kernel, stage), out_shape=out, in...  22.5 us
    ppermute x6, starting transfers between devices, head_swap(): lax.ppermute(value, 'ctx', [(i, exchanged(i, r)) for i in range(CTX)])  11.6 us
    ppermute x6, waiting for transfers between devices, head_swap(): lax.ppermute(value, 'ctx', [(i, exchanged(i, r)) for i in range(CTX)])  10.6 us
    ppermute x3, starting transfers between devices, step_swap(): return lax.ppermute(value, 'tp', [(i, i ^ step) for i in range(8)])  8.68 us
    ppermute x3, waiting for transfers between devices, step_swap(): return lax.ppermute(value, 'tp', [(i, i ^ step) for i in range(8)])  5.43 us
    ppermute x9, waiting for transfers between devices, core_swap(): return lax.ppermute(value, 'ctx', [(i, i ^ 1) for i in range(CTX)])  4.94 us
    ppermute x4, waiting for transfers between devices, class_swap(): return lax.ppermute(value, 'ctx', [(i, i ^ 2) for i in range(CTX)])  4.47 us
    pallas_call x1, Pallas kernels, pack(): pl.pallas_call(pack_kernel, out_shape=[shape((count, TOK), BF16) for coun...  4.41 us
  transfers between devices with their start and end apart: 24, of which 16 were waited for; matrix products, arithmetic and copies ran while one was open for 0% of the time, Pallas kernels for 30%

profile of v11, /device:TPU:0, one launch (start us, length us, event | category | flops | bytes accessed | tf_op | source)
XLA Modules:
  0.0 96.1 jit_solution(7578849072232014154)
XLA Ops:
  0.7 0.6 pad_add_fusion.info
  1.3 4.4 %shard_map.122 = (bf16[224,512]{1,0:T(8,128)(2,1)}, bf16[448,512]{1,0:T(8,128)(2,1)}, bf16[672,512]{1,0:T(8,128)(2,1)}, bf16[672,512]{1,0:T(8,128)(2,1)}, bf16[672,512]{1,0:T(8,128)(2,1)}) custom-call(s32[4]{0:T(128)} %pad_add_fusion.info, bf16[512,896]{1,0:T(8,128)(2,1)} %q_in.1, bf16[512,896]{1,0:T(8,128)(2,1)} %k_in.1, bf16[512,896]{1,0:T(8,128)(2,1)} %v_in.1), custom_call_target="tpu_custom_call" | custom-call | tf_op jit(solution)/shard_map/pallas_call | solution.py:347
  5.8 0.1 collective-permute-start.3
  5.9 1.7 %collective-permute-start.2 = (bf16[448,512]{1,0:T(8,128)(2,1)}, bf16[448,512]{1,0:T(8,128)(2,1)S(1)}, u32[]{:S(2)}, u32[]{:S(2)}) collective-permute-start(bf16[448,512]{1,0:T(8,128)(2,1)} %get-tuple-element.79.refs_3_), channel_id=1, source_target_pairs={{0,16},{8,24},{16,0},{24,8},{32,48},{40,56},{48,32},{56,40},{64,80... | collective-permute-start | bytes 1376264 | tf_op jit(solution)/shard_map/ppermute | solution.py:38
  7.5 2.1 %collective-permute-start = (bf16[672,512]{1,0:T(8,128)(2,1)}, bf16[672,512]{1,0:T(8,128)(2,1)S(1)}, u32[]{:S(2)}, u32[]{:S(2)}) collective-permute-start(bf16[672,512]{1,0:T(8,128)(2,1)} %get-tuple-element.77), channel_id=1, source_target_pairs={{0,48},{8,56},{16,32},{24,40},{32,16},{40,24},{48,0},{56,8},{64,11... | collective-permute-start | bytes 2064392 | tf_op jit(solution)/shard_map/ppermute | solution.py:34
  9.6 1.6 %collective-permute-start.1 = (bf16[672,512]{1,0:T(8,128)(2,1)}, bf16[672,512]{1,0:T(8,128)(2,1)S(1)}, u32[]{:S(2)}, u32[]{:S(2)}) collective-permute-start(bf16[672,512]{1,0:T(8,128)(2,1)} %get-tuple-element.78), channel_id=1, source_target_pairs={{0,64},{8,72},{16,80},{24,88},{32,96},{40,104},{48,112},{56,120},{... | collective-permute-start | bytes 2064392 | tf_op jit(solution)/shard_map/ppermute | solution.py:34
  11.2 0.0 collective-permute-done.3.refs_4_
  11.2 3.6 %shard_map.123 = (f32[512,896]{1,0:T(8,128)S(1)}, f32[72,896]{1,0:T(8,128)S(1)}, bf16[80,896]{1,0:T(8,128)(2,1)S(1)}, f32[512,14]{1,0:T(8,128)S(1)}) custom-call(bf16[512,896]{1,0:T(8,128)(2,1)S(1)} %copy-done.1, bf16[64,512]{1,0:T(8,128)(2,1)S(1)} %bitcast.12, bf16[64,512]{1,0:T(8,128)(2,1)S(1)} %bitcast.10, f32[14,512]{1,0:T(8,128)S(1)} %bitcast.13, ...), custom_call_target="tpu_custom_call" | custom-call | flops 1000 | bytes 1000 | tf_op jit(solution)/shard_map/pallas_call | solution.py:403
  14.9 0.1 collective-permute-start.4
  15.0 1.4 %collective-permute-done.4.got_ref = bf16[80,896]{1,0:T(8,128)(2,1)S(1)} collective-permute-done((bf16[80,896]{1,0:T(8,128)(2,1)S(1)}, bf16[80,896]{1,0:T(8,128)(2,1)S(1)}, u32[]{:S(2)}, u32[]{:S(2)}) %collective-permute-start.4) | collective-permute-done | bytes 143392 | tf_op jit(solution)/shard_map/ppermute | solution.py:42
  16.4 0.7 shard_map.124
  17.0 2.0 %collective-permute-done.2.refs_7_ = bf16[448,512]{1,0:T(8,128)(2,1)S(1)} collective-permute-done((bf16[448,512]{1,0:T(8,128)(2,1)}, bf16[448,512]{1,0:T(8,128)(2,1)S(1)}, u32[]{:S(2)}, u32[]{:S(2)}) %collective-permute-start.2) | collective-permute-done | bytes 458784 | tf_op jit(solution)/shard_map/ppermute | solution.py:38
  19.0 0.0 collective-permute-start.5
  19.0 1.6 %collective-permute-start.6 = (bf16[80,896]{1,0:T(8,128)(2,1)S(1)}, bf16[80,896]{1,0:T(8,128)(2,1)S(1)}, u32[]{:S(2)}, u32[]{:S(2)}) collective-permute-start(bf16[80,896]{1,0:T(8,128)(2,1)S(1)} %get-tuple-element.83), channel_id=1, source_target_pairs={{0,16},{8,24},{16,0},{24,8},{32,48},{40,56},{48,32},{56,40},{64,80... | collective-permute-start | bytes 430088 | tf_op jit(solution)/shard_map/ppermute | solution.py:38
  20.6 5.8 %collective-permute-done.refs_1_ = bf16[672,512]{1,0:T(8,128)(2,1)S(1)} collective-permute-done((bf16[672,512]{1,0:T(8,128)(2,1)}, bf16[672,512]{1,0:T(8,128)(2,1)S(1)}, u32[]{:S(2)}, u32[]{:S(2)}) %collective-permute-start) | collective-permute-done | bytes 688160 | tf_op jit(solution)/shard_map/ppermute | solution.py:34
  26.4 0.6 collective-permute-done.1.refs_2_
  27.0 0.0 collective-permute-done.6.got_ref
  27.0 0.0 collective-permute-done.5.refs_8_
  27.1 2.6 %collective-permute-start.7 = (bf16[672,512]{1,0:T(8,128)(2,1)S(1)}, bf16[672,512]{1,0:T(8,128)(2,1)S(1)}, u32[]{:S(2)}, u32[]{:S(2)}) collective-permute-start(bf16[672,512]{1,0:T(8,128)(2,1)S(1)} %copy-done.11), channel_id=1, source_target_pairs={{0,112},{8,120},{16,96},{24,104},{32,80},{40,88},{48,64},{56,72},{... | collective-permute-start | bytes 2064392 | tf_op jit(solution)/shard_map/ppermute | solution.py:34
  29.6 0.7 shard_map.125
  30.4 0.1 collective-permute-start.8
  30.5 0.5 collective-permute-start.9
  31.0 0.1 pad_maximum_fusion
  31.1 0.1 collective-permute-start.10
  31.2 1.1 %collective-permute-done.8.refs_5_ = bf16[448,512]{1,0:T(8,128)(2,1)S(1)} collective-permute-done((bf16[448,512]{1,0:T(8,128)(2,1)S(1)}, bf16[448,512]{1,0:T(8,128)(2,1)S(1)}, u32[]{:S(2)}, u32[]{:S(2)}) %collective-permute-start.8) | collective-permute-done | bytes 458784 | tf_op jit(solution)/shard_map/ppermute | solution.py:42
  32.3 0.7 collective-permute-done.9.refs_6_
  33.0 9.2 %shard_map.126 = (f32[4,224,512]{2,1,0:T(8,128)S(1)}, f32[4,16,512]{2,1,0:T(8,128)S(1)}, bf16[4,1024,224]{2,1,0:T(8,128)(2,1)S(1)}, bf16[4,224,1024]{2,1,0:T(8,128)(2,1)S(1)}, f32[8,128]{1,0:T(8,128)S(1)}) custom-call(s32[4]{0:T(128)S(1)} %copy-done.6, bf16[224,512]{1,0:T(8,128)(2,1)S(1)} %copy-done, bf16[672,512]{1,0:T(8,128)(2,1)S(1)} %collective-permute-done.refs_1_, ...), custom_call_target="tpu_custom_call" | custom-call | flops 1000 | bytes 1000 | tf_op jit(solution)/shard_map/pallas_call | solution.py:377
  42.2 3.4 %collective-permute-done.7.refs_3_ = bf16[672,512]{1,0:T(8,128)(2,1)S(1)} collective-permute-done((bf16[672,512]{1,0:T(8,128)(2,1)S(1)}, bf16[672,512]{1,0:T(8,128)(2,1)S(1)}, u32[]{:S(2)}, u32[]{:S(2)}) %collective-permute-start.7) | collective-permute-done | bytes 688160 | tf_op jit(solution)/shard_map/ppermute | solution.py:34
  45.6 0.1 collective-permute-start.12
  45.7 0.5 collective-permute-start.13
  46.2 0.7 collective-permute-start.11
  46.9 0.3 collective-permute-done.12.refs_4_
  47.2 0.3 collective-permute-done.13.refs_5_
  47.5 5.9 %shard_map.127 = (f32[4,224,512]{2,1,0:T(8,128)S(1)}, f32[4,16,512]{2,1,0:T(8,128)S(1)}, f32[8,128]{1,0:T(8,128)S(1)}) custom-call(s32[4]{0:T(128)S(1)} %copy-done.6, bf16[224,512]{1,0:T(8,128)(2,1)S(1)} %copy-done, bf16[672,512]{1,0:T(8,128)(2,1)S(1)} %collective-permute-done.refs_1_, bf16[672,512]{1,0:T(8,128)(2,1)S(1)} %collective-permute-done.1.refs_2_, ...), custom_call_target="tpu_custom_call" | custom-call | flops 1000 | bytes 1000 | tf_op jit(solution)/shard_map/pallas_call | solution.py:377
  53.4 4.3 %collective-permute-done.11.got_ref = bf16[80,896]{1,0:T(8,128)(2,1)S(1)} collective-permute-done((bf16[80,896]{1,0:T(8,128)(2,1)S(1)}, bf16[80,896]{1,0:T(8,128)(2,1)S(1)}, u32[]{:S(2)}, u32[]{:S(2)}) %collective-permute-start.11) | collective-permute-done | bytes 143392 | tf_op jit(solution)/shard_map/ppermute | solution.py:46
  57.7 0.0 collective-permute-done.10.refs_4_
  57.7 0.0 collective-permute-start.16
  57.8 0.1 collective-permute-start.14
  57.9 0.7 shard_map.128
  58.5 0.5 collective-permute-start.15
  59.1 1.2 %collective-permute-done.16.refs_5_ = bf16[896,512]{1,0:T(8,128)(2,1)S(1)} collective-permute-done((bf16[896,512]{1,0:T(8,128)(2,1)S(1)}, bf16[896,512]{1,0:T(8,128)(2,1)S(1)}, u32[]{:S(2)}, u32[]{:S(2)}) %collective-permute-start.16) | collective-permute-done | bytes 917536 | tf_op jit(solution)/shard_map/ppermute | solution.py:42
  60.2 5.4 %shard_map.129 = (f32[4,224,512]{2,1,0:T(8,128)S(1)}, f32[4,16,512]{2,1,0:T(8,128)S(1)}, f32[8,128]{1,0:T(8,128)S(1)}) custom-call(s32[4]{0:T(128)S(1)} %copy-done.6, bf16[224,512]{1,0:T(8,128)(2,1)S(1)} %copy-done, bf16[672,512]{1,0:T(8,128)(2,1)S(1)} %collective-permute-done.refs_1_, bf16[672,512]{1,0:T(8,128)(2,1)S(1)} %collective-permute-done.1.refs_2_, ...), custom_call_target="tpu_custom_call" | custom-call | flops 1000 | bytes 1000 | tf_op jit(solution)/shard_map/pallas_call | solution.py:377
  65.6 0.0 collective-permute-done.15.got_ref
  65.6 1.4 %shard_map.130 = (f32[72,896]{1,0:T(8,128)}, f32[72,896]{1,0:T(8,128)S(1)}, bf16[80,896]{1,0:T(8,128)(2,1)}) custom-call(s32[4]{0:T(128)S(1)} %copy-done.6, bf16[80,896]{1,0:T(8,128)(2,1)S(1)} %collective-permute-done.15.got_ref, f32[72,896]{1,0:T(8,128)S(1)} %get-tuple-element.124.total_ref, f32[72,896]{1,0:T(8,128)S(1)} %get-tuple-element.125.before_ref), custom_call_target="tpu_custom_call" | custom-call | flops 1000 | bytes 1000 | tf_op jit(solution)/shard_map/pallas_call | solution.py:420
  67.0 1.3 %shard_map.131 = (f32[512,896]{1,0:T(8,128)S(1)}, f32[1,512]{1,0:T(1,128)S(1)}) custom-call(f32[72,896]{1,0:T(8,128)S(1)} %get-tuple-element.126.state_ref, f32[512,896]{1,0:T(8,128)S(1)} %get-tuple-element.127.mixed_ref, f32[512,14]{1,0:T(8,128)S(1)} %get-tuple-element.128.cum_ref, bf16[64,512]{1,0:T(8,128)(2,1)S(1)} %bitcast.11, bf16[512,896]{1,0:T(8,128)(2,1)S(1)} %copy-done.2), custom_call_target="tpu_custom_call" | custom-call | flops 1000 | bytes 1000 | tf_op jit(solution)/shard_map/pallas_call | solution.py:432
  68.3 2.5 %collective-permute-done.14.refs_4_ = bf16[448,512]{1,0:T(8,128)(2,1)S(1)} collective-permute-done((bf16[448,512]{1,0:T(8,128)(2,1)S(1)}, bf16[448,512]{1,0:T(8,128)(2,1)S(1)}, u32[]{:S(2)}, u32[]{:S(2)}) %collective-permute-start.14) | collective-permute-done | bytes 458784 | tf_op jit(solution)/shard_map/ppermute | solution.py:38
  70.8 0.0 collective-permute-start.17
  70.8 2.9 %collective-permute-start.18 = (f32[1,512]{1,0:T(1,128)S(1)}, f32[1,512]{1,0:T(1,128)S(1)}, u32[]{:S(2)}, u32[]{:S(2)}) collective-permute-start(f32[1,512]{1,0:T(1,128)S(1)} %get-tuple-element.133), channel_id=1, source_target_pairs={{0,4},{1,5},{2,6},{3,7},{4,0},{5,1},{6,2},{7,3},{8,12},{9,13},{10,... | collective-permute-start | bytes 6152 | tf_op jit(solution)/shard_map/ppermute | solution.py:50
  73.7 2.2 %collective-permute-done.18 = f32[1,512]{1,0:T(1,128)S(1)} collective-permute-done((f32[1,512]{1,0:T(1,128)S(1)}, f32[1,512]{1,0:T(1,128)S(1)}, u32[]{:S(2)}, u32[]{:S(2)}) %collective-permute-start.18) | collective-permute-done | bytes 2080 | tf_op jit(solution)/shard_map/ppermute | solution.py:50
  75.9 0.0 collective-permute-done.17.refs_5_
  75.9 0.0 copy-start.10
  75.9 2.1 %shard_map.132 = (bf16[224,512]{1,0:T(8,128)(2,1)S(1)}, bf16[224,512]{1,0:T(8,128)(2,1)S(1)}, bf16[224,512]{1,0:T(8,128)(2,1)S(1)}, bf16[224,512]{1,0:T(8,128)(2,1)S(1)}, f32[8,128]{1,0:T(8,128)S(1)}) custom-call(s32[4]{0:T(128)S(1)} %copy-done.6, bf16[224,512]{1,0:T(8,128)(2,1)S(1)} %copy-done, bf16[672,512]{1,0:T(8,128)(2,1)S(1)} %collective-permute-done.refs_1_, ...), custom_call_target="tpu_custom_call" | custom-call | flops 1000 | bytes 1000 | tf_op jit(solution)/shard_map/pallas_call | solution.py:377
  78.0 1.6 %collective-permute-start.19 = (bf16[224,512]{1,0:T(8,128)(2,1)S(1)}, bf16[224,512]{1,0:T(8,128)(2,1)S(1)}, u32[]{:S(2)}, u32[]{:S(2)}) collective-permute-start(bf16[224,512]{1,0:T(8,128)(2,1)S(1)} %get-tuple-element.142), channel_id=1, source_target_pairs={{0,48},{8,56},{16,32},{24,40},{32,16},{40,24},{48,0},{56,8},{64,11... | collective-permute-start | bytes 688136 | tf_op jit(solution)/shard_map/ppermute | solution.py:34
  79.6 2.6 %collective-permute-start.20 = (bf16[224,512]{1,0:T(8,128)(2,1)S(1)}, bf16[224,512]{1,0:T(8,128)(2,1)S(1)}, u32[]{:S(2)}, u32[]{:S(2)}) collective-permute-start(bf16[224,512]{1,0:T(8,128)(2,1)S(1)} %get-tuple-element.143), channel_id=1, source_target_pairs={{0,64},{8,72},{16,80},{24,88},{32,96},{40,104},{48,112},{56,120},{... | collective-permute-start | bytes 688136 | tf_op jit(solution)/shard_map/ppermute | solution.py:34
  82.2 1.2 %collective-permute-start.21 = (bf16[224,512]{1,0:T(8,128)(2,1)S(1)}, bf16[224,512]{1,0:T(8,128)(2,1)S(1)}, u32[]{:S(2)}, u32[]{:S(2)}) collective-permute-start(bf16[224,512]{1,0:T(8,128)(2,1)S(1)} %get-tuple-element.144), channel_id=1, source_target_pairs={{0,112},{8,120},{16,96},{24,104},{32,80},{40,88},{48,64},{56,72},{... | collective-permute-start | bytes 688136 | tf_op jit(solution)/shard_map/ppermute | solution.py:34
  83.3 1.9 %collective-permute-start.22 = (f32[1,512]{1,0:T(1,128)S(1)}, f32[1,512]{1,0:T(1,128)S(1)}, u32[]{:S(2)}, u32[]{:S(2)}) collective-permute-start(f32[1,512]{1,0:T(1,128)S(1)} %add.24), channel_id=1, source_target_pairs={{0,1},{1,0},{2,3},{3,2},{4,5},{5,4},{6,7},{7,6},{8,9},{9,8},{10,11... | collective-permute-start | bytes 6152 | tf_op jit(solution)/shard_map/ppermute | solution.py:50
  85.3 1.7 %collective-permute-done.22 = f32[1,512]{1,0:T(1,128)S(1)} collective-permute-done((f32[1,512]{1,0:T(1,128)S(1)}, f32[1,512]{1,0:T(1,128)S(1)}, u32[]{:S(2)}, u32[]{:S(2)}) %collective-permute-start.22) | collective-permute-done | bytes 2080 | tf_op jit(solution)/shard_map/ppermute | solution.py:50
  86.9 3.9 %collective-permute-start.23 = (f32[1,512]{1,0:T(1,128)S(1)}, f32[1,512]{1,0:T(1,128)S(1)}, u32[]{:S(2)}, u32[]{:S(2)}) collective-permute-start(f32[1,512]{1,0:T(1,128)S(1)} %add.25), channel_id=1, source_target_pairs={{0,2},{1,3},{2,0},{3,1},{4,6},{5,7},{6,4},{7,5},{8,10},{9,11},{10,... | collective-permute-start | bytes 6152 | tf_op jit(solution)/shard_map/ppermute | solution.py:50
  90.8 1.6 %collective-permute-done.23 = f32[1,512]{1,0:T(1,128)S(1)} collective-permute-done((f32[1,512]{1,0:T(1,128)S(1)}, f32[1,512]{1,0:T(1,128)S(1)}, u32[]{:S(2)}, u32[]{:S(2)}) %collective-permute-start.23) | collective-permute-done | bytes 2080 | tf_op jit(solution)/shard_map/ppermute | solution.py:50
  92.4 0.0 collective-permute-done.19.refs_1_
  92.4 0.0 collective-permute-done.20.refs_2_
  92.4 0.7 collective-permute-done.21.refs_3_
  93.1 1.1 %multiply_convert_fusion = bf16[512,896]{1,0:T(8,128)(2,1)} fusion(f32[512,896]{1,0:T(8,128)S(1)} %get-tuple-element.150, f32[896]{0:T(1024)S(1)} %copy-done.10, f32[512]{0:T(512)S(1)} %bitcast.16), kind=kLoop, calls=%fused_computation | loop fusion | flops 1376256 | bytes 2758144 | tf_op jit(solution)/shard_map/convert_element_type | solution.py:520
  94.3 1.8 %shard_map.133 = bf16[512,896]{1,0:T(8,128)(2,1)} custom-call(s32[4]{0:T(128)S(1)} %copy-done.6, f32[8,128]{1,0:T(8,128)S(1)} %get-tuple-element.140._, bf16[224,512]{1,0:T(8,128)(2,1)S(1)} %get-tuple-element.146.refs_0_, bf16[224,512]{1,0:T(8,128)(2,1)S(1)} %collective-permute-done.19.refs_1_, bf16[224,512]{1,0:T(8,128)(2,1)S(1)} %collective-permute-done.20.refs_2_, ...), custom_call_target="tpu_custom_call" | custom-call | tf_op jit(solution)/shard_map/pallas_call | solution.py:390
  (32 shorter events, 0.2 us)
Async XLA Ops:
  0.6 10.6 %copy-start.1 = (bf16[512,896]{1,0:T(8,128)(2,1)S(1)}, bf16[512,896]{1,0:T(8,128)(2,1)}, u32[]{:S(2)}) copy-start(bf16[512,896]{1,0:T(8,128)(2,1)} %x_ref) | copy-start | bytes 2752516
  0.6 10.6 %copy-start.4 = (bf16[512,64]{0,1:T(8,128)(2,1)S(1)}, bf16[512,64]{0,1:T(8,128)(2,1)}, u32[]{:S(2)}) copy-start(bf16[512,64]{0,1:T(8,128)(2,1)} %param.17) | copy-start | bytes 196612
  0.7 10.6 %copy-start.5 = (bf16[512,64]{0,1:T(8,128)(2,1)S(1)}, bf16[512,64]{0,1:T(8,128)(2,1)}, u32[]{:S(2)}) copy-start(bf16[512,64]{0,1:T(8,128)(2,1)} %param.16) | copy-start | bytes 196612
  0.7 10.6 %copy-start.7 = (f32[512,14]{0,1:T(8,128)S(1)}, f32[512,14]{0,1:T(8,128)}, u32[]{:S(2)}) copy-start(f32[512,14]{0,1:T(8,128)} %param.18) | copy-start | bytes 86020
  0.7 10.6 %copy-start.8 = (f32[14]{0:T(128)S(1)}, f32[14]{0:T(128)}, u32[]{:S(2)}) copy-start(f32[14]{0:T(128)} %param.19) | copy-start | bytes 172
  0.7 10.6 %copy-start.9 = (f32[14]{0:T(128)S(1)}, f32[14]{0:T(128)}, u32[]{:S(2)}) copy-start(f32[14]{0:T(128)} %param.20) | copy-start | bytes 172
  1.3 15.0 %copy-start.6 = (s32[4]{0:T(128)S(1)}, s32[4]{0:T(128)}, u32[]{:S(2)}) copy-start(s32[4]{0:T(128)} %pad_add_fusion.info) | copy-start | bytes 52
  5.8 21.3 %copy-start.11 = (bf16[672,512]{1,0:T(8,128)(2,1)S(1)}, bf16[672,512]{1,0:T(8,128)(2,1)}, u32[]{:S(2)}) copy-start(bf16[672,512]{1,0:T(8,128)(2,1)} %get-tuple-element.86) | copy-start | bytes 2064388
  5.8 5.4 %collective-permute-start.3 = (bf16[448,512]{1,0:T(8,128)(2,1)}, bf16[448,512]{1,0:T(8,128)(2,1)S(1)}, u32[]{:S(2)}, u32[]{:S(2)}) collective-permute-start(bf16[448,512]{1,0:T(8,128)(2,1)} %get-tuple-element.79.refs_3_), channel_id=1, source_target_pairs={{0,8},{8,0},{16,24},{24,16},{32,40},{40,32},{48,56},{56,48},{64,72... | collective-permute-start | bytes 1376264 | tf_op jit(solution)/shard_map/ppermute | solution.py:42
  5.9 13.1 %collective-permute-start.2 = (bf16[448,512]{1,0:T(8,128)(2,1)}, bf16[448,512]{1,0:T(8,128)(2,1)S(1)}, u32[]{:S(2)}, u32[]{:S(2)}) collective-permute-start(bf16[448,512]{1,0:T(8,128)(2,1)} %get-tuple-element.79.refs_3_), channel_id=1, source_target_pairs={{0,16},{8,24},{16,0},{24,8},{32,48},{40,56},{48,32},{56,40},{64,80... | collective-permute-start | bytes 1376264 | tf_op jit(solution)/shard_map/ppermute | solution.py:38
  7.5 18.9 %collective-permute-start = (bf16[672,512]{1,0:T(8,128)(2,1)}, bf16[672,512]{1,0:T(8,128)(2,1)S(1)}, u32[]{:S(2)}, u32[]{:S(2)}) collective-permute-start(bf16[672,512]{1,0:T(8,128)(2,1)} %get-tuple-element.77), channel_id=1, source_target_pairs={{0,48},{8,56},{16,32},{24,40},{32,16},{40,24},{48,0},{56,8},{64,11... | collective-permute-start | bytes 2064392 | tf_op jit(solution)/shard_map/ppermute | solution.py:34
  9.6 17.4 %collective-permute-start.1 = (bf16[672,512]{1,0:T(8,128)(2,1)}, bf16[672,512]{1,0:T(8,128)(2,1)S(1)}, u32[]{:S(2)}, u32[]{:S(2)}) collective-permute-start(bf16[672,512]{1,0:T(8,128)(2,1)} %get-tuple-element.78), channel_id=1, source_target_pairs={{0,64},{8,72},{16,80},{24,88},{32,96},{40,104},{48,112},{56,120},{... | collective-permute-start | bytes 2064392 | tf_op jit(solution)/shard_map/ppermute | solution.py:34
  14.9 1.4 %collective-permute-start.4 = (bf16[80,896]{1,0:T(8,128)(2,1)S(1)}, bf16[80,896]{1,0:T(8,128)(2,1)S(1)}, u32[]{:S(2)}, u32[]{:S(2)}) collective-permute-start(bf16[80,896]{1,0:T(8,128)(2,1)S(1)} %get-tuple-element.81), channel_id=1, source_target_pairs={{0,8},{8,0},{16,24},{24,16},{32,40},{40,32},{48,56},{56,48},{64,72... | collective-permute-start | bytes 430088 | tf_op jit(solution)/shard_map/ppermute | solution.py:42
  19.0 8.0 %collective-permute-start.5 = (bf16[448,512]{1,0:T(8,128)(2,1)S(1)}, bf16[448,512]{1,0:T(8,128)(2,1)S(1)}, u32[]{:S(2)}, u32[]{:S(2)}) collective-permute-start(bf16[448,512]{1,0:T(8,128)(2,1)S(1)} %collective-permute-done.2.refs_7_), channel_id=1, source_target_pairs={{0,8},{8,0},{16,24},{24,16},{32,40},{40,32},{48,56},{56,48},{64,72... | collective-permute-start | bytes 1376264 | tf_op jit(solution)/shard_map/ppermute | solution.py:42
  19.0 8.0 %collective-permute-start.6 = (bf16[80,896]{1,0:T(8,128)(2,1)S(1)}, bf16[80,896]{1,0:T(8,128)(2,1)S(1)}, u32[]{:S(2)}, u32[]{:S(2)}) collective-permute-start(bf16[80,896]{1,0:T(8,128)(2,1)S(1)} %get-tuple-element.83), channel_id=1, source_target_pairs={{0,16},{8,24},{16,0},{24,8},{32,48},{40,56},{48,32},{56,40},{64,80... | collective-permute-start | bytes 430088 | tf_op jit(solution)/shard_map/ppermute | solution.py:38
  27.1 18.5 %collective-permute-start.7 = (bf16[672,512]{1,0:T(8,128)(2,1)S(1)}, bf16[672,512]{1,0:T(8,128)(2,1)S(1)}, u32[]{:S(2)}, u32[]{:S(2)}) collective-permute-start(bf16[672,512]{1,0:T(8,128)(2,1)S(1)} %copy-done.11), channel_id=1, source_target_pairs={{0,112},{8,120},{16,96},{24,104},{32,80},{40,88},{48,64},{56,72},{... | collective-permute-start | bytes 2064392 | tf_op jit(solution)/shard_map/ppermute | solution.py:34
  30.3 2.7 %copy-start = (bf16[224,512]{1,0:T(8,128)(2,1)S(1)}, bf16[224,512]{1,0:T(8,128)(2,1)}, u32[]{:S(2)}) copy-start(bf16[224,512]{1,0:T(8,128)(2,1)} %get-tuple-element.87.refs_0_) | copy-start | bytes 688132
  30.3 2.6 %copy-start.3 = (bf16[448,512]{1,0:T(8,128)(2,1)S(1)}, bf16[448,512]{1,0:T(8,128)(2,1)}, u32[]{:S(2)}) copy-start(bf16[448,512]{1,0:T(8,128)(2,1)} %get-tuple-element.79.refs_3_) | copy-start | bytes 1376260
  30.4 1.9 %collective-permute-start.8 = (bf16[448,512]{1,0:T(8,128)(2,1)S(1)}, bf16[448,512]{1,0:T(8,128)(2,1)S(1)}, u32[]{:S(2)}, u32[]{:S(2)}) collective-permute-start(bf16[448,512]{1,0:T(8,128)(2,1)S(1)} %slice.15), channel_id=1, source_target_pairs={{0,8},{8,0},{16,24},{24,16},{32,40},{40,32},{48,56},{56,48},{64,72... | collective-permute-start | bytes 1376264 | tf_op jit(solution)/shard_map/ppermute | solution.py:42
  30.5 2.5 %collective-permute-start.9 = (bf16[448,512]{1,0:T(8,128)(2,1)S(1)}, bf16[448,512]{1,0:T(8,128)(2,1)S(1)}, u32[]{:S(2)}, u32[]{:S(2)}) collective-permute-start(bf16[448,512]{1,0:T(8,128)(2,1)S(1)} %slice.16), channel_id=1, source_target_pairs={{0,8},{8,0},{16,24},{24,16},{32,40},{40,32},{48,56},{56,48},{64,72... | collective-permute-start | bytes 1376264 | tf_op jit(solution)/shard_map/ppermute | solution.py:42
  31.1 26.7 %collective-permute-start.10 = (bf16[896,512]{1,0:T(8,128)(2,1)S(1)}, bf16[896,512]{1,0:T(8,128)(2,1)S(1)}, u32[]{:S(2)}, u32[]{:S(2)}) collective-permute-start(bf16[896,512]{1,0:T(8,128)(2,1)S(1)} %pad_maximum_fusion), channel_id=1, source_target_pairs={{0,16},{8,24},{16,0},{24,8},{32,48},{40,56},{48,32},{56,40},{64,80... | collective-permute-start | bytes 2752520 | tf_op jit(solution)/shard_map/ppermute | solution.py:38
  45.6 1.6 %collective-permute-start.12 = (bf16[224,512]{1,0:T(8,128)(2,1)S(1)}, bf16[224,512]{1,0:T(8,128)(2,1)S(1)}, u32[]{:S(2)}, u32[]{:S(2)}) collective-permute-start(bf16[224,512]{1,0:T(8,128)(2,1)S(1)} %get-tuple-element.153), channel_id=1, source_target_pairs={{0,8},{8,0},{16,24},{24,16},{32,40},{40,32},{48,56},{56,48},{64,72... | collective-permute-start | bytes 688136 | tf_op jit(solution)/shard_map/ppermute | solution.py:42
  45.7 1.8 %collective-permute-start.13 = (bf16[224,512]{1,0:T(8,128)(2,1)S(1)}, bf16[224,512]{1,0:T(8,128)(2,1)S(1)}, u32[]{:S(2)}, u32[]{:S(2)}) collective-permute-start(bf16[224,512]{1,0:T(8,128)(2,1)S(1)} %get-tuple-element.152), channel_id=1, source_target_pairs={{0,8},{8,0},{16,24},{24,16},{32,40},{40,32},{48,56},{56,48},{64,72... | collective-permute-start | bytes 688136 | tf_op jit(solution)/shard_map/ppermute | solution.py:42
  46.2 11.5 %collective-permute-start.11 = (bf16[80,896]{1,0:T(8,128)(2,1)S(1)}, bf16[80,896]{1,0:T(8,128)(2,1)S(1)}, u32[]{:S(2)}, u32[]{:S(2)}) collective-permute-start(bf16[80,896]{1,0:T(8,128)(2,1)S(1)} %get-tuple-element.103), channel_id=1, source_target_pairs={{0,32},{8,40},{16,48},{24,56},{32,0},{40,8},{48,16},{56,24},{64,96... | collective-permute-start | bytes 430088 | tf_op jit(solution)/shard_map/ppermute | solution.py:46
  57.7 2.5 %collective-permute-start.16 = (bf16[896,512]{1,0:T(8,128)(2,1)S(1)}, bf16[896,512]{1,0:T(8,128)(2,1)S(1)}, u32[]{:S(2)}, u32[]{:S(2)}) collective-permute-start(bf16[896,512]{1,0:T(8,128)(2,1)S(1)} %collective-permute-done.10.refs_4_), channel_id=1, source_target_pairs={{0,8},{8,0},{16,24},{24,16},{32,40},{40,32},{48,56},{56,48},{64,72... | collective-permute-start | bytes 2752520 | tf_op jit(solution)/shard_map/ppermute | solution.py:42
  57.8 13.0 %collective-permute-start.14 = (bf16[448,512]{1,0:T(8,128)(2,1)S(1)}, bf16[448,512]{1,0:T(8,128)(2,1)S(1)}, u32[]{:S(2)}, u32[]{:S(2)}) collective-permute-start(bf16[448,512]{1,0:T(8,128)(2,1)S(1)} %slice.17), channel_id=1, source_target_pairs={{0,16},{8,24},{16,0},{24,8},{32,48},{40,56},{48,32},{56,40},{64,80... | collective-permute-start | bytes 1376264 | tf_op jit(solution)/shard_map/ppermute | solution.py:38
  58.5 7.1 %collective-permute-start.15 = (bf16[80,896]{1,0:T(8,128)(2,1)S(1)}, bf16[80,896]{1,0:T(8,128)(2,1)S(1)}, u32[]{:S(2)}, u32[]{:S(2)}) collective-permute-start(bf16[80,896]{1,0:T(8,128)(2,1)S(1)} %get-tuple-element.117), channel_id=1, source_target_pairs={{0,64},{8,72},{16,80},{24,88},{32,96},{40,104},{48,112},{56,120},{... | collective-permute-start | bytes 430088 | tf_op jit(solution)/shard_map/ppermute | solution.py:46
  60.2 6.8 %copy-start.2 = (bf16[512,896]{1,0:T(8,128)(2,1)S(1)}, bf16[512,896]{1,0:T(8,128)(2,1)}, u32[]{:S(2)}) copy-start(bf16[512,896]{1,0:T(8,128)(2,1)} %gate_ref.1) | copy-start | bytes 2752516
  70.8 5.1 %collective-permute-start.17 = (bf16[448,512]{1,0:T(8,128)(2,1)S(1)}, bf16[448,512]{1,0:T(8,128)(2,1)S(1)}, u32[]{:S(2)}, u32[]{:S(2)}) collective-permute-start(bf16[448,512]{1,0:T(8,128)(2,1)S(1)} %collective-permute-done.14.refs_4_), channel_id=1, source_target_pairs={{0,8},{8,0},{16,24},{24,16},{32,40},{40,32},{48,56},{56,48},{64,72... | collective-permute-start | bytes 1376264 | tf_op jit(solution)/shard_map/ppermute | solution.py:42
  70.8 5.1 %collective-permute-start.18 = (f32[1,512]{1,0:T(1,128)S(1)}, f32[1,512]{1,0:T(1,128)S(1)}, u32[]{:S(2)}, u32[]{:S(2)}) collective-permute-start(f32[1,512]{1,0:T(1,128)S(1)} %get-tuple-element.133), channel_id=1, source_target_pairs={{0,4},{1,5},{2,6},{3,7},{4,0},{5,1},{6,2},{7,3},{8,12},{9,13},{10,... | collective-permute-start | bytes 6152 | tf_op jit(solution)/shard_map/ppermute | solution.py:50
  75.9 17.2 %copy-start.10 = (f32[896]{0:T(1024)S(1)}, f32[896]{0:T(1024)}, u32[]{:S(2)}) copy-start(f32[896]{0:T(1024)} %param.21) | copy-start | bytes 10756
  78.0 14.3 %collective-permute-start.19 = (bf16[224,512]{1,0:T(8,128)(2,1)S(1)}, bf16[224,512]{1,0:T(8,128)(2,1)S(1)}, u32[]{:S(2)}, u32[]{:S(2)}) collective-permute-start(bf16[224,512]{1,0:T(8,128)(2,1)S(1)} %get-tuple-element.142), channel_id=1, source_target_pairs={{0,48},{8,56},{16,32},{24,40},{32,16},{40,24},{48,0},{56,8},{64,11... | collective-permute-start | bytes 688136 | tf_op jit(solution)/shard_map/ppermute | solution.py:34
  79.6 12.8 %collective-permute-start.20 = (bf16[224,512]{1,0:T(8,128)(2,1)S(1)}, bf16[224,512]{1,0:T(8,128)(2,1)S(1)}, u32[]{:S(2)}, u32[]{:S(2)}) collective-permute-start(bf16[224,512]{1,0:T(8,128)(2,1)S(1)} %get-tuple-element.143), channel_id=1, source_target_pairs={{0,64},{8,72},{16,80},{24,88},{32,96},{40,104},{48,112},{56,120},{... | collective-permute-start | bytes 688136 | tf_op jit(solution)/shard_map/ppermute | solution.py:34
  82.2 10.9 %collective-permute-start.21 = (bf16[224,512]{1,0:T(8,128)(2,1)S(1)}, bf16[224,512]{1,0:T(8,128)(2,1)S(1)}, u32[]{:S(2)}, u32[]{:S(2)}) collective-permute-start(bf16[224,512]{1,0:T(8,128)(2,1)S(1)} %get-tuple-element.144), channel_id=1, source_target_pairs={{0,112},{8,120},{16,96},{24,104},{32,80},{40,88},{48,64},{56,72},{... | collective-permute-start | bytes 688136 | tf_op jit(solution)/shard_map/ppermute | solution.py:34
  83.3 3.6 %collective-permute-start.22 = (f32[1,512]{1,0:T(1,128)S(1)}, f32[1,512]{1,0:T(1,128)S(1)}, u32[]{:S(2)}, u32[]{:S(2)}) collective-permute-start(f32[1,512]{1,0:T(1,128)S(1)} %add.24), channel_id=1, source_target_pairs={{0,1},{1,0},{2,3},{3,2},{4,5},{5,4},{6,7},{7,6},{8,9},{9,8},{10,11... | collective-permute-start | bytes 6152 | tf_op jit(solution)/shard_map/ppermute | solution.py:50
  86.9 5.4 %collective-permute-start.23 = (f32[1,512]{1,0:T(1,128)S(1)}, f32[1,512]{1,0:T(1,128)S(1)}, u32[]{:S(2)}, u32[]{:S(2)}) collective-permute-start(f32[1,512]{1,0:T(1,128)S(1)} %add.25), channel_id=1, source_target_pairs={{0,2},{1,3},{2,0},{3,1},{4,6},{5,7},{6,4},{7,5},{8,10},{9,11},{10,... | collective-permute-start | bytes 6152 | tf_op jit(solution)/shard_map/ppermute | solution.py:50
